TPU v7x, 32 devices: a whole 2x2x4 slice. The times are simulated.
32 devices in a mesh: gx: 8 (over z, y), gy: 4 (over x, core).
Axes of the slice: x: 2, y: 2, z: 4, core: 2. Of those that a mesh axis runs over, the one named last changes fastest.
Arguments:
- atmospheric_constituents: float32 [5, 72, 32, 1024], P(None, None, 'gy', 'gx'), may hold values from 0.001 to 2
- thermal_ratio: float32 [72, 32, 1024], P(None, 'gy', 'gx'), may hold values from 0.5 to 1.5
- flow_velocity: float32 [2, 72, 32, 1024], P(None, None, 'gy', 'gx'), may hold values from -4 to 4
- solar_elevation_factor: float32 [32, 1024], P('gy', 'gx'), may hold values from 0.1 to 1
- ground_reflectivity: float32 [32, 1024], P('gy', 'gx'), may hold values from 0.05 to 0.6
- sunlit_indicator: int32 [32, 1024], P('gy', 'gx'), may hold values from 0 to 1, as said below
- molecular_optics_lookup: float32 [3, 112, 72], replicated, may hold values from 0.0001 to 0.05
- condensate_optics_lookup: float32 [7, 112], replicated, may hold values from 0.1 to 0.9
Outputs:
- radiative_warming_rate: float32 [72, 32, 1024], P(None, 'gy', 'gx')
- advected_thermal_ratio: float32 [72, 32, 1024], P(None, 'gy', 'gx')
Inputs may be any that keep to these rules, and one draw needn't show every extreme that they name: `sunlit_indicator`: A column's flag and that of the column 512 further along the last dimension in the same row (round the end) sum to one.
All inputs are finite; a program needn't handle non-finite values.
Results may differ from a plain program's by a relative error of at most 0.0003.
Values sent between devices are 32-bit elements; how exact they have to be, the bound alone decides.
No kernel may reach another device: no remote copies, remote signals or barrier semaphores. Data moves between devices by JAX's collectives and lax.ppermute only.
A program may use at most 128 MiB of HBM per device.

v0:
```python
import jax
import jax.numpy as jnp
import numpy as np
from jax import lax
from jax.sharding import PartitionSpec as P

NODES = 4


TIME_INCREMENT = 0.05


def shifted(value, axis, steps):
    count = lax.axis_size(axis)
    pairs = [(source, (source + steps) % count) for source in range(count)]
    return lax.ppermute(value, axis, pairs)


def padded_2(block, sides, width):
    for axis, dim in sides:
        count = lax.axis_size(axis)
        forward = [(i, i + 1) for i in range(count - 1)]
        forward.append((count - 1, 0))
        backward = [(target, source) for source, target in forward]
        low = lax.ppermute(
            lax.slice_in_dim(block, block.shape[dim] - width, None, axis=dim), axis, forward
        )
        high = lax.ppermute(lax.slice_in_dim(block, 0, width, axis=dim), axis, backward)
        block = jnp.concatenate([low, block, high], axis=dim)
    return block


def gll_derivative():
    points = np.array([-1.0, -1.0 / np.sqrt(5.0), 1.0 / np.sqrt(5.0), 1.0])
    legendre = 0.5 * (5.0 * points**3 - 3.0 * points)
    derivative = np.zeros((4, 4))
    for source in range(4):
        for target in range(4):
            if source != target:
                derivative[source, target] = legendre[source] / (
                    legendre[target] * (points[source] - points[target])
                )
    derivative[0, 0] = -3.0
    derivative[3, 3] = 3.0
    return derivative


def depth_terms(coeffs, optics_table, columns):
    vapour, ozone_amount, thickness, liquid, frozen, temper = columns
    weighted = thickness * temper * temper
    gas_depth = (
        coeffs[0][:, None] * (weighted * vapour)[None, :]
        + coeffs[1][:, None] * (weighted * ozone_amount)[None, :]
    )
    rayleigh = coeffs[2][:, None] * thickness[None, :]
    liquid_depth = optics_table[0][:, None] * liquid[None, :]
    ice_depth = optics_table[3][:, None] * frozen[None, :]
    liquid_scatter = optics_table[1][:, None] * liquid_depth
    ice_scatter = optics_table[4][:, None] * ice_depth
    scattering = rayleigh + liquid_scatter + ice_scatter
    absorption = gas_depth + (liquid_depth - liquid_scatter) + (ice_depth - ice_scatter)
    forward = optics_table[2][:, None] * liquid_scatter + optics_table[5][:, None] * ice_scatter
    return (scattering, absorption, forward)


def layer_optics(coeffs, optics_table, columns, cosine):
    scattering, absorption, forward = depth_terms(coeffs, optics_table, columns)
    optical_depth = scattering + absorption
    single_albedo = scattering / optical_depth
    asymmetry = forward / scattering
    eigen_rate = 2.0 * jnp.sqrt(absorption / optical_depth * (1.0 - single_albedo * asymmetry))
    gamma_one = 2.0 - single_albedo * (1.0 + asymmetry)
    gamma_two = single_albedo * (1.0 - asymmetry)
    shrink = jnp.expm1(-eigen_rate * optical_depth)
    decay_factor = 1.0 + shrink
    spread = -shrink * (2.0 + shrink)
    denominator = gamma_one * spread + eigen_rate * (1.0 + decay_factor * decay_factor)
    reflect = gamma_two * spread / denominator
    transmit = 2.0 * eigen_rate * decay_factor / denominator
    beam_loss = jnp.expm1(-optical_depth / cosine[None, :])
    reflect_beam = -0.5 * single_albedo * beam_loss * (1.0 - asymmetry)
    transmit_beam = -0.5 * single_albedo * beam_loss * (1.0 + asymmetry)
    return (reflect, transmit, reflect_beam, transmit_beam)


def block_nets(coeffs, optics_table, columns, cosine, ground):
    solar_weight = optics_table[6][:, None]
    plane = (optics_table.shape[1], cosine.shape[0])

    def beam_step(beam_flux, per_level):
        scattering, absorption, unused = depth_terms(per_level[0], optics_table, per_level[1:])
        direct = 1.0 + jnp.expm1(-(scattering + absorption) / cosine[None, :])
        return (beam_flux * direct, beam_flux)

    surface_beam, beams = lax.scan(
        beam_step, jnp.broadcast_to(cosine[None, :], plane), (coeffs,) + columns, unroll=8
    )
    ground_full = jnp.broadcast_to(ground[None, :], plane)

    def below_step(below, per_level):
        albedo_below, source_below = below
        beam_now = per_level[-1]
        reflect, transmit, reflect_beam, transmit_beam = layer_optics(
            per_level[0], optics_table, per_level[1:-1], cosine
        )
        inverse = 1.0 / (1.0 - reflect * albedo_below)
        albedo_here = reflect + transmit * transmit * albedo_below * inverse
        source_here = beam_now * reflect_beam + transmit * inverse * (
            source_below + albedo_below * beam_now * transmit_beam
        )
        gain_coef = transmit * inverse
        offset = inverse * (beam_now * transmit_beam + reflect * source_below)
        weight = solar_weight * (1.0 - albedo_below)
        upper_part = jnp.sum(solar_weight * (beam_now - source_here), axis=0)
        return ((albedo_here, source_here), (gain_coef, offset, weight, upper_part))

    unused_carry, (gains, offsets, weights, uppers) = lax.scan(
        below_step,
        (ground_full, ground_full * surface_beam),
        (coeffs,) + columns + (beams,),
        reverse=True,
        unroll=8,
    )

    def down_step(diffuse_now, per_level):
        gain_coef, offset, weight = per_level
        diffuse_new = gain_coef * diffuse_now + offset
        return (diffuse_new, jnp.sum(weight * diffuse_new, axis=0))

    unused_last, lowers = lax.scan(
        down_step, jnp.zeros(plane, jnp.float32), (gains, offsets, weights), unroll=8
    )
    bottom = jnp.sum(solar_weight * (surface_beam - ground_full * surface_beam), axis=0)
    upper_all = jnp.concatenate([uppers, bottom[None]], axis=0)
    lower_all = jnp.concatenate([jnp.zeros_like(bottom)[None], lowers], axis=0)
    return upper_all + lower_all


def shortwave(
    state_cols, temp_cols, cosine, ground, molecular_optics_lookup, condensate_optics_lookup
):
    gpoints = molecular_optics_lookup.shape[1]
    level_sum_entries = molecular_optics_lookup.shape[2]
    blocks = gpoints // 56
    group_width = gpoints // blocks
    gas_blocks = molecular_optics_lookup.reshape(
        3, blocks, group_width, level_sum_entries
    ).transpose(1, 3, 0, 2)
    table_blocks = condensate_optics_lookup.reshape(7, blocks, group_width).transpose(1, 0, 2)
    columns = (state_cols[0], state_cols[1], state_cols[2], state_cols[3], state_cols[4], temp_cols)

    def one_block(running, per_block):
        return (running + block_nets(per_block[0], per_block[1], columns, cosine, ground), 0.0)

    nets, unused = lax.scan(
        one_block,
        jnp.zeros((level_sum_entries + 1, cosine.shape[0]), jnp.float32),
        (gas_blocks, table_blocks),
    )
    return level_sum_entries / gpoints * (nets[:-1] - nets[1:])


def pair_average(values, before, beyond, node_index):
    return jnp.where(
        node_index == NODES - 1,
        0.5 * (values + beyond),
        jnp.where(node_index == 0, 0.5 * (before + values), values),
    )


def local(
    atmospheric_constituents,
    thermal_ratio,
    flow_velocity,
    solar_elevation_factor,
    ground_reflectivity,
    sunlit_indicator,
    molecular_optics_lookup,
    condensate_optics_lookup,
):
    level_sum_entries, resident_line_number, resident_span_size = thermal_ratio.shape
    resident_profile_number = resident_line_number * resident_span_size
    half_cols = resident_profile_number // 2
    flat_state = atmospheric_constituents.reshape(5, level_sum_entries, resident_profile_number)
    thermal_ratio_vector = thermal_ratio.reshape(level_sum_entries, resident_profile_number)
    cosine = solar_elevation_factor.reshape(resident_profile_number)
    ground = ground_reflectivity.reshape(resident_profile_number)
    day_flags = sunlit_indicator.reshape(resident_profile_number)
    surface_here = jnp.stack([cosine, ground])
    day_count = jnp.sum(day_flags)
    sent_count = day_count // 2
    kept_count = day_count - sent_count
    incoming = (resident_profile_number - day_count) // 2
    rank_end = jnp.cumsum(day_flags)
    slot_ids = jnp.arange(resident_profile_number, dtype=jnp.int32)
    located = jnp.minimum(
        jnp.searchsorted(rank_end, slot_ids, side="right"), resident_profile_number - 1
    )
    half_ids = slot_ids[:half_cols]
    outgoing_source_start = located[:half_cols]
    outgoing_sunlit_flags = half_ids < sent_count
    send_state = jnp.where(
        outgoing_sunlit_flags, jnp.take(flat_state, outgoing_source_start, axis=2), 0.0
    )
    outgoing_thermal_ratio = jnp.where(
        outgoing_sunlit_flags, jnp.take(thermal_ratio_vector, outgoing_source_start, axis=1), 0.0
    )
    send_surface = jnp.where(
        outgoing_sunlit_flags, jnp.take(surface_here, outgoing_source_start, axis=1), 0.0
    )
    partner = lax.axis_size("gx") // 2
    got_state, got_temp, got_surface = shifted(
        (send_state, outgoing_thermal_ratio, send_surface), "gx", partner
    )
    from_own = half_ids < kept_count
    retained_source_start = jnp.take(
        located, jnp.minimum(sent_count + half_ids, resident_profile_number - 1)
    )
    recv_from = jnp.clip(half_ids - kept_count, 0, half_cols - 1)
    work_state = jnp.where(
        from_own,
        jnp.take(flat_state, retained_source_start, axis=2),
        jnp.take(got_state, recv_from, axis=2),
    )
    work_temp = jnp.where(
        from_own,
        jnp.take(thermal_ratio_vector, retained_source_start, axis=1),
        jnp.take(got_temp, recv_from, axis=1),
    )
    work_surface = jnp.where(
        from_own,
        jnp.take(surface_here, retained_source_start, axis=1),
        jnp.take(got_surface, recv_from, axis=1),
    )
    work_heat = shortwave(
        work_state,
        work_temp,
        work_surface[0],
        work_surface[1],
        molecular_optics_lookup,
        condensate_optics_lookup,
    )
    back_from = jnp.minimum(kept_count + half_ids, half_cols - 1)
    send_back = jnp.where(half_ids < incoming, jnp.take(work_heat, back_from, axis=1), 0.0)
    returned = shifted(send_back, "gx", partner)
    rank_here = rank_end - 1
    went_away = rank_here < sent_count
    heat_flat = jnp.where(
        went_away,
        jnp.take(returned, jnp.clip(rank_here, 0, half_cols - 1), axis=1),
        jnp.take(work_heat, jnp.clip(rank_here - sent_count, 0, half_cols - 1), axis=1),
    )
    heat_flat = jnp.where(day_flags == 1, heat_flat, 0.0)
    radiative_warming_rate = heat_flat.reshape(
        level_sum_entries, resident_line_number, resident_span_size
    )
    derivative = gll_derivative()
    x_derivative = jnp.asarray(
        np.kron(np.eye(resident_span_size // NODES), derivative).T, jnp.float32
    )
    y_derivative = jnp.asarray(
        np.kron(np.eye(resident_line_number // NODES), derivative), jnp.float32
    )
    x_nodes = (jnp.arange(resident_span_size) % NODES)[None, None, :]
    y_nodes = (jnp.arange(resident_line_number) % NODES)[None, :, None]

    def averaged(values):
        padded = padded_2(values, (("gx", 2),), 1)
        along_x = pair_average(values, padded[:, :, :-2], padded[:, :, 2:], x_nodes)
        padded_y = padded_2(along_x, (("gy", 1),), 1)
        return pair_average(along_x, padded_y[:, :-2], padded_y[:, 2:], y_nodes)

    def warming_change_rate(field_now):
        slope_x = jnp.dot(
            field_now.reshape(-1, resident_span_size), x_derivative, precision=lax.Precision.HIGHEST
        ).reshape(field_now.shape)
        slope_y = jnp.einsum(
            "ij,ljx->lix", y_derivative, field_now, precision=lax.Precision.HIGHEST
        )
        return averaged(
            radiative_warming_rate - (flow_velocity[0] * slope_x + flow_velocity[1] * slope_y)
        )

    opening_advection_part = thermal_ratio + TIME_INCREMENT * warming_change_rate(thermal_ratio)
    middle_advection_part = 0.75 * thermal_ratio + 0.25 * (
        opening_advection_part + TIME_INCREMENT * warming_change_rate(opening_advection_part)
    )
    advected_thermal_ratio = 1.0 / 3.0 * thermal_ratio + 2.0 / 3.0 * (
        middle_advection_part + TIME_INCREMENT * warming_change_rate(middle_advection_part)
    )
    return (radiative_warming_rate, advected_thermal_ratio)


def solution(mesh):
    in_specs = (
        P(None, None, "gy", "gx"),
        P(None, "gy", "gx"),
        P(None, None, "gy", "gx"),
        P("gy", "gx"),
        P("gy", "gx"),
        P("gy", "gx"),
        P(),
        P(),
    )
    out_specs = (P(None, "gy", "gx"), P(None, "gy", "gx"))
    return jax.shard_map(local, mesh=mesh, in_specs=in_specs, out_specs=out_specs, check_vma=False)
```

profile of v0, /device:TPU:1, one launch (start us, length us, event | category | flops | bytes accessed | tf_op | source)
XLA Modules:
  0.0 782.3 jit_solution(15016031741877445505)
XLA Ops:
  7.6 50.7 %while.169 = (s32[]{:T(128)}, u32[1024]{0:T(1024)S(1)}, u32[1024]{0:T(1024)S(1)}, s32[1024]{0:T(1024)S(1)}, s32[]{:T(128)}, /*index=5*/s32[]{:T(128)}, s32[]{}) while((s32[]{:T(128)}, u32[1024]{0:T(1024)S(1)}, u32[1024]{0:T(1024)S(1)}, s32[1024]{0:T(1024)S(1)}, s32[]{:T(128)}, /*index=5*/s32[]{:T(128)}, s32[]{}) %tuple.522), condition=%wide.region_4.5_spmd.clone, body=%wide.region_3.4_spmd.clone.sunk | while | flops 19460 | bytes 63589 | solution.py:197
  7.6 4.5 gather_fusion
  12.3 4.5 gather_fusion
  16.9 4.5 gather_fusion
  21.5 4.5 gather_fusion
  26.1 4.5 gather_fusion
  30.7 4.5 gather_fusion
  35.3 4.5 gather_fusion
  39.9 4.5 gather_fusion
  44.5 4.5 gather_fusion
  49.1 4.5 gather_fusion
  53.8 4.5 gather_fusion
  58.4 3.2 copy.77
  61.6 4.6 gather_fusion.7
  66.8 3.8 bitcast_select_fusion.1
  72.0 3.1 collective-permute-start.1
  80.2 2.4 collective-permute-start
  88.7 4.5 gather_fusion.6
  97.1 32.9 %collective-permute-done = f32[2,512]{0,1:T(8,128)} collective-permute-done((f32[2,512]{0,1:T(8,128)}, f32[2,512]{0,1:T(8,128)}, u32[]{:S(2)}, u32[]{:S(2)}) %collective-permute-start) | collective-permute-done | bytes 4128 | tf_op jit(solution)/shard_map/ppermute | solution.py:16
  136.0 3.9 gather_fusion.3
  139.9 6.0 bitcast_select_fusion
  147.6 553.0 %while.173 = (s32[]{:T(128)}, f32[73,512]{1,0:T(8,128)S(1)}, f32[1,512]{1,0:T(1,128)S(1)}, f32[1,512]{1,0:T(1,128)S(1)}, f32[2,72,3,56]{1,3,0,2:T(8,128)S(1)}, /...) while((s32[]{:T(128)}, f32[73,512]{1,0:T(8,128)S(1)}, ...), condition=%wide.region_29.34_spmd.clone, body=%wide.region_5.33_spmd.clone.sunk | while | flops 48399896 | bytes 59970308 | solution.py:155
  148.0 4.2 broadcast.994.clone
  152.2 30.6 %while.174 = (s32[]{:T(128)}, f32[56,512]{1,0:T(8,128)S(1)}, f32[9,8,56,512]{3,2,1,0:T(8,128)}, f32[9,8,3,56]{3,2,1,0:T(4,128)S(1)}, f32[9,8,512]{2,1,0:T(8,128)...) while((s32[]{:T(128)}, f32[56,512]{1,0:T(8,128)S(1)}, ...), condition=%wide.region_7.11_spmd, body=%wide.region_6.10_spmd.sunk | while | flops 6553609 | bytes 4723025 | solution.py:95
  183.0 4.3 broadcast.994
  187.3 4.2 broadcast.994.clone.1
  191.6 4.2 broadcast.994.clone.2
  195.8 196.2 %while.175 = (s32[]{:T(128)}, f32[56,512]{1,0:T(8,128)S(1)}, f32[56,512]{1,0:T(8,128)S(1)}, f32[9,8,56,512]{3,2,1,0:T(8,128)}, f32[9,8,56,512]{3,2,1,0:T(8,128)}...) while((s32[]{:T(128)}, f32[56,512]{1,0:T(8,128)S(1)}, ...), condition=%wide.region_17.21_spmd, body=%wide.region_8.20_spmd.sunk | while | flops 40468488 | bytes 15987933 | solution.py:117
  196.3 4.9 multiply_reduce_fusion.10
  218.2 4.9 multiply_reduce_fusion.10
  239.9 4.9 multiply_reduce_fusion.10
  261.7 4.9 multiply_reduce_fusion.10
  283.5 4.9 multiply_reduce_fusion.10
  305.3 4.9 multiply_reduce_fusion.10
  327.1 4.9 multiply_reduce_fusion.10
  348.8 4.9 multiply_reduce_fusion.10
  370.6 4.9 multiply_reduce_fusion.10
  392.0 32.0 %while.176 = (s32[]{:T(128)}, f32[56,512]{1,0:T(8,128)S(1)}, f32[9,8,512]{2,1,0:T(8,128)S(1)}, f32[9,8,56,512]{3,2,1,0:T(8,128)}, f32[9,8,56,512]{3,2,1,0:T(8,12...) while((s32[]{:T(128)}, f32[56,512]{1,0:T(8,128)S(1)}, ...), condition=%wide.region_28.32_spmd.clone, body=%wide.region_19.31_spmd.clone.sunk | while | flops 1114122 | bytes 4669739 | solution.py:130
  424.3 4.2 broadcast.994.clone
  428.5 30.6 %while.174 = (s32[]{:T(128)}, f32[56,512]{1,0:T(8,128)S(1)}, f32[9,8,56,512]{3,2,1,0:T(8,128)}, f32[9,8,3,56]{3,2,1,0:T(4,128)S(1)}, f32[9,8,512]{2,1,0:T(8,128)...) while((s32[]{:T(128)}, f32[56,512]{1,0:T(8,128)S(1)}, ...), condition=%wide.region_7.11_spmd, body=%wide.region_6.10_spmd.sunk | while | flops 6553609 | bytes 4723025 | solution.py:95
  459.3 4.3 broadcast.994
  463.6 4.2 broadcast.994.clone.1
  467.8 4.2 broadcast.994.clone.2
  472.1 196.2 %while.175 = (s32[]{:T(128)}, f32[56,512]{1,0:T(8,128)S(1)}, f32[56,512]{1,0:T(8,128)S(1)}, f32[9,8,56,512]{3,2,1,0:T(8,128)}, f32[9,8,56,512]{3,2,1,0:T(8,128)}...) while((s32[]{:T(128)}, f32[56,512]{1,0:T(8,128)S(1)}, ...), condition=%wide.region_17.21_spmd, body=%wide.region_8.20_spmd.sunk | while | flops 40468488 | bytes 15987933 | solution.py:117
  472.6 4.9 multiply_reduce_fusion.10
  494.4 4.9 multiply_reduce_fusion.10
  516.2 4.9 multiply_reduce_fusion.10
  538.0 4.9 multiply_reduce_fusion.10
  559.8 4.9 multiply_reduce_fusion.10
  581.6 4.9 multiply_reduce_fusion.10
  603.4 4.9 multiply_reduce_fusion.10
  625.1 4.9 multiply_reduce_fusion.10
  646.9 4.9 multiply_reduce_fusion.10
  668.3 32.0 %while.176 = (s32[]{:T(128)}, f32[56,512]{1,0:T(8,128)S(1)}, f32[9,8,512]{2,1,0:T(8,128)S(1)}, f32[9,8,56,512]{3,2,1,0:T(8,128)}, f32[9,8,56,512]{3,2,1,0:T(8,12...) while((s32[]{:T(128)}, f32[56,512]{1,0:T(8,128)S(1)}, ...), condition=%wide.region_28.32_spmd.clone, body=%wide.region_19.31_spmd.clone.sunk | while | flops 1114122 | bytes 4669739 | solution.py:130
  702.3 2.8 gather_fusion.13
  705.2 10.2 %collective-permute-done.3 = f32[72,512]{0,1:T(8,128)S(1)} collective-permute-done((f32[72,512]{0,1:T(8,128)S(1)}, f32[72,512]{0,1:T(8,128)S(1)}, u32[]{:S(2)}, u32[]{:S(2)}) %collective-permute-start.3) | collective-permute-done | bytes 147488 | tf_op jit(solution)/shard_map/ppermute | solution.py:16
  715.4 2.8 gather_fusion.12
  721.0 3.3 collective-permute-start.4
  724.3 5.9 collective-permute-done.4
  730.2 5.5 collective-permute-done.5
  740.8 4.3 collective-permute-start.8
  745.1 5.7 collective-permute-done.8
  750.8 6.1 collective-permute-done.9
  764.2 12.4 %collective-permute-done.12 = f32[72,8,1]{2,0,1:T(8,128)S(1)} collective-permute-done((f32[72,8,1]{2,0,1:T(8,128)S(1)}, f32[72,8,1]{2,0,1:T(8,128)S(1)}, u32[]{:S(2)}, u32[]{:S(2)}) %collective-permute-start.12) | collective-permute-done | bytes 2336 | tf_op jit(solution)/shard_map/ppermute | solution.py:28
  (1377 shorter events, 471.8 us)
Async XLA Ops:
  7.6 50.8 %copy-start.4 = (f32[5,72,8,128]{3,2,1,0:T(8,128)S(1)}, f32[5,72,8,128]{3,2,1,0:T(8,128)}, u32[]{:S(2)}) copy-start(f32[5,72,8,128]{3,2,1,0:T(8,128)} %param.30) | copy-start | bytes 4423684
  58.3 16.8 %copy-start = (f32[72,8,128]{2,1,0:T(8,128)S(1)}, f32[72,8,128]{2,1,0:T(8,128)}, u32[]{:S(2)}) copy-start(f32[72,8,128]{2,1,0:T(8,128)} %param.31) | copy-start | bytes 884740
  58.4 18.9 %copy-start.16 = (f32[8,128]{1,0:T(8,128)S(1)}, f32[8,128]{1,0:T(8,128)}, u32[]{:S(2)}) copy-start(f32[8,128]{1,0:T(8,128)} %param.34) | copy-start | bytes 12292
  61.6 24.5 %copy-start.6 = (f32[2,72,8,128]{3,2,1,0:T(8,128)S(1)}, f32[2,72,8,128]{3,2,1,0:T(8,128)}, u32[]{:S(2)}) copy-start(f32[2,72,8,128]{3,2,1,0:T(8,128)} %param.32) | copy-start | bytes 1769476
  61.6 25.3 %copy-start.7 = (f32[8,8,1]{1,0,2:T(8,128)S(1)}, f32[8,8,1]{1,0,2:T(8,128)}, u32[]{:S(2)}) copy-start(f32[8,8,1]{1,0,2:T(8,128)} %constant.361) | copy-start | bytes 772
  72.0 62.0 %collective-permute-start.1 = (f32[5,72,512]{2,1,0:T(8,128)}, f32[5,72,512]{2,1,0:T(8,128)S(1)}, u32[]{:S(2)}, u32[]{:S(2)}) collective-permute-start(f32[5,72,512]{2,1,0:T(8,128)} %copy.78), channel_id=1, source_target_pairs={{0,16},{4,20},{8,24},{12,28},{16,0},{20,4},{24,8},{28,12},{1,17},{... | collective-permute-start | bytes 2211848 | tf_op jit(solution)/shard_map/ppermute | solution.py:16
  77.3 55.3 %collective-permute-start.2 = (f32[72,512]{0,1:T(8,128)}, f32[72,512]{0,1:T(8,128)S(1)}, u32[]{:S(2)}, u32[]{:S(2)}) collective-permute-start(f32[72,512]{0,1:T(8,128)} %bitcast_select_fusion.5), channel_id=1, source_target_pairs={{0,16},{4,20},{8,24},{12,28},{16,0},{20,4},{24,8},{28,12},{1,17},{... | collective-permute-start | bytes 442376 | tf_op jit(solution)/shard_map/ppermute | solution.py:16
  80.2 49.7 %collective-permute-start = (f32[2,512]{0,1:T(8,128)}, f32[2,512]{0,1:T(8,128)}, u32[]{:S(2)}, u32[]{:S(2)}) collective-permute-start(f32[2,512]{0,1:T(8,128)} %bitcast_select_fusion.7), channel_id=1, source_target_pairs={{0,16},{4,20},{8,24},{12,28},{16,0},{20,4},{24,8},{28,12},{1,17},{... | collective-permute-start | bytes 12296 | tf_op jit(solution)/shard_map/ppermute | solution.py:16
  147.6 553.4 %copy-start.12 = (s32[1024]{0:T(1024)S(1)}, s32[1024]{0:T(1024)}, u32[]{:S(2)}) copy-start(s32[1024]{0:T(1024)} %get-tuple-element.1414) | copy-start | bytes 12292
  147.6 554.4 %copy-start.17 = (pred[512]{0:T(512)(128)(4,1)S(1)}, pred[512]{0:T(512)(128)(4,1)}, u32[]{:S(2)}) copy-start(pred[512]{0:T(512)(128)(4,1)} %get-tuple-element.1407) | copy-start | bytes 1540
  147.6 554.4 %copy-start.18 = (pred[512]{0:T(512)(128)(4,1)S(1)}, pred[512]{0:T(512)(128)(4,1)}, u32[]{:S(2)}) copy-start(pred[512]{0:T(512)(128)(4,1)} %get-tuple-element.1412) | copy-start | bytes 1540
  147.6 554.7 %copy-start.9 = (s32[8,128]{1,0:T(8,128)S(1)}, s32[8,128]{1,0:T(8,128)}, u32[]{:S(2)}) copy-start(s32[8,128]{1,0:T(8,128)} %param.35) | copy-start | bytes 12292
  147.6 554.7 %copy-start.11 = (s32[1024]{0:T(1024)S(1)}, s32[1024]{0:T(1024)}, u32[]{:S(2)}) copy-start(s32[1024]{0:T(1024)} %get-tuple-element.1406) | copy-start | bytes 12292
  147.6 567.8 %copy-start.10 = (s32[1024]{0:T(1024)S(1)}, s32[1024]{0:T(1024)}, u32[]{:S(2)}) copy-start(s32[1024]{0:T(1024)} %get-tuple-element.1405) | copy-start | bytes 12292
  700.6 17.6 %copy-start.13 = (pred[1024]{0:T(1024)(128)(4,1)S(1)}, pred[1024]{0:T(1024)(128)(4,1)}, u32[]{:S(2)}) copy-start(pred[1024]{0:T(1024)(128)(4,1)} %get-tuple-element.1140) | copy-start | bytes 3076
  700.6 17.6 %copy-start.14 = (pred[1024]{0:T(1024)(128)(4,1)S(1)}, pred[1024]{0:T(1024)(128)(4,1)}, u32[]{:S(2)}) copy-start(pred[1024]{0:T(1024)(128)(4,1)} %get-tuple-element.1403) | copy-start | bytes 3076
  700.6 17.6 %copy-start.15 = (pred[1024]{0:T(1024)(128)(4,1)S(1)}, pred[1024]{0:T(1024)(128)(4,1)}, u32[]{:S(2)}) copy-start(pred[1024]{0:T(1024)(128)(4,1)} %get-tuple-element.1404) | copy-start | bytes 3076
  700.6 18.7 %copy-start.1 = (f32[72,8,128]{2,1,0:T(8,128)S(1)}, f32[72,8,128]{2,1,0:T(8,128)}, u32[]{:S(2)}) copy-start(f32[72,8,128]{2,1,0:T(8,128)} %param.31) | copy-start | bytes 884740
  700.6 18.7 %copy-start.2 = (f32[1,72,8,128]{3,2,1,0:T(8,128)S(1)}, f32[1,72,8,128]{3,2,1,0:T(8,128)}, u32[]{:S(2)}) copy-start(f32[1,72,8,128]{3,2,1,0:T(8,128)} %get-tuple-element.1387) | copy-start | bytes 884740
  700.6 18.7 %copy-start.3 = (f32[1,72,8,128]{3,2,1,0:T(8,128)S(1)}, f32[1,72,8,128]{3,2,1,0:T(8,128)}, u32[]{:S(2)}) copy-start(f32[1,72,8,128]{3,2,1,0:T(8,128)} %get-tuple-element.1388) | copy-start | bytes 884740
  700.6 18.7 %copy-start.5 = (f32[128,128,1]{1,0,2:T(8,128)S(1)}, f32[128,128,1]{1,0,2:T(8,128)}, u32[]{:S(2)}) copy-start(f32[128,128,1]{1,0,2:T(8,128)} %constant.360) | copy-start | bytes 196612
  700.7 39.1 %copy-start.8 = (f32[8,8,1]{1,0,2:T(8,128)S(1)}, f32[8,8,1]{1,0,2:T(8,128)}, u32[]{:S(2)}) copy-start(f32[8,8,1]{1,0,2:T(8,128)} %constant.361) | copy-start | bytes 772
  702.2 13.2 %collective-permute-start.3 = (f32[72,512]{0,1:T(8,128)S(1)}, f32[72,512]{0,1:T(8,128)S(1)}, u32[]{:S(2)}, u32[]{:S(2)}) collective-permute-start(f32[72,512]{0,1:T(8,128)S(1)} %bitcast_select_fusion.3), channel_id=1, source_target_pairs={{0,16},{4,20},{8,24},{12,28},{16,0},{20,4},{24,8},{28,12},{1,17},{... | collective-permute-start | bytes 442376 | tf_op jit(solution)/shard_map/ppermute | solution.py:16
  721.0 9.2 %collective-permute-start.4 = (f32[72,8,1]{2,0,1:T(8,128)S(1)}, f32[72,8,1]{2,0,1:T(8,128)S(1)}, u32[]{:S(2)}, u32[]{:S(2)}) collective-permute-start(f32[72,8,1]{2,0,1:T(8,128)S(1)} %get-tuple-element.1399), channel_id=1, source_target_pairs={{4,0},{8,4},{12,8},{16,12},{20,16},{24,20},{28,24},{0,28},{5,1},{9... | collective-permute-start | bytes 6920 | tf_op jit(solution)/shard_map/ppermute | solution.py:28
  724.3 11.4 %collective-permute-start.5 = (f32[72,8,1]{2,0,1:T(8,128)S(1)}, f32[72,8,1]{2,0,1:T(8,128)S(1)}, u32[]{:S(2)}, u32[]{:S(2)}) collective-permute-start(f32[72,8,1]{2,0,1:T(8,128)S(1)} %get-tuple-element.1400), channel_id=1, source_target_pairs={{0,4},{4,8},{8,12},{12,16},{16,20},{20,24},{24,28},{28,0},{1,5},{5... | collective-permute-start | bytes 6920 | tf_op jit(solution)/shard_map/ppermute | solution.py:25
  736.0 3.5 collective-permute-start.6
  737.2 2.4 collective-permute-start.7
  740.8 10.0 %collective-permute-start.8 = (f32[72,8,1]{2,0,1:T(8,128)S(1)}, f32[72,8,1]{2,0,1:T(8,128)S(1)}, u32[]{:S(2)}, u32[]{:S(2)}) collective-permute-start(f32[72,8,1]{2,0,1:T(8,128)S(1)} %get-tuple-element.1395), channel_id=1, source_target_pairs={{4,0},{8,4},{12,8},{16,12},{20,16},{24,20},{28,24},{0,28},{5,1},{9... | collective-permute-start | bytes 6920 | tf_op jit(solution)/shard_map/ppermute | solution.py:28
  745.1 11.8 %collective-permute-start.9 = (f32[72,8,1]{2,0,1:T(8,128)S(1)}, f32[72,8,1]{2,0,1:T(8,128)S(1)}, u32[]{:S(2)}, u32[]{:S(2)}) collective-permute-start(f32[72,8,1]{2,0,1:T(8,128)S(1)} %get-tuple-element.1396), channel_id=1, source_target_pairs={{0,4},{4,8},{8,12},{12,16},{16,20},{20,24},{24,28},{28,0},{1,5},{5... | collective-permute-start | bytes 6920 | tf_op jit(solution)/shard_map/ppermute | solution.py:25
  757.2 3.7 collective-permute-start.10
  757.8 3.2 collective-permute-start.11
  762.2 14.4 %collective-permute-start.12 = (f32[72,8,1]{2,0,1:T(8,128)S(1)}, f32[72,8,1]{2,0,1:T(8,128)S(1)}, u32[]{:S(2)}, u32[]{:S(2)}) collective-permute-start(f32[72,8,1]{2,0,1:T(8,128)S(1)} %get-tuple-element.1391), channel_id=1, source_target_pairs={{4,0},{8,4},{12,8},{16,12},{20,16},{24,20},{28,24},{0,28},{5,1},{9... | collective-permute-start | bytes 6920 | tf_op jit(solution)/shard_map/ppermute | solution.py:28
  764.2 12.4 %collective-permute-start.13 = (f32[72,8,1]{2,0,1:T(8,128)S(1)}, f32[72,8,1]{2,0,1:T(8,128)S(1)}, u32[]{:S(2)}, u32[]{:S(2)}) collective-permute-start(f32[72,8,1]{2,0,1:T(8,128)S(1)} %get-tuple-element.1392), channel_id=1, source_target_pairs={{0,4},{4,8},{8,12},{12,16},{16,20},{20,24},{24,28},{28,0},{1,5},{5... | collective-permute-start | bytes 6920 | tf_op jit(solution)/shard_map/ppermute | solution.py:25
  776.9 4.4 collective-permute-start.14
  778.8 2.5 collective-permute-start.15
where the time goes:
time: 790 us; the launch traced here: 782 us
  other arithmetic  459 us (58%)
  local copies, waits for them, and re-layouts  200 us (25%)
  waiting for transfers between devices  82.5 us (10%)
  starting transfers between devices  22.2 us (3%)
  loops' own time  9.14 us (1%)
    while x362, other arithmetic  238 us
    reduce_sum x18, other arithmetic, below_step(): upper_part = jnp.sum(solar_weight * (beam_now - source_here), axis=0)  88.9 us
    dynamic_update_slice x54, local copies, waits for them, and re-layouts, block_nets(): lax.scan(beam_step, jnp.broadcast_to(cosine[None, :], plane), (coeffs,) +...  61.6 us
    gather x11, local copies, waits for them, and re-layouts, local(): jnp.searchsorted(rank_end, slot_ids, side='right')  49.8 us
    ppermute x4, waiting for transfers between devices, shifted(): return lax.ppermute(value, axis, pairs)  43.1 us
    another operation x13, local copies, waits for them, and re-layouts  34.2 us
    reduce_sum x18, other arithmetic, down_step(): return (diffuse_new, jnp.sum(weight * diffuse_new, axis=0))  33.1 us
    concatenate x36, other arithmetic, block_nets(): lax.scan(below_step, (ground_full, ground_full * surface_beam), (coeffs,)...  30.9 us
  transfers between devices with their start and end apart: 16, of which 10 were waited for; matrix products, arithmetic and copies ran while one was open for 3% of the time, Pallas kernels for 0%

commit v1 on v0

v1 whole, which is shorter than its diff:
```python
import functools

import jax
import jax.numpy as jnp
import numpy as np
from jax import lax
from jax.experimental import pallas as pl
from jax.experimental.pallas import tpu as pltpu
from jax.sharding import PartitionSpec as P

NODES = 4
TIME_INCREMENT = 0.05
LOG2E = 1.4426950408889634

GROUP = 8
TERMS = 16
QUANTITIES = 6


def padded_2(block, sides, width):
    for axis, dim in sides:
        count = lax.axis_size(axis)
        forward = [(i, i + 1) for i in range(count - 1)]
        forward.append((count - 1, 0))
        backward = [(target, source) for source, target in forward]
        low = lax.ppermute(
            lax.slice_in_dim(block, block.shape[dim] - width, None, axis=dim), axis, forward
        )
        high = lax.ppermute(lax.slice_in_dim(block, 0, width, axis=dim), axis, backward)
        block = jnp.concatenate([low, block, high], axis=dim)
    return block


def gll_derivative():
    points = np.array([-1.0, -1.0 / np.sqrt(5.0), 1.0 / np.sqrt(5.0), 1.0])
    legendre = 0.5 * (5.0 * points**3 - 3.0 * points)
    derivative = np.zeros((4, 4))
    for source in range(4):
        for target in range(4):
            if source != target:
                derivative[source, target] = legendre[source] / (
                    legendre[target] * (points[source] - points[target])
                )
    derivative[0, 0] = -3.0
    derivative[3, 3] = 3.0
    return derivative


def high_low(values):
    high = lax.reduce_precision(values, exponent_bits=8, mantissa_bits=7)
    return high.astype(jnp.bfloat16), (values - high).astype(jnp.bfloat16)


def optics_matrices(molecular, condensate):
    gpoints, level_count = molecular.shape[1:]
    groups = level_count // GROUP
    k0, k1, k2 = molecular
    w = condensate[:, :, None]
    zero = jnp.zeros((gpoints, level_count), jnp.float32)
    full = functools.partial(jnp.broadcast_to, shape=(gpoints, level_count))
    ls, li = w[0] * w[1], w[3] * w[4]
    la, ia = w[0] * (1.0 - w[1]), w[3] * (1.0 - w[4])
    absorption = (k0, k1, zero, full(la), full(ia))
    away = (zero, zero, k2, full(ls * (1.0 - w[2])), full(li * (1.0 - w[5])))
    along = (zero, zero, k2, full(ls * (1.0 + w[2])), full(li * (1.0 + w[5])))
    depth = (k0, k1, k2, full(w[0]), full(w[3]))
    rows = [
        absorption,
        [a + b for a, b in zip(absorption, away)],
        [2.0 * a + b for a, b in zip(absorption, away)],
        [0.5 * b for b in away],
        [0.5 * b for b in along],
        depth,
        [-LOG2E * b for b in depth],
    ]
    table = jnp.stack([jnp.stack(list(row)) for row in rows])
    high, low = high_low(table)
    empty = jnp.zeros_like(high[:, :1])
    terms = jnp.concatenate([high, low, high, empty], axis=1)
    terms = terms.reshape(len(rows), TERMS, gpoints, groups, GROUP)
    terms = terms.transpose(3, 0, 2, 4, 1).reshape(groups, len(rows) * gpoints, GROUP * TERMS)
    return terms[:, : QUANTITIES * gpoints], terms[:, QUANTITIES * gpoints :]


def radiation_kernel(
    state_ref, temp_ref, cosine_ref, ground_ref, day_ref, optics_ref, slant_ref, weight_ref,
    heat_ref,
    terms_ref, slant_terms_ref, right_ref, slant_right_ref, beam_ref, gain_ref, offset_ref,
    clear_ref, open_ref, partial_ref,
):
    level_count = temp_ref.shape[0]
    gpoints = weight_ref.shape[0]
    groups = level_count // GROUP
    lanes = temp_ref.shape[2]
    row = pl.program_id(0)
    rows = pl.num_programs(0)

    @pl.when(row == 0)
    def prepare():
        right_ref[...] = jnp.zeros_like(right_ref)
        slant_right_ref[...] = jnp.zeros_like(slant_right_ref)
        slant = 1.0 / cosine_ref[...]

        def level(l, carry):
            thickness = state_ref[2, l]
            weighted = thickness * temp_ref[l] * temp_ref[l]
            values = (
                weighted * state_ref[0, l], weighted * state_ref[1, l], thickness,
                state_ref[3, l], state_ref[4, l],
            )
            for ref, scale in ((terms_ref, None), (slant_terms_ref, slant)):
                for k, value in enumerate(values):
                    value = value if scale is None else value * scale
                    high = value.astype(jnp.bfloat16).astype(jnp.float32)
                    for place, part in ((k, high), (k + 5, high), (k + 10, value - high)):
                        start = pl.multiple_of((l * TERMS + place) * 8, 8)
                        ref[pl.ds(start, 8), :] = part
                ref[pl.ds(pl.multiple_of((l * TERMS + 15) * 8, 8), 8), :] = jnp.zeros_like(slant)
            return carry

        lax.fori_loop(0, level_count, level, 0)

    def place_terms(group, carry):
        for j in range(GROUP):
            start = (group * GROUP + j) * TERMS * 8 + row
            for source, target in ((terms_ref, right_ref), (slant_terms_ref, slant_right_ref)):
                tile = source[pl.ds(start, TERMS, stride=8), :]
                target[group, TERMS * j : TERMS * (j + 1), lanes * j : lanes * (j + 1)] = (
                    tile.astype(jnp.bfloat16)
                )
        return carry

    lax.fori_loop(0, groups, place_terms, 0)

    top = weight_ref[...] * cosine_ref[pl.ds(row, 1), :]
    beam_ref[0] = top

    def beam_group(group, beam):
        exponents = jnp.dot(
            slant_ref[group], slant_right_ref[group], preferred_element_type=jnp.float32
        )
        for j in range(GROUP):
            beam = beam * jnp.exp2(exponents[:, lanes * j : lanes * (j + 1)])
            beam_ref[group * GROUP + j + 1] = beam
        return beam

    surface = lax.fori_loop(0, groups, beam_group, top)
    albedo = jnp.broadcast_to(ground_ref[pl.ds(row, 1), :], surface.shape)

    def below_group(step, carry):
        group = groups - 1 - step
        albedo, source, beam_below = carry
        for pair in reversed(range(GROUP // 2)):
            both = jnp.dot(
                optics_ref[group],
                right_ref[group, :, 2 * pair * lanes : 2 * (pair + 1) * lanes],
                preferred_element_type=jnp.float32,
            )
            for half in (1, 0):
                level = group * GROUP + 2 * pair + half
                part = both[:, half * lanes : (half + 1) * lanes]
                a, b, ab, away, along, depth = [
                    part[n * gpoints : (n + 1) * gpoints] for n in range(QUANTITIES)
                ]
                square = a * b
                inverse_root = lax.rsqrt(square)
                h = jnp.tanh(square * inverse_root)
                g = h * inverse_root
                spread = ab * g
                differ = (away + away) * g
                h2 = h * h
                one = 1.0 + h2
                inverse = 1.0 / ((one + spread) - differ * albedo)
                through = 1.0 - h2
                beam = beam_ref[level]
                factor = (beam - beam_below) * (1.0 / depth)
                up, down = factor * away, factor * along
                push = inverse * (source + albedo * down)
                gain_ref[level] = through * inverse
                offset_ref[level] = down + differ * push
                open_ref[level] = 1.0 - albedo
                clear_ref[level] = beam_below - source
                albedo = (differ + (one - spread) * albedo) * inverse
                source = up + through * push
                beam_below = beam
        return (albedo, source, beam_below)

    albedo, source, beam = lax.fori_loop(
        0, groups, below_group, (albedo, albedo * surface, surface)
    )

    def folded(net):
        return sum(net[8 * k : 8 * (k + 1)] for k in range(gpoints // 8))

    partial_ref[pl.ds(pl.multiple_of(row * 8, 8), 8), :] = folded(beam - source)

    def down_group(group, diffuse):
        for j in range(GROUP):
            level = group * GROUP + j
            diffuse = gain_ref[level] * diffuse + offset_ref[level]
            net = folded(clear_ref[level] + open_ref[level] * diffuse)
            start = pl.multiple_of(((level + 1) * rows + row) * 8, 8)
            partial_ref[pl.ds(start, 8), :] = net
        return diffuse

    lax.fori_loop(0, groups, down_group, jnp.zeros_like(surface))

    @pl.when(row == rows - 1)
    def finish():
        scale = jnp.where(day_ref[...] == 1, level_count / gpoints, 0.0)

        def flux(level):
            start = level * rows * 8
            return sum(
                partial_ref[pl.ds(start + k, rows, stride=8), :] for k in range(8)
            )

        def level_heat(level, upper):
            lower = flux(level + 1)
            heat_ref[level] = jnp.where(scale > 0.0, scale * (upper - lower), 0.0)
            return lower

        lax.fori_loop(0, level_count, level_heat, flux(0))


def radiation(state, temper, cosine, ground, day, molecular, condensate):
    level_count, rows, lanes = temper.shape
    gpoints = molecular.shape[1]
    optics, slant = optics_matrices(molecular, condensate)
    weight = jnp.broadcast_to(condensate[6][:, None], (gpoints, lanes))
    groups = level_count // GROUP
    full = (level_count, gpoints, lanes)
    whole = pl.BlockSpec(memory_space=pltpu.VMEM)
    return pl.pallas_call(
        radiation_kernel,
        out_shape=jax.ShapeDtypeStruct(temper.shape, jnp.float32),
        grid=(rows,),
        in_specs=[whole] * 8,
        out_specs=whole,
        scratch_shapes=[
            pltpu.VMEM((level_count * TERMS * 8, lanes), jnp.float32),
            pltpu.VMEM((level_count * TERMS * 8, lanes), jnp.float32),
            pltpu.VMEM((groups, GROUP * TERMS, GROUP * lanes), jnp.bfloat16),
            pltpu.VMEM((groups, GROUP * TERMS, GROUP * lanes), jnp.bfloat16),
            pltpu.VMEM((level_count + 1, gpoints, lanes), jnp.float32),
            pltpu.VMEM(full, jnp.float32),
            pltpu.VMEM(full, jnp.float32),
            pltpu.VMEM(full, jnp.float32),
            pltpu.VMEM(full, jnp.float32),
            pltpu.VMEM(((level_count + 1) * rows * 8, lanes), jnp.float32),
        ],
        compiler_params=pltpu.CompilerParams(vmem_limit_bytes=60 * 1024 * 1024),
        name="radiation",
    )(state, temper, cosine, ground, day, optics, slant, weight)


def pair_average(values, before, beyond, node_index):
    return jnp.where(
        node_index == NODES - 1,
        0.5 * (values + beyond),
        jnp.where(node_index == 0, 0.5 * (before + values), values),
    )


def local(
    atmospheric_constituents,
    thermal_ratio,
    flow_velocity,
    solar_elevation_factor,
    ground_reflectivity,
    sunlit_indicator,
    molecular_optics_lookup,
    condensate_optics_lookup,
):
    level_count, line_count, span = thermal_ratio.shape
    radiative_warming_rate = radiation(
        atmospheric_constituents, thermal_ratio, solar_elevation_factor, ground_reflectivity,
        sunlit_indicator, molecular_optics_lookup, condensate_optics_lookup,
    )
    derivative = gll_derivative()
    x_derivative = jnp.asarray(np.kron(np.eye(span // NODES), derivative).T, jnp.float32)
    y_derivative = jnp.asarray(np.kron(np.eye(line_count // NODES), derivative), jnp.float32)
    x_nodes = (jnp.arange(span) % NODES)[None, None, :]
    y_nodes = (jnp.arange(line_count) % NODES)[None, :, None]

    def averaged(values):
        padded = padded_2(values, (("gx", 2),), 1)
        along_x = pair_average(values, padded[:, :, :-2], padded[:, :, 2:], x_nodes)
        padded_y = padded_2(along_x, (("gy", 1),), 1)
        return pair_average(along_x, padded_y[:, :-2], padded_y[:, 2:], y_nodes)

    def warming_change_rate(field_now):
        slope_x = jnp.dot(
            field_now.reshape(-1, span), x_derivative, precision=lax.Precision.HIGHEST
        ).reshape(field_now.shape)
        slope_y = jnp.einsum(
            "ij,ljx->lix", y_derivative, field_now, precision=lax.Precision.HIGHEST
        )
        return averaged(
            radiative_warming_rate - (flow_velocity[0] * slope_x + flow_velocity[1] * slope_y)
        )

    opening = thermal_ratio + TIME_INCREMENT * warming_change_rate(thermal_ratio)
    middle = 0.75 * thermal_ratio + 0.25 * (
        opening + TIME_INCREMENT * warming_change_rate(opening)
    )
    advected_thermal_ratio = 1.0 / 3.0 * thermal_ratio + 2.0 / 3.0 * (
        middle + TIME_INCREMENT * warming_change_rate(middle)
    )
    return (radiative_warming_rate, advected_thermal_ratio)


def solution(mesh):
    in_specs = (
        P(None, None, "gy", "gx"),
        P(None, "gy", "gx"),
        P(None, None, "gy", "gx"),
        P("gy", "gx"),
        P("gy", "gx"),
        P("gy", "gx"),
        P(),
        P(),
    )
    out_specs = (P(None, "gy", "gx"), P(None, "gy", "gx"))
    return jax.shard_map(local, mesh=mesh, in_specs=in_specs, out_specs=out_specs, check_vma=False)
```

time: 790 us -> 182 us (0.23)
  other arithmetic: 459 us -> 8.94 us
  local copies, waits for them, and re-layouts: 200 us -> 13.3 us
  Pallas kernels: 0 us -> 93.8 us
  waiting for transfers between devices: 82.5 us -> 40.1 us
  loops' own time: 9.14 us -> 0 us
    while x362 -> x0, other arithmetic: 238 us -> none
    reduce_sum x37 -> x0, other arithmetic: 123 us -> none  [the longest x18 88.9 us: below_step(): upper_part = jnp.sum(solar_weight * (beam_now - source_here), axis=0)]
    pallas_call x0 -> x1, Pallas kernels: none -> 93.8 us  [radiation(): pl.pallas_call(radiation_kernel, out_shape=jax.ShapeDtypeStruct(temper.sh...]
    gather x24 -> x0, local copies, waits for them, and re-layouts: 78.9 us -> none  [the longest x11 49.8 us: local(): jnp.searchsorted(rank_end, slot_ids, side='right')]
    dynamic_update_slice x90 -> x0, local copies, waits for them, and re-layouts: 61.9 us -> none  [the longest x54 61.6 us: block_nets(): lax.scan(beam_step, jnp.broadcast_to(cosine[None, :], plane), (coeffs,) +...]
    ppermute x4 -> x0, waiting for transfers between devices: 43.1 us -> none  [shifted(): return lax.ppermute(value, axis, pairs)]
    add x39 -> x0, other arithmetic: 36.5 us -> none  [the longest x18 29.4 us: down_step(): diffuse_new = gain_coef * diffuse_now + offset]
    concatenate x54 -> x0, other arithmetic: 34.3 us -> none  [the longest x36 30.9 us: block_nets(): lax.scan(below_step, (ground_full, ground_full * surface_beam), (coeffs,)...]
  transfers between devices with their start and end apart: 16 -> 12, of which waited for: 10 -> 9; matrix products, arithmetic and copies ran while one was open for 3% -> 0% of each run, Pallas kernels for 0% -> 0%
where the time goes in v1:
time: 182 us; the launch traced here: 180 us
  Pallas kernels  93.8 us (52%)
  waiting for transfers between devices  40.1 us (22%)
  starting transfers between devices  19 us (10%)
  local copies, waits for them, and re-layouts  13.3 us (7%)
  other arithmetic  8.94 us (5%)
  matrix products  3.66 us (2%)
    pallas_call x1, Pallas kernels, radiation(): pl.pallas_call(radiation_kernel, out_shape=jax.ShapeDtypeStruct(temper.sh...  93.8 us
    ppermute x6, waiting for transfers between devices, padded_2(): lax.ppermute(lax.slice_in_dim(block, 0, width, axis=dim), axis, backward)  21.8 us
    ppermute x6, waiting for transfers between devices, padded_2(): lax.ppermute(lax.slice_in_dim(block, block.shape[dim] - width, None, axis...  18.3 us
    ppermute x6, starting transfers between devices, padded_2(): lax.ppermute(lax.slice_in_dim(block, 0, width, axis=dim), axis, backward)  15.2 us
    unnamed x20, local copies, waits for them, and re-layouts  3.86 us
    ppermute x6, starting transfers between devices, padded_2(): lax.ppermute(lax.slice_in_dim(block, block.shape[dim] - width, None, axis...  3.81 us
  transfers between devices with their start and end apart: 12, of which 9 were waited for; matrix products, arithmetic and copies ran while one was open for 0% of the time, Pallas kernels for 0%

profile of v1, /device:TPU:1, one launch (start us, length us, event | category | flops | bytes accessed | tf_op | source)
XLA Modules:
  0.0 179.8 jit_solution(946446293065183432)
XLA Ops:
  0.6 0.0 copy-start.3
  0.6 0.9 broadcast_multiply_fusion.3
  1.6 0.9 slice_bitcast_fusion
  2.4 0.9 unstack.14
  3.3 0.8 constant_dynamic-update-slice_fusion.9
  4.1 0.1 pad.43.clone
  4.2 0.8 constant_dynamic-update-slice_fusion.8
  5.0 0.8 constant_dynamic-update-slice_fusion.7
  5.7 0.8 constant_dynamic-update-slice_fusion.3
  6.5 0.8 constant_dynamic-update-slice_fusion.2
  7.3 0.9 broadcast_multiply_fusion
  8.3 0.1 fusion.63
  8.5 0.1 fusion.64
  8.6 0.1 fusion.68
  8.8 0.2 fusion
  9.0 0.1 pad.27.clone
  9.0 0.4 maximum_bitcast_fusion
  9.4 1.4 copy.21
  10.8 2.9 %reshape.235 = bf16[9,784,128]{1,2,0:T(8,128)(2,1)} reshape(bf16[9,7,112,8,16]{2,1,4,3,0:T(8,128)(2,1)S(1)} %copy.21) | data formatting | bytes 3612672 | tf_op jit(solution)/shard_map/reshape | solution.py:81
  13.8 1.2 slice.174
  15.0 0.0 slice-start
  15.0 1.5 slice-done
  16.5 2.2 %copy.28.optics_ref = bf16[9,672,128]{2,1,0:T(8,128)(2,1)} copy(bf16[9,672,128]{1,2,0:T(8,128)(2,1)S(1)} %slice-done) | data formatting | bytes 3096576
  18.6 0.9 copy.29.slant_ref
  19.5 0.4 fusion.10
  19.9 0.7 broadcast_in_dim.105.weight_ref
  20.6 93.8 %radiation.1 = f32[72,8,128]{2,1,0:T(8,128)} custom-call(f32[5,72,8,128]{3,2,1,0:T(8,128)} %state_ref.1, f32[72,8,128]{2,1,0:T(8,128)} %temp_ref.1, f32[8,128]{1,0:T(8,128)} %cosine_ref.1, f32[8,128]{1,0:T(8,128)} %ground_ref.1, s32[8,128]{1,0:T(8,128)} %day_ref.1, bf16[9,672,128]{2,1,0:T(8,128)(2,1)} %copy.28.optics_ref, ...), custom_call_target="tpu_custom_call" | custom-call | tf_op jit(solution)/shard_map/radiation/pallas_call | solution.py:234
  114.4 1.4 fusion.9
  115.8 0.1 fusion.82
  115.9 5.2 %collective-permute-start = (f32[72,8,1]{2,1,0:T(8,128)S(1)}, f32[72,8,1]{2,1,0:T(8,128)S(1)}, u32[]{:S(2)}, u32[]{:S(2)}) collective-permute-start(f32[72,8,1]{2,1,0:T(8,128)S(1)} %get-tuple-element.18), channel_id=1, source_target_pairs={{4,0},{8,4},{12,8},{16,12},{20,16},{24,20},{28,24},{0,28},{5,1},{9... | collective-permute-start | bytes 6920 | tf_op jit(solution)/shard_map/ppermute | solution.py:29
  121.1 0.0 collective-permute-start.1
  121.1 5.7 %collective-permute-done = f32[72,8,1]{2,1,0:T(8,128)S(1)} collective-permute-done((f32[72,8,1]{2,1,0:T(8,128)S(1)}, f32[72,8,1]{2,1,0:T(8,128)S(1)}, u32[]{:S(2)}, u32[]{:S(2)}) %collective-permute-start) | collective-permute-done | bytes 2336 | tf_op jit(solution)/shard_map/ppermute | solution.py:29
  126.7 5.2 %collective-permute-done.1 = f32[72,8,1]{2,1,0:T(8,128)S(1)} collective-permute-done((f32[72,8,1]{2,1,0:T(8,128)S(1)}, f32[72,8,1]{2,1,0:T(8,128)S(1)}, u32[]{:S(2)}, u32[]{:S(2)}) %collective-permute-start.1) | collective-permute-done | bytes 2336 | tf_op jit(solution)/shard_map/ppermute | solution.py:26
  132.0 0.3 fusion.54
  132.4 1.3 collective-permute-start.2
  133.6 1.2 collective-permute-start.3
  134.8 2.0 %collective-permute-done.2 = f32[72,1,128]{2,1,0:T(1,128)S(1)} collective-permute-done((f32[72,1,128]{2,1,0:T(1,128)S(1)}, f32[72,1,128]{2,1,0:T(1,128)S(1)}, u32[]{:S(2)}, u32[]{:S(2)}) %collective-permute-start.2) | collective-permute-done | bytes 36896 | tf_op jit(solution)/shard_map/ppermute | solution.py:29
  136.8 0.0 collective-permute-done.3
  136.8 0.6 fusion.6
  137.4 0.6 fusion.3
  138.0 0.1 fusion.80
  138.1 4.1 %collective-permute-start.4 = (f32[72,8,1]{2,1,0:T(8,128)S(1)}, f32[72,8,1]{2,1,0:T(8,128)S(1)}, u32[]{:S(2)}, u32[]{:S(2)}) collective-permute-start(f32[72,8,1]{2,1,0:T(8,128)S(1)} %get-tuple-element.14), channel_id=1, source_target_pairs={{4,0},{8,4},{12,8},{16,12},{20,16},{24,20},{28,24},{0,28},{5,1},{9... | collective-permute-start | bytes 6920 | tf_op jit(solution)/shard_map/ppermute | solution.py:29
  142.2 0.0 collective-permute-start.5
  142.2 6.0 %collective-permute-done.4 = f32[72,8,1]{2,1,0:T(8,128)S(1)} collective-permute-done((f32[72,8,1]{2,1,0:T(8,128)S(1)}, f32[72,8,1]{2,1,0:T(8,128)S(1)}, u32[]{:S(2)}, u32[]{:S(2)}) %collective-permute-start.4) | collective-permute-done | bytes 2336 | tf_op jit(solution)/shard_map/ppermute | solution.py:29
  148.2 5.1 %collective-permute-done.5 = f32[72,8,1]{2,1,0:T(8,128)S(1)} collective-permute-done((f32[72,8,1]{2,1,0:T(8,128)S(1)}, f32[72,8,1]{2,1,0:T(8,128)S(1)}, u32[]{:S(2)}, u32[]{:S(2)}) %collective-permute-start.5) | collective-permute-done | bytes 2336 | tf_op jit(solution)/shard_map/ppermute | solution.py:26
  153.3 0.3 fusion.40
  153.7 1.1 collective-permute-start.6
  154.8 1.1 collective-permute-start.7
  155.8 1.6 collective-permute-done.6
  157.4 0.0 collective-permute-done.7
  157.4 0.4 fusion.34
  157.8 0.4 fusion.5
  158.2 0.4 fusion.4
  158.6 0.1 fusion.78
  158.7 3.0 %collective-permute-start.8 = (f32[72,8,1]{2,1,0:T(8,128)S(1)}, f32[72,8,1]{2,1,0:T(8,128)S(1)}, u32[]{:S(2)}, u32[]{:S(2)}) collective-permute-start(f32[72,8,1]{2,1,0:T(8,128)S(1)} %get-tuple-element.10), channel_id=1, source_target_pairs={{4,0},{8,4},{12,8},{16,12},{20,16},{24,20},{28,24},{0,28},{5,1},{9... | collective-permute-start | bytes 6920 | tf_op jit(solution)/shard_map/ppermute | solution.py:29
  161.7 0.0 collective-permute-start.9
  161.7 5.0 %collective-permute-done.8 = f32[72,8,1]{2,1,0:T(8,128)S(1)} collective-permute-done((f32[72,8,1]{2,1,0:T(8,128)S(1)}, f32[72,8,1]{2,1,0:T(8,128)S(1)}, u32[]{:S(2)}, u32[]{:S(2)}) %collective-permute-start.8) | collective-permute-done | bytes 2336 | tf_op jit(solution)/shard_map/ppermute | solution.py:29
  166.8 7.9 %collective-permute-done.9 = f32[72,8,1]{2,1,0:T(8,128)S(1)} collective-permute-done((f32[72,8,1]{2,1,0:T(8,128)S(1)}, f32[72,8,1]{2,1,0:T(8,128)S(1)}, u32[]{:S(2)}, u32[]{:S(2)}) %collective-permute-start.9) | collective-permute-done | bytes 2336 | tf_op jit(solution)/shard_map/ppermute | solution.py:26
  174.7 0.3 fusion.24
  175.1 0.6 collective-permute-start.10
  175.7 1.6 collective-permute-start.11
  177.2 1.6 collective-permute-done.10
  178.8 0.0 collective-permute-done.11
  178.8 0.9 fusion.18
  (37 shorter events, 0.3 us)
Async XLA Ops:
  0.6 7.8 %copy-start.3 = (f32[3,112,72]{1,2,0:T(8,128)S(1)}, f32[3,112,72]{1,2,0:T(8,128)}, u32[]{:S(2)}) copy-start(f32[3,112,72]{1,2,0:T(8,128)} %param.16) | copy-start | bytes 290308
  15.0 1.5 slice-start
  16.5 3.0 %copy-start = (f32[72,8,128]{2,1,0:T(8,128)S(1)}, f32[72,8,128]{2,1,0:T(8,128)}, u32[]{:S(2)}) copy-start(f32[72,8,128]{2,1,0:T(8,128)} %temp_ref.1) | copy-start | bytes 884740
  16.5 3.0 %copy-start.4 = (f32[2,72,8,128]{3,2,1,0:T(8,128)S(1)}, f32[2,72,8,128]{3,2,1,0:T(8,128)}, u32[]{:S(2)}) copy-start(f32[2,72,8,128]{3,2,1,0:T(8,128)} %param.12) | copy-start | bytes 1769476
  16.5 3.0 %copy-start.5 = (f32[128,128,1]{1,0,2:T(8,128)S(1)}, f32[128,128,1]{1,0,2:T(8,128)}, u32[]{:S(2)}) copy-start(f32[128,128,1]{1,0,2:T(8,128)} %constant.59) | copy-start | bytes 196612
  20.6 93.8 %copy-start.1 = (f32[72,8,128]{2,1,0:T(8,128)S(1)}, f32[72,8,128]{2,1,0:T(8,128)}, u32[]{:S(2)}) copy-start(f32[72,8,128]{2,1,0:T(8,128)} %temp_ref.1) | copy-start | bytes 884740
  20.6 93.8 %copy-start.6 = (f32[8,8,1]{1,0,2:T(8,128)S(1)}, f32[8,8,1]{1,0,2:T(8,128)}, u32[]{:S(2)}) copy-start(f32[8,8,1]{1,0,2:T(8,128)} %constant.60) | copy-start | bytes 772
  115.9 10.8 %collective-permute-start = (f32[72,8,1]{2,1,0:T(8,128)S(1)}, f32[72,8,1]{2,1,0:T(8,128)S(1)}, u32[]{:S(2)}, u32[]{:S(2)}) collective-permute-start(f32[72,8,1]{2,1,0:T(8,128)S(1)} %get-tuple-element.18), channel_id=1, source_target_pairs={{4,0},{8,4},{12,8},{16,12},{20,16},{24,20},{28,24},{0,28},{5,1},{9... | collective-permute-start | bytes 6920 | tf_op jit(solution)/shard_map/ppermute | solution.py:29
  121.1 10.9 %collective-permute-start.1 = (f32[72,8,1]{2,1,0:T(8,128)S(1)}, f32[72,8,1]{2,1,0:T(8,128)S(1)}, u32[]{:S(2)}, u32[]{:S(2)}) collective-permute-start(f32[72,8,1]{2,1,0:T(8,128)S(1)} %get-tuple-element.19), channel_id=1, source_target_pairs={{0,4},{4,8},{8,12},{12,16},{16,20},{20,24},{24,28},{28,0},{1,5},{5... | collective-permute-start | bytes 6920 | tf_op jit(solution)/shard_map/ppermute | solution.py:26
  132.0 5.4 %copy-start.2 = (f32[72,8,128]{2,1,0:T(8,128)S(1)}, f32[72,8,128]{2,1,0:T(8,128)}, u32[]{:S(2)}) copy-start(f32[72,8,128]{2,1,0:T(8,128)} %radiation.1) | copy-start | bytes 884740
  132.4 4.4 %collective-permute-start.2 = (f32[72,1,128]{2,1,0:T(1,128)S(1)}, f32[72,1,128]{2,1,0:T(1,128)S(1)}, u32[]{:S(2)}, u32[]{:S(2)}) collective-permute-start(f32[72,1,128]{2,1,0:T(1,128)S(1)} %get-tuple-element.16), channel_id=1, source_target_pairs={{1,0},{2,1},{3,2},{0,3},{5,4},{6,5},{7,6},{4,7},{9,8},{10,9},{11,1... | collective-permute-start | bytes 110600 | tf_op jit(solution)/shard_map/ppermute | solution.py:29
  133.6 3.2 %collective-permute-start.3 = (f32[72,1,128]{2,1,0:T(1,128)S(1)}, f32[72,1,128]{2,1,0:T(1,128)S(1)}, u32[]{:S(2)}, u32[]{:S(2)}) collective-permute-start(f32[72,1,128]{2,1,0:T(1,128)S(1)} %get-tuple-element.17), channel_id=1, source_target_pairs={{0,1},{1,2},{2,3},{3,0},{4,5},{5,6},{6,7},{7,4},{8,9},{9,10},{10,1... | collective-permute-start | bytes 110600 | tf_op jit(solution)/shard_map/ppermute | solution.py:26
  138.1 10.1 %collective-permute-start.4 = (f32[72,8,1]{2,1,0:T(8,128)S(1)}, f32[72,8,1]{2,1,0:T(8,128)S(1)}, u32[]{:S(2)}, u32[]{:S(2)}) collective-permute-start(f32[72,8,1]{2,1,0:T(8,128)S(1)} %get-tuple-element.14), channel_id=1, source_target_pairs={{4,0},{8,4},{12,8},{16,12},{20,16},{24,20},{28,24},{0,28},{5,1},{9... | collective-permute-start | bytes 6920 | tf_op jit(solution)/shard_map/ppermute | solution.py:29
  142.2 11.1 %collective-permute-start.5 = (f32[72,8,1]{2,1,0:T(8,128)S(1)}, f32[72,8,1]{2,1,0:T(8,128)S(1)}, u32[]{:S(2)}, u32[]{:S(2)}) collective-permute-start(f32[72,8,1]{2,1,0:T(8,128)S(1)} %get-tuple-element.15), channel_id=1, source_target_pairs={{0,4},{4,8},{8,12},{12,16},{16,20},{20,24},{24,28},{28,0},{1,5},{5... | collective-permute-start | bytes 6920 | tf_op jit(solution)/shard_map/ppermute | solution.py:26
  153.7 3.7 %collective-permute-start.6 = (f32[72,1,128]{2,1,0:T(1,128)S(1)}, f32[72,1,128]{2,1,0:T(1,128)S(1)}, u32[]{:S(2)}, u32[]{:S(2)}) collective-permute-start(f32[72,1,128]{2,1,0:T(1,128)S(1)} %get-tuple-element.12), channel_id=1, source_target_pairs={{1,0},{2,1},{3,2},{0,3},{5,4},{6,5},{7,6},{4,7},{9,8},{10,9},{11,1... | collective-permute-start | bytes 110600 | tf_op jit(solution)/shard_map/ppermute | solution.py:29
  154.8 2.6 %collective-permute-start.7 = (f32[72,1,128]{2,1,0:T(1,128)S(1)}, f32[72,1,128]{2,1,0:T(1,128)S(1)}, u32[]{:S(2)}, u32[]{:S(2)}) collective-permute-start(f32[72,1,128]{2,1,0:T(1,128)S(1)} %get-tuple-element.13), channel_id=1, source_target_pairs={{0,1},{1,2},{2,3},{3,0},{4,5},{5,6},{6,7},{7,4},{8,9},{9,10},{10,1... | collective-permute-start | bytes 110600 | tf_op jit(solution)/shard_map/ppermute | solution.py:26
  158.7 8.0 %collective-permute-start.8 = (f32[72,8,1]{2,1,0:T(8,128)S(1)}, f32[72,8,1]{2,1,0:T(8,128)S(1)}, u32[]{:S(2)}, u32[]{:S(2)}) collective-permute-start(f32[72,8,1]{2,1,0:T(8,128)S(1)} %get-tuple-element.10), channel_id=1, source_target_pairs={{4,0},{8,4},{12,8},{16,12},{20,16},{24,20},{28,24},{0,28},{5,1},{9... | collective-permute-start | bytes 6920 | tf_op jit(solution)/shard_map/ppermute | solution.py:29
  161.7 13.0 %collective-permute-start.9 = (f32[72,8,1]{2,1,0:T(8,128)S(1)}, f32[72,8,1]{2,1,0:T(8,128)S(1)}, u32[]{:S(2)}, u32[]{:S(2)}) collective-permute-start(f32[72,8,1]{2,1,0:T(8,128)S(1)} %get-tuple-element.11), channel_id=1, source_target_pairs={{0,4},{4,8},{8,12},{12,16},{16,20},{20,24},{24,28},{28,0},{1,5},{5... | collective-permute-start | bytes 6920 | tf_op jit(solution)/shard_map/ppermute | solution.py:26
  175.1 3.8 %collective-permute-start.10 = (f32[72,1,128]{2,1,0:T(1,128)S(1)}, f32[72,1,128]{2,1,0:T(1,128)S(1)}, u32[]{:S(2)}, u32[]{:S(2)}) collective-permute-start(f32[72,1,128]{2,1,0:T(1,128)S(1)} %get-tuple-element.8), channel_id=1, source_target_pairs={{1,0},{2,1},{3,2},{0,3},{5,4},{6,5},{7,6},{4,7},{9,8},{10,9},{11,1... | collective-permute-start | bytes 110600 | tf_op jit(solution)/shard_map/ppermute | solution.py:29
  175.7 3.1 %collective-permute-start.11 = (f32[72,1,128]{2,1,0:T(1,128)S(1)}, f32[72,1,128]{2,1,0:T(1,128)S(1)}, u32[]{:S(2)}, u32[]{:S(2)}) collective-permute-start(f32[72,1,128]{2,1,0:T(1,128)S(1)} %get-tuple-element.9), channel_id=1, source_target_pairs={{0,1},{1,2},{2,3},{3,0},{4,5},{5,6},{6,7},{7,4},{8,9},{9,10},{10,1... | collective-permute-start | bytes 110600 | tf_op jit(solution)/shard_map/ppermute | solution.py:26

commit v2 on v1

v2 whole, which is shorter than its diff:
```python
import functools

import jax
import jax.numpy as jnp
import numpy as np
from jax import lax
from jax.experimental import pallas as pl
from jax.experimental.pallas import tpu as pltpu
from jax.sharding import PartitionSpec as P

NODES = 4
TIME_INCREMENT = 0.05
EDGE = 16
LOG2E = 1.4426950408889634

GROUP = 8
TERMS = 16
BLOCK = 4
QUANTITIES = 3


def gll_derivative():
    points = np.array([-1.0, -1.0 / np.sqrt(5.0), 1.0 / np.sqrt(5.0), 1.0])
    legendre = 0.5 * (5.0 * points**3 - 3.0 * points)
    derivative = np.zeros((4, 4))
    for source in range(4):
        for target in range(4):
            if source != target:
                derivative[source, target] = legendre[source] / (
                    legendre[target] * (points[source] - points[target])
                )
    derivative[0, 0] = -3.0
    derivative[3, 3] = 3.0
    return derivative


def high_low(values):
    high = values.astype(jnp.bfloat16)
    return high, (values - high.astype(jnp.float32)).astype(jnp.bfloat16)


def optics_matrices(molecular_ref, table_ref, optics_ref):
    gpoints, level_count = molecular_ref.shape[1:]
    groups = level_count // GROUP
    width = GROUP * TERMS
    level = lax.broadcasted_iota(jnp.int32, (level_count, groups * width), 0)
    lane = lax.broadcasted_iota(jnp.int32, (level_count, groups * width), 1)
    here = level == lane // TERMS
    term = lane % TERMS
    gases = []
    for k in range(3):
        high, low = high_low(molecular_ref[k])
        spread = [
            jnp.where(here & chosen, 1.0, 0.0).astype(jnp.bfloat16)
            for chosen in ((term == k) | (term == k + 10), term == k + 5)
        ]
        gases.append(
            jnp.dot(high, spread[0], preferred_element_type=jnp.float32)
            + jnp.dot(low, spread[1], preferred_element_type=jnp.float32)
        )
    w = [table_ref[:, n : n + 1] for n in range(6)]
    ls, li = w[0] * w[1], w[3] * w[4]
    la, ia = w[0] * (1.0 - w[1]), w[3] * (1.0 - w[4])
    term = lax.broadcasted_iota(jnp.int32, (gpoints, width), 1) % TERMS

    def water(*values):
        total = jnp.zeros((gpoints, width), jnp.float32)
        for k, value in zip((3, 4), values):
            high = value.astype(jnp.bfloat16).astype(jnp.float32)
            total = jnp.where((term == k) | (term == k + 10), high, total)
            total = jnp.where(term == k + 5, value - high, total)
        return total

    absorbed = gases[0] + gases[1]
    gas = absorbed + gases[2]
    pairs = (
        (absorbed, water(la, ia)),
        (gas, water(la + ls * (1.0 - w[2]), ia + li * (1.0 - w[5]))),
        (gas + gas, water(2.0 * w[0], 2.0 * w[3])),
    )
    for n, (values, constant) in enumerate(pairs):
        for group in range(groups):
            optics_ref[group, n * gpoints : (n + 1) * gpoints, :] = (
                values[:, group * width : (group + 1) * width] + constant
            ).astype(jnp.bfloat16)


def pack_edges(source_ref, base, part, first_ref, last_ref):
    lanes = source_ref.shape[-1]
    lane = lax.broadcasted_iota(jnp.int32, (8, lanes), 1)
    first = last = jnp.zeros((8, lanes), jnp.float32)
    for j in range(8):
        tile = source_ref[base * 8 + j]
        chosen = lane // EDGE == j
        first = jnp.where(chosen, tile if j == 0 else pltpu.roll(tile, EDGE * j, 1), first)
        turn = (EDGE * (j + 1)) % lanes
        last = jnp.where(chosen, tile if turn == 0 else pltpu.roll(tile, turn, 1), last)
    first_ref[part] = first
    last_ref[part] = last


def radiation_kernel(
    state_ref, temp_ref, cosine_ref, ground_ref, day_ref, molecular_ref, table_ref,
    heat_ref, first_ref, last_ref,
    optics_ref, weight_ref, terms_ref, right_ref, depths_ref, gain_ref, offset_ref, direct_ref, partial_ref, ratio_ref,
    source_ref, slant_ref,
):
    level_count = temp_ref.shape[0]
    gpoints = molecular_ref.shape[1]
    lanes = temp_ref.shape[2]
    row = pl.program_id(0)
    rows = pl.num_programs(0)
    blocks = level_count // BLOCK

    @pl.when(row == 0)
    def prepare():
        optics_matrices(molecular_ref, table_ref, optics_ref)
        weight_ref[...] = jnp.broadcast_to(table_ref[:, 6:7], (gpoints, lanes))
        right_ref[...] = jnp.zeros_like(right_ref)

        def level(l, carry):
            thickness = state_ref[2, l]
            weighted = thickness * temp_ref[l] * temp_ref[l]
            values = (
                weighted * state_ref[0, l], weighted * state_ref[1, l], thickness,
                state_ref[3, l], state_ref[4, l],
            )
            for k, value in enumerate(values):
                high = value.astype(jnp.bfloat16).astype(jnp.float32)
                for place, part in ((k, high), (k + 5, high), (k + 10, value - high)):
                    start = pl.multiple_of((l * TERMS + place) * 8, 8)
                    terms_ref[pl.ds(start, 8), :] = part
            last = pl.multiple_of((l * TERMS + 15) * 8, 8)
            terms_ref[pl.ds(last, 8), :] = jnp.zeros((8, lanes), jnp.float32)
            return carry

        lax.fori_loop(0, level_count, level, 0)

    def place_group(group, carry):
        for j in range(GROUP):
            start = (group * GROUP + j) * TERMS * 8 + row
            tile = terms_ref[pl.ds(start, TERMS, stride=8), :].astype(jnp.bfloat16)
            half = lanes * (j % 2)
            pair = group * (GROUP // 2) + j // 2
            right_ref[pair, TERMS * j : TERMS * (j + 1), half : half + lanes] = tile
        return carry

    lax.fori_loop(0, level_count // GROUP, place_group, 0)

    cosine = cosine_ref[pl.ds(row, 1), :]
    ground = ground_ref[pl.ds(row, 1), :]
    slant_ref[...] = jnp.broadcast_to((-0.5 * LOG2E) / cosine, (8, lanes))

    def over_rows(values):
        return jnp.broadcast_to(values[None], (gpoints // 8, 8, lanes)).reshape(gpoints, lanes)

    clear = 1.0 / (1.0 - ground)
    ratio_ref[...] = over_rows(jnp.broadcast_to((1.0 + ground) * clear, (8, lanes)))
    source_ref[...] = over_rows(jnp.broadcast_to(2.0 * ground * clear, (8, lanes)))

    def fill(block):
        for p in range(BLOCK // 2):
            pair = block * (BLOCK // 2) + p
            depths_ref[p] = jnp.dot(
                optics_ref[pair // (GROUP // 2)], right_ref[pair],
                preferred_element_type=jnp.float32,
            )

    def below_block(step, carry):
        block = blocks - 1 - step
        ratio, source = ratio_ref[...], source_ref[...]
        slant = over_rows(slant_ref[...])
        for j in reversed(range(BLOCK)):
            level = block * BLOCK + j
            part = depths_ref.at[j // 2, :, (j % 2) * lanes : (j % 2 + 1) * lanes]
            a, b, depth = [part[n * gpoints : (n + 1) * gpoints] for n in range(QUANTITIES)]
            away = b - a
            along = (depth - a) - b
            square = a * b
            inverse_root = lax.rsqrt(square)
            h = jnp.tanh(square * inverse_root)
            g = h * inverse_root
            g = g + g
            s, p = a * g, b * g
            h2 = h * h
            one = 1.0 + h2
            through = 1.0 - h2
            inverse = 1.0 / (one + s * ratio)
            direct = jnp.exp2(depth * slant)
            factor = (1.0 - direct) * (1.0 / depth)
            up, down = factor * away, factor * along
            push = inverse * (direct * source + (ratio - 1.0) * down)
            ratio = (one * ratio + p) * inverse
            gain = through * inverse
            source = through * push + (ratio + 1.0) * up
            gain_ref[level] = gain
            offset_ref[level] = (gain * up + down) - s * push
            direct_ref[level] = direct
        ratio_ref[...] = ratio
        source_ref[...] = source
        fill(jnp.maximum(block - 1, 0))
        return carry

    fill(blocks - 1)
    lax.fori_loop(0, blocks, below_block, 0)

    def folded(net):
        return sum(net[8 * k : 8 * (k + 1)] for k in range(gpoints // 8))

    beam = weight_ref[...] * cosine
    net = -(source_ref[...] * beam) / (1.0 + ratio_ref[...])
    partial_ref[pl.ds(pl.multiple_of(row * 8, 8), 8), :] = folded(beam) + folded(net)

    def down_group(group, carry):
        net, beam = carry
        for j in range(GROUP):
            level = group * GROUP + j
            net = gain_ref[level] * net + offset_ref[level] * beam
            beam = beam * direct_ref[level]
            start = pl.multiple_of(((level + 1) * rows + row) * 8, 8)
            partial_ref[pl.ds(start, 8), :] = folded(net) + folded(beam)
        return (net, beam)

    lax.fori_loop(0, level_count // GROUP, down_group, (net, beam))

    @pl.when(row == rows - 1)
    def finish():
        scale = jnp.where(day_ref[...] == 1, level_count / gpoints, 0.0)

        def flux(level):
            start = level * rows * 8
            return sum(
                partial_ref[pl.ds(start + k, rows, stride=8), :] for k in range(8)
            )

        def level_heat(level, upper):
            lower = flux(level + 1)
            heat_ref[level] = jnp.where(scale > 0.0, scale * (upper - lower), 0.0)
            return lower

        lax.fori_loop(0, level_count, level_heat, flux(0))

        def pack(part, carry):
            pack_edges(heat_ref, part, part, first_ref, last_ref)
            return carry

        lax.fori_loop(0, level_count // 8, pack, 0)


def radiation(state, temper, cosine, ground, day, molecular, condensate):
    level_count, rows, lanes = temper.shape
    gpoints = molecular.shape[1]
    full = pltpu.VMEM((level_count, gpoints, lanes), jnp.float32)
    plane = pltpu.VMEM((gpoints, lanes), jnp.float32)
    whole = pl.BlockSpec(memory_space=pltpu.VMEM)
    edge = jax.ShapeDtypeStruct((level_count // 8, rows, lanes), jnp.float32)
    return pl.pallas_call(
        radiation_kernel,
        out_shape=(jax.ShapeDtypeStruct(temper.shape, jnp.float32), edge, edge),
        grid=(rows,),
        in_specs=[whole] * 7,
        out_specs=(whole,) * 3,
        scratch_shapes=[
            pltpu.VMEM((level_count // GROUP, QUANTITIES * gpoints, GROUP * TERMS), jnp.bfloat16),
            plane,
            pltpu.VMEM((level_count * TERMS * 8, lanes), jnp.float32),
            pltpu.VMEM((level_count // 2, GROUP * TERMS, 2 * lanes), jnp.bfloat16),
            pltpu.VMEM((BLOCK // 2, QUANTITIES * gpoints, 2 * lanes), jnp.float32),
            full, full, full,
            pltpu.VMEM(((level_count + 1) * rows * 8, lanes), jnp.float32),
            plane, plane,
            pltpu.VMEM((8, lanes), jnp.float32),
        ],
        compiler_params=pltpu.CompilerParams(vmem_limit_bytes=60 * 1024 * 1024),
        cost_estimate=pl.CostEstimate(
            flops=45 * level_count * gpoints * rows * lanes, bytes_accessed=4 * 8 * temper.size,
            transcendentals=5 * level_count * gpoints * rows * lanes,
        ),
        name="radiation",
    )(state, temper, cosine, ground, day, molecular, condensate.T)


def pack_kernel(temp_ref, flow_ref, first_ref, last_ref):
    parts = temp_ref.shape[0] // 8
    for n, ref in enumerate((temp_ref, flow_ref.at[0], flow_ref.at[1])):
        def pack(part, carry, ref=ref, n=n):
            pack_edges(ref, part, n * parts + part, first_ref, last_ref)
            return carry

        lax.fori_loop(0, parts, pack, 0)


def packed_edges(temper, flow):
    level_count, rows, lanes = temper.shape
    whole = pl.BlockSpec(memory_space=pltpu.VMEM)
    edge = jax.ShapeDtypeStruct((3 * level_count // 8, rows, lanes), jnp.float32)
    return pl.pallas_call(
        pack_kernel, out_shape=(edge, edge), in_specs=[whole] * 2, out_specs=(whole, whole),
        name="pack",
    )(temper, flow)


def node_coefficients(shape, axis):
    derivative = gll_derivative()
    node = lax.broadcasted_iota(jnp.int32, shape, axis) % NODES
    result = {}
    for shift in range(1 - NODES, NODES):
        value = jnp.zeros(shape, jnp.float32)
        for i in range(NODES):
            if 0 <= i + shift < NODES and derivative[i, i + shift] != 0.0:
                value = jnp.where(node == i, np.float32(derivative[i, i + shift]), value)
        result[shift] = value
    return result


def slope(tile, weights, axis):
    size = tile.shape[axis]
    total = weights[0] * tile
    for shift, weight in weights.items():
        if shift:
            total = total + weight * pltpu.roll(tile, -shift % size, axis)
    return total


def along_x(main, side):
    lane = lax.broadcasted_iota(jnp.int32, main.shape, 1)
    lanes = main.shape[1]
    node = lane % NODES
    before = [pltpu.roll(tile, 1, 1) for tile in (main, side)]
    beyond = [pltpu.roll(tile, lanes - 1, 1) for tile in (main, side)]
    results = []
    for n, tile in enumerate((main, side)):
        back = jnp.where(lane == 0, before[1 - n], before[n])
        ahead = jnp.where(lane == lanes - 1, beyond[1 - n], beyond[n])
        other = jnp.where(node == NODES - 1, ahead, jnp.where(node == 0, back, tile))
        results.append(0.5 * (tile + other))
    return results


def along_y(tile, below, above):
    row = lax.broadcasted_iota(jnp.int32, tile.shape, 0)
    rows = tile.shape[0]
    node = row % NODES
    back = jnp.where(row == 0, below, pltpu.roll(tile, 1, 0))
    ahead = jnp.where(row == rows - 1, above, pltpu.roll(tile, rows - 1, 0))
    other = jnp.where(node == NODES - 1, ahead, jnp.where(node == 0, back, tile))
    return 0.5 * (tile + other)


def side_tile(after_ref, before_ref, part, j):
    lanes = after_ref.shape[-1]
    lane = lax.broadcasted_iota(jnp.int32, after_ref.shape[1:], 1)
    after, before = after_ref[part], before_ref[part]
    turn = (lanes - EDGE * j) % lanes
    after = after if turn == 0 else pltpu.roll(after, turn, 1)
    turn = (2 * lanes - EDGE * (j + 1)) % lanes
    before = before if turn == 0 else pltpu.roll(before, turn, 1)
    return jnp.where(lane < EDGE, after, jnp.where(lane >= lanes - EDGE, before, 0.0))


def write_lines(field_ref, low_ref, high_ref, level_count, rows):
    for n in range(2):
        start = n * level_count * rows
        low_ref[n] = field_ref[pl.ds(start, level_count, stride=rows), :]
        high_ref[n] = field_ref[pl.ds(start + rows - 1, level_count, stride=rows), :]


def first_stage_kernel(
    heat_ref, temp_ref, flow_ref, after_ref, before_ref, heat_after_ref, heat_before_ref,
    out_ref, low_ref, high_ref, flow_side_ref,
):
    level_count, rows, lanes = temp_ref.shape
    parts = level_count // 8
    x_weights = node_coefficients((rows, lanes), 1)
    y_weights = node_coefficients((rows, lanes), 0)

    def eight(part, carry):
        for j in range(8):
            level = part * 8 + j
            sides = [side_tile(after_ref, before_ref, n * parts + part, j) for n in range(3)]
            heat_side = side_tile(heat_after_ref, heat_before_ref, part, j)
            flow_side_ref[0, level], flow_side_ref[1, level] = sides[1], sides[2]
            raw = []
            for t, u, v, heat in (
                (temp_ref[level], flow_ref[0, level], flow_ref[1, level], heat_ref[level]),
                (*sides, heat_side),
            ):
                change = heat - (u * slope(t, x_weights, 1) + v * slope(t, y_weights, 0))
                raw.append(TIME_INCREMENT * change)
            for n, tile in enumerate(along_x(*raw)):
                start = pl.multiple_of((n * level_count + level) * rows, 8)
                out_ref[pl.ds(start, rows), :] = tile
        return carry

    lax.fori_loop(0, parts, eight, 0)
    write_lines(out_ref, low_ref, high_ref, level_count, rows)


def next_stage_kernel(
    share, field_ref, below_ref, above_ref, flow_ref, flow_side_ref, sum_ref,
    out_ref, low_ref, high_ref, total_ref,
):
    level_count, rows, lanes = flow_ref.shape[1:]
    x_weights = node_coefficients((rows, lanes), 1)
    y_weights = node_coefficients((rows, lanes), 0)

    def eight(part, carry):
        for j in range(8):
            level = part * 8 + j
            raw = []
            for n, flows in enumerate((flow_ref, flow_side_ref)):
                start = pl.multiple_of((n * level_count + level) * rows, 8)
                tile = along_y(
                    field_ref[pl.ds(start, rows), :],
                    below_ref[n, pl.ds(level, 1), :], above_ref[n, pl.ds(level, 1), :],
                )
                if n == 0:
                    total_ref[level] = sum_ref[level] + share * tile
                change = flows[0, level] * slope(tile, x_weights, 1)
                change = change + flows[1, level] * slope(tile, y_weights, 0)
                raw.append(-TIME_INCREMENT * change)
            for n, tile in enumerate(along_x(*raw)):
                start = pl.multiple_of((n * level_count + level) * rows, 8)
                out_ref[pl.ds(start, rows), :] = tile
        return carry

    lax.fori_loop(0, level_count // 8, eight, 0)
    write_lines(out_ref, low_ref, high_ref, level_count, rows)


def last_kernel(share, field_ref, below_ref, above_ref, sum_ref, total_ref):
    level_count, rows, lanes = sum_ref.shape

    def eight(part, carry):
        for j in range(8):
            level = part * 8 + j
            start = pl.multiple_of(level * rows, 8)
            tile = along_y(
                field_ref[pl.ds(start, rows), :],
                below_ref[0, pl.ds(level, 1), :], above_ref[0, pl.ds(level, 1), :],
            )
            total_ref[level] = sum_ref[level] + share * tile
        return carry

    lax.fori_loop(0, level_count // 8, eight, 0)


def shifted(value, axis, steps):
    count = lax.axis_size(axis)
    return lax.ppermute(value, axis, [(i, (i + steps) % count) for i in range(count)])


def local(
    atmospheric_constituents,
    thermal_ratio,
    flow_velocity,
    solar_elevation_factor,
    ground_reflectivity,
    sunlit_indicator,
    molecular_optics_lookup,
    condensate_optics_lookup,
):
    level_count, rows, lanes = thermal_ratio.shape
    field = jax.ShapeDtypeStruct(thermal_ratio.shape, jnp.float32)
    wide = jax.ShapeDtypeStruct((2 * level_count * rows, lanes), jnp.float32)
    line = jax.ShapeDtypeStruct((2, level_count, lanes), jnp.float32)
    whole = pl.BlockSpec(memory_space=pltpu.VMEM)

    def call(kernel, name, outs, *values):
        return pl.pallas_call(
            kernel, out_shape=outs, in_specs=[whole] * len(values),
            out_specs=jax.tree.map(lambda _: whole, outs), name=name,
        )(*values)

    first, last = packed_edges(thermal_ratio, flow_velocity)
    after, before = shifted(first, "gx", -1), shifted(last, "gx", 1)
    heat, heat_first, heat_last = radiation(
        atmospheric_constituents, thermal_ratio, solar_elevation_factor, ground_reflectivity,
        sunlit_indicator, molecular_optics_lookup, condensate_optics_lookup,
    )
    heat_after, heat_before = shifted(heat_first, "gx", -1), shifted(heat_last, "gx", 1)
    flow_side = jax.ShapeDtypeStruct(flow_velocity.shape, jnp.float32)
    wave, low, high, flow_side = call(
        first_stage_kernel, "first_stage", (wide, line, line, flow_side),
        heat, thermal_ratio, flow_velocity, after, before, heat_after, heat_before,
    )
    total = thermal_ratio
    for name, share in (("second_stage", 1.0), ("third_stage", 0.5)):
        below, above = shifted(high, "gy", 1), shifted(low, "gy", -1)
        wave, low, high, total = call(
            functools.partial(next_stage_kernel, share), name, (wide, line, line, field),
            wave, below, above, flow_velocity, flow_side, total,
        )
    below, above = shifted(high, "gy", 1), shifted(low, "gy", -1)
    total = call(
        functools.partial(last_kernel, 1.0 / 6.0), "last_stage", field, wave, below, above, total
    )
    return (heat, total)


def solution(mesh):
    in_specs = (
        P(None, None, "gy", "gx"),
        P(None, "gy", "gx"),
        P(None, None, "gy", "gx"),
        P("gy", "gx"),
        P("gy", "gx"),
        P("gy", "gx"),
        P(),
        P(),
    )
    out_specs = (P(None, "gy", "gx"), P(None, "gy", "gx"))
    return jax.shard_map(local, mesh=mesh, in_specs=in_specs, out_specs=out_specs, check_vma=False)
```

time: 182 us -> 144 us (0.79); the launches traced: 180 us -> 144 us
  waiting for transfers between devices: 40.1 us -> 16.8 us
  Pallas kernels: 93.8 us -> 107 us
  other arithmetic: 8.94 us -> 0 us
  local copies, waits for them, and re-layouts: 13.3 us -> 5.64 us
  starting transfers between devices: 19 us -> 14.1 us
  matrix products: 3.66 us -> 0 us
    ppermute x12 -> x10, waiting for transfers between devices: 40.1 us -> 16.8 us  [shifted(): lax.ppermute(value, axis, [(i, (i + steps) % count) for i in range(count)])]
    pallas_call x1 -> x6, Pallas kernels: 93.8 us -> 107 us  [the longest x1 84.2 us: radiation(): pl.pallas_call(radiation_kernel, out_shape=(jax.ShapeDtypeStruct(temper.s...]
    ppermute x12 -> x10, starting transfers between devices: 19 us -> 14.1 us  [shifted(): lax.ppermute(value, axis, [(i, (i + steps) % count) for i in range(count)])]
    dot_general x6 -> x0, matrix products: 3.66 us -> none  [the longest x3 2.31 us: warming_change_rate(): jnp.einsum('ij,ljx->lix', y_derivative, field_now, precision=lax.Precisio...]
    unnamed x9 -> x0, other arithmetic: 3.4 us -> none
    slice x9 -> x0, local copies, waits for them, and re-layouts: 3.25 us -> none  [the longest x3 2.68 us: optics_matrices(): return (terms[:, :QUANTITIES * gpoints], terms[:, QUANTITIES * gpoints:])]
    reshape x1 -> x0, local copies, waits for them, and re-layouts: 2.95 us -> none  [optics_matrices(): terms.transpose(3, 0, 2, 4, 1)]
    mul x2 -> x0, other arithmetic: 1.83 us -> none  [the longest x1 0.92 us: optics_matrices(): 0.5 * b]
  transfers between devices with their start and end apart: 12 -> 10, of which waited for: 9 -> 8; matrix products, arithmetic and copies ran while one was open for 0% -> 2% of each run, Pallas kernels for 0% -> 58%
where the time goes in v2:
time: 144 us
  Pallas kernels  107 us (74%)
  waiting for transfers between devices  16.8 us (12%)
  starting transfers between devices  14.1 us (10%)
  local copies, waits for them, and re-layouts  5.64 us (4%)
    pallas_call x1, Pallas kernels, radiation(): pl.pallas_call(radiation_kernel, out_shape=(jax.ShapeDtypeStruct(temper.s...  84.2 us
    pallas_call x4, Pallas kernels, call(): pl.pallas_call(kernel, out_shape=outs, in_specs=[whole] * len(values), ou...  18.8 us
    ppermute x10, waiting for transfers between devices, shifted(): lax.ppermute(value, axis, [(i, (i + steps) % count) for i in range(count)])  16.8 us
    ppermute x10, starting transfers between devices, shifted(): lax.ppermute(value, axis, [(i, (i + steps) % count) for i in range(count)])  14.1 us
    unnamed x22, local copies, waits for them, and re-layouts  5.64 us
    pallas_call x1, Pallas kernels, packed_edges(): pl.pallas_call(pack_kernel, out_shape=(edge, edge), in_specs=[whole] * 2,...  4.07 us
  transfers between devices with their start and end apart: 10, of which 8 were waited for; matrix products, arithmetic and copies ran while one was open for 2% of the time, Pallas kernels for 58%

profile of v2, /device:TPU:1, one launch (start us, length us, event | category | flops | bytes accessed | tf_op | source)
XLA Modules:
  0.0 144.1 jit_solution(6543130183728551347)
XLA Ops:
  0.6 4.1 %pack.1 = (f32[27,8,128]{2,1,0:T(8,128)}, f32[27,8,128]{2,1,0:T(8,128)}) custom-call(f32[72,8,128]{2,1,0:T(8,128)} %sum_ref.1, f32[2,72,8,128]{3,2,1,0:T(8,128)} %flow_ref.7), custom_call_target="tpu_custom_call" | custom-call | tf_op jit(solution)/shard_map/pack/pallas_call | solution.py:297
  4.7 5.1 %collective-permute-start = (f32[27,8,128]{2,1,0:T(8,128)}, f32[27,8,128]{2,1,0:T(8,128)S(1)}, u32[]{:S(2)}, u32[]{:S(2)}) collective-permute-start(f32[27,8,128]{2,1,0:T(8,128)} %get-tuple-element.20), channel_id=1, source_target_pairs={{0,28},{4,0},{8,4},{12,8},{16,12},{20,16},{24,20},{28,24},{1,29},{... | collective-permute-start | bytes 331784 | tf_op jit(solution)/shard_map/ppermute | solution.py:450
  9.8 0.0 collective-permute-start.1
  9.8 1.4 copy.10
  11.2 1.7 %copy.11.molecular_ref = f32[3,112,72]{2,1,0:T(8,128)} copy(f32[3,112,72]{1,2,0:T(8,128)} %param.14) | data formatting | bytes 193536 | tf_op args[6]
  12.9 84.2 %radiation.1 = (f32[72,8,128]{2,1,0:T(8,128)}, f32[9,8,128]{2,1,0:T(8,128)}, f32[9,8,128]{2,1,0:T(8,128)}) custom-call(f32[5,72,8,128]{3,2,1,0:T(8,128)} %state_ref.1, f32[72,8,128]{2,1,0:T(8,128)} %sum_ref.1, f32[8,128]{1,0:T(8,128)} %cosine_ref.1, f32[8,128]{1,0:T(8,128)} %ground_ref.1, s32[8,128]{1,0:T(8,128)} %day_ref.1, ...), custom_call_target="tpu_custom_call" | custom-call | flops 371589120 | bytes 2359296 | tf_op jit(solution)/shard_map/radiation/pallas_call | solution.py:257
  97.1 4.2 %collective-permute-start.2 = (f32[9,8,128]{2,1,0:T(8,128)}, f32[9,8,128]{2,1,0:T(8,128)S(1)}, u32[]{:S(2)}, u32[]{:S(2)}) collective-permute-start(f32[9,8,128]{2,1,0:T(8,128)} %get-tuple-element.22), channel_id=1, source_target_pairs={{0,28},{4,0},{8,4},{12,8},{16,12},{20,16},{24,20},{28,24},{1,29},{... | collective-permute-start | bytes 110600 | tf_op jit(solution)/shard_map/ppermute | solution.py:450
  101.2 0.0 collective-permute-start.3
  101.2 1.4 collective-permute-done.2.heat_after_ref
  102.6 0.0 copy-start.8
  102.6 4.3 %collective-permute-done.3.heat_before_ref = f32[9,8,128]{2,1,0:T(8,128)S(1)} collective-permute-done((f32[9,8,128]{2,1,0:T(8,128)}, f32[9,8,128]{2,1,0:T(8,128)S(1)}, u32[]{:S(2)}, u32[]{:S(2)}) %collective-permute-start.3) | collective-permute-done | bytes 36896 | tf_op jit(solution)/shard_map/ppermute | solution.py:450
  106.9 0.0 copy-start.9
  106.9 0.0 collective-permute-done.after_ref
  106.9 0.0 copy-start
  107.0 0.0 collective-permute-done.1.before_ref
  107.0 0.0 copy-start.1
  107.0 0.0 copy-done.8
  107.0 0.6 copy-done.9
  107.6 0.1 copy-done
  107.6 0.0 copy-done.1
  107.6 6.3 %first_stage.1 = (f32[1152,128]{1,0:T(8,128)}, f32[2,72,128]{2,1,0:T(8,128)}, f32[2,72,128]{2,1,0:T(8,128)}, f32[2,72,8,128]{3,2,1,0:T(8,128)}) custom-call(f32[72,8,128]{2,1,0:T(8,128)} %get-tuple-element.17.heat_ref, f32[72,8,128]{2,1,0:T(8,128)} %sum_ref.1, f32[2,72,8,128]{3,2,1,0:T(8,128)} %flow_ref.7, f32[27,8,128]{2,1,0:T(8,128)} %copy-done, ...), custom_call_target="tpu_custom_call" | custom-call | tf_op jit(solution)/shard_map/first_stage/pallas_call | solution.py:470
  113.9 3.8 %collective-permute-start.4 = (f32[2,72,128]{2,1,0:T(8,128)}, f32[2,72,128]{2,1,0:T(8,128)S(1)}, u32[]{:S(2)}, u32[]{:S(2)}) collective-permute-start(f32[2,72,128]{2,1,0:T(8,128)} %get-tuple-element.25), channel_id=1, source_target_pairs={{0,1},{1,2},{2,3},{3,0},{4,5},{5,6},{6,7},{7,4},{8,9},{9,10},{10,1... | collective-permute-start | bytes 221192 | tf_op jit(solution)/shard_map/ppermute | solution.py:450
  117.7 0.0 collective-permute-start.5
  117.7 1.7 %collective-permute-done.4.below_ref = f32[2,72,128]{2,1,0:T(8,128)S(1)} collective-permute-done((f32[2,72,128]{2,1,0:T(8,128)}, f32[2,72,128]{2,1,0:T(8,128)S(1)}, u32[]{:S(2)}, u32[]{:S(2)}) %collective-permute-start.4) | collective-permute-done | bytes 73760 | tf_op jit(solution)/shard_map/ppermute | solution.py:450
  119.4 0.0 copy-start.3
  119.4 2.3 %collective-permute-done.5.above_ref = f32[2,72,128]{2,1,0:T(8,128)S(1)} collective-permute-done((f32[2,72,128]{2,1,0:T(8,128)}, f32[2,72,128]{2,1,0:T(8,128)S(1)}, u32[]{:S(2)}, u32[]{:S(2)}) %collective-permute-start.5) | collective-permute-done | bytes 73760 | tf_op jit(solution)/shard_map/ppermute | solution.py:450
  121.7 0.0 copy-start.5
  121.7 0.0 copy-done.3
  121.7 0.6 copy-done.5
  122.3 5.2 %second_stage.1 = (f32[1152,128]{1,0:T(8,128)}, f32[2,72,128]{2,1,0:T(8,128)}, f32[2,72,128]{2,1,0:T(8,128)}, f32[72,8,128]{2,1,0:T(8,128)}) custom-call(f32[1152,128]{1,0:T(8,128)} %get-tuple-element.24.field_ref, f32[2,72,128]{2,1,0:T(8,128)} %copy-done.3, f32[2,72,128]{2,1,0:T(8,128)} %copy-done.5, f32[2,72,8,128]{3,2,1,0:T(8,128)} %flow_ref.7, ...), custom_call_target="tpu_custom_call" | custom-call | tf_op jit(solution)/shard_map/second_stage/pallas_call | solution.py:470
  127.5 0.1 collective-permute-start.6
  127.6 0.5 collective-permute-start.7
  128.0 1.3 collective-permute-done.6.below_ref
  129.3 0.0 copy-start.2
  129.3 2.3 %collective-permute-done.7.above_ref = f32[2,72,128]{2,1,0:T(8,128)S(1)} collective-permute-done((f32[2,72,128]{2,1,0:T(8,128)}, f32[2,72,128]{2,1,0:T(8,128)S(1)}, u32[]{:S(2)}, u32[]{:S(2)}) %collective-permute-start.7) | collective-permute-done | bytes 73760 | tf_op jit(solution)/shard_map/ppermute | solution.py:450
  131.6 0.0 copy-start.4
  131.6 0.0 copy-done.2
  131.6 0.6 copy-done.4
  132.2 5.2 %third_stage.1 = (f32[1152,128]{1,0:T(8,128)}, f32[2,72,128]{2,1,0:T(8,128)}, f32[2,72,128]{2,1,0:T(8,128)}, f32[72,8,128]{2,1,0:T(8,128)}) custom-call(f32[1152,128]{1,0:T(8,128)} %get-tuple-element.28.field_ref, f32[2,72,128]{2,1,0:T(8,128)} %copy-done.2, f32[2,72,128]{2,1,0:T(8,128)} %copy-done.4, f32[2,72,8,128]{3,2,1,0:T(8,128)} %flow_ref.7, ...), custom_call_target="tpu_custom_call" | custom-call | tf_op jit(solution)/shard_map/third_stage/pallas_call | solution.py:470
  137.4 0.1 collective-permute-start.8
  137.4 0.5 collective-permute-start.9
  137.9 1.3 collective-permute-done.8.below_ref
  139.2 0.0 copy-start.6
  139.2 2.3 %collective-permute-done.9.above_ref = f32[2,72,128]{2,1,0:T(8,128)S(1)} collective-permute-done((f32[2,72,128]{2,1,0:T(8,128)}, f32[2,72,128]{2,1,0:T(8,128)S(1)}, u32[]{:S(2)}, u32[]{:S(2)}) %collective-permute-start.9) | collective-permute-done | bytes 73760 | tf_op jit(solution)/shard_map/ppermute | solution.py:450
  141.4 0.0 copy-start.7
  141.4 0.0 copy-done.6
  141.4 0.6 copy-done.7
  142.0 2.1 %last_stage.1 = f32[72,8,128]{2,1,0:T(8,128)} custom-call(f32[1152,128]{1,0:T(8,128)} %get-tuple-element.32.field_ref, f32[2,72,128]{2,1,0:T(8,128)} %copy-done.6, f32[2,72,128]{2,1,0:T(8,128)} %copy-done.7, f32[72,8,128]{2,1,0:T(8,128)} %get-tuple-element.35.sum_ref), custom_call_target="tpu_custom_call" | custom-call | tf_op jit(solution)/shard_map/last_stage/pallas_call | solution.py:470
Async XLA Ops:
  4.7 102.3 %collective-permute-start = (f32[27,8,128]{2,1,0:T(8,128)}, f32[27,8,128]{2,1,0:T(8,128)S(1)}, u32[]{:S(2)}, u32[]{:S(2)}) collective-permute-start(f32[27,8,128]{2,1,0:T(8,128)} %get-tuple-element.20), channel_id=1, source_target_pairs={{0,28},{4,0},{8,4},{12,8},{16,12},{20,16},{24,20},{28,24},{1,29},{... | collective-permute-start | bytes 331784 | tf_op jit(solution)/shard_map/ppermute | solution.py:450
  9.8 97.2 %collective-permute-start.1 = (f32[27,8,128]{2,1,0:T(8,128)}, f32[27,8,128]{2,1,0:T(8,128)S(1)}, u32[]{:S(2)}, u32[]{:S(2)}) collective-permute-start(f32[27,8,128]{2,1,0:T(8,128)} %get-tuple-element.21), channel_id=1, source_target_pairs={{0,4},{4,8},{8,12},{12,16},{16,20},{20,24},{24,28},{28,0},{1,5},{5... | collective-permute-start | bytes 331784 | tf_op jit(solution)/shard_map/ppermute | solution.py:450
  97.1 5.5 %collective-permute-start.2 = (f32[9,8,128]{2,1,0:T(8,128)}, f32[9,8,128]{2,1,0:T(8,128)S(1)}, u32[]{:S(2)}, u32[]{:S(2)}) collective-permute-start(f32[9,8,128]{2,1,0:T(8,128)} %get-tuple-element.22), channel_id=1, source_target_pairs={{0,28},{4,0},{8,4},{12,8},{16,12},{20,16},{24,20},{28,24},{1,29},{... | collective-permute-start | bytes 110600 | tf_op jit(solution)/shard_map/ppermute | solution.py:450
  101.2 5.7 %collective-permute-start.3 = (f32[9,8,128]{2,1,0:T(8,128)}, f32[9,8,128]{2,1,0:T(8,128)S(1)}, u32[]{:S(2)}, u32[]{:S(2)}) collective-permute-start(f32[9,8,128]{2,1,0:T(8,128)} %get-tuple-element.23), channel_id=1, source_target_pairs={{0,4},{4,8},{8,12},{12,16},{16,20},{20,24},{24,28},{28,0},{1,5},{5... | collective-permute-start | bytes 110600 | tf_op jit(solution)/shard_map/ppermute | solution.py:450
  102.6 4.4 %copy-start.8 = (f32[9,8,128]{2,1,0:T(8,128)}, f32[9,8,128]{2,1,0:T(8,128)S(1)}, u32[]{:S(2)}) copy-start(f32[9,8,128]{2,1,0:T(8,128)S(1)} %collective-permute-done.2.heat_after_ref) | copy-start | bytes 110596
  106.9 0.6 copy-start.9
  106.9 0.7 copy-start
  107.0 0.7 copy-start.1
  113.9 5.5 %collective-permute-start.4 = (f32[2,72,128]{2,1,0:T(8,128)}, f32[2,72,128]{2,1,0:T(8,128)S(1)}, u32[]{:S(2)}, u32[]{:S(2)}) collective-permute-start(f32[2,72,128]{2,1,0:T(8,128)} %get-tuple-element.25), channel_id=1, source_target_pairs={{0,1},{1,2},{2,3},{3,0},{4,5},{5,6},{6,7},{7,4},{8,9},{9,10},{10,1... | collective-permute-start | bytes 221192 | tf_op jit(solution)/shard_map/ppermute | solution.py:450
  117.7 4.0 %collective-permute-start.5 = (f32[2,72,128]{2,1,0:T(8,128)}, f32[2,72,128]{2,1,0:T(8,128)S(1)}, u32[]{:S(2)}, u32[]{:S(2)}) collective-permute-start(f32[2,72,128]{2,1,0:T(8,128)} %get-tuple-element.26), channel_id=1, source_target_pairs={{0,3},{1,0},{2,1},{3,2},{4,7},{5,4},{6,5},{7,6},{8,11},{9,8},{10,9... | collective-permute-start | bytes 221192 | tf_op jit(solution)/shard_map/ppermute | solution.py:450
  119.4 2.3 %copy-start.3 = (f32[2,72,128]{2,1,0:T(8,128)}, f32[2,72,128]{2,1,0:T(8,128)S(1)}, u32[]{:S(2)}) copy-start(f32[2,72,128]{2,1,0:T(8,128)S(1)} %collective-permute-done.4.below_ref) | copy-start | bytes 221188
  121.7 0.6 copy-start.5
  127.5 1.8 %collective-permute-start.6 = (f32[2,72,128]{2,1,0:T(8,128)}, f32[2,72,128]{2,1,0:T(8,128)S(1)}, u32[]{:S(2)}, u32[]{:S(2)}) collective-permute-start(f32[2,72,128]{2,1,0:T(8,128)} %get-tuple-element.29), channel_id=1, source_target_pairs={{0,1},{1,2},{2,3},{3,0},{4,5},{5,6},{6,7},{7,4},{8,9},{9,10},{10,1... | collective-permute-start | bytes 221192 | tf_op jit(solution)/shard_map/ppermute | solution.py:450
  127.6 4.0 %collective-permute-start.7 = (f32[2,72,128]{2,1,0:T(8,128)}, f32[2,72,128]{2,1,0:T(8,128)S(1)}, u32[]{:S(2)}, u32[]{:S(2)}) collective-permute-start(f32[2,72,128]{2,1,0:T(8,128)} %get-tuple-element.30), channel_id=1, source_target_pairs={{0,3},{1,0},{2,1},{3,2},{4,7},{5,4},{6,5},{7,6},{8,11},{9,8},{10,9... | collective-permute-start | bytes 221192 | tf_op jit(solution)/shard_map/ppermute | solution.py:450
  129.3 2.3 %copy-start.2 = (f32[2,72,128]{2,1,0:T(8,128)}, f32[2,72,128]{2,1,0:T(8,128)S(1)}, u32[]{:S(2)}) copy-start(f32[2,72,128]{2,1,0:T(8,128)S(1)} %collective-permute-done.6.below_ref) | copy-start | bytes 221188
  131.6 0.6 copy-start.4
  137.4 1.8 %collective-permute-start.8 = (f32[2,72,128]{2,1,0:T(8,128)}, f32[2,72,128]{2,1,0:T(8,128)S(1)}, u32[]{:S(2)}, u32[]{:S(2)}) collective-permute-start(f32[2,72,128]{2,1,0:T(8,128)} %get-tuple-element.33), channel_id=1, source_target_pairs={{0,1},{1,2},{2,3},{3,0},{4,5},{5,6},{6,7},{7,4},{8,9},{9,10},{10,1... | collective-permute-start | bytes 221192 | tf_op jit(solution)/shard_map/ppermute | solution.py:450
  137.4 4.0 %collective-permute-start.9 = (f32[2,72,128]{2,1,0:T(8,128)}, f32[2,72,128]{2,1,0:T(8,128)S(1)}, u32[]{:S(2)}, u32[]{:S(2)}) collective-permute-start(f32[2,72,128]{2,1,0:T(8,128)} %get-tuple-element.34), channel_id=1, source_target_pairs={{0,3},{1,0},{2,1},{3,2},{4,7},{5,4},{6,5},{7,6},{8,11},{9,8},{10,9... | collective-permute-start | bytes 221192 | tf_op jit(solution)/shard_map/ppermute | solution.py:450
  139.2 2.3 %copy-start.6 = (f32[2,72,128]{2,1,0:T(8,128)}, f32[2,72,128]{2,1,0:T(8,128)S(1)}, u32[]{:S(2)}) copy-start(f32[2,72,128]{2,1,0:T(8,128)S(1)} %collective-permute-done.8.below_ref) | copy-start | bytes 221188
  141.4 0.6 copy-start.7

commit v3 on v2

v3 whole, which is shorter than its diff:
```python
import functools

import jax
import jax.numpy as jnp
import numpy as np
from jax import lax
from jax.experimental import pallas as pl
from jax.experimental.pallas import tpu as pltpu
from jax.sharding import PartitionSpec as P

NODES = 4
TIME_INCREMENT = 0.05
EDGE = 16
ROWS = 8
LOG2E = 1.4426950408889634

GROUP = 8
TERMS = 16
BLOCK = 4
QUANTITIES = 3


def gll_derivative():
    points = np.array([-1.0, -1.0 / np.sqrt(5.0), 1.0 / np.sqrt(5.0), 1.0])
    legendre = 0.5 * (5.0 * points**3 - 3.0 * points)
    derivative = np.zeros((4, 4))
    for source in range(4):
        for target in range(4):
            if source != target:
                derivative[source, target] = legendre[source] / (
                    legendre[target] * (points[source] - points[target])
                )
    derivative[0, 0] = -3.0
    derivative[3, 3] = 3.0
    return derivative


def high_low(values):
    high = values.astype(jnp.bfloat16)
    return high, (values - high.astype(jnp.float32)).astype(jnp.bfloat16)


def across(left, right, precision=None):
    return lax.dot_general(
        left, right, (((0,), (0,)), ((), ())), precision=precision,
        preferred_element_type=jnp.float32,
    )


def optics_matrices(molecular_ref, table_ref, optics_ref, weight_ref):
    level_count, gpoints = molecular_ref.shape[1:]
    groups = level_count // GROUP
    width = GROUP * TERMS
    level = lax.broadcasted_iota(jnp.int32, (level_count, groups * width), 0)
    lane = lax.broadcasted_iota(jnp.int32, (level_count, groups * width), 1)
    here = level == lane // TERMS
    term = lane % TERMS
    gases = []
    for k in range(3):
        high, low = high_low(molecular_ref[k])
        spread = [
            jnp.where(here & chosen, 1.0, 0.0).astype(jnp.bfloat16)
            for chosen in ((term == k) | (term == k + 10), term == k + 5)
        ]
        gases.append(across(high, spread[0]) + across(low, spread[1]))
    w = [table_ref[n : n + 1, :] for n in range(7)]
    ls, li = w[0] * w[1], w[3] * w[4]
    la, ia = w[0] * (1.0 - w[1]), w[3] * (1.0 - w[4])
    place = lax.broadcasted_iota(jnp.int32, (8, width), 0)
    term = lax.broadcasted_iota(jnp.int32, (8, width), 1) % TERMS
    pattern = jnp.zeros((8, width), jnp.float32)
    for n, chosen in enumerate((
        (term == 3) | (term == 13), term == 8, (term == 4) | (term == 14), term == 9
    )):
        pattern = jnp.where((place == n) & chosen, 1.0, pattern)
    empty = jnp.zeros((4, gpoints), jnp.float32)

    def water(*values):
        parts = []
        for value in values:
            high = value.astype(jnp.bfloat16).astype(jnp.float32)
            parts += [high, value - high]
        return across(jnp.concatenate(parts + [empty], axis=0), pattern, lax.Precision.HIGHEST)

    absorbed = gases[0] + gases[1]
    gas = absorbed + gases[2]
    pairs = (
        (absorbed, water(la, ia)),
        (gas, water(la + ls * (1.0 - w[2]), ia + li * (1.0 - w[5]))),
        (gas + gas, water(2.0 * w[0], 2.0 * w[3])),
    )
    for n, (values, constant) in enumerate(pairs):
        for group in range(groups):
            optics_ref[group, n * gpoints : (n + 1) * gpoints, :] = (
                values[:, group * width : (group + 1) * width] + constant
            ).astype(jnp.bfloat16)
    only = jnp.where(place == 0, 1.0, 0.0)
    weight = jnp.broadcast_to(w[6], (8, gpoints))
    weight_ref[...] = across(weight, only, lax.Precision.HIGHEST)


def radiation_kernel(
    state_ref, temp_ref, cosine_ref, ground_ref, day_ref, molecular_ref, table_ref,
    edge_ref, heat_ref, first_ref, last_ref,
    optics_ref, weight_ref, terms_ref, right_ref, depths_ref, gain_ref, offset_ref, direct_ref, partial_ref, ratio_ref,
    source_ref, slant_ref, strip_ref,
):
    level_count = temp_ref.shape[0]
    gpoints = molecular_ref.shape[2]
    lanes = temp_ref.shape[2]
    row = pl.program_id(0)
    rows = pl.num_programs(0)
    rows_static = temp_ref.shape[1]
    blocks = level_count // BLOCK

    @pl.when(row == 0)
    def prepare():
        optics_matrices(molecular_ref, table_ref, optics_ref, weight_ref)
        right_ref[...] = jnp.zeros_like(right_ref)

        def level(l, carry):
            thickness = state_ref[2, l]
            weighted = thickness * temp_ref[l] * temp_ref[l]
            values = (
                weighted * state_ref[0, l], weighted * state_ref[1, l], thickness,
                state_ref[3, l], state_ref[4, l],
            )
            for k, value in enumerate(values):
                high = value.astype(jnp.bfloat16).astype(jnp.float32)
                for place, part in ((k, high), (k + 5, high), (k + 10, value - high)):
                    start = pl.multiple_of((l * TERMS + place) * 8, 8)
                    terms_ref[pl.ds(start, 8), :] = part
            last = pl.multiple_of((l * TERMS + 15) * 8, 8)
            terms_ref[pl.ds(last, 8), :] = jnp.zeros((8, lanes), jnp.float32)
            return carry

        lax.fori_loop(0, level_count, level, 0)

    def place_group(group, carry):
        for j in range(GROUP):
            start = (group * GROUP + j) * TERMS * 8 + row
            tile = terms_ref[pl.ds(start, TERMS, stride=8), :].astype(jnp.bfloat16)
            half = lanes * (j % 2)
            pair = group * (GROUP // 2) + j // 2
            right_ref[pair, TERMS * j : TERMS * (j + 1), half : half + lanes] = tile
        return carry

    lax.fori_loop(0, level_count // GROUP, place_group, 0)

    cosine = cosine_ref[pl.ds(row, 1), :]
    ground = ground_ref[pl.ds(row, 1), :]
    slant_ref[...] = jnp.broadcast_to((-0.5 * LOG2E) / cosine, (8, lanes))

    def over_rows(values):
        return jnp.broadcast_to(values[None], (gpoints // 8, 8, lanes)).reshape(gpoints, lanes)

    clear = 1.0 / (1.0 - ground)
    ratio_ref[...] = over_rows(jnp.broadcast_to((1.0 + ground) * clear, (8, lanes)))
    source_ref[...] = over_rows(jnp.broadcast_to(2.0 * ground * clear, (8, lanes)))

    def fill(block):
        for p in range(BLOCK // 2):
            pair = block * (BLOCK // 2) + p
            depths_ref[p] = jnp.dot(
                optics_ref[pair // (GROUP // 2)], right_ref[pair],
                preferred_element_type=jnp.float32,
            )

    def below_block(step, carry):
        block = blocks - 1 - step
        ratio, source = ratio_ref[...], source_ref[...]
        slant = over_rows(slant_ref[...])
        for j in reversed(range(BLOCK)):
            level = block * BLOCK + j
            part = depths_ref.at[j // 2, :, (j % 2) * lanes : (j % 2 + 1) * lanes]
            a, b, depth = [part[n * gpoints : (n + 1) * gpoints] for n in range(QUANTITIES)]
            away = b - a
            along = (depth - a) - b
            square = a * b
            inverse_root = lax.rsqrt(square)
            h = jnp.tanh(square * inverse_root)
            g = h * inverse_root
            g = g + g
            s, p = a * g, b * g
            h2 = h * h
            one = 1.0 + h2
            through = 1.0 - h2
            inverse = 1.0 / (one + s * ratio)
            direct = jnp.exp2(depth * slant)
            factor = (1.0 - direct) * (1.0 / depth)
            up, down = factor * away, factor * along
            push = inverse * (direct * source + (ratio - 1.0) * down)
            ratio = (one * ratio + p) * inverse
            gain = through * inverse
            source = through * push + (ratio + 1.0) * up
            gain_ref[level] = gain
            offset_ref[level] = (gain * up + down) - s * push
            direct_ref[level] = direct
        ratio_ref[...] = ratio
        source_ref[...] = source
        fill(jnp.maximum(block - 1, 0))
        return carry

    fill(blocks - 1)
    lax.fori_loop(0, blocks, below_block, 0)

    def folded(net):
        return sum(net[8 * k : 8 * (k + 1)] for k in range(gpoints // 8))

    beam = weight_ref[...] * cosine
    net = -(source_ref[...] * beam) / (1.0 + ratio_ref[...])
    partial_ref[pl.ds(pl.multiple_of(row * 8, 8), 8), :] = folded(beam) + folded(net)

    def down_group(group, carry):
        net, beam = carry
        for j in range(GROUP):
            level = group * GROUP + j
            net = gain_ref[level] * net + offset_ref[level] * beam
            beam = beam * direct_ref[level]
            start = pl.multiple_of(((level + 1) * rows + row) * 8, 8)
            partial_ref[pl.ds(start, 8), :] = folded(net) + folded(beam)
        return (net, beam)

    lax.fori_loop(0, level_count // GROUP, down_group, (net, beam))

    @pl.when(row == rows - 1)
    def finish():
        scale = jnp.where(day_ref[...] == 1, level_count / gpoints, 0.0)

        def flux(level):
            start = level * rows * 8
            return sum(
                partial_ref[pl.ds(start + k, rows, stride=8), :] for k in range(8)
            )

        def level_heat(level, upper):
            lower = flux(level + 1)
            start = pl.multiple_of(level * 8, 8)
            heat_ref[pl.ds(start, 8), :] = jnp.where(scale > 0.0, scale * (upper - lower), 0.0)
            return lower

        lax.fori_loop(0, level_count, level_heat, flux(0))

        parts = level_count // 8
        for r in range(rows_static):
            for k in range(parts):
                strip_ref[8 * r : 8 * (r + 1), lanes * k : lanes * (k + 1)] = heat_ref[
                    pl.ds(8 * k * rows_static + r, 8, stride=rows_static), :
                ]
        packed = split_dot(strip_ref[...], edge_ref[...])
        first_ref[...] = packed[:, :lanes]
        last_ref[...] = packed[:, lanes:]


def radiation(state, temper, cosine, ground, day, molecular, condensate):
    level_count, rows, lanes = temper.shape
    gpoints = molecular.shape[1]
    full = pltpu.VMEM((level_count, gpoints, lanes), jnp.float32)
    plane = pltpu.VMEM((gpoints, lanes), jnp.float32)
    whole = pl.BlockSpec(memory_space=pltpu.VMEM)
    edge = jax.ShapeDtypeStruct((8 * rows, lanes), jnp.float32)
    return pl.pallas_call(
        radiation_kernel,
        out_shape=(jax.ShapeDtypeStruct((level_count * rows, lanes), jnp.float32), edge, edge),
        grid=(rows,),
        in_specs=[whole] * 8,
        out_specs=(whole,) * 3,
        scratch_shapes=[
            pltpu.VMEM((level_count // GROUP, QUANTITIES * gpoints, GROUP * TERMS), jnp.bfloat16),
            plane,
            pltpu.VMEM((level_count * TERMS * 8, lanes), jnp.float32),
            pltpu.VMEM((level_count // 2, GROUP * TERMS, 2 * lanes), jnp.bfloat16),
            pltpu.VMEM((BLOCK // 2, QUANTITIES * gpoints, 2 * lanes), jnp.float32),
            full, full, full,
            pltpu.VMEM(((level_count + 1) * rows * 8, lanes), jnp.float32),
            plane, plane,
            pltpu.VMEM((8, lanes), jnp.float32),
            pltpu.VMEM((8 * rows, level_count // 8 * lanes), jnp.float32),
        ],
        compiler_params=pltpu.CompilerParams(vmem_limit_bytes=60 * 1024 * 1024),
        cost_estimate=pl.CostEstimate(
            flops=45 * level_count * gpoints * rows * lanes, bytes_accessed=4 * 8 * temper.size,
            transcendentals=5 * level_count * gpoints * rows * lanes,
        ),
        name="radiation",
    )(
        state, temper, cosine, ground, day, molecular.transpose(0, 2, 1), condensate,
        edge_matrix(level_count, lanes),
    )


def edge_matrix(level_count, lanes):
    parts = level_count // 8
    width = lanes // parts
    matrix = np.zeros((parts * lanes, 2 * lanes), np.float32)
    for k in range(parts):
        for c in range(width):
            matrix[lanes * k + c, width * k + c] = 1.0
            matrix[lanes * (k + 1) - width + c, lanes + width * k + c] = 1.0
    return jnp.asarray(matrix, jnp.bfloat16)


def slope_matrices(lanes):
    whole = np.kron(np.eye(2 * lanes // NODES), gll_derivative().T).astype(np.float32)
    high = np.asarray(whole, jnp.bfloat16)
    low = np.asarray(whole - high.astype(np.float32), jnp.bfloat16)
    return jnp.asarray(high), jnp.asarray(low)


def average_matrix(lanes):
    size = 2 * lanes
    matrix = np.eye(size, dtype=np.float32)
    for c in range(NODES - 1, size, NODES):
        after = (c + 1) % size
        matrix[c, c] = matrix[after, after] = matrix[c, after] = matrix[after, c] = 0.5
    return jnp.asarray(matrix, jnp.bfloat16)


def split_dot(values, *matrices):
    high, low = high_low(values)
    total = jnp.dot(high, matrices[0], preferred_element_type=jnp.float32)
    total = total + jnp.dot(low, matrices[0], preferred_element_type=jnp.float32)
    if len(matrices) > 1:
        total = total + jnp.dot(high, matrices[1], preferred_element_type=jnp.float32)
    return total


def slope_y(rows_of):
    derivative = gll_derivative()
    result = []
    for r in range(len(rows_of)):
        first = r // NODES * NODES
        total = None
        for n in range(NODES):
            weight = derivative[r - first, n]
            if abs(weight) > 1e-12:
                term = np.float32(weight) * rows_of[first + n]
                total = term if total is None else total + term
        result.append(total)
    return result


def average_y(rows_of, below, above):
    result = list(rows_of)
    count = len(rows_of)
    for r in range(NODES - 1, count - 1, NODES):
        result[r] = result[r + 1] = 0.5 * (rows_of[r] + rows_of[r + 1])
    result[0] = 0.5 * (below + rows_of[0])
    result[count - 1] = 0.5 * (rows_of[count - 1] + above)
    return result


def own_change_kernel(
    temp_ref, temp_after_ref, temp_before_ref, flow_ref, flow_after_ref, flow_before_ref,
    high_ref, low_ref, change_ref, wind_ref, temp_wide_ref, slope_ref,
):
    level_count = change_ref.shape[0] // ROWS
    lanes = temp_ref.shape[-1]
    lane = lax.broadcasted_iota(jnp.int32, (level_count, lanes), 1)

    def tiles(own, after, before, r):
        span = pl.ds(r, level_count, stride=ROWS)
        side = jnp.where(lane < EDGE, after[span, :], 0.0)
        return own[span, :], jnp.where(lane >= lanes - EDGE, before[span, :], side)

    for r in range(ROWS):
        rows = slice(r * level_count, (r + 1) * level_count)
        pairs = [tiles(temp_ref, temp_after_ref, temp_before_ref, r)] + [
            tiles(flow_ref.at[n], flow_after_ref.at[n], flow_before_ref.at[n], r) for n in range(2)
        ]
        for half in range(2):
            span = slice(half * lanes, (half + 1) * lanes)
            temp_wide_ref[rows, span] = pairs[0][half]
            wind_ref[0, rows, span] = pairs[1][half]
            wind_ref[1, rows, span] = pairs[2][half]
    slope_ref[...] = split_dot(temp_wide_ref[...], high_ref[...], low_ref[...])
    advect(temp_wide_ref, slope_ref, wind_ref, change_ref, level_count)


def advect(field_ref, slope_ref, wind_ref, change_ref, level_count):
    spans = [slice(r * level_count, (r + 1) * level_count) for r in range(ROWS)]
    for half in range(2):
        lanes = field_ref.shape[1] // 2
        part = slice(half * lanes, (half + 1) * lanes)
        slopes = slope_y([field_ref[span, part] for span in spans])
        for span, slope in zip(spans, slopes):
            change = wind_ref[0, span, part] * slope_ref[span, part]
            change_ref[span, part] = -TIME_INCREMENT * (change + wind_ref[1, span, part] * slope)


def write_averaged(change, average_ref, out_ref, first_ref, last_ref):
    level_count = first_ref.shape[0]
    out_ref[...] = split_dot(change, average_ref[...])
    width = first_ref.shape[1]
    first_ref[...] = out_ref[:level_count, :width]
    last_ref[...] = out_ref[out_ref.shape[0] - level_count :, :width]


def first_stage_kernel(
    change_ref, heat_ref, after_ref, before_ref, edge_ref, average_ref,
    out_ref, first_ref, last_ref, sum_ref,
):
    level_count = first_ref.shape[0]
    lanes = heat_ref.shape[1]
    sides = split_dot(
        jnp.concatenate([after_ref[...], before_ref[...]], axis=1), edge_ref[...]
    )
    for r in range(ROWS):
        rows = slice(r * level_count, (r + 1) * level_count)
        own = heat_ref[pl.ds(r, level_count, stride=ROWS), :]
        sum_ref[rows, :lanes] = change_ref[rows, :lanes] + TIME_INCREMENT * own
        for k in range(level_count // 8):
            side = sides[8 * r : 8 * (r + 1), lanes * k : lanes * (k + 1)]
            here = slice(r * level_count + 8 * k, r * level_count + 8 * (k + 1))
            sum_ref[here, lanes:] = change_ref[here, lanes:] + TIME_INCREMENT * side
    write_averaged(sum_ref[...], average_ref, out_ref, first_ref, last_ref)


def next_stage_kernel(
    share, native, field_ref, below_ref, above_ref, wind_ref, sum_ref, high_ref, low_ref,
    average_ref, out_ref, first_ref, last_ref, total_ref, wave_ref, slope_ref, change_ref,
):
    level_count = below_ref.shape[0]
    lanes = sum_ref.shape[1]
    spans = [slice(r * level_count, (r + 1) * level_count) for r in range(ROWS)]
    for half in range(2):
        part = slice(half * lanes, (half + 1) * lanes)
        wave = average_y(
            [field_ref[span, part] for span in spans], below_ref[:, part], above_ref[:, part]
        )
        for r, (span, row) in enumerate(zip(spans, wave)):
            wave_ref[span, part] = row
            if half == 0:
                before = sum_ref[pl.ds(r, level_count, stride=ROWS), :] if native else sum_ref[span]
                total_ref[span] = before + share * row
    slope_ref[...] = split_dot(wave_ref[...], high_ref[...], low_ref[...])
    advect(wave_ref, slope_ref, wind_ref, change_ref, level_count)
    write_averaged(change_ref[...], average_ref, out_ref, first_ref, last_ref)


def last_kernel(share, field_ref, below_ref, above_ref, sum_ref, total_ref):
    level_count, lanes = below_ref.shape
    spans = [slice(r * level_count, (r + 1) * level_count) for r in range(ROWS)]
    wave = average_y([field_ref[span, :lanes] for span in spans], below_ref[...], above_ref[...])
    for r, (span, row) in enumerate(zip(spans, wave)):
        total_ref[pl.ds(r, level_count, stride=ROWS), :] = sum_ref[span] + share * row


def shifted(value, axis, steps):
    count = lax.axis_size(axis)
    return lax.ppermute(value, axis, [(i, (i + steps) % count) for i in range(count)])


def local(
    atmospheric_constituents,
    thermal_ratio,
    flow_velocity,
    solar_elevation_factor,
    ground_reflectivity,
    sunlit_indicator,
    molecular_optics_lookup,
    condensate_optics_lookup,
):
    level_count, rows, lanes = thermal_ratio.shape
    size = level_count * rows
    temper = thermal_ratio.reshape(size, lanes)
    flow = flow_velocity.reshape(2, size, lanes)
    field = jax.ShapeDtypeStruct((size, lanes), jnp.float32)
    wide = jax.ShapeDtypeStruct((size, 2 * lanes), jnp.float32)
    line = jax.ShapeDtypeStruct((level_count, 2 * lanes), jnp.float32)
    short = jax.ShapeDtypeStruct((level_count, lanes), jnp.float32)
    wide_scratch = pltpu.VMEM(wide.shape, jnp.float32)
    whole = pl.BlockSpec(memory_space=pltpu.VMEM)

    def call(kernel, name, outs, scratch, *values):
        return pl.pallas_call(
            kernel, out_shape=outs, in_specs=[whole] * len(values),
            out_specs=jax.tree.map(lambda _: whole, outs), scratch_shapes=[wide_scratch] * scratch,
            compiler_params=pltpu.CompilerParams(vmem_limit_bytes=40 * 1024 * 1024), name=name,
        )(*values)

    slopes = slope_matrices(lanes)
    average = average_matrix(lanes)
    temper_after, temper_before = shifted(temper, "gx", -1), shifted(temper, "gx", 1)
    flow_after, flow_before = shifted(flow, "gx", -1), shifted(flow, "gx", 1)
    heat, heat_first, heat_last = radiation(
        atmospheric_constituents, thermal_ratio, solar_elevation_factor, ground_reflectivity,
        sunlit_indicator, molecular_optics_lookup, condensate_optics_lookup,
    )
    heat_after, heat_before = shifted(heat_first, "gx", -1), shifted(heat_last, "gx", 1)
    change, wind = call(
        own_change_kernel, "own_change",
        (wide, jax.ShapeDtypeStruct((2, size, 2 * lanes), jnp.float32)), 2,
        temper, temper_after, temper_before, flow, flow_after, flow_before, *slopes,
    )
    wave, first, last = call(
        first_stage_kernel, "first_stage", (wide, line, line), 1,
        change, heat, heat_after, heat_before, edge_matrix(level_count, lanes).T, average,
    )
    below, above = shifted(last, "gy", 1), shifted(first, "gy", -1)
    wave, first, last, total = call(
        functools.partial(next_stage_kernel, 1.0, True), "second_stage",
        (wide, line, line, field), 3, wave, below, above, wind, temper, *slopes, average,
    )
    below, above = shifted(last, "gy", 1), shifted(first, "gy", -1)
    wave, first, last, total = call(
        functools.partial(next_stage_kernel, 0.5, False), "third_stage",
        (wide, short, short, field), 3, wave, below, above, wind, total, *slopes, average,
    )
    below, above = shifted(last, "gy", 1), shifted(first, "gy", -1)
    total = call(
        functools.partial(last_kernel, 1.0 / 6.0), "last_stage", field, 0,
        wave, below, above, total,
    )
    return (heat.reshape(thermal_ratio.shape), total.reshape(thermal_ratio.shape))


def solution(mesh):
    in_specs = (
        P(None, None, "gy", "gx"),
        P(None, "gy", "gx"),
        P(None, None, "gy", "gx"),
        P("gy", "gx"),
        P("gy", "gx"),
        P("gy", "gx"),
        P(),
        P(),
    )
    out_specs = (P(None, "gy", "gx"), P(None, "gy", "gx"))
    return jax.shard_map(local, mesh=mesh, in_specs=in_specs, out_specs=out_specs, check_vma=False)
```

time: 144 us -> 123 us (0.85)
  Pallas kernels: 107 us -> 88.1 us
  local copies, waits for them, and re-layouts: 5.64 us -> 0.03 us
  starting transfers between devices: 14.1 us -> 19 us
  waiting for transfers between devices: 16.8 us -> 14.8 us
    pallas_call x4 -> x5, Pallas kernels: 18.8 us -> 4 us  [call(): pl.pallas_call(kernel, out_shape=outs, in_specs=[whole] * len(values), ou...]
    unnamed x22 -> x14, local copies, waits for them, and re-layouts: 5.64 us -> 0.03 us
    ppermute x10 -> x12, starting transfers between devices: 14.1 us -> 19 us  [shifted(): lax.ppermute(value, axis, [(i, (i + steps) % count) for i in range(count)])]
    pallas_call x2 -> x1, Pallas kernels: 88.2 us -> 84.1 us  [radiation(): pl.pallas_call(radiation_kernel, out_shape=(jax.ShapeDtypeStruct((level_c...]
    ppermute x10 -> x12, waiting for transfers between devices: 16.8 us -> 14.8 us  [shifted(): lax.ppermute(value, axis, [(i, (i + steps) % count) for i in range(count)])]
  transfers between devices with their start and end apart: 10 -> 12, of which waited for: 8 -> 8; matrix products, arithmetic and copies ran while one was open for 2% -> 0% of each run, Pallas kernels for 58% -> 69%
where the time goes in v3:
time: 123 us
  Pallas kernels  88.1 us (72%)
  starting transfers between devices  19 us (15%)
  waiting for transfers between devices  14.8 us (12%)
    pallas_call x1, Pallas kernels, radiation(): pl.pallas_call(radiation_kernel, out_shape=(jax.ShapeDtypeStruct((level_c...  84.1 us
    ppermute x12, starting transfers between devices, shifted(): lax.ppermute(value, axis, [(i, (i + steps) % count) for i in range(count)])  19 us
    ppermute x12, waiting for transfers between devices, shifted(): lax.ppermute(value, axis, [(i, (i + steps) % count) for i in range(count)])  14.8 us
    pallas_call x5, Pallas kernels, call(): pl.pallas_call(kernel, out_shape=outs, in_specs=[whole] * len(values), ou...  4 us
  transfers between devices with their start and end apart: 12, of which 8 were waited for; matrix products, arithmetic and copies ran while one was open for 0% of the time, Pallas kernels for 69%

profile of v3, /device:TPU:1, one launch (start us, length us, event | category | flops | bytes accessed | tf_op | source)
XLA Modules:
  0.0 122.8 jit_solution(14292901226122653503)
XLA Ops:
  0.6 5.2 %collective-permute-start.2 = (f32[2,576,128]{2,1,0:T(8,128)}, f32[2,576,128]{2,1,0:T(8,128)S(1)}, u32[]{:S(2)}, u32[]{:S(2)}) collective-permute-start(f32[2,576,128]{2,1,0:T(8,128)} %bitcast.9), channel_id=1, source_target_pairs={{0,28},{4,0},{8,4},{12,8},{16,12},{20,16},{24,20},{28,24},{1,29},{... | collective-permute-start | bytes 1769480 | tf_op jit(solution)/shard_map/ppermute | solution.py:451
  5.8 0.0 collective-permute-start.3
  5.8 4.2 %collective-permute-start = (f32[576,128]{1,0:T(8,128)}, f32[576,128]{1,0:T(8,128)S(1)}, u32[]{:S(2)}, u32[]{:S(2)}) collective-permute-start(f32[576,128]{1,0:T(8,128)} %bitcast.5), channel_id=1, source_target_pairs={{0,28},{4,0},{8,4},{12,8},{16,12},{20,16},{24,20},{28,24},{1,29},{... | collective-permute-start | bytes 884744 | tf_op jit(solution)/shard_map/ppermute | solution.py:451
  10.0 0.0 collective-permute-start.1
  10.0 0.0 copy-start
  10.0 0.0 copy-start.1
  10.0 0.0 copy-start.2
  10.0 0.0 copy-start.5
  10.0 84.1 %radiation.1 = (f32[576,128]{1,0:T(8,128)}, f32[64,128]{1,0:T(8,128)}, f32[64,128]{1,0:T(8,128)}) custom-call(f32[5,72,8,128]{3,2,1,0:T(8,128)} %state_ref.1, f32[72,8,128]{2,1,0:T(8,128)} %temp_ref.1, f32[8,128]{1,0:T(8,128)} %cosine_ref.1, f32[8,128]{1,0:T(8,128)} %ground_ref.1, s32[8,128]{1,0:T(8,128)} %day_ref.1, f32[3,72,112]{2,1,0:T(8,128)} %bitcast.14, ...), custom_call_target="tpu_custom_call" | custom-call | flops 371589120 | bytes 2359296 | tf_op jit(solution)/shard_map/radiation/pallas_call | solution.py:262
  94.1 0.0 copy-start.3
  94.1 0.0 copy-start.4
  94.1 0.0 copy-start.6
  94.1 4.2 %collective-permute-start.4 = (f32[64,128]{1,0:T(8,128)}, f32[64,128]{1,0:T(8,128)S(1)}, u32[]{:S(2)}, u32[]{:S(2)}) collective-permute-start(f32[64,128]{1,0:T(8,128)} %get-tuple-element.20), channel_id=1, source_target_pairs={{0,28},{4,0},{8,4},{12,8},{16,12},{20,16},{24,20},{28,24},{1,29},{... | collective-permute-start | bytes 98312 | tf_op jit(solution)/shard_map/ppermute | solution.py:451
  98.3 0.0 collective-permute-done.temp_after_ref
  98.3 0.0 collective-permute-start.5
  98.3 0.0 collective-permute-done.1.temp_before_ref
  98.4 0.0 collective-permute-done.2.flow_after_ref
  98.4 0.0 collective-permute-done.3.flow_before_ref
  98.4 0.0 copy-done
  98.4 0.0 copy-done.1
  98.4 0.0 copy-done.2
  98.4 0.0 copy-done.5
  98.4 0.8 own_change.1
  99.2 0.5 collective-permute-done.4.after_ref
  99.7 4.3 %collective-permute-done.5.before_ref = f32[64,128]{1,0:T(8,128)S(1)} collective-permute-done((f32[64,128]{1,0:T(8,128)}, f32[64,128]{1,0:T(8,128)S(1)}, u32[]{:S(2)}, u32[]{:S(2)}) %collective-permute-start.5) | collective-permute-done | bytes 32800 | tf_op jit(solution)/shard_map/ppermute | solution.py:451
  104.0 0.0 copy-done.3
  104.0 0.0 copy-done.4
  104.0 0.0 copy-done.6
  104.0 0.6 first_stage.1
  104.6 4.4 %collective-permute-start.6 = (f32[72,256]{1,0:T(8,128)S(1)}, f32[72,256]{1,0:T(8,128)S(1)}, u32[]{:S(2)}, u32[]{:S(2)}) collective-permute-start(f32[72,256]{1,0:T(8,128)S(1)} %get-tuple-element.23), channel_id=1, source_target_pairs={{0,1},{1,2},{2,3},{3,0},{4,5},{5,6},{6,7},{7,4},{8,9},{9,10},{10,1... | collective-permute-start | bytes 221192 | tf_op jit(solution)/shard_map/ppermute | solution.py:451
  109.0 0.0 collective-permute-start.7
  109.0 1.4 %collective-permute-done.6.below_ref = f32[72,256]{1,0:T(8,128)S(1)} collective-permute-done((f32[72,256]{1,0:T(8,128)S(1)}, f32[72,256]{1,0:T(8,128)S(1)}, u32[]{:S(2)}, u32[]{:S(2)}) %collective-permute-start.6) | collective-permute-done | bytes 73760 | tf_op jit(solution)/shard_map/ppermute | solution.py:451
  110.4 2.4 %collective-permute-done.7.above_ref = f32[72,256]{1,0:T(8,128)S(1)} collective-permute-done((f32[72,256]{1,0:T(8,128)S(1)}, f32[72,256]{1,0:T(8,128)S(1)}, u32[]{:S(2)}, u32[]{:S(2)}) %collective-permute-start.7) | collective-permute-done | bytes 73760 | tf_op jit(solution)/shard_map/ppermute | solution.py:451
  112.8 0.9 second_stage.1
  113.7 0.1 collective-permute-start.8
  113.7 0.5 collective-permute-start.9
  114.2 0.9 collective-permute-done.8.below_ref
  115.1 2.4 %collective-permute-done.9.above_ref = f32[72,256]{1,0:T(8,128)S(1)} collective-permute-done((f32[72,256]{1,0:T(8,128)S(1)}, f32[72,256]{1,0:T(8,128)S(1)}, u32[]{:S(2)}, u32[]{:S(2)}) %collective-permute-start.9) | collective-permute-done | bytes 73760 | tf_op jit(solution)/shard_map/ppermute | solution.py:451
  117.6 0.9 third_stage.1
  118.5 0.1 collective-permute-start.10
  118.5 0.5 collective-permute-start.11
  119.0 0.7 collective-permute-done.10.below_ref
  119.7 2.2 %collective-permute-done.11.above_ref = f32[72,128]{1,0:T(8,128)S(1)} collective-permute-done((f32[72,128]{1,0:T(8,128)S(1)}, f32[72,128]{1,0:T(8,128)S(1)}, u32[]{:S(2)}, u32[]{:S(2)}) %collective-permute-start.11) | collective-permute-done | bytes 36896 | tf_op jit(solution)/shard_map/ppermute | solution.py:451
  122.0 0.8 last_stage.1
Async XLA Ops:
  0.6 97.7 %collective-permute-start.2 = (f32[2,576,128]{2,1,0:T(8,128)}, f32[2,576,128]{2,1,0:T(8,128)S(1)}, u32[]{:S(2)}, u32[]{:S(2)}) collective-permute-start(f32[2,576,128]{2,1,0:T(8,128)} %bitcast.9), channel_id=1, source_target_pairs={{0,28},{4,0},{8,4},{12,8},{16,12},{20,16},{24,20},{28,24},{1,29},{... | collective-permute-start | bytes 1769480 | tf_op jit(solution)/shard_map/ppermute | solution.py:451
  5.8 92.6 %collective-permute-start.3 = (f32[2,576,128]{2,1,0:T(8,128)}, f32[2,576,128]{2,1,0:T(8,128)S(1)}, u32[]{:S(2)}, u32[]{:S(2)}) collective-permute-start(f32[2,576,128]{2,1,0:T(8,128)} %bitcast.10), channel_id=1, source_target_pairs={{0,4},{4,8},{8,12},{12,16},{16,20},{20,24},{24,28},{28,0},{1,5},{5... | collective-permute-start | bytes 1769480 | tf_op jit(solution)/shard_map/ppermute | solution.py:451
  5.8 92.5 %collective-permute-start = (f32[576,128]{1,0:T(8,128)}, f32[576,128]{1,0:T(8,128)S(1)}, u32[]{:S(2)}, u32[]{:S(2)}) collective-permute-start(f32[576,128]{1,0:T(8,128)} %bitcast.5), channel_id=1, source_target_pairs={{0,28},{4,0},{8,4},{12,8},{16,12},{20,16},{24,20},{28,24},{1,29},{... | collective-permute-start | bytes 884744 | tf_op jit(solution)/shard_map/ppermute | solution.py:451
  10.0 88.4 %collective-permute-start.1 = (f32[576,128]{1,0:T(8,128)}, f32[576,128]{1,0:T(8,128)S(1)}, u32[]{:S(2)}, u32[]{:S(2)}) collective-permute-start(f32[576,128]{1,0:T(8,128)} %bitcast.6), channel_id=1, source_target_pairs={{0,4},{4,8},{8,12},{12,16},{16,20},{20,24},{24,28},{28,0},{1,5},{5... | collective-permute-start | bytes 884744 | tf_op jit(solution)/shard_map/ppermute | solution.py:451
  10.0 88.4 %copy-start = (f32[72,8,128]{2,1,0:T(8,128)S(1)}, f32[72,8,128]{2,1,0:T(8,128)}, u32[]{:S(2)}) copy-start(f32[72,8,128]{2,1,0:T(8,128)} %temp_ref.1) | copy-start | bytes 884740
  10.0 88.4 %copy-start.1 = (bf16[256,256]{1,0:T(8,128)(2,1)S(1)}, bf16[256,256]{1,0:T(8,128)(2,1)}, u32[]{:S(2)}) copy-start(bf16[256,256]{1,0:T(8,128)(2,1)} %constant.8.clone.high_ref) | copy-start | bytes 393220
  10.0 88.4 %copy-start.2 = (bf16[256,256]{1,0:T(8,128)(2,1)S(1)}, bf16[256,256]{1,0:T(8,128)(2,1)}, u32[]{:S(2)}) copy-start(bf16[256,256]{1,0:T(8,128)(2,1)} %constant.9.clone.low_ref) | copy-start | bytes 393220
  10.0 88.4 %copy-start.5 = (f32[2,72,8,128]{3,2,1,0:T(8,128)S(1)}, f32[2,72,8,128]{3,2,1,0:T(8,128)}, u32[]{:S(2)}) copy-start(f32[2,72,8,128]{3,2,1,0:T(8,128)} %param.15) | copy-start | bytes 1769476
  94.1 9.9 %copy-start.3 = (bf16[256,256]{1,0:T(8,128)(2,1)S(1)}, bf16[256,256]{1,0:T(8,128)(2,1)}, u32[]{:S(2)}) copy-start(bf16[256,256]{1,0:T(8,128)(2,1)} %constant.10.clone.average_ref) | copy-start | bytes 393220
  94.1 9.9 %copy-start.4 = (bf16[256,1152]{1,0:T(8,128)(2,1)S(1)}, bf16[256,1152]{1,0:T(8,128)(2,1)}, u32[]{:S(2)}) copy-start(bf16[256,1152]{1,0:T(8,128)(2,1)} %constant.12.edge_ref) | copy-start | bytes 1769476
  94.1 9.9 %copy-start.6 = (f32[576,128]{1,0:T(8,128)S(1)}, f32[576,128]{1,0:T(8,128)}, u32[]{:S(2)}) copy-start(f32[576,128]{1,0:T(8,128)} %get-tuple-element.18.heat_ref) | copy-start | bytes 884740
  94.1 5.5 %collective-permute-start.4 = (f32[64,128]{1,0:T(8,128)}, f32[64,128]{1,0:T(8,128)S(1)}, u32[]{:S(2)}, u32[]{:S(2)}) collective-permute-start(f32[64,128]{1,0:T(8,128)} %get-tuple-element.20), channel_id=1, source_target_pairs={{0,28},{4,0},{8,4},{12,8},{16,12},{20,16},{24,20},{28,24},{1,29},{... | collective-permute-start | bytes 98312 | tf_op jit(solution)/shard_map/ppermute | solution.py:451
  98.3 5.7 %collective-permute-start.5 = (f32[64,128]{1,0:T(8,128)}, f32[64,128]{1,0:T(8,128)S(1)}, u32[]{:S(2)}, u32[]{:S(2)}) collective-permute-start(f32[64,128]{1,0:T(8,128)} %get-tuple-element.21), channel_id=1, source_target_pairs={{0,4},{4,8},{8,12},{12,16},{16,20},{20,24},{24,28},{28,0},{1,5},{5... | collective-permute-start | bytes 98312 | tf_op jit(solution)/shard_map/ppermute | solution.py:451
  104.6 5.8 %collective-permute-start.6 = (f32[72,256]{1,0:T(8,128)S(1)}, f32[72,256]{1,0:T(8,128)S(1)}, u32[]{:S(2)}, u32[]{:S(2)}) collective-permute-start(f32[72,256]{1,0:T(8,128)S(1)} %get-tuple-element.23), channel_id=1, source_target_pairs={{0,1},{1,2},{2,3},{3,0},{4,5},{5,6},{6,7},{7,4},{8,9},{9,10},{10,1... | collective-permute-start | bytes 221192 | tf_op jit(solution)/shard_map/ppermute | solution.py:451
  109.0 3.8 %collective-permute-start.7 = (f32[72,256]{1,0:T(8,128)S(1)}, f32[72,256]{1,0:T(8,128)S(1)}, u32[]{:S(2)}, u32[]{:S(2)}) collective-permute-start(f32[72,256]{1,0:T(8,128)S(1)} %get-tuple-element.24), channel_id=1, source_target_pairs={{0,3},{1,0},{2,1},{3,2},{4,7},{5,4},{6,5},{7,6},{8,11},{9,8},{10,9... | collective-permute-start | bytes 221192 | tf_op jit(solution)/shard_map/ppermute | solution.py:451
  113.7 1.5 %collective-permute-start.8 = (f32[72,256]{1,0:T(8,128)S(1)}, f32[72,256]{1,0:T(8,128)S(1)}, u32[]{:S(2)}, u32[]{:S(2)}) collective-permute-start(f32[72,256]{1,0:T(8,128)S(1)} %get-tuple-element.27), channel_id=1, source_target_pairs={{0,1},{1,2},{2,3},{3,0},{4,5},{5,6},{6,7},{7,4},{8,9},{9,10},{10,1... | collective-permute-start | bytes 221192 | tf_op jit(solution)/shard_map/ppermute | solution.py:451
  113.7 3.8 %collective-permute-start.9 = (f32[72,256]{1,0:T(8,128)S(1)}, f32[72,256]{1,0:T(8,128)S(1)}, u32[]{:S(2)}, u32[]{:S(2)}) collective-permute-start(f32[72,256]{1,0:T(8,128)S(1)} %get-tuple-element.28), channel_id=1, source_target_pairs={{0,3},{1,0},{2,1},{3,2},{4,7},{5,4},{6,5},{7,6},{8,11},{9,8},{10,9... | collective-permute-start | bytes 221192 | tf_op jit(solution)/shard_map/ppermute | solution.py:451
  118.5 1.3 %collective-permute-start.10 = (f32[72,128]{1,0:T(8,128)S(1)}, f32[72,128]{1,0:T(8,128)S(1)}, u32[]{:S(2)}, u32[]{:S(2)}) collective-permute-start(f32[72,128]{1,0:T(8,128)S(1)} %get-tuple-element.31), channel_id=1, source_target_pairs={{0,1},{1,2},{2,3},{3,0},{4,5},{5,6},{6,7},{7,4},{8,9},{9,10},{10,1... | collective-permute-start | bytes 110600 | tf_op jit(solution)/shard_map/ppermute | solution.py:451
  118.5 3.4 %collective-permute-start.11 = (f32[72,128]{1,0:T(8,128)S(1)}, f32[72,128]{1,0:T(8,128)S(1)}, u32[]{:S(2)}, u32[]{:S(2)}) collective-permute-start(f32[72,128]{1,0:T(8,128)S(1)} %get-tuple-element.32), channel_id=1, source_target_pairs={{0,3},{1,0},{2,1},{3,2},{4,7},{5,4},{6,5},{7,6},{8,11},{9,8},{10,9... | collective-permute-start | bytes 110600 | tf_op jit(solution)/shard_map/ppermute | solution.py:451

commit v4 on v3

--- a/solution.py
+++ b/solution.py
@@ -16,8 +16,13 @@
 
 GROUP = 8
 TERMS = 16
-BLOCK = 4
+BLOCK = 8
 QUANTITIES = 3
+
+
+def shifted(value, axis, steps):
+    count = lax.axis_size(axis)
+    return lax.ppermute(value, axis, [(i, (i + steps) % count) for i in range(count)])
 
 
 def gll_derivative():
@@ -99,56 +104,44 @@
     weight_ref[...] = across(weight, only, lax.Precision.HIGHEST)
 
 
-def radiation_kernel(
-    state_ref, temp_ref, cosine_ref, ground_ref, day_ref, molecular_ref, table_ref,
-    edge_ref, heat_ref, first_ref, last_ref,
-    optics_ref, weight_ref, terms_ref, right_ref, depths_ref, gain_ref, offset_ref, direct_ref, partial_ref, ratio_ref,
-    source_ref, slant_ref, strip_ref,
+def layer_terms(state_ref, temp_ref, level):
+    thickness = state_ref[2, level]
+    weighted = thickness * temp_ref[level] * temp_ref[level]
+    return (
+        weighted * state_ref[0, level], weighted * state_ref[1, level], thickness,
+        state_ref[3, level], state_ref[4, level],
+    )
+
+
+def write_terms(terms_ref, level, values, lines):
+    parts = [None] * TERMS
+    for k, value in enumerate(values):
+        high = value.astype(jnp.bfloat16).astype(jnp.float32)
+        parts[k], parts[k + 5], parts[k + 10] = high, high, value - high
+    parts[15] = jnp.zeros_like(values[0])
+    for k, part in enumerate(parts):
+        start = (level * TERMS + k) * lines
+        start = pl.multiple_of(start, 8) if lines % 8 == 0 else start
+        terms_ref[pl.ds(start, lines), :] = part
+
+
+def sweep_row(
+    row, lines, count, cosine, ground, optics_ref, weight_ref, terms_ref, right_ref, depths_ref,
+    gain_ref, offset_ref, direct_ref, partial_ref, ratio_ref, source_ref, slant_ref,
 ):
-    level_count = temp_ref.shape[0]
-    gpoints = molecular_ref.shape[2]
-    lanes = temp_ref.shape[2]
-    row = pl.program_id(0)
-    rows = pl.num_programs(0)
-    rows_static = temp_ref.shape[1]
+    level_count, gpoints, lanes = gain_ref.shape
     blocks = level_count // BLOCK
-
-    @pl.when(row == 0)
-    def prepare():
-        optics_matrices(molecular_ref, table_ref, optics_ref, weight_ref)
-        right_ref[...] = jnp.zeros_like(right_ref)
-
-        def level(l, carry):
-            thickness = state_ref[2, l]
-            weighted = thickness * temp_ref[l] * temp_ref[l]
-            values = (
-                weighted * state_ref[0, l], weighted * state_ref[1, l], thickness,
-                state_ref[3, l], state_ref[4, l],
-            )
-            for k, value in enumerate(values):
-                high = value.astype(jnp.bfloat16).astype(jnp.float32)
-                for place, part in ((k, high), (k + 5, high), (k + 10, value - high)):
-                    start = pl.multiple_of((l * TERMS + place) * 8, 8)
-                    terms_ref[pl.ds(start, 8), :] = part
-            last = pl.multiple_of((l * TERMS + 15) * 8, 8)
-            terms_ref[pl.ds(last, 8), :] = jnp.zeros((8, lanes), jnp.float32)
-            return carry
-
-        lax.fori_loop(0, level_count, level, 0)
 
     def place_group(group, carry):
         for j in range(GROUP):
-            start = (group * GROUP + j) * TERMS * 8 + row
-            tile = terms_ref[pl.ds(start, TERMS, stride=8), :].astype(jnp.bfloat16)
+            start = (group * GROUP + j) * TERMS * lines + row
+            tile = terms_ref[pl.ds(start, TERMS, stride=lines), :].astype(jnp.bfloat16)
             half = lanes * (j % 2)
             pair = group * (GROUP // 2) + j // 2
             right_ref[pair, TERMS * j : TERMS * (j + 1), half : half + lanes] = tile
         return carry
 
     lax.fori_loop(0, level_count // GROUP, place_group, 0)
-
-    cosine = cosine_ref[pl.ds(row, 1), :]
-    ground = ground_ref[pl.ds(row, 1), :]
     slant_ref[...] = jnp.broadcast_to((-0.5 * LOG2E) / cosine, (8, lanes))
 
     def over_rows(values):
@@ -158,16 +151,14 @@
     ratio_ref[...] = over_rows(jnp.broadcast_to((1.0 + ground) * clear, (8, lanes)))
     source_ref[...] = over_rows(jnp.broadcast_to(2.0 * ground * clear, (8, lanes)))
 
-    def fill(block):
+    def below_block(step, carry):
+        block = blocks - 1 - step
         for p in range(BLOCK // 2):
             pair = block * (BLOCK // 2) + p
             depths_ref[p] = jnp.dot(
                 optics_ref[pair // (GROUP // 2)], right_ref[pair],
                 preferred_element_type=jnp.float32,
             )
-
-    def below_block(step, carry):
-        block = blocks - 1 - step
         ratio, source = ratio_ref[...], source_ref[...]
         slant = over_rows(slant_ref[...])
         for j in reversed(range(BLOCK)):
@@ -198,18 +189,21 @@
             direct_ref[level] = direct
         ratio_ref[...] = ratio
         source_ref[...] = source
-        fill(jnp.maximum(block - 1, 0))
         return carry
 
-    fill(blocks - 1)
     lax.fori_loop(0, blocks, below_block, 0)
 
     def folded(net):
         return sum(net[8 * k : 8 * (k + 1)] for k in range(gpoints // 8))
 
-    beam = weight_ref[...] * cosine
-    net = -(source_ref[...] * beam) / (1.0 + ratio_ref[...])
-    partial_ref[pl.ds(pl.multiple_of(row * 8, 8), 8), :] = folded(beam) + folded(net)
+    def top(step, carry):
+        beam = weight_ref[...] * cosine
+        net = -(source_ref[...] * beam) / (1.0 + ratio_ref[...])
+        partial_ref[pl.ds(pl.multiple_of(row * 8, 8), 8), :] = folded(beam) + folded(net)
+        return net, beam
+
+    nothing = jnp.zeros((gpoints, lanes), jnp.float32)
+    carry = lax.fori_loop(0, 1 + jnp.minimum(row, 0), top, (nothing, nothing))
 
     def down_group(group, carry):
         net, beam = carry
@@ -217,76 +211,228 @@
             level = group * GROUP + j
             net = gain_ref[level] * net + offset_ref[level] * beam
             beam = beam * direct_ref[level]
-            start = pl.multiple_of(((level + 1) * rows + row) * 8, 8)
+            start = pl.multiple_of(((level + 1) * count + row) * 8, 8)
             partial_ref[pl.ds(start, 8), :] = folded(net) + folded(beam)
         return (net, beam)
 
-    lax.fori_loop(0, level_count // GROUP, down_group, (net, beam))
-
-    @pl.when(row == rows - 1)
+    lax.fori_loop(0, level_count // GROUP, down_group, carry)
+
+
+def level_heating(partial_ref, level_count, gpoints, count, write):
+    def flux(level):
+        start = level * count * 8
+        return sum(partial_ref[pl.ds(start + k, count, stride=8), :] for k in range(8))
+
+    def step(level, upper):
+        lower = flux(level + 1)
+        write(level, (level_count / gpoints) * (upper - lower))
+        return lower
+
+    lax.fori_loop(0, level_count, step, flux(0))
+
+
+def home_kernel(
+    state_ref, temp_ref, cosine_ref, ground_ref, day_ref, molecular_ref, table_ref,
+    heat_ref, optics_ref, weight_ref, terms_ref, right_ref, *scratch,
+):
+    level_count, lines, lanes = temp_ref.shape
+    gpoints = weight_ref.shape[0]
+    row, count = pl.program_id(0), pl.num_programs(0)
+
+    @pl.when(row == 0)
+    def prepare():
+        optics_matrices(molecular_ref, table_ref, optics_ref, weight_ref)
+        right_ref[...] = jnp.zeros_like(right_ref)
+        heat_ref[...] = jnp.zeros_like(heat_ref)
+
+        def level(l, carry):
+            write_terms(terms_ref, l, layer_terms(state_ref, temp_ref, l), lines)
+            return carry
+
+        lax.fori_loop(0, level_count, level, 0)
+
+    sweep_row(
+        row, lines, count, cosine_ref[pl.ds(row, 1), :], ground_ref[pl.ds(row, 1), :],
+        optics_ref, weight_ref, terms_ref, right_ref, *scratch,
+    )
+
+    @pl.when(row == count - 1)
     def finish():
-        scale = jnp.where(day_ref[...] == 1, level_count / gpoints, 0.0)
-
-        def flux(level):
-            start = level * rows * 8
-            return sum(
-                partial_ref[pl.ds(start + k, rows, stride=8), :] for k in range(8)
+        home = lines // 2
+        day = day_ref[:home, :] == 1
+
+        def write(level, value):
+            start = pl.multiple_of(level * lines, 8)
+            heat_ref[pl.ds(start, home), :] = jnp.where(day, value, 0.0)
+
+        level_heating(scratch[4], level_count, gpoints, home, write)
+
+
+def pack_kernel(theirs_ref, state_ref, temp_ref, cosine_ref, ground_ref, out_ref, own_ref):
+    level_count, lines, lanes = temp_ref.shape
+    count = out_ref.shape[1]
+    first = theirs_ref[0]
+
+    def level(l, carry):
+        for k, value in enumerate(layer_terms(state_ref, temp_ref, l)):
+            own_ref[pl.ds(pl.multiple_of((5 * l + k) * lines, 8), lines), :] = value
+        return carry
+
+    lax.fori_loop(0, level_count, level, 0)
+
+    def copy(n, carry):
+        out_ref[n] = own_ref[pl.ds(n * lines + first, count), :]
+        return carry
+
+    lax.fori_loop(0, 5 * level_count, copy, 0, unroll=8)
+    out_ref[5 * level_count] = cosine_ref[pl.ds(first, count), :]
+    out_ref[5 * level_count + 1] = ground_ref[pl.ds(first, count), :]
+
+
+def shared_kernel(
+    mine_ref, state_ref, temp_ref, cosine_ref, ground_ref, day_ref, received_ref, optics_ref,
+    weight_ref, edge_ref, home_ref,
+    heat_ref, theirs_ref, first_ref, last_ref, their_first_ref, their_last_ref,
+    own_ref, strip_ref, surface_ref, terms_ref, right_ref, *scratch,
+):
+    level_count, lines, lanes = temp_ref.shape
+    gpoints = weight_ref.shape[0]
+    row, count = pl.program_id(0), pl.num_programs(0)
+    shared = received_ref.shape[1]
+    first = mine_ref[0]
+    day = day_ref[pl.ds(first, shared), :] == 1
+
+    @pl.when(row == 0)
+    def prepare():
+        right_ref[...] = jnp.zeros_like(right_ref)
+
+        def own(l, carry):
+            for k, value in enumerate(layer_terms(state_ref, temp_ref, l)):
+                own_ref[pl.ds(pl.multiple_of((5 * l + k) * lines, 8), lines), :] = value
+            return carry
+
+        lax.fori_loop(0, level_count, own, 0)
+
+        def level(l, carry):
+            values = [
+                jnp.where(
+                    day, own_ref[pl.ds((5 * l + k) * lines + first, shared), :],
+                    received_ref[5 * l + k],
+                )
+                for k in range(5)
+            ]
+            write_terms(terms_ref, l, values, shared)
+            return carry
+
+        lax.fori_loop(0, level_count, level, 0)
+        for n, ref in enumerate((cosine_ref, ground_ref)):
+            surface_ref[n, :shared, :] = jnp.where(
+                day, ref[pl.ds(first, shared), :], received_ref[5 * level_count + n]
             )
 
-        def level_heat(level, upper):
-            lower = flux(level + 1)
-            start = pl.multiple_of(level * 8, 8)
-            heat_ref[pl.ds(start, 8), :] = jnp.where(scale > 0.0, scale * (upper - lower), 0.0)
-            return lower
-
-        lax.fori_loop(0, level_count, level_heat, flux(0))
-
-        parts = level_count // 8
-        for r in range(rows_static):
-            for k in range(parts):
-                strip_ref[8 * r : 8 * (r + 1), lanes * k : lanes * (k + 1)] = heat_ref[
-                    pl.ds(8 * k * rows_static + r, 8, stride=rows_static), :
+    sweep_row(
+        row, shared, count, surface_ref[0, pl.ds(row, 1), :], surface_ref[1, pl.ds(row, 1), :],
+        optics_ref, weight_ref, terms_ref, right_ref, *scratch,
+    )
+
+    @pl.when(row == count - 1)
+    def finish():
+        heat_ref[...] = home_ref[...]
+
+        def write(level, value):
+            heat_ref[pl.ds(level * lines + first, shared), :] = jnp.where(day, value, 0.0)
+            theirs_ref[pl.ds(level * shared, shared), :] = jnp.where(day, 0.0, value)
+
+        level_heating(scratch[4], level_count, gpoints, shared, write)
+        strip_ref[...] = jnp.zeros_like(strip_ref)
+        for k in range(level_count // 8):
+            span = slice(lanes * k, lanes * (k + 1))
+            for r in range(lines):
+                strip_ref[8 * r : 8 * (r + 1), span] = heat_ref[
+                    pl.ds(8 * k * lines + r, 8, stride=lines), :
+                ]
+            for r in range(shared):
+                start = pl.multiple_of(8 * (lines + first + r), 8)
+                strip_ref[pl.ds(start, 8), span] = theirs_ref[
+                    pl.ds(8 * k * shared + r, 8, stride=shared), :
                 ]
         packed = split_dot(strip_ref[...], edge_ref[...])
-        first_ref[...] = packed[:, :lanes]
-        last_ref[...] = packed[:, lanes:]
+        half = 8 * lines
+        first_ref[...] = packed[:half, :lanes]
+        last_ref[...] = packed[:half, lanes:]
+        their_first_ref[...] = packed[half:, :lanes]
+        their_last_ref[...] = packed[half:, lanes:]
 
 
 def radiation(state, temper, cosine, ground, day, molecular, condensate):
     level_count, rows, lanes = temper.shape
     gpoints = molecular.shape[1]
+    home, shared = rows // 2, rows // 4
+    partner = lax.axis_size("gx") // 2
+    low = lax.axis_index("gx") < partner
+    mine = jnp.where(low, home, home + shared).astype(jnp.int32).reshape(1)
+    theirs = jnp.where(low, home + shared, home).astype(jnp.int32).reshape(1)
     full = pltpu.VMEM((level_count, gpoints, lanes), jnp.float32)
     plane = pltpu.VMEM((gpoints, lanes), jnp.float32)
     whole = pl.BlockSpec(memory_space=pltpu.VMEM)
-    edge = jax.ShapeDtypeStruct((8 * rows, lanes), jnp.float32)
-    return pl.pallas_call(
-        radiation_kernel,
-        out_shape=(jax.ShapeDtypeStruct((level_count * rows, lanes), jnp.float32), edge, edge),
-        grid=(rows,),
-        in_specs=[whole] * 8,
-        out_specs=(whole,) * 3,
-        scratch_shapes=[
-            pltpu.VMEM((level_count // GROUP, QUANTITIES * gpoints, GROUP * TERMS), jnp.bfloat16),
-            plane,
-            pltpu.VMEM((level_count * TERMS * 8, lanes), jnp.float32),
+    scalar = pl.BlockSpec(memory_space=pltpu.SMEM)
+    field = jax.ShapeDtypeStruct((level_count * rows, lanes), jnp.float32)
+    own = pltpu.VMEM((5 * level_count * rows, lanes), jnp.float32)
+    params = pltpu.CompilerParams(vmem_limit_bytes=60 * 1024 * 1024)
+
+    def scratch(lines, count):
+        return [
+            pltpu.VMEM((level_count * TERMS * lines, lanes), jnp.float32),
             pltpu.VMEM((level_count // 2, GROUP * TERMS, 2 * lanes), jnp.bfloat16),
             pltpu.VMEM((BLOCK // 2, QUANTITIES * gpoints, 2 * lanes), jnp.float32),
             full, full, full,
-            pltpu.VMEM(((level_count + 1) * rows * 8, lanes), jnp.float32),
+            pltpu.VMEM(((level_count + 1) * count * 8, lanes), jnp.float32),
             plane, plane,
             pltpu.VMEM((8, lanes), jnp.float32),
-            pltpu.VMEM((8 * rows, level_count // 8 * lanes), jnp.float32),
-        ],
-        compiler_params=pltpu.CompilerParams(vmem_limit_bytes=60 * 1024 * 1024),
-        cost_estimate=pl.CostEstimate(
-            flops=45 * level_count * gpoints * rows * lanes, bytes_accessed=4 * 8 * temper.size,
-            transcendentals=5 * level_count * gpoints * rows * lanes,
+        ]
+
+    def cost(count):
+        cells = level_count * gpoints * count * lanes
+        return pl.CostEstimate(
+            flops=45 * cells, bytes_accessed=32 * temper.size, transcendentals=5 * cells
+        )
+
+    sent = pl.pallas_call(
+        pack_kernel,
+        out_shape=jax.ShapeDtypeStruct((5 * level_count + 2, shared, lanes), jnp.float32),
+        in_specs=[scalar] + [whole] * 4, out_specs=whole, scratch_shapes=[own],
+        compiler_params=params, name="pack",
+    )(theirs, state, temper, cosine, ground)
+    received = shifted(sent, "gx", partner)
+    optics = (level_count // GROUP, QUANTITIES * gpoints, GROUP * TERMS)
+    heat, optics, weight = pl.pallas_call(
+        home_kernel,
+        out_shape=(
+            field, jax.ShapeDtypeStruct(optics, jnp.bfloat16),
+            jax.ShapeDtypeStruct((gpoints, lanes), jnp.float32),
         ),
-        name="radiation",
+        grid=(home,), in_specs=[whole] * 7, out_specs=(whole,) * 3,
+        scratch_shapes=scratch(rows, home), compiler_params=params, cost_estimate=cost(home),
+        name="home_radiation",
+    )(state, temper, cosine, ground, day, molecular.transpose(0, 2, 1), condensate)
+    edge = jax.ShapeDtypeStruct((8 * rows, lanes), jnp.float32)
+    return pl.pallas_call(
+        shared_kernel,
+        out_shape=(
+            field, jax.ShapeDtypeStruct((level_count * shared, lanes), jnp.float32),
+            edge, edge, edge, edge,
+        ),
+        grid=(shared,), in_specs=[scalar] + [whole] * 10, out_specs=(whole,) * 6,
+        scratch_shapes=[
+            own,
+            pltpu.VMEM((16 * rows, level_count // 8 * lanes), jnp.float32),
+            pltpu.VMEM((2, 8, lanes), jnp.float32),
+        ] + scratch(shared, shared),
+        compiler_params=params, cost_estimate=cost(shared), name="shared_radiation",
     )(
-        state, temper, cosine, ground, day, molecular.transpose(0, 2, 1), condensate,
-        edge_matrix(level_count, lanes),
-    )
+        mine, state, temper, cosine, ground, day, received, optics, weight,
+        edge_matrix(level_count, lanes), heat,
+    ) + (theirs,)
 
 
 def edge_matrix(level_count, lanes):
@@ -397,17 +543,27 @@
 
 
 def first_stage_kernel(
-    change_ref, heat_ref, after_ref, before_ref, edge_ref, average_ref,
-    out_ref, first_ref, last_ref, sum_ref,
+    theirs_ref, change_ref, heat_ref, returned_ref, after_ref, before_ref, after_more_ref,
+    before_more_ref, edge_ref, average_ref,
+    out_ref, first_ref, last_ref, heat_out_ref, sum_ref,
 ):
     level_count = first_ref.shape[0]
     lanes = heat_ref.shape[1]
-    sides = split_dot(
-        jnp.concatenate([after_ref[...], before_ref[...]], axis=1), edge_ref[...]
-    )
+    shared = returned_ref.shape[0] // level_count
+    after = after_ref[...] + after_more_ref[...]
+    before = before_ref[...] + before_more_ref[...]
+    sides = split_dot(jnp.concatenate([after, before], axis=1), edge_ref[...])
     for r in range(ROWS):
         rows = slice(r * level_count, (r + 1) * level_count)
-        own = heat_ref[pl.ds(r, level_count, stride=ROWS), :]
+        span = pl.ds(r, level_count, stride=ROWS)
+        own = heat_ref[span, :]
+        if r >= ROWS // 2:
+            n = r % shared
+            here = theirs_ref[0] == r - n
+            own = own + jnp.where(
+                here, returned_ref[pl.ds(n, level_count, stride=shared), :], 0.0
+            )
+        heat_out_ref[span, :] = own
         sum_ref[rows, :lanes] = change_ref[rows, :lanes] + TIME_INCREMENT * own
         for k in range(level_count // 8):
             side = sides[8 * r : 8 * (r + 1), lanes * k : lanes * (k + 1)]
@@ -446,11 +602,6 @@
         total_ref[pl.ds(r, level_count, stride=ROWS), :] = sum_ref[span] + share * row
 
 
-def shifted(value, axis, steps):
-    count = lax.axis_size(axis)
-    return lax.ppermute(value, axis, [(i, (i + steps) % count) for i in range(count)])
-
-
 def local(
     atmospheric_constituents,
     thermal_ratio,
@@ -471,10 +622,12 @@
     short = jax.ShapeDtypeStruct((level_count, lanes), jnp.float32)
     wide_scratch = pltpu.VMEM(wide.shape, jnp.float32)
     whole = pl.BlockSpec(memory_space=pltpu.VMEM)
+    scalar = pl.BlockSpec(memory_space=pltpu.SMEM)
 
     def call(kernel, name, outs, scratch, *values):
         return pl.pallas_call(
-            kernel, out_shape=outs, in_specs=[whole] * len(values),
+            kernel, out_shape=outs,
+            in_specs=[scalar if value.size == 1 else whole for value in values],
             out_specs=jax.tree.map(lambda _: whole, outs), scratch_shapes=[wide_scratch] * scratch,
             compiler_params=pltpu.CompilerParams(vmem_limit_bytes=40 * 1024 * 1024), name=name,
         )(*values)
@@ -483,19 +636,24 @@
     average = average_matrix(lanes)
     temper_after, temper_before = shifted(temper, "gx", -1), shifted(temper, "gx", 1)
     flow_after, flow_before = shifted(flow, "gx", -1), shifted(flow, "gx", 1)
-    heat, heat_first, heat_last = radiation(
+    heat, heat_theirs, heat_first, heat_last, their_first, their_last, theirs = radiation(
         atmospheric_constituents, thermal_ratio, solar_elevation_factor, ground_reflectivity,
         sunlit_indicator, molecular_optics_lookup, condensate_optics_lookup,
     )
+    partner = lax.axis_size("gx") // 2
     heat_after, heat_before = shifted(heat_first, "gx", -1), shifted(heat_last, "gx", 1)
+    after_more = shifted(their_first, "gx", partner - 1)
+    before_more = shifted(their_last, "gx", partner + 1)
+    returned = shifted(heat_theirs, "gx", partner)
     change, wind = call(
         own_change_kernel, "own_change",
         (wide, jax.ShapeDtypeStruct((2, size, 2 * lanes), jnp.float32)), 2,
         temper, temper_after, temper_before, flow, flow_after, flow_before, *slopes,
     )
-    wave, first, last = call(
-        first_stage_kernel, "first_stage", (wide, line, line), 1,
-        change, heat, heat_after, heat_before, edge_matrix(level_count, lanes).T, average,
+    wave, first, last, heat = call(
+        first_stage_kernel, "first_stage", (wide, line, line, field), 1,
+        theirs, change, heat, returned, heat_after, heat_before, after_more, before_more,
+        edge_matrix(level_count, lanes).T, average,
     )
     below, above = shifted(last, "gy", 1), shifted(first, "gy", -1)
     wave, first, last, total = call(

time: 123 us -> 112 us (0.911)
  Pallas kernels: 88.1 us -> 75 us
  starting transfers between devices: 19 us -> 23.7 us
  waiting for transfers between devices: 14.8 us -> 11.9 us
    pallas_call x6 -> x8, Pallas kernels: 88.1 us -> 75 us  [the longest x1 42.7 us: radiation(): pl.pallas_call(home_kernel, out_shape=(field, jax.ShapeDtypeStruct(optics...]
    ppermute x12 -> x16, starting transfers between devices: 19 us -> 23.7 us  [shifted(): lax.ppermute(value, axis, [(i, (i + steps) % count) for i in range(count)])]
    ppermute x12 -> x16, waiting for transfers between devices: 14.8 us -> 11.9 us  [shifted(): lax.ppermute(value, axis, [(i, (i + steps) % count) for i in range(count)])]
  transfers between devices with their start and end apart: 12 -> 16, of which waited for: 8 -> 8; matrix products, arithmetic and copies ran while one was open for 0% -> 0% of each run, Pallas kernels for 69% -> 64%
where the time goes in v4:
time: 112 us
  Pallas kernels  75 us (67%)
  starting transfers between devices  23.7 us (21%)
  waiting for transfers between devices  11.9 us (11%)
    pallas_call x1, Pallas kernels, radiation(): pl.pallas_call(home_kernel, out_shape=(field, jax.ShapeDtypeStruct(optics...  42.7 us
    pallas_call x1, Pallas kernels, radiation(): pl.pallas_call(shared_kernel, out_shape=(field, jax.ShapeDtypeStruct((lev...  24.7 us
    ppermute x16, starting transfers between devices, shifted(): lax.ppermute(value, axis, [(i, (i + steps) % count) for i in range(count)])  23.7 us
    ppermute x16, waiting for transfers between devices, shifted(): lax.ppermute(value, axis, [(i, (i + steps) % count) for i in range(count)])  11.9 us
    pallas_call x5, Pallas kernels, call(): pl.pallas_call(kernel, out_shape=outs, in_specs=[scalar if value.size ==...  4.55 us
    pallas_call x1, Pallas kernels, radiation(): pl.pallas_call(pack_kernel, out_shape=jax.ShapeDtypeStruct((5 * level_cou...  3.05 us
  transfers between devices with their start and end apart: 16, of which 8 were waited for; matrix products, arithmetic and copies ran while one was open for 0% of the time, Pallas kernels for 64%

profile of v4, /device:TPU:1, one launch (start us, length us, event | category | flops | bytes accessed | tf_op | source)
XLA Modules:
  0.0 112.1 jit_solution(7574775936765695953)
XLA Ops:
  0.6 0.0 copy-start
  0.6 5.2 %collective-permute-start.2 = (f32[2,576,128]{2,1,0:T(8,128)}, f32[2,576,128]{2,1,0:T(8,128)S(1)}, u32[]{:S(2)}, u32[]{:S(2)}) collective-permute-start(f32[2,576,128]{2,1,0:T(8,128)} %bitcast.11), channel_id=1, source_target_pairs={{0,28},{4,0},{8,4},{12,8},{16,12},{20,16},{24,20},{28,24},{1,29},{... | collective-permute-start | bytes 1769480 | tf_op jit(solution)/shard_map/ppermute | solution.py:25
  5.8 0.0 collective-permute-start.3
  5.8 3.1 %pack.1 = f32[362,2,128]{2,1,0:T(2,128)} custom-call(s32[1]{0:T(128)} %bitcast.theirs_ref, f32[5,72,8,128]{3,2,1,0:T(8,128)} %state_ref.5, f32[72,8,128]{2,1,0:T(8,128)} %temp_ref.5, f32[8,128]{1,0:T(8,128)} %cosine_ref.5, f32[8,128]{1,0:T(8,128)} %ground_ref.5), custom_call_target="tpu_custom_call" | custom-call | tf_op jit(solution)/shard_map/pack/pallas_call | solution.py:400
  8.9 0.0 collective-permute-start.4
  8.9 0.0 copy-done
  8.9 4.2 %collective-permute-start = (f32[576,128]{1,0:T(8,128)S(1)}, f32[576,128]{1,0:T(8,128)S(1)}, u32[]{:S(2)}, u32[]{:S(2)}) collective-permute-start(f32[576,128]{1,0:T(8,128)S(1)} %bitcast.7), channel_id=1, source_target_pairs={{0,28},{4,0},{8,4},{12,8},{16,12},{20,16},{24,20},{28,24},{1,29},{... | collective-permute-start | bytes 884744 | tf_op jit(solution)/shard_map/ppermute | solution.py:25
  13.0 0.0 collective-permute-start.1
  13.0 42.7 %home_radiation.1 = (f32[576,128]{1,0:T(8,128)}, bf16[9,336,128]{2,1,0:T(8,128)(2,1)}, f32[112,128]{1,0:T(8,128)}) custom-call(f32[5,72,8,128]{3,2,1,0:T(8,128)} %state_ref.5, f32[72,8,128]{2,1,0:T(8,128)} %temp_ref.5, f32[8,128]{1,0:T(8,128)} %cosine_ref.5, f32[8,128]{1,0:T(8,128)} %ground_ref.5, s32[8,128]{1,0:T(8,128)} %day_ref.3, ...), custom_call_target="tpu_custom_call" | custom-call | flops 185794560 | bytes 2359296 | tf_op jit(solution)/shard_map/home_radiation/pallas_call | solution.py:408
  55.7 0.0 collective-permute-done.4.received_ref
  55.7 0.0 copy-start.8
  55.7 0.8 copy-done.8
  56.5 0.0 copy-start.1
  56.5 0.0 copy-start.2
  56.5 0.0 copy-start.3
  56.5 0.0 copy-start.5
  56.5 24.7 %shared_radiation.1 = (f32[576,128]{1,0:T(8,128)}, f32[144,128]{1,0:T(8,128)}, f32[64,128]{1,0:T(8,128)}, f32[64,128]{1,0:T(8,128)}, f32[64,128]{1,0:T(8,128)}, /*index=5*/f32[64,128]{1,0:T(8,128)}) custom-call(s32[1]{0:T(128)} %bitcast.3.mine_ref, f32[5,72,8,128]{3,2,1,0:T(8,128)} %state_ref.5, f32[72,8,128]{2,1,0:T(8,128)} %temp_ref.5, ...), custom_call_target="tpu_custom_call" | custom-call | flops 92897280 | bytes 2359296 | tf_op jit(solution)/shard_map/shared_radiation/pallas_call | solution.py:419
  81.2 0.0 copy-start.4
  81.2 0.0 copy-start.6
  81.2 0.0 copy-start.7
  81.2 1.5 %collective-permute-start.5 = (f32[144,128]{1,0:T(8,128)}, f32[144,128]{1,0:T(8,128)S(1)}, u32[]{:S(2)}, u32[]{:S(2)}) collective-permute-start(f32[144,128]{1,0:T(8,128)} %get-tuple-element.30), channel_id=1, source_target_pairs={{0,16},{4,20},{8,24},{12,28},{16,0},{20,4},{24,8},{28,12},{1,17},{... | collective-permute-start | bytes 221192 | tf_op jit(solution)/shard_map/ppermute | solution.py:25
  82.8 0.0 collective-permute-done.temp_after_ref
  82.8 3.3 %collective-permute-start.6 = (f32[64,128]{1,0:T(8,128)}, f32[64,128]{1,0:T(8,128)S(1)}, u32[]{:S(2)}, u32[]{:S(2)}) collective-permute-start(f32[64,128]{1,0:T(8,128)} %get-tuple-element.31), channel_id=1, source_target_pairs={{0,28},{4,0},{8,4},{12,8},{16,12},{20,16},{24,20},{28,24},{1,29},{... | collective-permute-start | bytes 98312 | tf_op jit(solution)/shard_map/ppermute | solution.py:25
  86.0 0.0 collective-permute-done.1.temp_before_ref
  86.0 0.0 collective-permute-start.7
  86.0 0.0 collective-permute-done.2.flow_after_ref
  86.1 2.1 %collective-permute-start.8 = (f32[64,128]{1,0:T(8,128)}, f32[64,128]{1,0:T(8,128)S(1)}, u32[]{:S(2)}, u32[]{:S(2)}) collective-permute-start(f32[64,128]{1,0:T(8,128)} %get-tuple-element.33), channel_id=1, source_target_pairs={{0,12},{4,16},{8,20},{12,24},{16,28},{20,0},{24,4},{28,8},{1,13},{... | collective-permute-start | bytes 98312 | tf_op jit(solution)/shard_map/ppermute | solution.py:25
  88.1 0.0 collective-permute-done.3.flow_before_ref
  88.1 1.2 %collective-permute-start.9 = (f32[64,128]{1,0:T(8,128)}, f32[64,128]{1,0:T(8,128)S(1)}, u32[]{:S(2)}, u32[]{:S(2)}) collective-permute-start(f32[64,128]{1,0:T(8,128)} %get-tuple-element.34), channel_id=1, source_target_pairs={{0,20},{4,24},{8,28},{12,0},{16,4},{20,8},{24,12},{28,16},{1,21},{... | collective-permute-start | bytes 98312 | tf_op jit(solution)/shard_map/ppermute | solution.py:25
  89.4 0.0 copy-done.1
  89.4 0.0 copy-done.2
  89.4 0.0 copy-done.3
  89.4 0.0 copy-done.5
  89.4 0.8 own_change.1
  90.2 0.0 collective-permute-done.6.after_ref
  90.2 1.5 %collective-permute-done.7.before_ref = f32[64,128]{1,0:T(8,128)S(1)} collective-permute-done((f32[64,128]{1,0:T(8,128)}, f32[64,128]{1,0:T(8,128)S(1)}, u32[]{:S(2)}, u32[]{:S(2)}) %collective-permute-start.7) | collective-permute-done | bytes 32800 | tf_op jit(solution)/shard_map/ppermute | solution.py:25
  91.7 0.0 collective-permute-done.8.after_more_ref
  91.7 0.3 collective-permute-done.9.before_more_ref
  92.1 0.0 collective-permute-done.5.returned_ref
  92.1 0.0 copy-done.4
  92.1 0.0 copy-done.6
  92.1 0.0 copy-done.7
  92.1 1.2 %first_stage.1 = (f32[576,256]{1,0:T(8,128)S(1)}, f32[72,256]{1,0:T(8,128)S(1)}, f32[72,256]{1,0:T(8,128)S(1)}, f32[576,128]{1,0:T(8,128)}) custom-call(s32[1]{0:T(128)} %bitcast.theirs_ref, f32[576,256]{1,0:T(8,128)S(1)} %get-tuple-element.25.change_ref, f32[576,128]{1,0:T(8,128)S(1)} %copy-done.7, f32[144,128]{1,0:T(8,128)S(1)} %collective-permute-done.5.returned_ref, ...), custom_call_target="tpu_custom_call" | custom-call | tf_op jit(solution)/shard_map/first_stage/pallas_call | solution.py:628
  93.2 5.1 %collective-permute-start.10 = (f32[72,256]{1,0:T(8,128)S(1)}, f32[72,256]{1,0:T(8,128)S(1)}, u32[]{:S(2)}, u32[]{:S(2)}) collective-permute-start(f32[72,256]{1,0:T(8,128)S(1)} %get-tuple-element.37), channel_id=1, source_target_pairs={{0,1},{1,2},{2,3},{3,0},{4,5},{5,6},{6,7},{7,4},{8,9},{9,10},{10,1... | collective-permute-start | bytes 221192 | tf_op jit(solution)/shard_map/ppermute | solution.py:25
  98.4 0.0 collective-permute-start.11
  98.4 1.4 %collective-permute-done.10.below_ref = f32[72,256]{1,0:T(8,128)S(1)} collective-permute-done((f32[72,256]{1,0:T(8,128)S(1)}, f32[72,256]{1,0:T(8,128)S(1)}, u32[]{:S(2)}, u32[]{:S(2)}) %collective-permute-start.10) | collective-permute-done | bytes 73760 | tf_op jit(solution)/shard_map/ppermute | solution.py:25
  99.8 2.4 %collective-permute-done.11.above_ref = f32[72,256]{1,0:T(8,128)S(1)} collective-permute-done((f32[72,256]{1,0:T(8,128)S(1)}, f32[72,256]{1,0:T(8,128)S(1)}, u32[]{:S(2)}, u32[]{:S(2)}) %collective-permute-start.11) | collective-permute-done | bytes 73760 | tf_op jit(solution)/shard_map/ppermute | solution.py:25
  102.1 0.9 second_stage.1
  103.0 0.1 collective-permute-start.12
  103.1 0.5 collective-permute-start.13
  103.6 0.9 collective-permute-done.12.below_ref
  104.5 2.4 %collective-permute-done.13.above_ref = f32[72,256]{1,0:T(8,128)S(1)} collective-permute-done((f32[72,256]{1,0:T(8,128)S(1)}, f32[72,256]{1,0:T(8,128)S(1)}, u32[]{:S(2)}, u32[]{:S(2)}) %collective-permute-start.13) | collective-permute-done | bytes 73760 | tf_op jit(solution)/shard_map/ppermute | solution.py:25
  106.9 0.9 third_stage.1
  107.8 0.1 collective-permute-start.14
  107.9 0.5 collective-permute-start.15
  108.4 0.7 collective-permute-done.14.below_ref
  109.1 2.2 %collective-permute-done.15.above_ref = f32[72,128]{1,0:T(8,128)S(1)} collective-permute-done((f32[72,128]{1,0:T(8,128)S(1)}, f32[72,128]{1,0:T(8,128)S(1)}, u32[]{:S(2)}, u32[]{:S(2)}) %collective-permute-start.15) | collective-permute-done | bytes 36896 | tf_op jit(solution)/shard_map/ppermute | solution.py:25
  111.3 0.8 last_stage.1
Async XLA Ops:
  0.6 8.2 %copy-start = (f32[72,8,128]{2,1,0:T(8,128)S(1)}, f32[72,8,128]{2,1,0:T(8,128)}, u32[]{:S(2)}) copy-start(f32[72,8,128]{2,1,0:T(8,128)} %temp_ref.5) | copy-start | bytes 884740
  0.6 85.4 %collective-permute-start.2 = (f32[2,576,128]{2,1,0:T(8,128)}, f32[2,576,128]{2,1,0:T(8,128)S(1)}, u32[]{:S(2)}, u32[]{:S(2)}) collective-permute-start(f32[2,576,128]{2,1,0:T(8,128)} %bitcast.11), channel_id=1, source_target_pairs={{0,28},{4,0},{8,4},{12,8},{16,12},{20,16},{24,20},{28,24},{1,29},{... | collective-permute-start | bytes 1769480 | tf_op jit(solution)/shard_map/ppermute | solution.py:25
  5.8 82.3 %collective-permute-start.3 = (f32[2,576,128]{2,1,0:T(8,128)}, f32[2,576,128]{2,1,0:T(8,128)S(1)}, u32[]{:S(2)}, u32[]{:S(2)}) collective-permute-start(f32[2,576,128]{2,1,0:T(8,128)} %bitcast.12), channel_id=1, source_target_pairs={{0,4},{4,8},{8,12},{12,16},{16,20},{20,24},{24,28},{28,0},{1,5},{5... | collective-permute-start | bytes 1769480 | tf_op jit(solution)/shard_map/ppermute | solution.py:25
  8.9 46.9 %collective-permute-start.4 = (f32[362,2,128]{2,1,0:T(2,128)}, f32[362,2,128]{2,1,0:T(2,128)S(1)}, u32[]{:S(2)}, u32[]{:S(2)}) collective-permute-start(f32[362,2,128]{2,1,0:T(2,128)} %pack.1), channel_id=1, source_target_pairs={{0,16},{4,20},{8,24},{12,28},{16,0},{20,4},{24,8},{28,12},{1,17},{... | collective-permute-start | bytes 1112072 | tf_op jit(solution)/shard_map/ppermute | solution.py:25
  8.9 73.9 %collective-permute-start = (f32[576,128]{1,0:T(8,128)S(1)}, f32[576,128]{1,0:T(8,128)S(1)}, u32[]{:S(2)}, u32[]{:S(2)}) collective-permute-start(f32[576,128]{1,0:T(8,128)S(1)} %bitcast.7), channel_id=1, source_target_pairs={{0,28},{4,0},{8,4},{12,8},{16,12},{20,16},{24,20},{28,24},{1,29},{... | collective-permute-start | bytes 884744 | tf_op jit(solution)/shard_map/ppermute | solution.py:25
  13.0 73.0 %collective-permute-start.1 = (f32[576,128]{1,0:T(8,128)S(1)}, f32[576,128]{1,0:T(8,128)S(1)}, u32[]{:S(2)}, u32[]{:S(2)}) collective-permute-start(f32[576,128]{1,0:T(8,128)S(1)} %bitcast.8), channel_id=1, source_target_pairs={{0,4},{4,8},{8,12},{12,16},{16,20},{20,24},{24,28},{28,0},{1,5},{5... | collective-permute-start | bytes 884744 | tf_op jit(solution)/shard_map/ppermute | solution.py:25
  55.7 0.8 copy-start.8
  56.5 32.9 %copy-start.1 = (f32[72,8,128]{2,1,0:T(8,128)S(1)}, f32[72,8,128]{2,1,0:T(8,128)}, u32[]{:S(2)}) copy-start(f32[72,8,128]{2,1,0:T(8,128)} %temp_ref.5) | copy-start | bytes 884740
  56.5 32.9 %copy-start.2 = (bf16[256,256]{1,0:T(8,128)(2,1)S(1)}, bf16[256,256]{1,0:T(8,128)(2,1)}, u32[]{:S(2)}) copy-start(bf16[256,256]{1,0:T(8,128)(2,1)} %constant.18.clone.high_ref) | copy-start | bytes 393220
  56.5 32.9 %copy-start.3 = (bf16[256,256]{1,0:T(8,128)(2,1)S(1)}, bf16[256,256]{1,0:T(8,128)(2,1)}, u32[]{:S(2)}) copy-start(bf16[256,256]{1,0:T(8,128)(2,1)} %constant.19.clone.low_ref) | copy-start | bytes 393220
  56.5 32.9 %copy-start.5 = (f32[2,72,8,128]{3,2,1,0:T(8,128)S(1)}, f32[2,72,8,128]{3,2,1,0:T(8,128)}, u32[]{:S(2)}) copy-start(f32[2,72,8,128]{3,2,1,0:T(8,128)} %param.15) | copy-start | bytes 1769476
  81.2 10.8 %copy-start.4 = (bf16[256,256]{1,0:T(8,128)(2,1)S(1)}, bf16[256,256]{1,0:T(8,128)(2,1)}, u32[]{:S(2)}) copy-start(bf16[256,256]{1,0:T(8,128)(2,1)} %constant.20.clone.average_ref) | copy-start | bytes 393220
  81.2 10.8 %copy-start.6 = (bf16[256,1152]{1,0:T(8,128)(2,1)S(1)}, bf16[256,1152]{1,0:T(8,128)(2,1)}, u32[]{:S(2)}) copy-start(bf16[256,1152]{1,0:T(8,128)(2,1)} %constant.22.edge_ref) | copy-start | bytes 1769476
  81.2 10.8 %copy-start.7 = (f32[576,128]{1,0:T(8,128)S(1)}, f32[576,128]{1,0:T(8,128)}, u32[]{:S(2)}) copy-start(f32[576,128]{1,0:T(8,128)} %get-tuple-element.29.heat_ref) | copy-start | bytes 884740
  81.2 10.8 %collective-permute-start.5 = (f32[144,128]{1,0:T(8,128)}, f32[144,128]{1,0:T(8,128)S(1)}, u32[]{:S(2)}, u32[]{:S(2)}) collective-permute-start(f32[144,128]{1,0:T(8,128)} %get-tuple-element.30), channel_id=1, source_target_pairs={{0,16},{4,20},{8,24},{12,28},{16,0},{20,4},{24,8},{28,12},{1,17},{... | collective-permute-start | bytes 221192 | tf_op jit(solution)/shard_map/ppermute | solution.py:25
  82.8 7.4 %collective-permute-start.6 = (f32[64,128]{1,0:T(8,128)}, f32[64,128]{1,0:T(8,128)S(1)}, u32[]{:S(2)}, u32[]{:S(2)}) collective-permute-start(f32[64,128]{1,0:T(8,128)} %get-tuple-element.31), channel_id=1, source_target_pairs={{0,28},{4,0},{8,4},{12,8},{16,12},{20,16},{24,20},{28,24},{1,29},{... | collective-permute-start | bytes 98312 | tf_op jit(solution)/shard_map/ppermute | solution.py:25
  86.0 5.7 %collective-permute-start.7 = (f32[64,128]{1,0:T(8,128)}, f32[64,128]{1,0:T(8,128)S(1)}, u32[]{:S(2)}, u32[]{:S(2)}) collective-permute-start(f32[64,128]{1,0:T(8,128)} %get-tuple-element.32), channel_id=1, source_target_pairs={{0,4},{4,8},{8,12},{12,16},{16,20},{20,24},{24,28},{28,0},{1,5},{5... | collective-permute-start | bytes 98312 | tf_op jit(solution)/shard_map/ppermute | solution.py:25
  86.1 5.7 %collective-permute-start.8 = (f32[64,128]{1,0:T(8,128)}, f32[64,128]{1,0:T(8,128)S(1)}, u32[]{:S(2)}, u32[]{:S(2)}) collective-permute-start(f32[64,128]{1,0:T(8,128)} %get-tuple-element.33), channel_id=1, source_target_pairs={{0,12},{4,16},{8,20},{12,24},{16,28},{20,0},{24,4},{28,8},{1,13},{... | collective-permute-start | bytes 98312 | tf_op jit(solution)/shard_map/ppermute | solution.py:25
  88.1 3.9 %collective-permute-start.9 = (f32[64,128]{1,0:T(8,128)}, f32[64,128]{1,0:T(8,128)S(1)}, u32[]{:S(2)}, u32[]{:S(2)}) collective-permute-start(f32[64,128]{1,0:T(8,128)} %get-tuple-element.34), channel_id=1, source_target_pairs={{0,20},{4,24},{8,28},{12,0},{16,4},{20,8},{24,12},{28,16},{1,21},{... | collective-permute-start | bytes 98312 | tf_op jit(solution)/shard_map/ppermute | solution.py:25
  93.2 6.5 %collective-permute-start.10 = (f32[72,256]{1,0:T(8,128)S(1)}, f32[72,256]{1,0:T(8,128)S(1)}, u32[]{:S(2)}, u32[]{:S(2)}) collective-permute-start(f32[72,256]{1,0:T(8,128)S(1)} %get-tuple-element.37), channel_id=1, source_target_pairs={{0,1},{1,2},{2,3},{3,0},{4,5},{5,6},{6,7},{7,4},{8,9},{9,10},{10,1... | collective-permute-start | bytes 221192 | tf_op jit(solution)/shard_map/ppermute | solution.py:25
  98.4 3.8 %collective-permute-start.11 = (f32[72,256]{1,0:T(8,128)S(1)}, f32[72,256]{1,0:T(8,128)S(1)}, u32[]{:S(2)}, u32[]{:S(2)}) collective-permute-start(f32[72,256]{1,0:T(8,128)S(1)} %get-tuple-element.38), channel_id=1, source_target_pairs={{0,3},{1,0},{2,1},{3,2},{4,7},{5,4},{6,5},{7,6},{8,11},{9,8},{10,9... | collective-permute-start | bytes 221192 | tf_op jit(solution)/shard_map/ppermute | solution.py:25
  103.0 1.5 %collective-permute-start.12 = (f32[72,256]{1,0:T(8,128)S(1)}, f32[72,256]{1,0:T(8,128)S(1)}, u32[]{:S(2)}, u32[]{:S(2)}) collective-permute-start(f32[72,256]{1,0:T(8,128)S(1)} %get-tuple-element.41), channel_id=1, source_target_pairs={{0,1},{1,2},{2,3},{3,0},{4,5},{5,6},{6,7},{7,4},{8,9},{9,10},{10,1... | collective-permute-start | bytes 221192 | tf_op jit(solution)/shard_map/ppermute | solution.py:25
  103.1 3.8 %collective-permute-start.13 = (f32[72,256]{1,0:T(8,128)S(1)}, f32[72,256]{1,0:T(8,128)S(1)}, u32[]{:S(2)}, u32[]{:S(2)}) collective-permute-start(f32[72,256]{1,0:T(8,128)S(1)} %get-tuple-element.42), channel_id=1, source_target_pairs={{0,3},{1,0},{2,1},{3,2},{4,7},{5,4},{6,5},{7,6},{8,11},{9,8},{10,9... | collective-permute-start | bytes 221192 | tf_op jit(solution)/shard_map/ppermute | solution.py:25
  107.8 1.3 %collective-permute-start.14 = (f32[72,128]{1,0:T(8,128)S(1)}, f32[72,128]{1,0:T(8,128)S(1)}, u32[]{:S(2)}, u32[]{:S(2)}) collective-permute-start(f32[72,128]{1,0:T(8,128)S(1)} %get-tuple-element.45), channel_id=1, source_target_pairs={{0,1},{1,2},{2,3},{3,0},{4,5},{5,6},{6,7},{7,4},{8,9},{9,10},{10,1... | collective-permute-start | bytes 110600 | tf_op jit(solution)/shard_map/ppermute | solution.py:25
  107.9 3.4 %collective-permute-start.15 = (f32[72,128]{1,0:T(8,128)S(1)}, f32[72,128]{1,0:T(8,128)S(1)}, u32[]{:S(2)}, u32[]{:S(2)}) collective-permute-start(f32[72,128]{1,0:T(8,128)S(1)} %get-tuple-element.46), channel_id=1, source_target_pairs={{0,3},{1,0},{2,1},{3,2},{4,7},{5,4},{6,5},{7,6},{8,11},{9,8},{10,9... | collective-permute-start | bytes 110600 | tf_op jit(solution)/shard_map/ppermute | solution.py:25

commit v5 on v4

--- a/solution.py
+++ b/solution.py
@@ -16,8 +16,10 @@
 
 GROUP = 8
 TERMS = 16
-BLOCK = 8
-QUANTITIES = 3
+BLOCK = 12
+PARTIAL = 5
+CHUNKS = 2
+QUANTITIES = 4
 
 
 def shifted(value, axis, steps):
@@ -93,12 +95,15 @@
         (absorbed, water(la, ia)),
         (gas, water(la + ls * (1.0 - w[2]), ia + li * (1.0 - w[5]))),
         (gas + gas, water(2.0 * w[0], 2.0 * w[3])),
-    )
-    for n, (values, constant) in enumerate(pairs):
-        for group in range(groups):
-            optics_ref[group, n * gpoints : (n + 1) * gpoints, :] = (
-                values[:, group * width : (group + 1) * width] + constant
-            ).astype(jnp.bfloat16)
+        (gases[2], water(ls * (1.0 + w[2]), li * (1.0 + w[5]))),
+    )
+    chunk = gpoints // CHUNKS
+    for group in range(groups):
+        span = slice(group * width, (group + 1) * width)
+        tables = [values[:, span] + constant for values, constant in pairs]
+        for c in range(CHUNKS):
+            rows = [table[c * chunk : (c + 1) * chunk] for table in tables]
+            optics_ref[group, c] = jnp.concatenate(rows, axis=0).astype(jnp.bfloat16)
     only = jnp.where(place == 0, 1.0, 0.0)
     weight = jnp.broadcast_to(w[6], (8, gpoints))
     weight_ref[...] = across(weight, only, lax.Precision.HIGHEST)
@@ -126,15 +131,18 @@
 
 
 def sweep_row(
-    row, lines, count, cosine, ground, optics_ref, weight_ref, terms_ref, right_ref, depths_ref,
-    gain_ref, offset_ref, direct_ref, partial_ref, ratio_ref, source_ref, slant_ref,
+    row, line, lines, count, cosine, ground, optics_ref, weight_ref, terms_ref, right_ref,
+    depths_0, depths_1, gain_ref, offset_ref, direct_ref, partial_ref, ratio_ref, source_ref, slant_ref,
 ):
     level_count, gpoints, lanes = gain_ref.shape
     blocks = level_count // BLOCK
+    chunk = gpoints // CHUNKS
+    slots = (depths_0, depths_1)
+    once = 1 + jnp.minimum(row, 0)
 
     def place_group(group, carry):
         for j in range(GROUP):
-            start = (group * GROUP + j) * TERMS * lines + row
+            start = (group * GROUP + j) * TERMS * lines + line
             tile = terms_ref[pl.ds(start, TERMS, stride=lines), :].astype(jnp.bfloat16)
             half = lanes * (j % 2)
             pair = group * (GROUP // 2) + j // 2
@@ -151,22 +159,24 @@
     ratio_ref[...] = over_rows(jnp.broadcast_to((1.0 + ground) * clear, (8, lanes)))
     source_ref[...] = over_rows(jnp.broadcast_to(2.0 * ground * clear, (8, lanes)))
 
-    def below_block(step, carry):
-        block = blocks - 1 - step
+    def fill(block, c):
         for p in range(BLOCK // 2):
             pair = block * (BLOCK // 2) + p
-            depths_ref[p] = jnp.dot(
-                optics_ref[pair // (GROUP // 2)], right_ref[pair],
+            slots[c % 2][p] = jnp.dot(
+                optics_ref[pair // (GROUP // 2), c], right_ref[pair],
                 preferred_element_type=jnp.float32,
             )
-        ratio, source = ratio_ref[...], source_ref[...]
-        slant = over_rows(slant_ref[...])
+
+    def below(block, c):
+        span = slice(c * chunk, (c + 1) * chunk)
+        ratio, source = ratio_ref[span], source_ref[span]
+        slant = jnp.broadcast_to(slant_ref[...][None], (chunk // 8, 8, lanes))
+        slant = slant.reshape(chunk, lanes)
         for j in reversed(range(BLOCK)):
             level = block * BLOCK + j
-            part = depths_ref.at[j // 2, :, (j % 2) * lanes : (j % 2 + 1) * lanes]
-            a, b, depth = [part[n * gpoints : (n + 1) * gpoints] for n in range(QUANTITIES)]
+            part = slots[c % 2].at[j // 2, :, (j % 2) * lanes : (j % 2 + 1) * lanes]
+            a, b, depth, along = [part[n * chunk : (n + 1) * chunk] for n in range(QUANTITIES)]
             away = b - a
-            along = (depth - a) - b
             square = a * b
             inverse_root = lax.rsqrt(square)
             h = jnp.tanh(square * inverse_root)
@@ -184,13 +194,27 @@
             ratio = (one * ratio + p) * inverse
             gain = through * inverse
             source = through * push + (ratio + 1.0) * up
-            gain_ref[level] = gain
-            offset_ref[level] = (gain * up + down) - s * push
-            direct_ref[level] = direct
-        ratio_ref[...] = ratio
-        source_ref[...] = source
+            gain_ref[level, span] = gain
+            offset_ref[level, span] = (gain * up + down) - s * push
+            direct_ref[level, span] = direct
+        ratio_ref[span] = ratio
+        source_ref[span] = source
+
+    def below_block(step, carry):
+        block = blocks - 1 - step
+        for c in range(CHUNKS):
+            def turn(n, carry, c=c):
+                below(block, c)
+                if c + 1 < CHUNKS:
+                    fill(block, c + 1)
+                else:
+                    fill(jnp.maximum(block - 1, 0), 0)
+                return carry
+
+            lax.fori_loop(0, once, turn, 0)
         return carry
 
+    fill(blocks - 1, 0)
     lax.fori_loop(0, blocks, below_block, 0)
 
     def folded(net):
@@ -203,7 +227,7 @@
         return net, beam
 
     nothing = jnp.zeros((gpoints, lanes), jnp.float32)
-    carry = lax.fori_loop(0, 1 + jnp.minimum(row, 0), top, (nothing, nothing))
+    carry = lax.fori_loop(0, once, top, (nothing, nothing))
 
     def down_group(group, carry):
         net, beam = carry
@@ -232,7 +256,7 @@
 
 
 def home_kernel(
-    state_ref, temp_ref, cosine_ref, ground_ref, day_ref, molecular_ref, table_ref,
+    first, state_ref, temp_ref, cosine_ref, ground_ref, day_ref, molecular_ref, table_ref,
     heat_ref, optics_ref, weight_ref, terms_ref, right_ref, *scratch,
 ):
     level_count, lines, lanes = temp_ref.shape
@@ -242,149 +266,183 @@
     @pl.when(row == 0)
     def prepare():
         optics_matrices(molecular_ref, table_ref, optics_ref, weight_ref)
-        right_ref[...] = jnp.zeros_like(right_ref)
         heat_ref[...] = jnp.zeros_like(heat_ref)
-
-        def level(l, carry):
-            write_terms(terms_ref, l, layer_terms(state_ref, temp_ref, l), lines)
-            return carry
-
-        lax.fori_loop(0, level_count, level, 0)
-
+        prepare_terms(state_ref, temp_ref, terms_ref, right_ref)
+
+    line = first + row
     sweep_row(
-        row, lines, count, cosine_ref[pl.ds(row, 1), :], ground_ref[pl.ds(row, 1), :],
+        row, line, lines, count, cosine_ref[pl.ds(line, 1), :], ground_ref[pl.ds(line, 1), :],
         optics_ref, weight_ref, terms_ref, right_ref, *scratch,
     )
 
     @pl.when(row == count - 1)
     def finish():
-        home = lines // 2
-        day = day_ref[:home, :] == 1
+        size = heat_ref.shape[0] // level_count
+        rows = slice(first, first + size)
+        day = day_ref[rows, :] == 1
 
         def write(level, value):
-            start = pl.multiple_of(level * lines, 8)
-            heat_ref[pl.ds(start, home), :] = jnp.where(day, value, 0.0)
-
-        level_heating(scratch[4], level_count, gpoints, home, write)
-
-
-def pack_kernel(theirs_ref, state_ref, temp_ref, cosine_ref, ground_ref, out_ref, own_ref):
+            heat_ref[pl.ds(level * size, size), :] = jnp.where(day, value, 0.0)
+
+        level_heating(scratch[PARTIAL], level_count, gpoints, size, write)
+
+
+def prepare_terms(state_ref, temp_ref, terms_ref, right_ref):
     level_count, lines, lanes = temp_ref.shape
-    count = out_ref.shape[1]
-    first = theirs_ref[0]
+    right_ref[...] = jnp.zeros_like(right_ref)
+
+    def level(l, carry):
+        write_terms(terms_ref, l, layer_terms(state_ref, temp_ref, l), lines)
+        return carry
+
+    lax.fori_loop(0, level_count, level, 0, unroll=2)
+
+
+def pack_kernel(
+    places_ref, state_ref, temp_ref, flow_ref, cosine_ref, ground_ref,
+    sent_ref, kept_ref, fields_ref, own_ref,
+):
+    level_count, lines, lanes = temp_ref.shape
+    count = sent_ref.shape[1]
 
     def level(l, carry):
         for k, value in enumerate(layer_terms(state_ref, temp_ref, l)):
             own_ref[pl.ds(pl.multiple_of((5 * l + k) * lines, 8), lines), :] = value
+        fields_ref[0, l] = temp_ref[l]
+        fields_ref[1, l] = flow_ref[0, l]
+        fields_ref[2, l] = flow_ref[1, l]
         return carry
 
-    lax.fori_loop(0, level_count, level, 0)
-
-    def copy(n, carry):
-        out_ref[n] = own_ref[pl.ds(n * lines + first, count), :]
-        return carry
-
-    lax.fori_loop(0, 5 * level_count, copy, 0, unroll=8)
-    out_ref[5 * level_count] = cosine_ref[pl.ds(first, count), :]
-    out_ref[5 * level_count + 1] = ground_ref[pl.ds(first, count), :]
+    lax.fori_loop(0, level_count, level, 0, unroll=4)
+    for n, ref in enumerate((kept_ref, sent_ref)):
+        first = places_ref[n]
+
+        def copy(n, carry, ref=ref, first=first):
+            ref[n] = own_ref[pl.ds(n * lines + first, count), :]
+            return carry
+
+        lax.fori_loop(0, 5 * level_count, copy, 0, unroll=8)
+        ref[5 * level_count] = cosine_ref[pl.ds(first, count), :]
+        ref[5 * level_count + 1] = ground_ref[pl.ds(first, count), :]
 
 
 def shared_kernel(
-    mine_ref, state_ref, temp_ref, cosine_ref, ground_ref, day_ref, received_ref, optics_ref,
-    weight_ref, edge_ref, home_ref,
-    heat_ref, theirs_ref, first_ref, last_ref, their_first_ref, their_last_ref,
-    own_ref, strip_ref, surface_ref, terms_ref, right_ref, *scratch,
-):
-    level_count, lines, lanes = temp_ref.shape
+    places_ref, kept_ref, received_ref, day_ref, optics_ref, weight_ref, edge_ref,
+    mine_ref, theirs_ref, their_first_ref, their_last_ref,
+    surface_ref, strip_ref, terms_ref, right_ref, *scratch,
+):
+    level_count = kept_ref.shape[0] // 5
+    shared, lanes = kept_ref.shape[1:]
     gpoints = weight_ref.shape[0]
     row, count = pl.program_id(0), pl.num_programs(0)
-    shared = received_ref.shape[1]
-    first = mine_ref[0]
+    first = places_ref[0]
     day = day_ref[pl.ds(first, shared), :] == 1
 
     @pl.when(row == 0)
     def prepare():
         right_ref[...] = jnp.zeros_like(right_ref)
 
-        def own(l, carry):
-            for k, value in enumerate(layer_terms(state_ref, temp_ref, l)):
-                own_ref[pl.ds(pl.multiple_of((5 * l + k) * lines, 8), lines), :] = value
-            return carry
-
-        lax.fori_loop(0, level_count, own, 0)
-
         def level(l, carry):
             values = [
-                jnp.where(
-                    day, own_ref[pl.ds((5 * l + k) * lines + first, shared), :],
-                    received_ref[5 * l + k],
-                )
-                for k in range(5)
+                jnp.where(day, kept_ref[5 * l + k], received_ref[5 * l + k]) for k in range(5)
             ]
             write_terms(terms_ref, l, values, shared)
             return carry
 
-        lax.fori_loop(0, level_count, level, 0)
-        for n, ref in enumerate((cosine_ref, ground_ref)):
-            surface_ref[n, :shared, :] = jnp.where(
-                day, ref[pl.ds(first, shared), :], received_ref[5 * level_count + n]
-            )
+        lax.fori_loop(0, level_count, level, 0, unroll=4)
+        for n in range(2):
+            place = 5 * level_count + n
+            surface_ref[n, :shared, :] = jnp.where(day, kept_ref[place], received_ref[place])
 
     sweep_row(
-        row, shared, count, surface_ref[0, pl.ds(row, 1), :], surface_ref[1, pl.ds(row, 1), :],
-        optics_ref, weight_ref, terms_ref, right_ref, *scratch,
+        row, row, shared, count, surface_ref[0, pl.ds(row, 1), :],
+        surface_ref[1, pl.ds(row, 1), :], optics_ref, weight_ref, terms_ref, right_ref, *scratch,
     )
 
     @pl.when(row == count - 1)
     def finish():
-        heat_ref[...] = home_ref[...]
-
         def write(level, value):
-            heat_ref[pl.ds(level * lines + first, shared), :] = jnp.where(day, value, 0.0)
-            theirs_ref[pl.ds(level * shared, shared), :] = jnp.where(day, 0.0, value)
-
-        level_heating(scratch[4], level_count, gpoints, shared, write)
+            span = pl.ds(level * shared, shared)
+            mine_ref[span, :] = jnp.where(day, value, 0.0)
+            theirs_ref[span, :] = jnp.where(day, 0.0, value)
+
+        level_heating(scratch[PARTIAL], level_count, gpoints, shared, write)
         strip_ref[...] = jnp.zeros_like(strip_ref)
-        for k in range(level_count // 8):
-            span = slice(lanes * k, lanes * (k + 1))
-            for r in range(lines):
-                strip_ref[8 * r : 8 * (r + 1), span] = heat_ref[
-                    pl.ds(8 * k * lines + r, 8, stride=lines), :
-                ]
-            for r in range(shared):
-                start = pl.multiple_of(8 * (lines + first + r), 8)
-                strip_ref[pl.ds(start, 8), span] = theirs_ref[
-                    pl.ds(8 * k * shared + r, 8, stride=shared), :
-                ]
+        for r in range(shared):
+            start = pl.multiple_of(8 * (first + r), 8)
+            write_strip(theirs_ref, r, shared, strip_ref, start)
         packed = split_dot(strip_ref[...], edge_ref[...])
-        half = 8 * lines
-        first_ref[...] = packed[:half, :lanes]
-        last_ref[...] = packed[:half, lanes:]
-        their_first_ref[...] = packed[half:, :lanes]
-        their_last_ref[...] = packed[half:, lanes:]
-
-
-def radiation(state, temper, cosine, ground, day, molecular, condensate):
+        their_first_ref[...] = packed[:, :lanes]
+        their_last_ref[...] = packed[:, lanes:]
+
+
+def write_strip(source_ref, r, lines, strip_ref, start):
+    lanes = source_ref.shape[1]
+    for k in range(strip_ref.shape[1] // lanes):
+        strip_ref[pl.ds(start, 8), lanes * k : lanes * (k + 1)] = source_ref[
+            pl.ds(8 * k * lines + r, 8, stride=lines), :
+        ]
+
+
+def last_home_kernel(
+    places_ref, state_ref, temp_ref, cosine_ref, ground_ref, day_ref, optics_ref, weight_ref,
+    edge_ref, home_ref, mine_ref,
+    heat_ref, first_ref, last_ref, strip_ref, terms_ref, right_ref, *scratch,
+):
+    level_count, lines, lanes = temp_ref.shape
+    gpoints = weight_ref.shape[0]
+    row = pl.program_id(0)
+    line = lines // 2 - 1
+    prepare_terms(state_ref, temp_ref, terms_ref, right_ref)
+    sweep_row(
+        row, line, lines, 1, cosine_ref[pl.ds(line, 1), :], ground_ref[pl.ds(line, 1), :],
+        optics_ref, weight_ref, terms_ref, right_ref, *scratch,
+    )
+    first = places_ref[0]
+    shared = mine_ref.shape[0] // level_count
+    day = day_ref[line : line + 1, :] == 1
+    heat_ref[...] = jnp.zeros_like(heat_ref)
+
+    def write(level, value):
+        start = pl.multiple_of(level * lines, 8)
+        heat_ref[pl.ds(start, line), :] = home_ref[pl.ds(level * line, line), :]
+        heat_ref[pl.ds(start + line, 1), :] = jnp.where(day, value, 0.0)
+        heat_ref[pl.ds(start + first, shared), :] = mine_ref[pl.ds(level * shared, shared), :]
+
+    level_heating(scratch[PARTIAL], level_count, gpoints, 1, write)
+    for r in range(lines):
+        write_strip(heat_ref, r, lines, strip_ref, 8 * r)
+    packed = split_dot(strip_ref[...], edge_ref[...])
+    first_ref[...] = packed[:, :lanes]
+    last_ref[...] = packed[:, lanes:]
+
+
+def radiation(state, temper, flow, cosine, ground, day, molecular, condensate):
     level_count, rows, lanes = temper.shape
     gpoints = molecular.shape[1]
     home, shared = rows // 2, rows // 4
     partner = lax.axis_size("gx") // 2
     low = lax.axis_index("gx") < partner
-    mine = jnp.where(low, home, home + shared).astype(jnp.int32).reshape(1)
-    theirs = jnp.where(low, home + shared, home).astype(jnp.int32).reshape(1)
+    places = jnp.where(
+        low, jnp.array([home, home + shared], jnp.int32), jnp.array([home + shared, home], jnp.int32)
+    )
     full = pltpu.VMEM((level_count, gpoints, lanes), jnp.float32)
     plane = pltpu.VMEM((gpoints, lanes), jnp.float32)
     whole = pl.BlockSpec(memory_space=pltpu.VMEM)
     scalar = pl.BlockSpec(memory_space=pltpu.SMEM)
-    field = jax.ShapeDtypeStruct((level_count * rows, lanes), jnp.float32)
-    own = pltpu.VMEM((5 * level_count * rows, lanes), jnp.float32)
     params = pltpu.CompilerParams(vmem_limit_bytes=60 * 1024 * 1024)
+    part = (QUANTITIES * gpoints // CHUNKS, GROUP * TERMS)
+    strip = pltpu.VMEM((8 * rows, level_count // 8 * lanes), jnp.float32)
+
+    def field(lines):
+        return jax.ShapeDtypeStruct((level_count * lines, lanes), jnp.float32)
 
     def scratch(lines, count):
         return [
             pltpu.VMEM((level_count * TERMS * lines, lanes), jnp.float32),
             pltpu.VMEM((level_count // 2, GROUP * TERMS, 2 * lanes), jnp.bfloat16),
-            pltpu.VMEM((BLOCK // 2, QUANTITIES * gpoints, 2 * lanes), jnp.float32),
+            pltpu.VMEM((BLOCK // 2, part[0], 2 * lanes), jnp.float32),
+            pltpu.VMEM((BLOCK // 2, part[0], 2 * lanes), jnp.float32),
             full, full, full,
             pltpu.VMEM(((level_count + 1) * count * 8, lanes), jnp.float32),
             plane, plane,
@@ -397,42 +455,54 @@
             flops=45 * cells, bytes_accessed=32 * temper.size, transcendentals=5 * cells
         )
 
-    sent = pl.pallas_call(
+    state_rows = jax.ShapeDtypeStruct((5 * level_count + 2, shared, lanes), jnp.float32)
+    sent, kept, fields = pl.pallas_call(
         pack_kernel,
-        out_shape=jax.ShapeDtypeStruct((5 * level_count + 2, shared, lanes), jnp.float32),
-        in_specs=[scalar] + [whole] * 4, out_specs=whole, scratch_shapes=[own],
+        out_shape=(
+            state_rows, state_rows,
+            jax.ShapeDtypeStruct((3, level_count, rows, lanes), jnp.float32),
+        ),
+        in_specs=[scalar] + [whole] * 5, out_specs=(whole,) * 3,
+        scratch_shapes=[pltpu.VMEM((5 * level_count * rows, lanes), jnp.float32)],
         compiler_params=params, name="pack",
-    )(theirs, state, temper, cosine, ground)
+    )(places, state, temper, flow, cosine, ground)
     received = shifted(sent, "gx", partner)
-    optics = (level_count // GROUP, QUANTITIES * gpoints, GROUP * TERMS)
-    heat, optics, weight = pl.pallas_call(
-        home_kernel,
+    fields_after, fields_before = shifted(fields, "gx", -1), shifted(fields, "gx", 1)
+    early = home - 1
+    home_heat, optics, weight = pl.pallas_call(
+        functools.partial(home_kernel, 0),
         out_shape=(
-            field, jax.ShapeDtypeStruct(optics, jnp.bfloat16),
+            field(early),
+            jax.ShapeDtypeStruct((level_count // GROUP, CHUNKS) + part, jnp.bfloat16),
             jax.ShapeDtypeStruct((gpoints, lanes), jnp.float32),
         ),
-        grid=(home,), in_specs=[whole] * 7, out_specs=(whole,) * 3,
-        scratch_shapes=scratch(rows, home), compiler_params=params, cost_estimate=cost(home),
+        grid=(early,), in_specs=[whole] * 7, out_specs=(whole,) * 3,
+        scratch_shapes=scratch(rows, early), compiler_params=params, cost_estimate=cost(early),
         name="home_radiation",
     )(state, temper, cosine, ground, day, molecular.transpose(0, 2, 1), condensate)
     edge = jax.ShapeDtypeStruct((8 * rows, lanes), jnp.float32)
-    return pl.pallas_call(
+    edges = edge_matrix(level_count, lanes)
+    mine, theirs, their_first, their_last = pl.pallas_call(
         shared_kernel,
-        out_shape=(
-            field, jax.ShapeDtypeStruct((level_count * shared, lanes), jnp.float32),
-            edge, edge, edge, edge,
-        ),
-        grid=(shared,), in_specs=[scalar] + [whole] * 10, out_specs=(whole,) * 6,
-        scratch_shapes=[
-            own,
-            pltpu.VMEM((16 * rows, level_count // 8 * lanes), jnp.float32),
-            pltpu.VMEM((2, 8, lanes), jnp.float32),
-        ] + scratch(shared, shared),
+        out_shape=(field(shared), field(shared), edge, edge),
+        grid=(shared,), in_specs=[scalar] + [whole] * 6, out_specs=(whole,) * 4,
+        scratch_shapes=[pltpu.VMEM((2, 8, lanes), jnp.float32), strip] + scratch(shared, shared),
         compiler_params=params, cost_estimate=cost(shared), name="shared_radiation",
-    )(
-        mine, state, temper, cosine, ground, day, received, optics, weight,
-        edge_matrix(level_count, lanes), heat,
-    ) + (theirs,)
+    )(places, kept, received, day, optics, weight, edges)
+    returned = shifted(theirs, "gx", partner)
+    after_more = shifted(their_first, "gx", partner - 1)
+    before_more = shifted(their_last, "gx", partner + 1)
+    heat, first, last = pl.pallas_call(
+        last_home_kernel,
+        out_shape=(field(rows), edge, edge),
+        grid=(1,), in_specs=[scalar] + [whole] * 10, out_specs=(whole,) * 3,
+        scratch_shapes=[strip] + scratch(rows, 1),
+        compiler_params=params, cost_estimate=cost(1), name="last_home_radiation",
+    )(places, state, temper, cosine, ground, day, optics, weight, edges, home_heat, mine)
+    after, before = shifted(first, "gx", -1), shifted(last, "gx", 1)
+    return (
+        heat, returned, places, after, before, after_more, before_more, fields_after, fields_before
+    )
 
 
 def edge_matrix(level_count, lanes):
@@ -497,7 +567,7 @@
 
 
 def own_change_kernel(
-    temp_ref, temp_after_ref, temp_before_ref, flow_ref, flow_after_ref, flow_before_ref,
+    temp_ref, flow_ref, after_ref, before_ref,
     high_ref, low_ref, change_ref, wind_ref, temp_wide_ref, slope_ref,
 ):
     level_count = change_ref.shape[0] // ROWS
@@ -511,8 +581,9 @@
 
     for r in range(ROWS):
         rows = slice(r * level_count, (r + 1) * level_count)
-        pairs = [tiles(temp_ref, temp_after_ref, temp_before_ref, r)] + [
-            tiles(flow_ref.at[n], flow_after_ref.at[n], flow_before_ref.at[n], r) for n in range(2)
+        pairs = [
+            tiles(own, after_ref.at[n], before_ref.at[n], r)
+            for n, own in enumerate((temp_ref, flow_ref.at[0], flow_ref.at[1]))
         ]
         for half in range(2):
             span = slice(half * lanes, (half + 1) * lanes)
@@ -543,7 +614,7 @@
 
 
 def first_stage_kernel(
-    theirs_ref, change_ref, heat_ref, returned_ref, after_ref, before_ref, after_more_ref,
+    places_ref, change_ref, heat_ref, returned_ref, after_ref, before_ref, after_more_ref,
     before_more_ref, edge_ref, average_ref,
     out_ref, first_ref, last_ref, heat_out_ref, sum_ref,
 ):
@@ -559,7 +630,7 @@
         own = heat_ref[span, :]
         if r >= ROWS // 2:
             n = r % shared
-            here = theirs_ref[0] == r - n
+            here = places_ref[1] == r - n
             own = own + jnp.where(
                 here, returned_ref[pl.ds(n, level_count, stride=shared), :], 0.0
             )
@@ -627,32 +698,29 @@
     def call(kernel, name, outs, scratch, *values):
         return pl.pallas_call(
             kernel, out_shape=outs,
-            in_specs=[scalar if value.size == 1 else whole for value in values],
+            in_specs=[scalar if value.ndim == 1 else whole for value in values],
             out_specs=jax.tree.map(lambda _: whole, outs), scratch_shapes=[wide_scratch] * scratch,
             compiler_params=pltpu.CompilerParams(vmem_limit_bytes=40 * 1024 * 1024), name=name,
         )(*values)
 
     slopes = slope_matrices(lanes)
     average = average_matrix(lanes)
-    temper_after, temper_before = shifted(temper, "gx", -1), shifted(temper, "gx", 1)
-    flow_after, flow_before = shifted(flow, "gx", -1), shifted(flow, "gx", 1)
-    heat, heat_theirs, heat_first, heat_last, their_first, their_last, theirs = radiation(
-        atmospheric_constituents, thermal_ratio, solar_elevation_factor, ground_reflectivity,
-        sunlit_indicator, molecular_optics_lookup, condensate_optics_lookup,
-    )
-    partner = lax.axis_size("gx") // 2
-    heat_after, heat_before = shifted(heat_first, "gx", -1), shifted(heat_last, "gx", 1)
-    after_more = shifted(their_first, "gx", partner - 1)
-    before_more = shifted(their_last, "gx", partner + 1)
-    returned = shifted(heat_theirs, "gx", partner)
+    (
+        heat, returned, places, after, before, after_more, before_more, fields_after, fields_before
+    ) = radiation(
+        atmospheric_constituents, thermal_ratio, flow_velocity, solar_elevation_factor,
+        ground_reflectivity, sunlit_indicator, molecular_optics_lookup, condensate_optics_lookup,
+    )
+    fields_after = fields_after.reshape(3, size, lanes)
+    fields_before = fields_before.reshape(3, size, lanes)
     change, wind = call(
         own_change_kernel, "own_change",
         (wide, jax.ShapeDtypeStruct((2, size, 2 * lanes), jnp.float32)), 2,
-        temper, temper_after, temper_before, flow, flow_after, flow_before, *slopes,
+        temper, flow, fields_after, fields_before, *slopes,
     )
     wave, first, last, heat = call(
         first_stage_kernel, "first_stage", (wide, line, line, field), 1,
-        theirs, change, heat, returned, heat_after, heat_before, after_more, before_more,
+        places, change, heat, returned, after, before, after_more, before_more,
         edge_matrix(level_count, lanes).T, average,
     )
     below, above = shifted(last, "gy", 1), shifted(first, "gy", -1)

time: 112 us -> 110 us (0.982); the launches traced: 112 us -> 109 us
  starting transfers between devices: 23.7 us -> 15.7 us
  waiting for transfers between devices: 11.9 us -> 18.7 us
  Pallas kernels: 75 us -> 71.4 us
  other arithmetic: 0 us -> 1.25 us
    ppermute x16 -> x14, starting transfers between devices: 23.7 us -> 15.7 us  [shifted(): lax.ppermute(value, axis, [(i, (i + steps) % count) for i in range(count)])]
    ppermute x16 -> x14, waiting for transfers between devices: 11.9 us -> 18.7 us  [shifted(): lax.ppermute(value, axis, [(i, (i + steps) % count) for i in range(count)])]
    pallas_call x8 -> x9, Pallas kernels: 75 us -> 71.4 us  [the longest x1 29.3 us: radiation(): pl.pallas_call(functools.partial(home_kernel, 0), out_shape=(field(early)...]
    select_n x0 -> x1, other arithmetic: none -> 1.25 us  [radiation(): jnp.where(low, jnp.array([home, home + shared], jnp.int32), jnp.array([ho...]
  transfers between devices with their start and end apart: 16 -> 14, of which waited for: 8 -> 10; matrix products, arithmetic and copies ran while one was open for 0% -> 0% of each run, Pallas kernels for 64% -> 58%
where the time goes in v5:
time: 110 us; the launch traced here: 109 us
  Pallas kernels  71.4 us (65%)
  waiting for transfers between devices  18.7 us (17%)
  starting transfers between devices  15.7 us (14%)
  other arithmetic  1.25 us (1%)
    pallas_call x1, Pallas kernels, radiation(): pl.pallas_call(functools.partial(home_kernel, 0), out_shape=(field(early)...  29.3 us
    pallas_call x1, Pallas kernels, radiation(): pl.pallas_call(shared_kernel, out_shape=(field(shared), field(shared), ed...  20.7 us
    ppermute x14, waiting for transfers between devices, shifted(): lax.ppermute(value, axis, [(i, (i + steps) % count) for i in range(count)])  18.7 us
    ppermute x14, starting transfers between devices, shifted(): lax.ppermute(value, axis, [(i, (i + steps) % count) for i in range(count)])  15.7 us
    pallas_call x1, Pallas kernels, radiation(): pl.pallas_call(last_home_kernel, out_shape=(field(rows), edge, edge), gri...  12.7 us
    pallas_call x5, Pallas kernels, call(): pl.pallas_call(kernel, out_shape=outs, in_specs=[scalar if value.ndim ==...  5.1 us
    pallas_call x1, Pallas kernels, radiation(): pl.pallas_call(pack_kernel, out_shape=(state_rows, state_rows, jax.ShapeD...  3.67 us
  transfers between devices with their start and end apart: 14, of which 10 were waited for; matrix products, arithmetic and copies ran while one was open for 0% of the time, Pallas kernels for 58%

profile of v5, /device:TPU:1, one launch (start us, length us, event | category | flops | bytes accessed | tf_op | source)
XLA Modules:
  0.0 108.7 jit_solution(2644790871977622707)
XLA Ops:
  0.6 1.2 %broadcast_select_fusion.places_ref = s32[2]{0:T(128)} fusion(s32[2]{0:T(128)} %constant.23.clone, s32[2]{0:T(128)} %constant.24.clone, pred[]{:T(512)S(6)} %lt.3), kind=kLoop, calls=%fused_computation | loop fusion | flops 2 | bytes 25 | tf_op jit(solution)/shard_map/jit(_where)/select_n | solution.py:426
  1.9 3.7 %pack.1 = (f32[362,2,128]{2,1,0:T(2,128)}, f32[362,2,128]{2,1,0:T(2,128)}, f32[3,72,8,128]{3,2,1,0:T(8,128)}) custom-call(s32[2]{0:T(128)} %broadcast_select_fusion.places_ref, f32[5,72,8,128]{3,2,1,0:T(8,128)} %state_ref.5, f32[72,8,128]{2,1,0:T(8,128)} %temp_ref.5, f32[2,72,8,128]{3,2,1,0:T(8,128)} %flow_ref.1, f32[8,128]{1,0:T(8,128)} %cosine_ref.5, ...), custom_call_target="tpu_custom_call" | custom-call | tf_op jit(solution)/shard_map/pack/pallas_call | solution.py:459
  5.5 2.1 %collective-permute-start.1 = (f32[3,72,8,128]{3,2,1,0:T(8,128)}, f32[3,72,8,128]{3,2,1,0:T(8,128)S(1)}, u32[]{:S(2)}, u32[]{:S(2)}) collective-permute-start(f32[3,72,8,128]{3,2,1,0:T(8,128)} %get-tuple-element.29), channel_id=1, source_target_pairs={{0,4},{4,8},{8,12},{12,16},{16,20},{20,24},{24,28},{28,0},{1,5},{5... | collective-permute-start | bytes 2654216 | tf_op jit(solution)/shard_map/ppermute | solution.py:27
  7.6 3.0 %collective-permute-start = (f32[3,72,8,128]{3,2,1,0:T(8,128)}, f32[3,72,8,128]{3,2,1,0:T(8,128)S(1)}, u32[]{:S(2)}, u32[]{:S(2)}) collective-permute-start(f32[3,72,8,128]{3,2,1,0:T(8,128)} %get-tuple-element.29), channel_id=1, source_target_pairs={{0,28},{4,0},{8,4},{12,8},{16,12},{20,16},{24,20},{28,24},{1,29},{... | collective-permute-start | bytes 2654216 | tf_op jit(solution)/shard_map/ppermute | solution.py:27
  10.7 0.4 collective-permute-start.2
  11.1 29.3 %home_radiation.1 = (f32[216,128]{1,0:T(8,128)}, bf16[9,2,224,128]{3,2,1,0:T(8,128)(2,1)}, f32[112,128]{1,0:T(8,128)}) custom-call(f32[5,72,8,128]{3,2,1,0:T(8,128)} %state_ref.5, f32[72,8,128]{2,1,0:T(8,128)} %temp_ref.5, f32[8,128]{1,0:T(8,128)} %cosine_ref.5, f32[8,128]{1,0:T(8,128)} %ground_ref.5, s32[8,128]{1,0:T(8,128)} %day_ref.5, ...), custom_call_target="tpu_custom_call" | custom-call | flops 139345920 | bytes 2359296 | tf_op jit(solution)/shard_map/home_radiation/pallas_call | solution.py:472
  40.3 5.6 %collective-permute-done.2.received_ref = f32[362,2,128]{2,1,0:T(2,128)S(1)} collective-permute-done((f32[362,2,128]{2,1,0:T(2,128)}, f32[362,2,128]{2,1,0:T(2,128)S(1)}, u32[]{:S(2)}, u32[]{:S(2)}) %collective-permute-start.2) | collective-permute-done | bytes 370720 | tf_op jit(solution)/shard_map/ppermute | solution.py:27
  46.0 0.0 copy-start.8
  46.0 0.7 copy-done.8
  46.7 20.7 %shared_radiation.1 = (f32[144,128]{1,0:T(8,128)}, f32[144,128]{1,0:T(8,128)}, f32[64,128]{1,0:T(8,128)}, f32[64,128]{1,0:T(8,128)}) custom-call(s32[2]{0:T(128)} %broadcast_select_fusion.places_ref, f32[362,2,128]{2,1,0:T(2,128)} %get-tuple-element.34.kept_ref, f32[362,2,128]{2,1,0:T(2,128)} %copy-done.8, s32[8,128]{1,0:T(8,128)} %day_ref.5, ...), custom_call_target="tpu_custom_call" | custom-call | flops 92897280 | bytes 2359296 | tf_op jit(solution)/shard_map/shared_radiation/pallas_call | solution.py:485
  67.4 0.0 collective-permute-start.3
  67.4 0.0 copy-start.10
  67.4 0.0 copy-start.9
  67.4 0.0 copy-start
  67.5 0.0 copy-start.1
  67.5 0.0 copy-start.2
  67.5 0.0 copy-start.3
  67.5 12.7 %last_home_radiation.1 = (f32[576,128]{1,0:T(8,128)}, f32[64,128]{1,0:T(8,128)}, f32[64,128]{1,0:T(8,128)}) custom-call(s32[2]{0:T(128)} %broadcast_select_fusion.places_ref, f32[5,72,8,128]{3,2,1,0:T(8,128)} %state_ref.5, f32[72,8,128]{2,1,0:T(8,128)} %temp_ref.5, f32[8,128]{1,0:T(8,128)} %cosine_ref.5, f32[8,128]{1,0:T(8,128)} %ground_ref.5, ...), custom_call_target="tpu_custom_call" | custom-call | flops 46448640 | bytes 2359296 | tf_op jit(solution)/shard_map/last_home_radiation/pallas_call | solution.py:495
  80.2 0.0 copy-start.4
  80.2 0.0 copy-start.5
  80.2 0.0 copy-start.6
  80.2 0.0 copy-start.7
  80.2 1.2 %collective-permute-start.4 = (f32[64,128]{1,0:T(8,128)}, f32[64,128]{1,0:T(8,128)S(1)}, u32[]{:S(2)}, u32[]{:S(2)}) collective-permute-start(f32[64,128]{1,0:T(8,128)} %get-tuple-element.39), channel_id=1, source_target_pairs={{0,28},{4,0},{8,4},{12,8},{16,12},{20,16},{24,20},{28,24},{1,29},{... | collective-permute-start | bytes 98312 | tf_op jit(solution)/shard_map/ppermute | solution.py:27
  81.4 0.3 collective-permute-start.5
  81.7 0.0 collective-permute-done.1
  81.7 0.0 copy-done.10
  81.7 4.2 %collective-permute-start.6 = (f32[64,128]{1,0:T(8,128)S(1)}, f32[64,128]{1,0:T(8,128)S(1)}, u32[]{:S(2)}, u32[]{:S(2)}) collective-permute-start(f32[64,128]{1,0:T(8,128)S(1)} %copy-done.10), channel_id=1, source_target_pairs={{0,12},{4,16},{8,20},{12,24},{16,28},{20,0},{24,4},{28,8},{1,13},{... | collective-permute-start | bytes 98312 | tf_op jit(solution)/shard_map/ppermute | solution.py:27
  85.9 0.0 collective-permute-done
  85.9 0.0 copy-done.9
  85.9 0.0 collective-permute-start.7
  86.0 0.0 copy-done
  86.0 0.0 copy-done.1
  86.0 0.0 copy-done.2
  86.0 0.0 copy-done.3
  86.0 0.8 own_change.1
  86.8 0.0 collective-permute-done.4.after_ref
  86.8 0.3 collective-permute-done.5.before_ref
  87.1 0.3 collective-permute-done.6.after_more_ref
  87.5 2.4 %collective-permute-done.7.before_more_ref = f32[64,128]{1,0:T(8,128)S(1)} collective-permute-done((f32[64,128]{1,0:T(8,128)S(1)}, f32[64,128]{1,0:T(8,128)S(1)}, u32[]{:S(2)}, u32[]{:S(2)}) %collective-permute-start.7) | collective-permute-done | bytes 32800 | tf_op jit(solution)/shard_map/ppermute | solution.py:27
  89.9 0.0 collective-permute-done.3.returned_ref
  89.9 0.0 copy-done.4
  89.9 0.0 copy-done.5
  89.9 0.0 copy-done.6
  89.9 0.0 copy-done.7
  89.9 1.7 %first_stage.1 = (f32[576,256]{1,0:T(8,128)S(1)}, f32[72,256]{1,0:T(8,128)S(1)}, f32[72,256]{1,0:T(8,128)S(1)}, f32[576,128]{1,0:T(8,128)}) custom-call(s32[2]{0:T(128)S(1)} %copy-done.7, f32[576,256]{1,0:T(8,128)S(1)} %get-tuple-element.30.change_ref, f32[576,128]{1,0:T(8,128)S(1)} %copy-done.6, f32[144,128]{1,0:T(8,128)S(1)} %collective-permute-done.3.returned_ref, ...), custom_call_target="tpu_custom_call" | custom-call | tf_op jit(solution)/shard_map/first_stage/pallas_call | solution.py:699
  91.6 3.3 %collective-permute-start.8 = (f32[72,256]{1,0:T(8,128)S(1)}, f32[72,256]{1,0:T(8,128)S(1)}, u32[]{:S(2)}, u32[]{:S(2)}) collective-permute-start(f32[72,256]{1,0:T(8,128)S(1)} %get-tuple-element.45), channel_id=1, source_target_pairs={{0,1},{1,2},{2,3},{3,0},{4,5},{5,6},{6,7},{7,4},{8,9},{9,10},{10,1... | collective-permute-start | bytes 221192 | tf_op jit(solution)/shard_map/ppermute | solution.py:27
  94.9 0.0 collective-permute-start.9
  94.9 1.4 %collective-permute-done.8.below_ref = f32[72,256]{1,0:T(8,128)S(1)} collective-permute-done((f32[72,256]{1,0:T(8,128)S(1)}, f32[72,256]{1,0:T(8,128)S(1)}, u32[]{:S(2)}, u32[]{:S(2)}) %collective-permute-start.8) | collective-permute-done | bytes 73760 | tf_op jit(solution)/shard_map/ppermute | solution.py:27
  96.3 2.4 %collective-permute-done.9.above_ref = f32[72,256]{1,0:T(8,128)S(1)} collective-permute-done((f32[72,256]{1,0:T(8,128)S(1)}, f32[72,256]{1,0:T(8,128)S(1)}, u32[]{:S(2)}, u32[]{:S(2)}) %collective-permute-start.9) | collective-permute-done | bytes 73760 | tf_op jit(solution)/shard_map/ppermute | solution.py:27
  98.7 0.9 second_stage.1
  99.6 0.1 collective-permute-start.10
  99.7 0.5 collective-permute-start.11
  100.2 0.9 collective-permute-done.10.below_ref
  101.1 2.4 %collective-permute-done.11.above_ref = f32[72,256]{1,0:T(8,128)S(1)} collective-permute-done((f32[72,256]{1,0:T(8,128)S(1)}, f32[72,256]{1,0:T(8,128)S(1)}, u32[]{:S(2)}, u32[]{:S(2)}) %collective-permute-start.11) | collective-permute-done | bytes 73760 | tf_op jit(solution)/shard_map/ppermute | solution.py:27
  103.5 0.9 third_stage.1
  104.4 0.1 collective-permute-start.12
  104.5 0.5 collective-permute-start.13
  105.0 0.7 collective-permute-done.12.below_ref
  105.7 2.2 %collective-permute-done.13.above_ref = f32[72,128]{1,0:T(8,128)S(1)} collective-permute-done((f32[72,128]{1,0:T(8,128)S(1)}, f32[72,128]{1,0:T(8,128)S(1)}, u32[]{:S(2)}, u32[]{:S(2)}) %collective-permute-start.13) | collective-permute-done | bytes 36896 | tf_op jit(solution)/shard_map/ppermute | solution.py:27
  107.9 0.8 last_stage.1
Async XLA Ops:
  5.5 76.2 %collective-permute-start.1 = (f32[3,72,8,128]{3,2,1,0:T(8,128)}, f32[3,72,8,128]{3,2,1,0:T(8,128)S(1)}, u32[]{:S(2)}, u32[]{:S(2)}) collective-permute-start(f32[3,72,8,128]{3,2,1,0:T(8,128)} %get-tuple-element.29), channel_id=1, source_target_pairs={{0,4},{4,8},{8,12},{12,16},{16,20},{20,24},{24,28},{28,0},{1,5},{5... | collective-permute-start | bytes 2654216 | tf_op jit(solution)/shard_map/ppermute | solution.py:27
  7.6 78.3 %collective-permute-start = (f32[3,72,8,128]{3,2,1,0:T(8,128)}, f32[3,72,8,128]{3,2,1,0:T(8,128)S(1)}, u32[]{:S(2)}, u32[]{:S(2)}) collective-permute-start(f32[3,72,8,128]{3,2,1,0:T(8,128)} %get-tuple-element.29), channel_id=1, source_target_pairs={{0,28},{4,0},{8,4},{12,8},{16,12},{20,16},{24,20},{28,24},{1,29},{... | collective-permute-start | bytes 2654216 | tf_op jit(solution)/shard_map/ppermute | solution.py:27
  10.7 35.3 %collective-permute-start.2 = (f32[362,2,128]{2,1,0:T(2,128)}, f32[362,2,128]{2,1,0:T(2,128)S(1)}, u32[]{:S(2)}, u32[]{:S(2)}) collective-permute-start(f32[362,2,128]{2,1,0:T(2,128)} %get-tuple-element.35), channel_id=1, source_target_pairs={{0,16},{4,20},{8,24},{12,28},{16,0},{20,4},{24,8},{28,12},{1,17},{... | collective-permute-start | bytes 1112072 | tf_op jit(solution)/shard_map/ppermute | solution.py:27
  46.0 0.7 copy-start.8
  67.4 22.4 %collective-permute-start.3 = (f32[144,128]{1,0:T(8,128)}, f32[144,128]{1,0:T(8,128)S(1)}, u32[]{:S(2)}, u32[]{:S(2)}) collective-permute-start(f32[144,128]{1,0:T(8,128)} %get-tuple-element.38), channel_id=1, source_target_pairs={{0,16},{4,20},{8,24},{12,28},{16,0},{20,4},{24,8},{28,12},{1,17},{... | collective-permute-start | bytes 221192 | tf_op jit(solution)/shard_map/ppermute | solution.py:27
  67.4 14.3 %copy-start.10 = (f32[64,128]{1,0:T(8,128)S(1)}, f32[64,128]{1,0:T(8,128)}, u32[]{:S(2)}) copy-start(f32[64,128]{1,0:T(8,128)} %get-tuple-element.41) | copy-start | bytes 98308
  67.4 18.5 %copy-start.9 = (f32[64,128]{1,0:T(8,128)S(1)}, f32[64,128]{1,0:T(8,128)}, u32[]{:S(2)}) copy-start(f32[64,128]{1,0:T(8,128)} %get-tuple-element.42) | copy-start | bytes 98308
  67.4 18.5 %copy-start = (f32[72,8,128]{2,1,0:T(8,128)S(1)}, f32[72,8,128]{2,1,0:T(8,128)}, u32[]{:S(2)}) copy-start(f32[72,8,128]{2,1,0:T(8,128)} %temp_ref.5) | copy-start | bytes 884740
  67.5 18.5 %copy-start.1 = (f32[2,72,8,128]{3,2,1,0:T(8,128)S(1)}, f32[2,72,8,128]{3,2,1,0:T(8,128)}, u32[]{:S(2)}) copy-start(f32[2,72,8,128]{3,2,1,0:T(8,128)} %flow_ref.1) | copy-start | bytes 1769476
  67.5 18.5 %copy-start.2 = (bf16[256,256]{1,0:T(8,128)(2,1)S(1)}, bf16[256,256]{1,0:T(8,128)(2,1)}, u32[]{:S(2)}) copy-start(bf16[256,256]{1,0:T(8,128)(2,1)} %constant.21.clone.low_ref) | copy-start | bytes 393220
  67.5 18.5 %copy-start.3 = (bf16[256,256]{1,0:T(8,128)(2,1)S(1)}, bf16[256,256]{1,0:T(8,128)(2,1)}, u32[]{:S(2)}) copy-start(bf16[256,256]{1,0:T(8,128)(2,1)} %constant.20.clone.high_ref) | copy-start | bytes 393220
  80.2 9.7 %copy-start.4 = (bf16[256,256]{1,0:T(8,128)(2,1)S(1)}, bf16[256,256]{1,0:T(8,128)(2,1)}, u32[]{:S(2)}) copy-start(bf16[256,256]{1,0:T(8,128)(2,1)} %constant.22.clone.average_ref) | copy-start | bytes 393220
  80.2 9.7 %copy-start.5 = (bf16[256,1152]{1,0:T(8,128)(2,1)S(1)}, bf16[256,1152]{1,0:T(8,128)(2,1)}, u32[]{:S(2)}) copy-start(bf16[256,1152]{1,0:T(8,128)(2,1)} %constant.26.edge_ref) | copy-start | bytes 1769476
  80.2 9.7 %copy-start.6 = (f32[576,128]{1,0:T(8,128)S(1)}, f32[576,128]{1,0:T(8,128)}, u32[]{:S(2)}) copy-start(f32[576,128]{1,0:T(8,128)} %get-tuple-element.37.heat_ref) | copy-start | bytes 884740
  80.2 9.7 %copy-start.7 = (s32[2]{0:T(128)S(1)}, s32[2]{0:T(128)}, u32[]{:S(2)}) copy-start(s32[2]{0:T(128)} %broadcast_select_fusion.places_ref) | copy-start | bytes 28
  80.2 6.6 %collective-permute-start.4 = (f32[64,128]{1,0:T(8,128)}, f32[64,128]{1,0:T(8,128)S(1)}, u32[]{:S(2)}, u32[]{:S(2)}) collective-permute-start(f32[64,128]{1,0:T(8,128)} %get-tuple-element.39), channel_id=1, source_target_pairs={{0,28},{4,0},{8,4},{12,8},{16,12},{20,16},{24,20},{28,24},{1,29},{... | collective-permute-start | bytes 98312 | tf_op jit(solution)/shard_map/ppermute | solution.py:27
  81.4 5.7 %collective-permute-start.5 = (f32[64,128]{1,0:T(8,128)}, f32[64,128]{1,0:T(8,128)S(1)}, u32[]{:S(2)}, u32[]{:S(2)}) collective-permute-start(f32[64,128]{1,0:T(8,128)} %get-tuple-element.40), channel_id=1, source_target_pairs={{0,4},{4,8},{8,12},{12,16},{16,20},{20,24},{24,28},{28,0},{1,5},{5... | collective-permute-start | bytes 98312 | tf_op jit(solution)/shard_map/ppermute | solution.py:27
  81.7 5.7 %collective-permute-start.6 = (f32[64,128]{1,0:T(8,128)S(1)}, f32[64,128]{1,0:T(8,128)S(1)}, u32[]{:S(2)}, u32[]{:S(2)}) collective-permute-start(f32[64,128]{1,0:T(8,128)S(1)} %copy-done.10), channel_id=1, source_target_pairs={{0,12},{4,16},{8,20},{12,24},{16,28},{20,0},{24,4},{28,8},{1,13},{... | collective-permute-start | bytes 98312 | tf_op jit(solution)/shard_map/ppermute | solution.py:27
  85.9 3.9 %collective-permute-start.7 = (f32[64,128]{1,0:T(8,128)S(1)}, f32[64,128]{1,0:T(8,128)S(1)}, u32[]{:S(2)}, u32[]{:S(2)}) collective-permute-start(f32[64,128]{1,0:T(8,128)S(1)} %copy-done.9), channel_id=1, source_target_pairs={{0,20},{4,24},{8,28},{12,0},{16,4},{20,8},{24,12},{28,16},{1,21},{... | collective-permute-start | bytes 98312 | tf_op jit(solution)/shard_map/ppermute | solution.py:27
  91.6 4.7 %collective-permute-start.8 = (f32[72,256]{1,0:T(8,128)S(1)}, f32[72,256]{1,0:T(8,128)S(1)}, u32[]{:S(2)}, u32[]{:S(2)}) collective-permute-start(f32[72,256]{1,0:T(8,128)S(1)} %get-tuple-element.45), channel_id=1, source_target_pairs={{0,1},{1,2},{2,3},{3,0},{4,5},{5,6},{6,7},{7,4},{8,9},{9,10},{10,1... | collective-permute-start | bytes 221192 | tf_op jit(solution)/shard_map/ppermute | solution.py:27
  94.9 3.8 %collective-permute-start.9 = (f32[72,256]{1,0:T(8,128)S(1)}, f32[72,256]{1,0:T(8,128)S(1)}, u32[]{:S(2)}, u32[]{:S(2)}) collective-permute-start(f32[72,256]{1,0:T(8,128)S(1)} %get-tuple-element.46), channel_id=1, source_target_pairs={{0,3},{1,0},{2,1},{3,2},{4,7},{5,4},{6,5},{7,6},{8,11},{9,8},{10,9... | collective-permute-start | bytes 221192 | tf_op jit(solution)/shard_map/ppermute | solution.py:27
  99.6 1.5 %collective-permute-start.10 = (f32[72,256]{1,0:T(8,128)S(1)}, f32[72,256]{1,0:T(8,128)S(1)}, u32[]{:S(2)}, u32[]{:S(2)}) collective-permute-start(f32[72,256]{1,0:T(8,128)S(1)} %get-tuple-element.49), channel_id=1, source_target_pairs={{0,1},{1,2},{2,3},{3,0},{4,5},{5,6},{6,7},{7,4},{8,9},{9,10},{10,1... | collective-permute-start | bytes 221192 | tf_op jit(solution)/shard_map/ppermute | solution.py:27
  99.7 3.8 %collective-permute-start.11 = (f32[72,256]{1,0:T(8,128)S(1)}, f32[72,256]{1,0:T(8,128)S(1)}, u32[]{:S(2)}, u32[]{:S(2)}) collective-permute-start(f32[72,256]{1,0:T(8,128)S(1)} %get-tuple-element.50), channel_id=1, source_target_pairs={{0,3},{1,0},{2,1},{3,2},{4,7},{5,4},{6,5},{7,6},{8,11},{9,8},{10,9... | collective-permute-start | bytes 221192 | tf_op jit(solution)/shard_map/ppermute | solution.py:27
  104.4 1.3 %collective-permute-start.12 = (f32[72,128]{1,0:T(8,128)S(1)}, f32[72,128]{1,0:T(8,128)S(1)}, u32[]{:S(2)}, u32[]{:S(2)}) collective-permute-start(f32[72,128]{1,0:T(8,128)S(1)} %get-tuple-element.53), channel_id=1, source_target_pairs={{0,1},{1,2},{2,3},{3,0},{4,5},{5,6},{6,7},{7,4},{8,9},{9,10},{10,1... | collective-permute-start | bytes 110600 | tf_op jit(solution)/shard_map/ppermute | solution.py:27
  104.5 3.4 %collective-permute-start.13 = (f32[72,128]{1,0:T(8,128)S(1)}, f32[72,128]{1,0:T(8,128)S(1)}, u32[]{:S(2)}, u32[]{:S(2)}) collective-permute-start(f32[72,128]{1,0:T(8,128)S(1)} %get-tuple-element.54), channel_id=1, source_target_pairs={{0,3},{1,0},{2,1},{3,2},{4,7},{5,4},{6,5},{7,6},{8,11},{9,8},{10,9... | collective-permute-start | bytes 110600 | tf_op jit(solution)/shard_map/ppermute | solution.py:27

commit v6 on v5

--- a/solution.py
+++ b/solution.py
@@ -10,7 +10,6 @@
 
 NODES = 4
 TIME_INCREMENT = 0.05
-EDGE = 16
 ROWS = 8
 LOG2E = 1.4426950408889634
 
@@ -110,8 +109,10 @@
 
 
 def layer_terms(state_ref, temp_ref, level):
+    lines = state_ref.shape[2]
     thickness = state_ref[2, level]
-    weighted = thickness * temp_ref[level] * temp_ref[level]
+    temper = temp_ref[pl.ds(pl.multiple_of(level * lines, 8), lines), :]
+    weighted = thickness * temper * temper
     return (
         weighted * state_ref[0, level], weighted * state_ref[1, level], thickness,
         state_ref[3, level], state_ref[4, level],
@@ -252,14 +253,14 @@
         write(level, (level_count / gpoints) * (upper - lower))
         return lower
 
-    lax.fori_loop(0, level_count, step, flux(0))
+    lax.fori_loop(0, level_count, step, flux(0), unroll=4)
 
 
 def home_kernel(
     first, state_ref, temp_ref, cosine_ref, ground_ref, day_ref, molecular_ref, table_ref,
     heat_ref, optics_ref, weight_ref, terms_ref, right_ref, *scratch,
 ):
-    level_count, lines, lanes = temp_ref.shape
+    level_count, lines, lanes = state_ref.shape[1:]
     gpoints = weight_ref.shape[0]
     row, count = pl.program_id(0), pl.num_programs(0)
 
@@ -288,46 +289,56 @@
 
 
 def prepare_terms(state_ref, temp_ref, terms_ref, right_ref):
-    level_count, lines, lanes = temp_ref.shape
+    level_count, lines = state_ref.shape[1:3]
     right_ref[...] = jnp.zeros_like(right_ref)
 
     def level(l, carry):
         write_terms(terms_ref, l, layer_terms(state_ref, temp_ref, l), lines)
         return carry
 
-    lax.fori_loop(0, level_count, level, 0, unroll=2)
+    lax.fori_loop(0, level_count, level, 0, unroll=4)
+
+
+def shared_places(lines):
+    low = lax.axis_index("gx") < lax.axis_size("gx") // 2
+    early, late = lines // 2, lines // 2 + lines // 4
+    return jnp.where(low, early, late), jnp.where(low, late, early)
 
 
 def pack_kernel(
-    places_ref, state_ref, temp_ref, flow_ref, cosine_ref, ground_ref,
-    sent_ref, kept_ref, fields_ref, own_ref,
-):
-    level_count, lines, lanes = temp_ref.shape
-    count = sent_ref.shape[1]
+    state_ref, temp_ref, flow_ref, cosine_ref, ground_ref, edge_ref,
+    sent_ref, kept_ref, line_ref, first_ref, last_ref, own_ref, strip_ref,
+):
+    level_count, lines, lanes = state_ref.shape[1:]
 
     def level(l, carry):
         for k, value in enumerate(layer_terms(state_ref, temp_ref, l)):
             own_ref[pl.ds(pl.multiple_of((5 * l + k) * lines, 8), lines), :] = value
-        fields_ref[0, l] = temp_ref[l]
-        fields_ref[1, l] = flow_ref[0, l]
-        fields_ref[2, l] = flow_ref[1, l]
         return carry
 
     lax.fori_loop(0, level_count, level, 0, unroll=4)
-    for n, ref in enumerate((kept_ref, sent_ref)):
-        first = places_ref[n]
-
-        def copy(n, carry, ref=ref, first=first):
-            ref[n] = own_ref[pl.ds(n * lines + first, count), :]
-            return carry
-
-        lax.fori_loop(0, 5 * level_count, copy, 0, unroll=8)
-        ref[5 * level_count] = cosine_ref[pl.ds(first, count), :]
-        ref[5 * level_count + 1] = ground_ref[pl.ds(first, count), :]
+    mine, theirs = shared_places(lines)
+    copies = ((kept_ref, mine), (sent_ref, theirs), (line_ref, lines // 2 - 1))
+
+    def copy(n, carry):
+        for ref, place in copies:
+            ref[n] = own_ref[pl.ds(n * lines + place, ref.shape[1]), :]
+        return carry
+
+    lax.fori_loop(0, 5 * level_count, copy, 0, unroll=8)
+    for ref, place in copies:
+        ref[5 * level_count] = cosine_ref[pl.ds(place, ref.shape[1]), :]
+        ref[5 * level_count + 1] = ground_ref[pl.ds(place, ref.shape[1]), :]
+    for n, ref in enumerate((temp_ref, flow_ref.at[0], flow_ref.at[1])):
+        for r in range(lines):
+            write_strip(ref, r, lines, strip_ref, 8 * (lines * n + r))
+    packed = split_dot(strip_ref[...], edge_ref[...])
+    first_ref[...] = packed[:, :lanes]
+    last_ref[...] = packed[:, lanes:]
 
 
 def shared_kernel(
-    places_ref, kept_ref, received_ref, day_ref, optics_ref, weight_ref, edge_ref,
+    kept_ref, received_ref, day_ref, optics_ref, weight_ref, edge_ref,
     mine_ref, theirs_ref, their_first_ref, their_last_ref,
     surface_ref, strip_ref, terms_ref, right_ref, *scratch,
 ):
@@ -335,7 +346,7 @@
     shared, lanes = kept_ref.shape[1:]
     gpoints = weight_ref.shape[0]
     row, count = pl.program_id(0), pl.num_programs(0)
-    first = places_ref[0]
+    first = shared_places(day_ref.shape[0])[0]
     day = day_ref[pl.ds(first, shared), :] == 1
 
     @pl.when(row == 0)
@@ -385,20 +396,26 @@
 
 
 def last_home_kernel(
-    places_ref, state_ref, temp_ref, cosine_ref, ground_ref, day_ref, optics_ref, weight_ref,
-    edge_ref, home_ref, mine_ref,
+    line_ref, day_ref, optics_ref, weight_ref, edge_ref, home_ref, mine_ref,
     heat_ref, first_ref, last_ref, strip_ref, terms_ref, right_ref, *scratch,
 ):
-    level_count, lines, lanes = temp_ref.shape
+    lines, lanes = day_ref.shape
+    level_count = line_ref.shape[0] // 5
     gpoints = weight_ref.shape[0]
     row = pl.program_id(0)
     line = lines // 2 - 1
-    prepare_terms(state_ref, temp_ref, terms_ref, right_ref)
+    right_ref[...] = jnp.zeros_like(right_ref)
+
+    def level(l, carry):
+        write_terms(terms_ref, l, [line_ref[5 * l + k] for k in range(5)], 1)
+        return carry
+
+    lax.fori_loop(0, level_count, level, 0, unroll=4)
     sweep_row(
-        row, line, lines, 1, cosine_ref[pl.ds(line, 1), :], ground_ref[pl.ds(line, 1), :],
+        row, 0, 1, 1, line_ref[5 * level_count], line_ref[5 * level_count + 1],
         optics_ref, weight_ref, terms_ref, right_ref, *scratch,
     )
-    first = places_ref[0]
+    first = shared_places(lines)[0]
     shared = mine_ref.shape[0] // level_count
     day = day_ref[line : line + 1, :] == 1
     heat_ref[...] = jnp.zeros_like(heat_ref)
@@ -422,14 +439,11 @@
     gpoints = molecular.shape[1]
     home, shared = rows // 2, rows // 4
     partner = lax.axis_size("gx") // 2
-    low = lax.axis_index("gx") < partner
-    places = jnp.where(
-        low, jnp.array([home, home + shared], jnp.int32), jnp.array([home + shared, home], jnp.int32)
-    )
+    temper = temper.reshape(level_count * rows, lanes)
+    flow = flow.reshape(2, level_count * rows, lanes)
     full = pltpu.VMEM((level_count, gpoints, lanes), jnp.float32)
     plane = pltpu.VMEM((gpoints, lanes), jnp.float32)
     whole = pl.BlockSpec(memory_space=pltpu.VMEM)
-    scalar = pl.BlockSpec(memory_space=pltpu.SMEM)
     params = pltpu.CompilerParams(vmem_limit_bytes=60 * 1024 * 1024)
     part = (QUANTITIES * gpoints // CHUNKS, GROUP * TERMS)
     strip = pltpu.VMEM((8 * rows, level_count // 8 * lanes), jnp.float32)
@@ -452,22 +466,26 @@
     def cost(count):
         cells = level_count * gpoints * count * lanes
         return pl.CostEstimate(
-            flops=45 * cells, bytes_accessed=32 * temper.size, transcendentals=5 * cells
+            flops=10000 * cells, bytes_accessed=32 * temper.size, transcendentals=5 * cells
         )
 
-    state_rows = jax.ShapeDtypeStruct((5 * level_count + 2, shared, lanes), jnp.float32)
-    sent, kept, fields = pl.pallas_call(
+    def state_rows(count):
+        return jax.ShapeDtypeStruct((5 * level_count + 2, count, lanes), jnp.float32)
+
+    edges = edge_matrix(level_count, lanes)
+    three = jax.ShapeDtypeStruct((3 * 8 * rows, lanes), jnp.float32)
+    sent, kept, line, fields_first, fields_last = pl.pallas_call(
         pack_kernel,
-        out_shape=(
-            state_rows, state_rows,
-            jax.ShapeDtypeStruct((3, level_count, rows, lanes), jnp.float32),
-        ),
-        in_specs=[scalar] + [whole] * 5, out_specs=(whole,) * 3,
-        scratch_shapes=[pltpu.VMEM((5 * level_count * rows, lanes), jnp.float32)],
+        out_shape=(state_rows(shared), state_rows(shared), state_rows(1), three, three),
+        in_specs=[whole] * 6, out_specs=(whole,) * 5,
+        scratch_shapes=[
+            pltpu.VMEM((5 * level_count * rows, lanes), jnp.float32),
+            pltpu.VMEM((3 * 8 * rows, level_count // 8 * lanes), jnp.float32),
+        ],
         compiler_params=params, name="pack",
-    )(places, state, temper, flow, cosine, ground)
+    )(state, temper, flow, cosine, ground, edges)
     received = shifted(sent, "gx", partner)
-    fields_after, fields_before = shifted(fields, "gx", -1), shifted(fields, "gx", 1)
+    fields_after, fields_before = shifted(fields_first, "gx", -1), shifted(fields_last, "gx", 1)
     early = home - 1
     home_heat, optics, weight = pl.pallas_call(
         functools.partial(home_kernel, 0),
@@ -481,27 +499,26 @@
         name="home_radiation",
     )(state, temper, cosine, ground, day, molecular.transpose(0, 2, 1), condensate)
     edge = jax.ShapeDtypeStruct((8 * rows, lanes), jnp.float32)
-    edges = edge_matrix(level_count, lanes)
     mine, theirs, their_first, their_last = pl.pallas_call(
         shared_kernel,
         out_shape=(field(shared), field(shared), edge, edge),
-        grid=(shared,), in_specs=[scalar] + [whole] * 6, out_specs=(whole,) * 4,
+        grid=(shared,), in_specs=[whole] * 6, out_specs=(whole,) * 4,
         scratch_shapes=[pltpu.VMEM((2, 8, lanes), jnp.float32), strip] + scratch(shared, shared),
         compiler_params=params, cost_estimate=cost(shared), name="shared_radiation",
-    )(places, kept, received, day, optics, weight, edges)
+    )(kept, received, day, optics, weight, edges)
     returned = shifted(theirs, "gx", partner)
     after_more = shifted(their_first, "gx", partner - 1)
     before_more = shifted(their_last, "gx", partner + 1)
     heat, first, last = pl.pallas_call(
         last_home_kernel,
         out_shape=(field(rows), edge, edge),
-        grid=(1,), in_specs=[scalar] + [whole] * 10, out_specs=(whole,) * 3,
-        scratch_shapes=[strip] + scratch(rows, 1),
+        grid=(1,), in_specs=[whole] * 7, out_specs=(whole,) * 3,
+        scratch_shapes=[strip] + scratch(1, 1),
         compiler_params=params, cost_estimate=cost(1), name="last_home_radiation",
-    )(places, state, temper, cosine, ground, day, optics, weight, edges, home_heat, mine)
+    )(line, day, optics, weight, edges, home_heat, mine)
     after, before = shifted(first, "gx", -1), shifted(last, "gx", 1)
     return (
-        heat, returned, places, after, before, after_more, before_more, fields_after, fields_before
+        heat, returned, after, before, after_more, before_more, fields_after, fields_before
     )
 
 
@@ -566,30 +583,30 @@
     return result
 
 
+def unpacked(after_ref, before_ref, edge_ref):
+    both = jnp.concatenate([after_ref[...], before_ref[...]], axis=1)
+    return split_dot(both, edge_ref[...])
+
+
 def own_change_kernel(
-    temp_ref, flow_ref, after_ref, before_ref,
-    high_ref, low_ref, change_ref, wind_ref, temp_wide_ref, slope_ref,
+    temp_ref, flow_ref, after_ref, before_ref, edge_ref, high_ref, low_ref,
+    change_ref, wind_ref, temp_wide_ref, slope_ref,
 ):
     level_count = change_ref.shape[0] // ROWS
     lanes = temp_ref.shape[-1]
-    lane = lax.broadcasted_iota(jnp.int32, (level_count, lanes), 1)
-
-    def tiles(own, after, before, r):
-        span = pl.ds(r, level_count, stride=ROWS)
-        side = jnp.where(lane < EDGE, after[span, :], 0.0)
-        return own[span, :], jnp.where(lane >= lanes - EDGE, before[span, :], side)
-
-    for r in range(ROWS):
-        rows = slice(r * level_count, (r + 1) * level_count)
-        pairs = [
-            tiles(own, after_ref.at[n], before_ref.at[n], r)
-            for n, own in enumerate((temp_ref, flow_ref.at[0], flow_ref.at[1]))
-        ]
-        for half in range(2):
-            span = slice(half * lanes, (half + 1) * lanes)
-            temp_wide_ref[rows, span] = pairs[0][half]
-            wind_ref[0, rows, span] = pairs[1][half]
-            wind_ref[1, rows, span] = pairs[2][half]
+    sides = unpacked(after_ref, before_ref, edge_ref)
+    fields = (
+        (temp_ref, temp_wide_ref), (flow_ref.at[0], wind_ref.at[0]), (flow_ref.at[1], wind_ref.at[1])
+    )
+    for n, (own, wide) in enumerate(fields):
+        for r in range(ROWS):
+            start = r * level_count
+            wide[start : start + level_count, :lanes] = own[pl.ds(r, level_count, stride=ROWS), :]
+            here = 8 * (ROWS * n + r)
+            for k in range(level_count // 8):
+                wide[start + 8 * k : start + 8 * (k + 1), lanes:] = sides[
+                    here : here + 8, lanes * k : lanes * (k + 1)
+                ]
     slope_ref[...] = split_dot(temp_wide_ref[...], high_ref[...], low_ref[...])
     advect(temp_wide_ref, slope_ref, wind_ref, change_ref, level_count)
 
@@ -614,7 +631,7 @@
 
 
 def first_stage_kernel(
-    places_ref, change_ref, heat_ref, returned_ref, after_ref, before_ref, after_more_ref,
+    change_ref, heat_ref, returned_ref, after_ref, before_ref, after_more_ref,
     before_more_ref, edge_ref, average_ref,
     out_ref, first_ref, last_ref, heat_out_ref, sum_ref,
 ):
@@ -630,7 +647,7 @@
         own = heat_ref[span, :]
         if r >= ROWS // 2:
             n = r % shared
-            here = places_ref[1] == r - n
+            here = shared_places(ROWS)[1] == r - n
             own = own + jnp.where(
                 here, returned_ref[pl.ds(n, level_count, stride=shared), :], 0.0
             )
@@ -693,12 +710,11 @@
     short = jax.ShapeDtypeStruct((level_count, lanes), jnp.float32)
     wide_scratch = pltpu.VMEM(wide.shape, jnp.float32)
     whole = pl.BlockSpec(memory_space=pltpu.VMEM)
-    scalar = pl.BlockSpec(memory_space=pltpu.SMEM)
 
     def call(kernel, name, outs, scratch, *values):
         return pl.pallas_call(
             kernel, out_shape=outs,
-            in_specs=[scalar if value.ndim == 1 else whole for value in values],
+            in_specs=[whole] * len(values),
             out_specs=jax.tree.map(lambda _: whole, outs), scratch_shapes=[wide_scratch] * scratch,
             compiler_params=pltpu.CompilerParams(vmem_limit_bytes=40 * 1024 * 1024), name=name,
         )(*values)
@@ -706,22 +722,20 @@
     slopes = slope_matrices(lanes)
     average = average_matrix(lanes)
     (
-        heat, returned, places, after, before, after_more, before_more, fields_after, fields_before
+        heat, returned, after, before, after_more, before_more, fields_after, fields_before
     ) = radiation(
         atmospheric_constituents, thermal_ratio, flow_velocity, solar_elevation_factor,
         ground_reflectivity, sunlit_indicator, molecular_optics_lookup, condensate_optics_lookup,
     )
-    fields_after = fields_after.reshape(3, size, lanes)
-    fields_before = fields_before.reshape(3, size, lanes)
+    back = edge_matrix(level_count, lanes).T
     change, wind = call(
         own_change_kernel, "own_change",
         (wide, jax.ShapeDtypeStruct((2, size, 2 * lanes), jnp.float32)), 2,
-        temper, flow, fields_after, fields_before, *slopes,
+        temper, flow, fields_after, fields_before, back, *slopes,
     )
     wave, first, last, heat = call(
         first_stage_kernel, "first_stage", (wide, line, line, field), 1,
-        places, change, heat, returned, after, before, after_more, before_more,
-        edge_matrix(level_count, lanes).T, average,
+        change, heat, returned, after, before, after_more, before_more, back, average,
     )
     below, above = shifted(last, "gy", 1), shifted(first, "gy", -1)
     wave, first, last, total = call(

time: 110 us -> 103 us (0.936)
  waiting for transfers between devices: 18.7 us -> 11.5 us
  starting transfers between devices: 15.7 us -> 20.4 us
  Pallas kernels: 71.4 us -> 69 us
  other arithmetic: 1.25 us -> 0 us
    ppermute x14, waiting for transfers between devices: 18.7 us -> 11.5 us  [shifted(): lax.ppermute(value, axis, [(i, (i + steps) % count) for i in range(count)])]
    ppermute x14, starting transfers between devices: 15.7 us -> 20.4 us  [shifted(): lax.ppermute(value, axis, [(i, (i + steps) % count) for i in range(count)])]
    select_n x1 -> x0, other arithmetic: 1.25 us -> none  [radiation(): jnp.where(low, jnp.array([home, home + shared], jnp.int32), jnp.array([ho...]
    pallas_call x1, Pallas kernels: 12.7 us -> 11.6 us  [radiation(): pl.pallas_call(last_home_kernel, out_shape=(field(rows), edge, edge), gri...]
  transfers between devices with their start and end apart: 14 -> 14, of which waited for: 10 -> 7; matrix products, arithmetic and copies ran while one was open for 0% -> 0% of each run, Pallas kernels for 58% -> 60%
where the time goes in v6:
time: 103 us; the launch traced here: 102 us
  Pallas kernels  69 us (67%)
  starting transfers between devices  20.4 us (20%)
  waiting for transfers between devices  11.5 us (11%)
    pallas_call x1, Pallas kernels, radiation(): pl.pallas_call(functools.partial(home_kernel, 0), out_shape=(field(early)...  28.8 us
    ppermute x14, starting transfers between devices, shifted(): lax.ppermute(value, axis, [(i, (i + steps) % count) for i in range(count)])  20.4 us
    pallas_call x1, Pallas kernels, radiation(): pl.pallas_call(shared_kernel, out_shape=(field(shared), field(shared), ed...  20.1 us
    pallas_call x1, Pallas kernels, radiation(): pl.pallas_call(last_home_kernel, out_shape=(field(rows), edge, edge), gri...  11.6 us
    ppermute x14, waiting for transfers between devices, shifted(): lax.ppermute(value, axis, [(i, (i + steps) % count) for i in range(count)])  11.5 us
    pallas_call x5, Pallas kernels, call(): pl.pallas_call(kernel, out_shape=outs, in_specs=[whole] * len(values), ou...  4.58 us
    pallas_call x1, Pallas kernels, radiation(): pl.pallas_call(pack_kernel, out_shape=(state_rows(shared), state_rows(sha...  3.89 us
  transfers between devices with their start and end apart: 14, of which 7 were waited for; matrix products, arithmetic and copies ran while one was open for 0% of the time, Pallas kernels for 60%

profile of v6, /device:TPU:1, one launch (start us, length us, event | category | flops | bytes accessed | tf_op | source)
XLA Modules:
  0.0 102.4 jit_solution(1679451070993560309)
XLA Ops:
  0.6 3.9 %pack.1 = (f32[362,2,128]{2,1,0:T(2,128)}, f32[362,2,128]{2,1,0:T(2,128)}, f32[362,1,128]{2,1,0:T(1,128)}, f32[192,128]{1,0:T(8,128)}, f32[192,128]{1,0:T(8,128)}) custom-call(f32[5,72,8,128]{3,2,1,0:T(8,128)} %state_ref.3, f32[576,128]{1,0:T(8,128)} %bitcast.5, f32[2,576,128]{2,1,0:T(8,128)} %bitcast.9, f32[8,128]{1,0:T(8,128)} %cosine_ref.3, ...), custom_call_target="tpu_custom_call" | custom-call | tf_op jit(solution)/shard_map/pack/pallas_call | solution.py:477
  4.5 5.1 %collective-permute-start = (f32[192,128]{1,0:T(8,128)}, f32[192,128]{1,0:T(8,128)S(1)}, u32[]{:S(2)}, u32[]{:S(2)}) collective-permute-start(f32[192,128]{1,0:T(8,128)} %get-tuple-element.31), channel_id=1, source_target_pairs={{0,28},{4,0},{8,4},{12,8},{16,12},{20,16},{24,20},{28,24},{1,29},{... | collective-permute-start | bytes 294920 | tf_op jit(solution)/shard_map/ppermute | solution.py:26
  9.6 0.0 collective-permute-start.1
  9.6 0.0 collective-permute-start.2
  9.6 28.8 %home_radiation.1 = (f32[216,128]{1,0:T(8,128)}, bf16[9,2,224,128]{3,2,1,0:T(8,128)(2,1)}, f32[112,128]{1,0:T(8,128)}) custom-call(f32[5,72,8,128]{3,2,1,0:T(8,128)} %state_ref.3, f32[576,128]{1,0:T(8,128)} %bitcast.6, f32[8,128]{1,0:T(8,128)} %cosine_ref.3, f32[8,128]{1,0:T(8,128)} %ground_ref.3, s32[8,128]{1,0:T(8,128)} %day_ref.5, ...), custom_call_target="tpu_custom_call" | custom-call | flops 30965760000 | bytes 2359296 | tf_op jit(solution)/shard_map/home_radiation/pallas_call | solution.py:490
  38.5 0.0 collective-permute-done.2.received_ref
  38.5 0.0 copy-start.7
  38.5 0.7 copy-done.7
  39.2 20.1 %shared_radiation.1 = (f32[144,128]{1,0:T(8,128)}, f32[144,128]{1,0:T(8,128)}, f32[64,128]{1,0:T(8,128)}, f32[64,128]{1,0:T(8,128)}) custom-call(f32[362,2,128]{2,1,0:T(2,128)} %get-tuple-element.38.kept_ref, f32[362,2,128]{2,1,0:T(2,128)} %copy-done.7, s32[8,128]{1,0:T(8,128)} %day_ref.5, bf16[9,2,224,128]{3,2,1,0:T(8,128)(2,1)} %get-tuple-element.35.optics_ref, ...), custom_call_target="tpu_custom_call" | custom-call | flops 20643840000 | bytes 2359296 | tf_op jit(solution)/shard_map/shared_radiation/pallas_call | solution.py:502
  59.3 2.4 %collective-permute-start.3 = (f32[144,128]{1,0:T(8,128)}, f32[144,128]{1,0:T(8,128)S(1)}, u32[]{:S(2)}, u32[]{:S(2)}) collective-permute-start(f32[144,128]{1,0:T(8,128)} %get-tuple-element.42), channel_id=1, source_target_pairs={{0,16},{4,20},{8,24},{12,28},{16,0},{20,4},{24,8},{28,12},{1,17},{... | collective-permute-start | bytes 221192 | tf_op jit(solution)/shard_map/ppermute | solution.py:26
  61.7 0.0 copy-start.9
  61.7 0.0 copy-start.8
  61.7 0.0 copy-start
  61.7 0.0 copy-start.1
  61.7 0.0 copy-start.2
  61.7 0.0 copy-start.4
  61.7 0.0 copy-start.5
  61.7 11.6 %last_home_radiation.1 = (f32[576,128]{1,0:T(8,128)}, f32[64,128]{1,0:T(8,128)}, f32[64,128]{1,0:T(8,128)}) custom-call(f32[362,1,128]{2,1,0:T(1,128)} %get-tuple-element.34.line_ref, s32[8,128]{1,0:T(8,128)} %day_ref.5, bf16[9,2,224,128]{3,2,1,0:T(8,128)(2,1)} %get-tuple-element.35.optics_ref, f32[112,128]{1,0:T(8,128)} %get-tuple-element.36.weight_ref, ...), custom_call_target="tpu_custom_call" | custom-call | flops 10321920000 | bytes 2359296 | tf_op jit(solution)/shard_map/last_home_radiation/pallas_call | solution.py:512
  73.3 0.0 copy-start.3
  73.3 0.0 copy-start.6
  73.3 4.2 %collective-permute-start.4 = (f32[64,128]{1,0:T(8,128)}, f32[64,128]{1,0:T(8,128)S(1)}, u32[]{:S(2)}, u32[]{:S(2)}) collective-permute-start(f32[64,128]{1,0:T(8,128)} %get-tuple-element.43), channel_id=1, source_target_pairs={{0,28},{4,0},{8,4},{12,8},{16,12},{20,16},{24,20},{28,24},{1,29},{... | collective-permute-start | bytes 98312 | tf_op jit(solution)/shard_map/ppermute | solution.py:26
  77.5 0.0 collective-permute-start.5
  77.5 0.0 collective-permute-done.after_ref
  77.5 0.0 copy-done.9
  77.5 0.3 collective-permute-start.6
  77.8 0.0 collective-permute-done.1.before_ref
  77.8 0.0 copy-done.8
  77.8 3.0 %collective-permute-start.7 = (f32[64,128]{1,0:T(8,128)S(1)}, f32[64,128]{1,0:T(8,128)S(1)}, u32[]{:S(2)}, u32[]{:S(2)}) collective-permute-start(f32[64,128]{1,0:T(8,128)S(1)} %copy-done.8), channel_id=1, source_target_pairs={{0,20},{4,24},{8,28},{12,0},{16,4},{20,8},{24,12},{28,16},{1,21},{... | collective-permute-start | bytes 98312 | tf_op jit(solution)/shard_map/ppermute | solution.py:26
  80.8 0.0 copy-done
  80.8 0.0 copy-done.1
  80.8 0.0 copy-done.2
  80.8 0.0 copy-done.4
  80.8 0.0 copy-done.5
  80.8 0.8 own_change.1
  81.7 0.0 collective-permute-done.4.after_ref
  81.7 1.5 %collective-permute-done.5.before_ref = f32[64,128]{1,0:T(8,128)S(1)} collective-permute-done((f32[64,128]{1,0:T(8,128)}, f32[64,128]{1,0:T(8,128)S(1)}, u32[]{:S(2)}, u32[]{:S(2)}) %collective-permute-start.5) | collective-permute-done | bytes 32800 | tf_op jit(solution)/shard_map/ppermute | solution.py:26
  83.1 0.0 collective-permute-done.6.after_more_ref
  83.1 0.0 collective-permute-done.7.before_more_ref
  83.1 0.0 collective-permute-done.3.returned_ref
  83.1 0.0 copy-done.3
  83.2 0.0 copy-done.6
  83.2 1.1 %first_stage.1 = (f32[576,256]{1,0:T(8,128)S(1)}, f32[72,256]{1,0:T(8,128)S(1)}, f32[72,256]{1,0:T(8,128)S(1)}, f32[576,128]{1,0:T(8,128)}) custom-call(f32[576,256]{1,0:T(8,128)S(1)} %get-tuple-element.33.change_ref, f32[576,128]{1,0:T(8,128)S(1)} %copy-done.6, f32[144,128]{1,0:T(8,128)S(1)} %collective-permute-done.3.returned_ref, ...), custom_call_target="tpu_custom_call" | custom-call | tf_op jit(solution)/shard_map/first_stage/pallas_call | solution.py:715
  84.3 4.3 %collective-permute-start.8 = (f32[72,256]{1,0:T(8,128)S(1)}, f32[72,256]{1,0:T(8,128)S(1)}, u32[]{:S(2)}, u32[]{:S(2)}) collective-permute-start(f32[72,256]{1,0:T(8,128)S(1)} %get-tuple-element.49), channel_id=1, source_target_pairs={{0,1},{1,2},{2,3},{3,0},{4,5},{5,6},{6,7},{7,4},{8,9},{9,10},{10,1... | collective-permute-start | bytes 221192 | tf_op jit(solution)/shard_map/ppermute | solution.py:26
  88.6 0.0 collective-permute-start.9
  88.6 1.4 %collective-permute-done.8.below_ref = f32[72,256]{1,0:T(8,128)S(1)} collective-permute-done((f32[72,256]{1,0:T(8,128)S(1)}, f32[72,256]{1,0:T(8,128)S(1)}, u32[]{:S(2)}, u32[]{:S(2)}) %collective-permute-start.8) | collective-permute-done | bytes 73760 | tf_op jit(solution)/shard_map/ppermute | solution.py:26
  90.1 2.4 %collective-permute-done.9.above_ref = f32[72,256]{1,0:T(8,128)S(1)} collective-permute-done((f32[72,256]{1,0:T(8,128)S(1)}, f32[72,256]{1,0:T(8,128)S(1)}, u32[]{:S(2)}, u32[]{:S(2)}) %collective-permute-start.9) | collective-permute-done | bytes 73760 | tf_op jit(solution)/shard_map/ppermute | solution.py:26
  92.4 0.9 second_stage.1
  93.3 0.1 collective-permute-start.10
  93.4 0.5 collective-permute-start.11
  93.9 0.9 collective-permute-done.10.below_ref
  94.8 2.4 %collective-permute-done.11.above_ref = f32[72,256]{1,0:T(8,128)S(1)} collective-permute-done((f32[72,256]{1,0:T(8,128)S(1)}, f32[72,256]{1,0:T(8,128)S(1)}, u32[]{:S(2)}, u32[]{:S(2)}) %collective-permute-start.11) | collective-permute-done | bytes 73760 | tf_op jit(solution)/shard_map/ppermute | solution.py:26
  97.2 0.9 third_stage.1
  98.1 0.1 collective-permute-start.12
  98.2 0.5 collective-permute-start.13
  98.7 0.7 collective-permute-done.12.below_ref
  99.4 2.2 %collective-permute-done.13.above_ref = f32[72,128]{1,0:T(8,128)S(1)} collective-permute-done((f32[72,128]{1,0:T(8,128)S(1)}, f32[72,128]{1,0:T(8,128)S(1)}, u32[]{:S(2)}, u32[]{:S(2)}) %collective-permute-start.13) | collective-permute-done | bytes 36896 | tf_op jit(solution)/shard_map/ppermute | solution.py:26
  101.6 0.8 last_stage.1
Async XLA Ops:
  4.5 72.9 %collective-permute-start = (f32[192,128]{1,0:T(8,128)}, f32[192,128]{1,0:T(8,128)S(1)}, u32[]{:S(2)}, u32[]{:S(2)}) collective-permute-start(f32[192,128]{1,0:T(8,128)} %get-tuple-element.31), channel_id=1, source_target_pairs={{0,28},{4,0},{8,4},{12,8},{16,12},{20,16},{24,20},{28,24},{1,29},{... | collective-permute-start | bytes 294920 | tf_op jit(solution)/shard_map/ppermute | solution.py:26
  9.6 68.1 %collective-permute-start.1 = (f32[192,128]{1,0:T(8,128)}, f32[192,128]{1,0:T(8,128)S(1)}, u32[]{:S(2)}, u32[]{:S(2)}) collective-permute-start(f32[192,128]{1,0:T(8,128)} %get-tuple-element.32), channel_id=1, source_target_pairs={{0,4},{4,8},{8,12},{12,16},{16,20},{20,24},{24,28},{28,0},{1,5},{5... | collective-permute-start | bytes 294920 | tf_op jit(solution)/shard_map/ppermute | solution.py:26
  9.6 28.8 %collective-permute-start.2 = (f32[362,2,128]{2,1,0:T(2,128)}, f32[362,2,128]{2,1,0:T(2,128)S(1)}, u32[]{:S(2)}, u32[]{:S(2)}) collective-permute-start(f32[362,2,128]{2,1,0:T(2,128)} %get-tuple-element.39), channel_id=1, source_target_pairs={{0,16},{4,20},{8,24},{12,28},{16,0},{20,4},{24,8},{28,12},{1,17},{... | collective-permute-start | bytes 1112072 | tf_op jit(solution)/shard_map/ppermute | solution.py:26
  38.5 0.7 copy-start.7
  59.3 23.8 %collective-permute-start.3 = (f32[144,128]{1,0:T(8,128)}, f32[144,128]{1,0:T(8,128)S(1)}, u32[]{:S(2)}, u32[]{:S(2)}) collective-permute-start(f32[144,128]{1,0:T(8,128)} %get-tuple-element.42), channel_id=1, source_target_pairs={{0,16},{4,20},{8,24},{12,28},{16,0},{20,4},{24,8},{28,12},{1,17},{... | collective-permute-start | bytes 221192 | tf_op jit(solution)/shard_map/ppermute | solution.py:26
  61.7 15.8 %copy-start.9 = (f32[64,128]{1,0:T(8,128)S(1)}, f32[64,128]{1,0:T(8,128)}, u32[]{:S(2)}) copy-start(f32[64,128]{1,0:T(8,128)} %get-tuple-element.45) | copy-start | bytes 98308
  61.7 16.1 %copy-start.8 = (f32[64,128]{1,0:T(8,128)S(1)}, f32[64,128]{1,0:T(8,128)}, u32[]{:S(2)}) copy-start(f32[64,128]{1,0:T(8,128)} %get-tuple-element.46) | copy-start | bytes 98308
  61.7 19.1 %copy-start = (f32[72,8,128]{2,1,0:T(8,128)S(1)}, f32[72,8,128]{2,1,0:T(8,128)}, u32[]{:S(2)}) copy-start(f32[72,8,128]{2,1,0:T(8,128)} %param.14) | copy-start | bytes 884740
  61.7 19.1 %copy-start.1 = (bf16[256,1152]{1,0:T(8,128)(2,1)S(1)}, bf16[256,1152]{1,0:T(8,128)(2,1)}, u32[]{:S(2)}) copy-start(bf16[256,1152]{1,0:T(8,128)(2,1)} %constant.12.edge_ref) | copy-start | bytes 1769476
  61.7 19.1 %copy-start.2 = (f32[2,72,8,128]{3,2,1,0:T(8,128)S(1)}, f32[2,72,8,128]{3,2,1,0:T(8,128)}, u32[]{:S(2)}) copy-start(f32[2,72,8,128]{3,2,1,0:T(8,128)} %param.15) | copy-start | bytes 1769476
  61.7 19.1 %copy-start.4 = (bf16[256,256]{1,0:T(8,128)(2,1)S(1)}, bf16[256,256]{1,0:T(8,128)(2,1)}, u32[]{:S(2)}) copy-start(bf16[256,256]{1,0:T(8,128)(2,1)} %constant.9.clone.low_ref) | copy-start | bytes 393220
  61.7 19.1 %copy-start.5 = (bf16[256,256]{1,0:T(8,128)(2,1)S(1)}, bf16[256,256]{1,0:T(8,128)(2,1)}, u32[]{:S(2)}) copy-start(bf16[256,256]{1,0:T(8,128)(2,1)} %constant.8.clone.high_ref) | copy-start | bytes 393220
  73.3 9.8 %copy-start.3 = (bf16[256,256]{1,0:T(8,128)(2,1)S(1)}, bf16[256,256]{1,0:T(8,128)(2,1)}, u32[]{:S(2)}) copy-start(bf16[256,256]{1,0:T(8,128)(2,1)} %constant.10.clone.average_ref) | copy-start | bytes 393220
  73.3 9.9 %copy-start.6 = (f32[576,128]{1,0:T(8,128)S(1)}, f32[576,128]{1,0:T(8,128)}, u32[]{:S(2)}) copy-start(f32[576,128]{1,0:T(8,128)} %get-tuple-element.41.heat_ref) | copy-start | bytes 884740
  73.3 8.4 %collective-permute-start.4 = (f32[64,128]{1,0:T(8,128)}, f32[64,128]{1,0:T(8,128)S(1)}, u32[]{:S(2)}, u32[]{:S(2)}) collective-permute-start(f32[64,128]{1,0:T(8,128)} %get-tuple-element.43), channel_id=1, source_target_pairs={{0,28},{4,0},{8,4},{12,8},{16,12},{20,16},{24,20},{28,24},{1,29},{... | collective-permute-start | bytes 98312 | tf_op jit(solution)/shard_map/ppermute | solution.py:26
  77.5 5.7 %collective-permute-start.5 = (f32[64,128]{1,0:T(8,128)}, f32[64,128]{1,0:T(8,128)S(1)}, u32[]{:S(2)}, u32[]{:S(2)}) collective-permute-start(f32[64,128]{1,0:T(8,128)} %get-tuple-element.44), channel_id=1, source_target_pairs={{0,4},{4,8},{8,12},{12,16},{16,20},{20,24},{24,28},{28,0},{1,5},{5... | collective-permute-start | bytes 98312 | tf_op jit(solution)/shard_map/ppermute | solution.py:26
  77.5 5.7 %collective-permute-start.6 = (f32[64,128]{1,0:T(8,128)S(1)}, f32[64,128]{1,0:T(8,128)S(1)}, u32[]{:S(2)}, u32[]{:S(2)}) collective-permute-start(f32[64,128]{1,0:T(8,128)S(1)} %copy-done.9), channel_id=1, source_target_pairs={{0,12},{4,16},{8,20},{12,24},{16,28},{20,0},{24,4},{28,8},{1,13},{... | collective-permute-start | bytes 98312 | tf_op jit(solution)/shard_map/ppermute | solution.py:26
  77.8 5.4 %collective-permute-start.7 = (f32[64,128]{1,0:T(8,128)S(1)}, f32[64,128]{1,0:T(8,128)S(1)}, u32[]{:S(2)}, u32[]{:S(2)}) collective-permute-start(f32[64,128]{1,0:T(8,128)S(1)} %copy-done.8), channel_id=1, source_target_pairs={{0,20},{4,24},{8,28},{12,0},{16,4},{20,8},{24,12},{28,16},{1,21},{... | collective-permute-start | bytes 98312 | tf_op jit(solution)/shard_map/ppermute | solution.py:26
  84.3 5.7 %collective-permute-start.8 = (f32[72,256]{1,0:T(8,128)S(1)}, f32[72,256]{1,0:T(8,128)S(1)}, u32[]{:S(2)}, u32[]{:S(2)}) collective-permute-start(f32[72,256]{1,0:T(8,128)S(1)} %get-tuple-element.49), channel_id=1, source_target_pairs={{0,1},{1,2},{2,3},{3,0},{4,5},{5,6},{6,7},{7,4},{8,9},{9,10},{10,1... | collective-permute-start | bytes 221192 | tf_op jit(solution)/shard_map/ppermute | solution.py:26
  88.6 3.8 %collective-permute-start.9 = (f32[72,256]{1,0:T(8,128)S(1)}, f32[72,256]{1,0:T(8,128)S(1)}, u32[]{:S(2)}, u32[]{:S(2)}) collective-permute-start(f32[72,256]{1,0:T(8,128)S(1)} %get-tuple-element.50), channel_id=1, source_target_pairs={{0,3},{1,0},{2,1},{3,2},{4,7},{5,4},{6,5},{7,6},{8,11},{9,8},{10,9... | collective-permute-start | bytes 221192 | tf_op jit(solution)/shard_map/ppermute | solution.py:26
  93.3 1.5 %collective-permute-start.10 = (f32[72,256]{1,0:T(8,128)S(1)}, f32[72,256]{1,0:T(8,128)S(1)}, u32[]{:S(2)}, u32[]{:S(2)}) collective-permute-start(f32[72,256]{1,0:T(8,128)S(1)} %get-tuple-element.53), channel_id=1, source_target_pairs={{0,1},{1,2},{2,3},{3,0},{4,5},{5,6},{6,7},{7,4},{8,9},{9,10},{10,1... | collective-permute-start | bytes 221192 | tf_op jit(solution)/shard_map/ppermute | solution.py:26
  93.4 3.8 %collective-permute-start.11 = (f32[72,256]{1,0:T(8,128)S(1)}, f32[72,256]{1,0:T(8,128)S(1)}, u32[]{:S(2)}, u32[]{:S(2)}) collective-permute-start(f32[72,256]{1,0:T(8,128)S(1)} %get-tuple-element.54), channel_id=1, source_target_pairs={{0,3},{1,0},{2,1},{3,2},{4,7},{5,4},{6,5},{7,6},{8,11},{9,8},{10,9... | collective-permute-start | bytes 221192 | tf_op jit(solution)/shard_map/ppermute | solution.py:26
  98.1 1.3 %collective-permute-start.12 = (f32[72,128]{1,0:T(8,128)S(1)}, f32[72,128]{1,0:T(8,128)S(1)}, u32[]{:S(2)}, u32[]{:S(2)}) collective-permute-start(f32[72,128]{1,0:T(8,128)S(1)} %get-tuple-element.57), channel_id=1, source_target_pairs={{0,1},{1,2},{2,3},{3,0},{4,5},{5,6},{6,7},{7,4},{8,9},{9,10},{10,1... | collective-permute-start | bytes 110600 | tf_op jit(solution)/shard_map/ppermute | solution.py:26
  98.2 3.4 %collective-permute-start.13 = (f32[72,128]{1,0:T(8,128)S(1)}, f32[72,128]{1,0:T(8,128)S(1)}, u32[]{:S(2)}, u32[]{:S(2)}) collective-permute-start(f32[72,128]{1,0:T(8,128)S(1)} %get-tuple-element.58), channel_id=1, source_target_pairs={{0,3},{1,0},{2,1},{3,2},{4,7},{5,4},{6,5},{7,6},{8,11},{9,8},{10,9... | collective-permute-start | bytes 110600 | tf_op jit(solution)/shard_map/ppermute | solution.py:26

commit v7 on v6

--- a/solution.py
+++ b/solution.py
@@ -339,8 +339,7 @@
 
 def shared_kernel(
     kept_ref, received_ref, day_ref, optics_ref, weight_ref, edge_ref,
-    mine_ref, theirs_ref, their_first_ref, their_last_ref,
-    surface_ref, strip_ref, terms_ref, right_ref, *scratch,
+    mine_ref, theirs_ref, surface_ref, strip_ref, terms_ref, right_ref, *scratch,
 ):
     level_count = kept_ref.shape[0] // 5
     shared, lanes = kept_ref.shape[1:]
@@ -383,8 +382,10 @@
             start = pl.multiple_of(8 * (first + r), 8)
             write_strip(theirs_ref, r, shared, strip_ref, start)
         packed = split_dot(strip_ref[...], edge_ref[...])
-        their_first_ref[...] = packed[:, :lanes]
-        their_last_ref[...] = packed[:, lanes:]
+        size = level_count * shared
+        half = packed.shape[0]
+        theirs_ref[size : size + half, :] = packed[:, :lanes]
+        theirs_ref[size + half :, :] = packed[:, lanes:]
 
 
 def write_strip(source_ref, r, lines, strip_ref, start):
@@ -486,6 +487,9 @@
     )(state, temper, flow, cosine, ground, edges)
     received = shifted(sent, "gx", partner)
     fields_after, fields_before = shifted(fields_first, "gx", -1), shifted(fields_last, "gx", 1)
+    received, fields_after, fields_before = lax.optimization_barrier(
+        (received, fields_after, fields_before)
+    )
     early = home - 1
     home_heat, optics, weight = pl.pallas_call(
         functools.partial(home_kernel, 0),
@@ -499,16 +503,17 @@
         name="home_radiation",
     )(state, temper, cosine, ground, day, molecular.transpose(0, 2, 1), condensate)
     edge = jax.ShapeDtypeStruct((8 * rows, lanes), jnp.float32)
-    mine, theirs, their_first, their_last = pl.pallas_call(
+    theirs_size = level_count * shared + 16 * rows
+    mine, theirs = pl.pallas_call(
         shared_kernel,
-        out_shape=(field(shared), field(shared), edge, edge),
-        grid=(shared,), in_specs=[whole] * 6, out_specs=(whole,) * 4,
+        out_shape=(field(shared), jax.ShapeDtypeStruct((theirs_size, lanes), jnp.float32)),
+        grid=(shared,), in_specs=[whole] * 6, out_specs=(whole,) * 2,
         scratch_shapes=[pltpu.VMEM((2, 8, lanes), jnp.float32), strip] + scratch(shared, shared),
         compiler_params=params, cost_estimate=cost(shared), name="shared_radiation",
     )(kept, received, day, optics, weight, edges)
     returned = shifted(theirs, "gx", partner)
-    after_more = shifted(their_first, "gx", partner - 1)
-    before_more = shifted(their_last, "gx", partner + 1)
+    after_more = shifted(theirs, "gx", partner - 1)
+    before_more = shifted(theirs, "gx", partner + 1)
     heat, first, last = pl.pallas_call(
         last_home_kernel,
         out_shape=(field(rows), edge, edge),
@@ -637,9 +642,10 @@
 ):
     level_count = first_ref.shape[0]
     lanes = heat_ref.shape[1]
-    shared = returned_ref.shape[0] // level_count
-    after = after_ref[...] + after_more_ref[...]
-    before = before_ref[...] + before_more_ref[...]
+    shared = ROWS // 4
+    size, half = level_count * shared, after_ref.shape[0]
+    after = after_ref[...] + after_more_ref[size : size + half, :]
+    before = before_ref[...] + before_more_ref[size + half :, :]
     sides = split_dot(jnp.concatenate([after, before], axis=1), edge_ref[...])
     for r in range(ROWS):
         rows = slice(r * level_count, (r + 1) * level_count)

time: 103 us -> 106 us (1.029)
  waiting for transfers between devices: 11.5 us -> 14.8 us
    ppermute x14, waiting for transfers between devices: 11.5 us -> 14.8 us  [shifted(): lax.ppermute(value, axis, [(i, (i + steps) % count) for i in range(count)])]
  transfers between devices with their start and end apart: 14 -> 14, of which waited for: 7 -> 8; matrix products, arithmetic and copies ran while one was open for 0% -> 0% of each run, Pallas kernels for 60% -> 39%
where the time goes in v7:
time: 106 us
  Pallas kernels  69 us (65%)
  starting transfers between devices  20.9 us (20%)
  waiting for transfers between devices  14.8 us (14%)
    pallas_call x1, Pallas kernels, radiation(): pl.pallas_call(functools.partial(home_kernel, 0), out_shape=(field(early)...  28.8 us
    ppermute x14, starting transfers between devices, shifted(): lax.ppermute(value, axis, [(i, (i + steps) % count) for i in range(count)])  20.9 us
    pallas_call x1, Pallas kernels, radiation(): pl.pallas_call(shared_kernel, out_shape=(field(shared), jax.ShapeDtypeStr...  20.1 us
    ppermute x14, waiting for transfers between devices, shifted(): lax.ppermute(value, axis, [(i, (i + steps) % count) for i in range(count)])  14.8 us
    pallas_call x1, Pallas kernels, radiation(): pl.pallas_call(last_home_kernel, out_shape=(field(rows), edge, edge), gri...  11.6 us
    pallas_call x5, Pallas kernels, call(): pl.pallas_call(kernel, out_shape=outs, in_specs=[whole] * len(values), ou...  4.58 us
    pallas_call x1, Pallas kernels, radiation(): pl.pallas_call(pack_kernel, out_shape=(state_rows(shared), state_rows(sha...  3.91 us
  transfers between devices with their start and end apart: 14, of which 8 were waited for; matrix products, arithmetic and copies ran while one was open for 0% of the time, Pallas kernels for 39%

profile of v7, /device:TPU:1, one launch (start us, length us, event | category | flops | bytes accessed | tf_op | source)
XLA Modules:
  0.0 106.2 jit_solution(157108321954772400)
XLA Ops:
  0.6 3.9 %pack.1 = (f32[362,2,128]{2,1,0:T(2,128)}, f32[362,2,128]{2,1,0:T(2,128)}, f32[362,1,128]{2,1,0:T(1,128)}, f32[192,128]{1,0:T(8,128)}, f32[192,128]{1,0:T(8,128)}) custom-call(f32[5,72,8,128]{3,2,1,0:T(8,128)} %state_ref.3, f32[576,128]{1,0:T(8,128)} %bitcast.5, f32[2,576,128]{2,1,0:T(8,128)} %bitcast.9, f32[8,128]{1,0:T(8,128)} %cosine_ref.3, ...), custom_call_target="tpu_custom_call" | custom-call | tf_op jit(solution)/shard_map/pack/pallas_call | solution.py:478
  4.5 5.1 %collective-permute-start.1 = (f32[192,128]{1,0:T(8,128)}, f32[192,128]{1,0:T(8,128)S(1)}, u32[]{:S(2)}, u32[]{:S(2)}) collective-permute-start(f32[192,128]{1,0:T(8,128)} %get-tuple-element.33), channel_id=1, source_target_pairs={{0,28},{4,0},{8,4},{12,8},{16,12},{20,16},{24,20},{28,24},{1,29},{... | collective-permute-start | bytes 294920 | tf_op jit(solution)/shard_map/ppermute | solution.py:26
  9.6 0.0 collective-permute-start.2
  9.6 0.0 collective-permute-start
  9.7 28.8 %home_radiation.1 = (f32[216,128]{1,0:T(8,128)}, bf16[9,2,224,128]{3,2,1,0:T(8,128)(2,1)}, f32[112,128]{1,0:T(8,128)}) custom-call(f32[5,72,8,128]{3,2,1,0:T(8,128)} %state_ref.3, f32[576,128]{1,0:T(8,128)} %bitcast.6, f32[8,128]{1,0:T(8,128)} %cosine_ref.3, f32[8,128]{1,0:T(8,128)} %ground_ref.3, s32[8,128]{1,0:T(8,128)} %day_ref.5, ...), custom_call_target="tpu_custom_call" | custom-call | flops 30965760000 | bytes 2359296 | tf_op jit(solution)/shard_map/home_radiation/pallas_call | solution.py:494
  38.4 0.0 collective-permute-done.1.after_ref
  38.5 0.0 collective-permute-done.2.before_ref
  38.5 0.0 collective-permute-done.received_ref
  38.5 0.0 copy-start.7
  38.5 0.7 copy-done.7
  39.2 20.1 %shared_radiation.1 = (f32[144,128]{1,0:T(8,128)}, f32[272,128]{1,0:T(8,128)}) custom-call(f32[362,2,128]{2,1,0:T(2,128)} %get-tuple-element.42.kept_ref, f32[362,2,128]{2,1,0:T(2,128)} %copy-done.7, s32[8,128]{1,0:T(8,128)} %day_ref.5, bf16[9,2,224,128]{3,2,1,0:T(8,128)(2,1)} %get-tuple-element.39.optics_ref, f32[112,128]{1,0:T(8,128)} %get-tuple-element.40.weight_ref, ...), custom_call_target="tpu_custom_call" | custom-call | flops 20643840000 | bytes 2359296 | tf_op jit(solution)/shard_map/shared_radiation/pallas_call | solution.py:507
  59.3 1.4 %collective-permute-start.7 = (f32[272,128]{1,0:T(8,128)}, f32[272,128]{1,0:T(8,128)S(1)}, u32[]{:S(2)}, u32[]{:S(2)}) collective-permute-start(f32[272,128]{1,0:T(8,128)} %get-tuple-element.46), channel_id=1, source_target_pairs={{0,20},{4,24},{8,28},{12,0},{16,4},{20,8},{24,12},{28,16},{1,21},{... | collective-permute-start | bytes 417800 | tf_op jit(solution)/shard_map/ppermute | solution.py:26
  60.7 3.0 %collective-permute-start.6 = (f32[272,128]{1,0:T(8,128)}, f32[272,128]{1,0:T(8,128)S(1)}, u32[]{:S(2)}, u32[]{:S(2)}) collective-permute-start(f32[272,128]{1,0:T(8,128)} %get-tuple-element.46), channel_id=1, source_target_pairs={{0,12},{4,16},{8,20},{12,24},{16,28},{20,0},{24,4},{28,8},{1,13},{... | collective-permute-start | bytes 417800 | tf_op jit(solution)/shard_map/ppermute | solution.py:26
  63.7 0.3 collective-permute-start.3
  64.0 0.0 copy-start
  64.0 0.0 copy-start.1
  64.0 0.0 copy-start.2
  64.0 0.0 copy-start.4
  64.0 0.0 copy-start.5
  64.0 11.6 %last_home_radiation.1 = (f32[576,128]{1,0:T(8,128)}, f32[64,128]{1,0:T(8,128)}, f32[64,128]{1,0:T(8,128)}) custom-call(f32[362,1,128]{2,1,0:T(1,128)} %get-tuple-element.38.line_ref, s32[8,128]{1,0:T(8,128)} %day_ref.5, bf16[9,2,224,128]{3,2,1,0:T(8,128)(2,1)} %get-tuple-element.39.optics_ref, f32[112,128]{1,0:T(8,128)} %get-tuple-element.40.weight_ref, ...), custom_call_target="tpu_custom_call" | custom-call | flops 10321920000 | bytes 2359296 | tf_op jit(solution)/shard_map/last_home_radiation/pallas_call | solution.py:517
  75.6 0.0 copy-start.3
  75.6 0.0 copy-start.6
  75.6 5.1 %collective-permute-start.4 = (f32[64,128]{1,0:T(8,128)}, f32[64,128]{1,0:T(8,128)S(1)}, u32[]{:S(2)}, u32[]{:S(2)}) collective-permute-start(f32[64,128]{1,0:T(8,128)} %get-tuple-element.47), channel_id=1, source_target_pairs={{0,28},{4,0},{8,4},{12,8},{16,12},{20,16},{24,20},{28,24},{1,29},{... | collective-permute-start | bytes 98312 | tf_op jit(solution)/shard_map/ppermute | solution.py:26
  80.7 0.0 collective-permute-start.5
  80.7 0.0 copy-done
  80.7 0.0 copy-done.1
  80.7 0.0 copy-done.2
  80.7 0.0 copy-done.4
  80.7 0.0 copy-done.5
  80.7 0.8 own_change.1
  81.6 0.5 collective-permute-done.4.after_ref
  82.0 4.3 %collective-permute-done.5.before_ref = f32[64,128]{1,0:T(8,128)S(1)} collective-permute-done((f32[64,128]{1,0:T(8,128)}, f32[64,128]{1,0:T(8,128)S(1)}, u32[]{:S(2)}, u32[]{:S(2)}) %collective-permute-start.5) | collective-permute-done | bytes 32800 | tf_op jit(solution)/shard_map/ppermute | solution.py:26
  86.4 0.0 collective-permute-done.7.before_more_ref
  86.4 0.0 collective-permute-done.6.after_more_ref
  86.4 0.0 collective-permute-done.3.returned_ref
  86.4 0.0 copy-done.3
  86.4 0.0 copy-done.6
  86.4 1.2 %first_stage.1 = (f32[576,256]{1,0:T(8,128)S(1)}, f32[72,256]{1,0:T(8,128)S(1)}, f32[72,256]{1,0:T(8,128)S(1)}, f32[576,128]{1,0:T(8,128)}) custom-call(f32[576,256]{1,0:T(8,128)S(1)} %get-tuple-element.37.change_ref, f32[576,128]{1,0:T(8,128)S(1)} %copy-done.6, f32[272,128]{1,0:T(8,128)S(1)} %collective-permute-done.3.returned_ref, ...), custom_call_target="tpu_custom_call" | custom-call | tf_op jit(solution)/shard_map/first_stage/pallas_call | solution.py:721
  87.6 4.9 %collective-permute-start.8 = (f32[72,256]{1,0:T(8,128)S(1)}, f32[72,256]{1,0:T(8,128)S(1)}, u32[]{:S(2)}, u32[]{:S(2)}) collective-permute-start(f32[72,256]{1,0:T(8,128)S(1)} %get-tuple-element.51), channel_id=1, source_target_pairs={{0,1},{1,2},{2,3},{3,0},{4,5},{5,6},{6,7},{7,4},{8,9},{9,10},{10,1... | collective-permute-start | bytes 221192 | tf_op jit(solution)/shard_map/ppermute | solution.py:26
  92.4 0.0 collective-permute-start.9
  92.4 1.4 %collective-permute-done.8.below_ref = f32[72,256]{1,0:T(8,128)S(1)} collective-permute-done((f32[72,256]{1,0:T(8,128)S(1)}, f32[72,256]{1,0:T(8,128)S(1)}, u32[]{:S(2)}, u32[]{:S(2)}) %collective-permute-start.8) | collective-permute-done | bytes 73760 | tf_op jit(solution)/shard_map/ppermute | solution.py:26
  93.8 2.4 %collective-permute-done.9.above_ref = f32[72,256]{1,0:T(8,128)S(1)} collective-permute-done((f32[72,256]{1,0:T(8,128)S(1)}, f32[72,256]{1,0:T(8,128)S(1)}, u32[]{:S(2)}, u32[]{:S(2)}) %collective-permute-start.9) | collective-permute-done | bytes 73760 | tf_op jit(solution)/shard_map/ppermute | solution.py:26
  96.2 0.9 second_stage.1
  97.1 0.1 collective-permute-start.10
  97.2 0.5 collective-permute-start.11
  97.7 0.9 collective-permute-done.10.below_ref
  98.6 2.4 %collective-permute-done.11.above_ref = f32[72,256]{1,0:T(8,128)S(1)} collective-permute-done((f32[72,256]{1,0:T(8,128)S(1)}, f32[72,256]{1,0:T(8,128)S(1)}, u32[]{:S(2)}, u32[]{:S(2)}) %collective-permute-start.11) | collective-permute-done | bytes 73760 | tf_op jit(solution)/shard_map/ppermute | solution.py:26
  101.0 0.9 third_stage.1
  101.9 0.1 collective-permute-start.12
  102.0 0.5 collective-permute-start.13
  102.5 0.7 collective-permute-done.12.below_ref
  103.2 2.2 %collective-permute-done.13.above_ref = f32[72,128]{1,0:T(8,128)S(1)} collective-permute-done((f32[72,128]{1,0:T(8,128)S(1)}, f32[72,128]{1,0:T(8,128)S(1)}, u32[]{:S(2)}, u32[]{:S(2)}) %collective-permute-start.13) | collective-permute-done | bytes 36896 | tf_op jit(solution)/shard_map/ppermute | solution.py:26
  105.4 0.8 last_stage.1
Async XLA Ops:
  4.5 33.9 %collective-permute-start.1 = (f32[192,128]{1,0:T(8,128)}, f32[192,128]{1,0:T(8,128)S(1)}, u32[]{:S(2)}, u32[]{:S(2)}) collective-permute-start(f32[192,128]{1,0:T(8,128)} %get-tuple-element.33), channel_id=1, source_target_pairs={{0,28},{4,0},{8,4},{12,8},{16,12},{20,16},{24,20},{28,24},{1,29},{... | collective-permute-start | bytes 294920 | tf_op jit(solution)/shard_map/ppermute | solution.py:26
  9.6 28.8 %collective-permute-start.2 = (f32[192,128]{1,0:T(8,128)}, f32[192,128]{1,0:T(8,128)S(1)}, u32[]{:S(2)}, u32[]{:S(2)}) collective-permute-start(f32[192,128]{1,0:T(8,128)} %get-tuple-element.34), channel_id=1, source_target_pairs={{0,4},{4,8},{8,12},{12,16},{16,20},{20,24},{24,28},{28,0},{1,5},{5... | collective-permute-start | bytes 294920 | tf_op jit(solution)/shard_map/ppermute | solution.py:26
  9.6 28.8 %collective-permute-start = (f32[362,2,128]{2,1,0:T(2,128)}, f32[362,2,128]{2,1,0:T(2,128)S(1)}, u32[]{:S(2)}, u32[]{:S(2)}) collective-permute-start(f32[362,2,128]{2,1,0:T(2,128)} %get-tuple-element.32), channel_id=1, source_target_pairs={{0,16},{4,20},{8,24},{12,28},{16,0},{20,4},{24,8},{28,12},{1,17},{... | collective-permute-start | bytes 1112072 | tf_op jit(solution)/shard_map/ppermute | solution.py:26
  38.5 0.7 copy-start.7
  59.3 27.1 %collective-permute-start.7 = (f32[272,128]{1,0:T(8,128)}, f32[272,128]{1,0:T(8,128)S(1)}, u32[]{:S(2)}, u32[]{:S(2)}) collective-permute-start(f32[272,128]{1,0:T(8,128)} %get-tuple-element.46), channel_id=1, source_target_pairs={{0,20},{4,24},{8,28},{12,0},{16,4},{20,8},{24,12},{28,16},{1,21},{... | collective-permute-start | bytes 417800 | tf_op jit(solution)/shard_map/ppermute | solution.py:26
  60.7 25.7 %collective-permute-start.6 = (f32[272,128]{1,0:T(8,128)}, f32[272,128]{1,0:T(8,128)S(1)}, u32[]{:S(2)}, u32[]{:S(2)}) collective-permute-start(f32[272,128]{1,0:T(8,128)} %get-tuple-element.46), channel_id=1, source_target_pairs={{0,12},{4,16},{8,20},{12,24},{16,28},{20,0},{24,4},{28,8},{1,13},{... | collective-permute-start | bytes 417800 | tf_op jit(solution)/shard_map/ppermute | solution.py:26
  63.7 22.6 %collective-permute-start.3 = (f32[272,128]{1,0:T(8,128)}, f32[272,128]{1,0:T(8,128)S(1)}, u32[]{:S(2)}, u32[]{:S(2)}) collective-permute-start(f32[272,128]{1,0:T(8,128)} %get-tuple-element.46), channel_id=1, source_target_pairs={{0,16},{4,20},{8,24},{12,28},{16,0},{20,4},{24,8},{28,12},{1,17},{... | collective-permute-start | bytes 417800 | tf_op jit(solution)/shard_map/ppermute | solution.py:26
  64.0 16.7 %copy-start = (f32[72,8,128]{2,1,0:T(8,128)S(1)}, f32[72,8,128]{2,1,0:T(8,128)}, u32[]{:S(2)}) copy-start(f32[72,8,128]{2,1,0:T(8,128)} %param.14) | copy-start | bytes 884740
  64.0 16.7 %copy-start.1 = (f32[2,72,8,128]{3,2,1,0:T(8,128)S(1)}, f32[2,72,8,128]{3,2,1,0:T(8,128)}, u32[]{:S(2)}) copy-start(f32[2,72,8,128]{3,2,1,0:T(8,128)} %param.15) | copy-start | bytes 1769476
  64.0 16.7 %copy-start.2 = (bf16[256,1152]{1,0:T(8,128)(2,1)S(1)}, bf16[256,1152]{1,0:T(8,128)(2,1)}, u32[]{:S(2)}) copy-start(bf16[256,1152]{1,0:T(8,128)(2,1)} %constant.12.edge_ref) | copy-start | bytes 1769476
  64.0 16.7 %copy-start.4 = (bf16[256,256]{1,0:T(8,128)(2,1)S(1)}, bf16[256,256]{1,0:T(8,128)(2,1)}, u32[]{:S(2)}) copy-start(bf16[256,256]{1,0:T(8,128)(2,1)} %constant.9.clone.low_ref) | copy-start | bytes 393220
  64.0 16.7 %copy-start.5 = (bf16[256,256]{1,0:T(8,128)(2,1)S(1)}, bf16[256,256]{1,0:T(8,128)(2,1)}, u32[]{:S(2)}) copy-start(bf16[256,256]{1,0:T(8,128)(2,1)} %constant.8.clone.high_ref) | copy-start | bytes 393220
  75.6 10.7 %copy-start.3 = (bf16[256,256]{1,0:T(8,128)(2,1)S(1)}, bf16[256,256]{1,0:T(8,128)(2,1)}, u32[]{:S(2)}) copy-start(bf16[256,256]{1,0:T(8,128)(2,1)} %constant.10.clone.average_ref) | copy-start | bytes 393220
  75.6 10.8 %copy-start.6 = (f32[576,128]{1,0:T(8,128)S(1)}, f32[576,128]{1,0:T(8,128)}, u32[]{:S(2)}) copy-start(f32[576,128]{1,0:T(8,128)} %get-tuple-element.45.heat_ref) | copy-start | bytes 884740
  75.6 6.4 %collective-permute-start.4 = (f32[64,128]{1,0:T(8,128)}, f32[64,128]{1,0:T(8,128)S(1)}, u32[]{:S(2)}, u32[]{:S(2)}) collective-permute-start(f32[64,128]{1,0:T(8,128)} %get-tuple-element.47), channel_id=1, source_target_pairs={{0,28},{4,0},{8,4},{12,8},{16,12},{20,16},{24,20},{28,24},{1,29},{... | collective-permute-start | bytes 98312 | tf_op jit(solution)/shard_map/ppermute | solution.py:26
  80.7 5.7 %collective-permute-start.5 = (f32[64,128]{1,0:T(8,128)}, f32[64,128]{1,0:T(8,128)S(1)}, u32[]{:S(2)}, u32[]{:S(2)}) collective-permute-start(f32[64,128]{1,0:T(8,128)} %get-tuple-element.48), channel_id=1, source_target_pairs={{0,4},{4,8},{8,12},{12,16},{16,20},{20,24},{24,28},{28,0},{1,5},{5... | collective-permute-start | bytes 98312 | tf_op jit(solution)/shard_map/ppermute | solution.py:26
  87.6 6.3 %collective-permute-start.8 = (f32[72,256]{1,0:T(8,128)S(1)}, f32[72,256]{1,0:T(8,128)S(1)}, u32[]{:S(2)}, u32[]{:S(2)}) collective-permute-start(f32[72,256]{1,0:T(8,128)S(1)} %get-tuple-element.51), channel_id=1, source_target_pairs={{0,1},{1,2},{2,3},{3,0},{4,5},{5,6},{6,7},{7,4},{8,9},{9,10},{10,1... | collective-permute-start | bytes 221192 | tf_op jit(solution)/shard_map/ppermute | solution.py:26
  92.4 3.8 %collective-permute-start.9 = (f32[72,256]{1,0:T(8,128)S(1)}, f32[72,256]{1,0:T(8,128)S(1)}, u32[]{:S(2)}, u32[]{:S(2)}) collective-permute-start(f32[72,256]{1,0:T(8,128)S(1)} %get-tuple-element.52), channel_id=1, source_target_pairs={{0,3},{1,0},{2,1},{3,2},{4,7},{5,4},{6,5},{7,6},{8,11},{9,8},{10,9... | collective-permute-start | bytes 221192 | tf_op jit(solution)/shard_map/ppermute | solution.py:26
  97.1 1.5 %collective-permute-start.10 = (f32[72,256]{1,0:T(8,128)S(1)}, f32[72,256]{1,0:T(8,128)S(1)}, u32[]{:S(2)}, u32[]{:S(2)}) collective-permute-start(f32[72,256]{1,0:T(8,128)S(1)} %get-tuple-element.55), channel_id=1, source_target_pairs={{0,1},{1,2},{2,3},{3,0},{4,5},{5,6},{6,7},{7,4},{8,9},{9,10},{10,1... | collective-permute-start | bytes 221192 | tf_op jit(solution)/shard_map/ppermute | solution.py:26
  97.2 3.8 %collective-permute-start.11 = (f32[72,256]{1,0:T(8,128)S(1)}, f32[72,256]{1,0:T(8,128)S(1)}, u32[]{:S(2)}, u32[]{:S(2)}) collective-permute-start(f32[72,256]{1,0:T(8,128)S(1)} %get-tuple-element.56), channel_id=1, source_target_pairs={{0,3},{1,0},{2,1},{3,2},{4,7},{5,4},{6,5},{7,6},{8,11},{9,8},{10,9... | collective-permute-start | bytes 221192 | tf_op jit(solution)/shard_map/ppermute | solution.py:26
  101.9 1.3 %collective-permute-start.12 = (f32[72,128]{1,0:T(8,128)S(1)}, f32[72,128]{1,0:T(8,128)S(1)}, u32[]{:S(2)}, u32[]{:S(2)}) collective-permute-start(f32[72,128]{1,0:T(8,128)S(1)} %get-tuple-element.59), channel_id=1, source_target_pairs={{0,1},{1,2},{2,3},{3,0},{4,5},{5,6},{6,7},{7,4},{8,9},{9,10},{10,1... | collective-permute-start | bytes 110600 | tf_op jit(solution)/shard_map/ppermute | solution.py:26
  102.0 3.4 %collective-permute-start.13 = (f32[72,128]{1,0:T(8,128)S(1)}, f32[72,128]{1,0:T(8,128)S(1)}, u32[]{:S(2)}, u32[]{:S(2)}) collective-permute-start(f32[72,128]{1,0:T(8,128)S(1)} %get-tuple-element.60), channel_id=1, source_target_pairs={{0,3},{1,0},{2,1},{3,2},{4,7},{5,4},{6,5},{7,6},{8,11},{9,8},{10,9... | collective-permute-start | bytes 110600 | tf_op jit(solution)/shard_map/ppermute | solution.py:26

commit v8 on v7

--- a/solution.py
+++ b/solution.py
@@ -338,8 +338,8 @@
 
 
 def shared_kernel(
-    kept_ref, received_ref, day_ref, optics_ref, weight_ref, edge_ref,
-    mine_ref, theirs_ref, surface_ref, strip_ref, terms_ref, right_ref, *scratch,
+    kept_ref, received_ref, day_ref, optics_ref, weight_ref,
+    mine_ref, theirs_ref, surface_ref, terms_ref, right_ref, *scratch,
 ):
     level_count = kept_ref.shape[0] // 5
     shared, lanes = kept_ref.shape[1:]
@@ -377,15 +377,6 @@
             theirs_ref[span, :] = jnp.where(day, 0.0, value)
 
         level_heating(scratch[PARTIAL], level_count, gpoints, shared, write)
-        strip_ref[...] = jnp.zeros_like(strip_ref)
-        for r in range(shared):
-            start = pl.multiple_of(8 * (first + r), 8)
-            write_strip(theirs_ref, r, shared, strip_ref, start)
-        packed = split_dot(strip_ref[...], edge_ref[...])
-        size = level_count * shared
-        half = packed.shape[0]
-        theirs_ref[size : size + half, :] = packed[:, :lanes]
-        theirs_ref[size + half :, :] = packed[:, lanes:]
 
 
 def write_strip(source_ref, r, lines, strip_ref, start):
@@ -397,14 +388,10 @@
 
 
 def last_home_kernel(
-    line_ref, day_ref, optics_ref, weight_ref, edge_ref, home_ref, mine_ref,
-    heat_ref, first_ref, last_ref, strip_ref, terms_ref, right_ref, *scratch,
-):
-    lines, lanes = day_ref.shape
+    line_ref, day_ref, optics_ref, weight_ref, heat_ref, terms_ref, right_ref, *scratch,
+):
     level_count = line_ref.shape[0] // 5
-    gpoints = weight_ref.shape[0]
     row = pl.program_id(0)
-    line = lines // 2 - 1
     right_ref[...] = jnp.zeros_like(right_ref)
 
     def level(l, carry):
@@ -416,20 +403,34 @@
         row, 0, 1, 1, line_ref[5 * level_count], line_ref[5 * level_count + 1],
         optics_ref, weight_ref, terms_ref, right_ref, *scratch,
     )
-    first = shared_places(lines)[0]
-    shared = mine_ref.shape[0] // level_count
+    line = day_ref.shape[0] // 2 - 1
     day = day_ref[line : line + 1, :] == 1
-    heat_ref[...] = jnp.zeros_like(heat_ref)
 
     def write(level, value):
-        start = pl.multiple_of(level * lines, 8)
-        heat_ref[pl.ds(start, line), :] = home_ref[pl.ds(level * line, line), :]
-        heat_ref[pl.ds(start + line, 1), :] = jnp.where(day, value, 0.0)
-        heat_ref[pl.ds(start + first, shared), :] = mine_ref[pl.ds(level * shared, shared), :]
-
-    level_heating(scratch[PARTIAL], level_count, gpoints, 1, write)
+        heat_ref[pl.ds(level, 1), :] = jnp.where(day, value, 0.0)
+
+    level_heating(scratch[PARTIAL], level_count, weight_ref.shape[0], 1, write)
+
+
+def join_kernel(
+    home_ref, line_ref, mine_ref, returned_ref, edge_ref, heat_ref, first_ref, last_ref, strip_ref
+):
+    level_count, lanes = line_ref.shape
+    lines = heat_ref.shape[0] // level_count
+    home, shared = lines // 2, lines // 4
+    place = shared_places(lines)[0]
     for r in range(lines):
-        write_strip(heat_ref, r, lines, strip_ref, 8 * r)
+        if r < home - 1:
+            row = home_ref[pl.ds(r, level_count, stride=home - 1), :]
+        elif r == home - 1:
+            row = line_ref[...]
+        else:
+            n = (r - home) % shared
+            span = pl.ds(n, level_count, stride=shared)
+            row = jnp.where(place == r - n, mine_ref[span, :], returned_ref[span, :])
+        heat_ref[pl.ds(r, level_count, stride=lines), :] = row
+        for k in range(level_count // 8):
+            strip_ref[8 * r : 8 * (r + 1), lanes * k : lanes * (k + 1)] = row[8 * k : 8 * (k + 1)]
     packed = split_dot(strip_ref[...], edge_ref[...])
     first_ref[...] = packed[:, :lanes]
     last_ref[...] = packed[:, lanes:]
@@ -503,28 +504,27 @@
         name="home_radiation",
     )(state, temper, cosine, ground, day, molecular.transpose(0, 2, 1), condensate)
     edge = jax.ShapeDtypeStruct((8 * rows, lanes), jnp.float32)
-    theirs_size = level_count * shared + 16 * rows
     mine, theirs = pl.pallas_call(
         shared_kernel,
-        out_shape=(field(shared), jax.ShapeDtypeStruct((theirs_size, lanes), jnp.float32)),
-        grid=(shared,), in_specs=[whole] * 6, out_specs=(whole,) * 2,
-        scratch_shapes=[pltpu.VMEM((2, 8, lanes), jnp.float32), strip] + scratch(shared, shared),
+        out_shape=(field(shared), field(shared)),
+        grid=(shared,), in_specs=[whole] * 5, out_specs=(whole,) * 2,
+        scratch_shapes=[pltpu.VMEM((2, 8, lanes), jnp.float32)] + scratch(shared, shared),
         compiler_params=params, cost_estimate=cost(shared), name="shared_radiation",
-    )(kept, received, day, optics, weight, edges)
+    )(kept, received, day, optics, weight)
     returned = shifted(theirs, "gx", partner)
-    after_more = shifted(theirs, "gx", partner - 1)
-    before_more = shifted(theirs, "gx", partner + 1)
+    line_heat = pl.pallas_call(
+        last_home_kernel,
+        out_shape=field(1),
+        grid=(1,), in_specs=[whole] * 4, out_specs=whole, scratch_shapes=scratch(1, 1),
+        compiler_params=params, cost_estimate=cost(1), name="last_home_radiation",
+    )(line, day, optics, weight)
     heat, first, last = pl.pallas_call(
-        last_home_kernel,
-        out_shape=(field(rows), edge, edge),
-        grid=(1,), in_specs=[whole] * 7, out_specs=(whole,) * 3,
-        scratch_shapes=[strip] + scratch(1, 1),
-        compiler_params=params, cost_estimate=cost(1), name="last_home_radiation",
-    )(line, day, optics, weight, edges, home_heat, mine)
+        join_kernel, out_shape=(field(rows), edge, edge),
+        in_specs=[whole] * 5, out_specs=(whole,) * 3, scratch_shapes=[strip],
+        compiler_params=params, name="join",
+    )(home_heat, line_heat, mine, returned, edges)
     after, before = shifted(first, "gx", -1), shifted(last, "gx", 1)
-    return (
-        heat, returned, after, before, after_more, before_more, fields_after, fields_before
-    )
+    return heat, after, before, fields_after, fields_before
 
 
 def edge_matrix(level_count, lanes):
@@ -636,28 +636,15 @@
 
 
 def first_stage_kernel(
-    change_ref, heat_ref, returned_ref, after_ref, before_ref, after_more_ref,
-    before_more_ref, edge_ref, average_ref,
-    out_ref, first_ref, last_ref, heat_out_ref, sum_ref,
+    change_ref, heat_ref, after_ref, before_ref, edge_ref, average_ref,
+    out_ref, first_ref, last_ref, sum_ref,
 ):
     level_count = first_ref.shape[0]
     lanes = heat_ref.shape[1]
-    shared = ROWS // 4
-    size, half = level_count * shared, after_ref.shape[0]
-    after = after_ref[...] + after_more_ref[size : size + half, :]
-    before = before_ref[...] + before_more_ref[size + half :, :]
-    sides = split_dot(jnp.concatenate([after, before], axis=1), edge_ref[...])
+    sides = unpacked(after_ref, before_ref, edge_ref)
     for r in range(ROWS):
         rows = slice(r * level_count, (r + 1) * level_count)
-        span = pl.ds(r, level_count, stride=ROWS)
-        own = heat_ref[span, :]
-        if r >= ROWS // 2:
-            n = r % shared
-            here = shared_places(ROWS)[1] == r - n
-            own = own + jnp.where(
-                here, returned_ref[pl.ds(n, level_count, stride=shared), :], 0.0
-            )
-        heat_out_ref[span, :] = own
+        own = heat_ref[pl.ds(r, level_count, stride=ROWS), :]
         sum_ref[rows, :lanes] = change_ref[rows, :lanes] + TIME_INCREMENT * own
         for k in range(level_count // 8):
             side = sides[8 * r : 8 * (r + 1), lanes * k : lanes * (k + 1)]
@@ -727,9 +714,7 @@
 
     slopes = slope_matrices(lanes)
     average = average_matrix(lanes)
-    (
-        heat, returned, after, before, after_more, before_more, fields_after, fields_before
-    ) = radiation(
+    heat, after, before, fields_after, fields_before = radiation(
         atmospheric_constituents, thermal_ratio, flow_velocity, solar_elevation_factor,
         ground_reflectivity, sunlit_indicator, molecular_optics_lookup, condensate_optics_lookup,
     )
@@ -739,9 +724,9 @@
         (wide, jax.ShapeDtypeStruct((2, size, 2 * lanes), jnp.float32)), 2,
         temper, flow, fields_after, fields_before, back, *slopes,
     )
-    wave, first, last, heat = call(
-        first_stage_kernel, "first_stage", (wide, line, line, field), 1,
-        change, heat, returned, after, before, after_more, before_more, back, average,
+    wave, first, last = call(
+        first_stage_kernel, "first_stage", (wide, line, line), 1,
+        change, heat, after, before, back, average,
     )
     below, above = shifted(last, "gy", 1), shifted(first, "gy", -1)
     wave, first, last, total = call(

time: 106 us -> 104 us (0.981)
  starting transfers between devices: 20.9 us -> 17.1 us
    ppermute x14 -> x12, starting transfers between devices: 20.9 us -> 17.1 us  [shifted(): lax.ppermute(value, axis, [(i, (i + steps) % count) for i in range(count)])]
    pallas_call x2 -> x3, Pallas kernels: 31.7 us -> 32.7 us  [the longest x1 19.5 us: radiation(): pl.pallas_call(shared_kernel, out_shape=(field(shared), field(shared)), g...]
    ppermute x14 -> x12, waiting for transfers between devices: 14.8 us -> 14.8 us  [shifted(): lax.ppermute(value, axis, [(i, (i + steps) % count) for i in range(count)])]
  transfers between devices with their start and end apart: 14 -> 12, of which waited for: 8 -> 8; matrix products, arithmetic and copies ran while one was open for 0% -> 0% of each run, Pallas kernels for 39% -> 39%
where the time goes in v8:
time: 104 us; the launch traced here: 103 us
  Pallas kernels  69.4 us (67%)
  starting transfers between devices  17.1 us (16%)
  waiting for transfers between devices  14.8 us (14%)
  local copies, waits for them, and re-layouts  1.39 us (1%)
    pallas_call x1, Pallas kernels, radiation(): pl.pallas_call(functools.partial(home_kernel, 0), out_shape=(field(early)...  28.8 us
    pallas_call x1, Pallas kernels, radiation(): pl.pallas_call(shared_kernel, out_shape=(field(shared), field(shared)), g...  19.5 us
    ppermute x12, starting transfers between devices, shifted(): lax.ppermute(value, axis, [(i, (i + steps) % count) for i in range(count)])  17.1 us
    ppermute x12, waiting for transfers between devices, shifted(): lax.ppermute(value, axis, [(i, (i + steps) % count) for i in range(count)])  14.8 us
    pallas_call x1, Pallas kernels, radiation(): pl.pallas_call(last_home_kernel, out_shape=field(1), grid=(1,), in_specs=...  11 us
    pallas_call x5, Pallas kernels, call(): pl.pallas_call(kernel, out_shape=outs, in_specs=[whole] * len(values), ou...  4 us
    pallas_call x1, Pallas kernels, radiation(): pl.pallas_call(pack_kernel, out_shape=(state_rows(shared), state_rows(sha...  3.89 us
    pallas_call x1, Pallas kernels, radiation(): pl.pallas_call(join_kernel, out_shape=(field(rows), edge, edge), in_specs...  2.16 us
  transfers between devices with their start and end apart: 12, of which 8 were waited for; matrix products, arithmetic and copies ran while one was open for 0% of the time, Pallas kernels for 39%

profile of v8, /device:TPU:1, one launch (start us, length us, event | category | flops | bytes accessed | tf_op | source)
XLA Modules:
  0.0 103.5 jit_solution(14214188021162249422)
XLA Ops:
  0.6 3.9 %pack.1 = (f32[362,2,128]{2,1,0:T(2,128)}, f32[362,2,128]{2,1,0:T(2,128)}, f32[362,1,128]{2,1,0:T(1,128)}, f32[192,128]{1,0:T(8,128)}, f32[192,128]{1,0:T(8,128)}) custom-call(f32[5,72,8,128]{3,2,1,0:T(8,128)} %state_ref.3, f32[576,128]{1,0:T(8,128)} %bitcast.5, f32[2,576,128]{2,1,0:T(8,128)} %bitcast.9, f32[8,128]{1,0:T(8,128)} %cosine_ref.3, ...), custom_call_target="tpu_custom_call" | custom-call | tf_op jit(solution)/shard_map/pack/pallas_call | solution.py:479
  4.5 5.1 %collective-permute-start.1 = (f32[192,128]{1,0:T(8,128)}, f32[192,128]{1,0:T(8,128)S(1)}, u32[]{:S(2)}, u32[]{:S(2)}) collective-permute-start(f32[192,128]{1,0:T(8,128)} %get-tuple-element.37), channel_id=1, source_target_pairs={{0,28},{4,0},{8,4},{12,8},{16,12},{20,16},{24,20},{28,24},{1,29},{... | collective-permute-start | bytes 294920 | tf_op jit(solution)/shard_map/ppermute | solution.py:26
  9.6 0.0 collective-permute-start.2
  9.6 0.0 collective-permute-start
  9.6 28.8 %home_radiation.1 = (f32[216,128]{1,0:T(8,128)}, bf16[9,2,224,128]{3,2,1,0:T(8,128)(2,1)}, f32[112,128]{1,0:T(8,128)}) custom-call(f32[5,72,8,128]{3,2,1,0:T(8,128)} %state_ref.3, f32[576,128]{1,0:T(8,128)} %bitcast.6, f32[8,128]{1,0:T(8,128)} %cosine_ref.3, f32[8,128]{1,0:T(8,128)} %ground_ref.3, s32[8,128]{1,0:T(8,128)} %day_ref.5, ...), custom_call_target="tpu_custom_call" | custom-call | flops 30965760000 | bytes 2359296 | tf_op jit(solution)/shard_map/home_radiation/pallas_call | solution.py:495
  38.4 0.0 collective-permute-done.1.after_ref
  38.4 0.0 collective-permute-done.2.before_ref
  38.4 0.0 collective-permute-done.received_ref
  38.4 0.0 copy-start.8
  38.5 0.7 copy-done.8
  39.2 19.5 %shared_radiation.1 = (f32[144,128]{1,0:T(8,128)}, f32[144,128]{1,0:T(8,128)}) custom-call(f32[362,2,128]{2,1,0:T(2,128)} %get-tuple-element.35.kept_ref, f32[362,2,128]{2,1,0:T(2,128)} %copy-done.8, s32[8,128]{1,0:T(8,128)} %day_ref.5, bf16[9,2,224,128]{3,2,1,0:T(8,128)(2,1)} %get-tuple-element.33.optics_ref, f32[112,128]{1,0:T(8,128)} %get-tuple-element.34.weight_ref), custom_call_target="tpu_custom_call" | custom-call | flops 20643840000 | bytes 2359296 | tf_op jit(solution)/shard_map/shared_radiation/pallas_call | solution.py:507
  58.7 2.4 %collective-permute-start.3 = (f32[144,128]{1,0:T(8,128)}, f32[144,128]{1,0:T(8,128)S(1)}, u32[]{:S(2)}, u32[]{:S(2)}) collective-permute-start(f32[144,128]{1,0:T(8,128)} %get-tuple-element.41), channel_id=1, source_target_pairs={{0,16},{4,20},{8,24},{12,28},{16,0},{20,4},{24,8},{28,12},{1,17},{... | collective-permute-start | bytes 221192 | tf_op jit(solution)/shard_map/ppermute | solution.py:26
  61.1 0.0 copy-start
  61.1 0.0 copy-start.1
  61.1 0.0 copy-start.2
  61.1 0.0 copy-start.4
  61.1 0.0 copy-start.5
  61.1 11.0 %last_home_radiation.1.line_ref = f32[72,128]{1,0:T(8,128)} custom-call(f32[362,1,128]{2,1,0:T(1,128)} %get-tuple-element.32.line_ref, s32[8,128]{1,0:T(8,128)} %day_ref.5, bf16[9,2,224,128]{3,2,1,0:T(8,128)(2,1)} %get-tuple-element.33.optics_ref, f32[112,128]{1,0:T(8,128)} %get-tuple-element.34.weight_ref), custom_call_target="tpu_custom_call" | custom-call | flops 10321920000 | bytes 2359296 | tf_op jit(solution)/shard_map/last_home_radiation/pallas_call | solution.py:515
  72.1 0.0 copy-start.3
  72.1 0.0 collective-permute-done.3.returned_ref
  72.1 0.0 copy-start.7
  72.1 0.6 copy-done.7
  72.7 2.2 %join.1 = (f32[576,128]{1,0:T(8,128)}, f32[64,128]{1,0:T(8,128)}, f32[64,128]{1,0:T(8,128)}) custom-call(f32[216,128]{1,0:T(8,128)} %get-tuple-element.31.home_ref, f32[72,128]{1,0:T(8,128)} %last_home_radiation.1.line_ref, f32[144,128]{1,0:T(8,128)} %get-tuple-element.40.mine_ref, f32[144,128]{1,0:T(8,128)} %copy-done.7, ...), custom_call_target="tpu_custom_call" | custom-call | tf_op jit(solution)/shard_map/join/pallas_call | solution.py:521
  74.9 0.0 copy-start.6
  74.9 4.2 %collective-permute-start.4 = (f32[64,128]{1,0:T(8,128)}, f32[64,128]{1,0:T(8,128)S(1)}, u32[]{:S(2)}, u32[]{:S(2)}) collective-permute-start(f32[64,128]{1,0:T(8,128)} %get-tuple-element.46), channel_id=1, source_target_pairs={{0,28},{4,0},{8,4},{12,8},{16,12},{20,16},{24,20},{28,24},{1,29},{... | collective-permute-start | bytes 98312 | tf_op jit(solution)/shard_map/ppermute | solution.py:26
  79.1 0.0 collective-permute-start.5
  79.1 0.0 copy-done
  79.1 0.0 copy-done.1
  79.1 0.0 copy-done.2
  79.1 0.0 copy-done.4
  79.1 0.0 copy-done.5
  79.1 0.8 own_change.1
  79.9 0.5 collective-permute-done.4.after_ref
  80.4 4.3 %collective-permute-done.5.before_ref = f32[64,128]{1,0:T(8,128)S(1)} collective-permute-done((f32[64,128]{1,0:T(8,128)}, f32[64,128]{1,0:T(8,128)S(1)}, u32[]{:S(2)}, u32[]{:S(2)}) %collective-permute-start.5) | collective-permute-done | bytes 32800 | tf_op jit(solution)/shard_map/ppermute | solution.py:26
  84.7 0.0 copy-done.3
  84.7 0.0 copy-done.6
  84.7 0.6 first_stage.1
  85.3 4.4 %collective-permute-start.6 = (f32[72,256]{1,0:T(8,128)S(1)}, f32[72,256]{1,0:T(8,128)S(1)}, u32[]{:S(2)}, u32[]{:S(2)}) collective-permute-start(f32[72,256]{1,0:T(8,128)S(1)} %get-tuple-element.49), channel_id=1, source_target_pairs={{0,1},{1,2},{2,3},{3,0},{4,5},{5,6},{6,7},{7,4},{8,9},{9,10},{10,1... | collective-permute-start | bytes 221192 | tf_op jit(solution)/shard_map/ppermute | solution.py:26
  89.7 0.0 collective-permute-start.7
  89.7 1.4 %collective-permute-done.6.below_ref = f32[72,256]{1,0:T(8,128)S(1)} collective-permute-done((f32[72,256]{1,0:T(8,128)S(1)}, f32[72,256]{1,0:T(8,128)S(1)}, u32[]{:S(2)}, u32[]{:S(2)}) %collective-permute-start.6) | collective-permute-done | bytes 73760 | tf_op jit(solution)/shard_map/ppermute | solution.py:26
  91.1 2.4 %collective-permute-done.7.above_ref = f32[72,256]{1,0:T(8,128)S(1)} collective-permute-done((f32[72,256]{1,0:T(8,128)S(1)}, f32[72,256]{1,0:T(8,128)S(1)}, u32[]{:S(2)}, u32[]{:S(2)}) %collective-permute-start.7) | collective-permute-done | bytes 73760 | tf_op jit(solution)/shard_map/ppermute | solution.py:26
  93.5 0.9 second_stage.1
  94.4 0.1 collective-permute-start.8
  94.4 0.5 collective-permute-start.9
  94.9 0.9 collective-permute-done.8.below_ref
  95.8 2.4 %collective-permute-done.9.above_ref = f32[72,256]{1,0:T(8,128)S(1)} collective-permute-done((f32[72,256]{1,0:T(8,128)S(1)}, f32[72,256]{1,0:T(8,128)S(1)}, u32[]{:S(2)}, u32[]{:S(2)}) %collective-permute-start.9) | collective-permute-done | bytes 73760 | tf_op jit(solution)/shard_map/ppermute | solution.py:26
  98.3 0.9 third_stage.1
  99.2 0.1 collective-permute-start.10
  99.2 0.5 collective-permute-start.11
  99.7 0.7 collective-permute-done.10.below_ref
  100.4 2.2 %collective-permute-done.11.above_ref = f32[72,128]{1,0:T(8,128)S(1)} collective-permute-done((f32[72,128]{1,0:T(8,128)S(1)}, f32[72,128]{1,0:T(8,128)S(1)}, u32[]{:S(2)}, u32[]{:S(2)}) %collective-permute-start.11) | collective-permute-done | bytes 36896 | tf_op jit(solution)/shard_map/ppermute | solution.py:26
  102.7 0.8 last_stage.1
Async XLA Ops:
  4.5 33.9 %collective-permute-start.1 = (f32[192,128]{1,0:T(8,128)}, f32[192,128]{1,0:T(8,128)S(1)}, u32[]{:S(2)}, u32[]{:S(2)}) collective-permute-start(f32[192,128]{1,0:T(8,128)} %get-tuple-element.37), channel_id=1, source_target_pairs={{0,28},{4,0},{8,4},{12,8},{16,12},{20,16},{24,20},{28,24},{1,29},{... | collective-permute-start | bytes 294920 | tf_op jit(solution)/shard_map/ppermute | solution.py:26
  9.6 28.8 %collective-permute-start.2 = (f32[192,128]{1,0:T(8,128)}, f32[192,128]{1,0:T(8,128)S(1)}, u32[]{:S(2)}, u32[]{:S(2)}) collective-permute-start(f32[192,128]{1,0:T(8,128)} %get-tuple-element.38), channel_id=1, source_target_pairs={{0,4},{4,8},{8,12},{12,16},{16,20},{20,24},{24,28},{28,0},{1,5},{5... | collective-permute-start | bytes 294920 | tf_op jit(solution)/shard_map/ppermute | solution.py:26
  9.6 28.8 %collective-permute-start = (f32[362,2,128]{2,1,0:T(2,128)}, f32[362,2,128]{2,1,0:T(2,128)S(1)}, u32[]{:S(2)}, u32[]{:S(2)}) collective-permute-start(f32[362,2,128]{2,1,0:T(2,128)} %get-tuple-element.36), channel_id=1, source_target_pairs={{0,16},{4,20},{8,24},{12,28},{16,0},{20,4},{24,8},{28,12},{1,17},{... | collective-permute-start | bytes 1112072 | tf_op jit(solution)/shard_map/ppermute | solution.py:26
  38.4 0.7 copy-start.8
  58.7 13.4 %collective-permute-start.3 = (f32[144,128]{1,0:T(8,128)}, f32[144,128]{1,0:T(8,128)S(1)}, u32[]{:S(2)}, u32[]{:S(2)}) collective-permute-start(f32[144,128]{1,0:T(8,128)} %get-tuple-element.41), channel_id=1, source_target_pairs={{0,16},{4,20},{8,24},{12,28},{16,0},{20,4},{24,8},{28,12},{1,17},{... | collective-permute-start | bytes 221192 | tf_op jit(solution)/shard_map/ppermute | solution.py:26
  61.1 18.0 %copy-start = (f32[72,8,128]{2,1,0:T(8,128)S(1)}, f32[72,8,128]{2,1,0:T(8,128)}, u32[]{:S(2)}) copy-start(f32[72,8,128]{2,1,0:T(8,128)} %param.14) | copy-start | bytes 884740
  61.1 18.0 %copy-start.1 = (bf16[256,1152]{1,0:T(8,128)(2,1)S(1)}, bf16[256,1152]{1,0:T(8,128)(2,1)}, u32[]{:S(2)}) copy-start(bf16[256,1152]{1,0:T(8,128)(2,1)} %constant.12.edge_ref) | copy-start | bytes 1769476
  61.1 18.0 %copy-start.2 = (f32[2,72,8,128]{3,2,1,0:T(8,128)S(1)}, f32[2,72,8,128]{3,2,1,0:T(8,128)}, u32[]{:S(2)}) copy-start(f32[2,72,8,128]{3,2,1,0:T(8,128)} %param.15) | copy-start | bytes 1769476
  61.1 18.0 %copy-start.4 = (bf16[256,256]{1,0:T(8,128)(2,1)S(1)}, bf16[256,256]{1,0:T(8,128)(2,1)}, u32[]{:S(2)}) copy-start(bf16[256,256]{1,0:T(8,128)(2,1)} %constant.9.clone.low_ref) | copy-start | bytes 393220
  61.1 18.0 %copy-start.5 = (bf16[256,256]{1,0:T(8,128)(2,1)S(1)}, bf16[256,256]{1,0:T(8,128)(2,1)}, u32[]{:S(2)}) copy-start(bf16[256,256]{1,0:T(8,128)(2,1)} %constant.8.clone.high_ref) | copy-start | bytes 393220
  72.1 12.6 %copy-start.3 = (bf16[256,256]{1,0:T(8,128)(2,1)S(1)}, bf16[256,256]{1,0:T(8,128)(2,1)}, u32[]{:S(2)}) copy-start(bf16[256,256]{1,0:T(8,128)(2,1)} %constant.10.clone.average_ref) | copy-start | bytes 393220
  72.1 0.6 copy-start.7
  74.9 9.8 %copy-start.6 = (f32[576,128]{1,0:T(8,128)S(1)}, f32[576,128]{1,0:T(8,128)}, u32[]{:S(2)}) copy-start(f32[576,128]{1,0:T(8,128)} %get-tuple-element.42.heat_ref) | copy-start | bytes 884740
  74.9 5.5 %collective-permute-start.4 = (f32[64,128]{1,0:T(8,128)}, f32[64,128]{1,0:T(8,128)S(1)}, u32[]{:S(2)}, u32[]{:S(2)}) collective-permute-start(f32[64,128]{1,0:T(8,128)} %get-tuple-element.46), channel_id=1, source_target_pairs={{0,28},{4,0},{8,4},{12,8},{16,12},{20,16},{24,20},{28,24},{1,29},{... | collective-permute-start | bytes 98312 | tf_op jit(solution)/shard_map/ppermute | solution.py:26
  79.1 5.7 %collective-permute-start.5 = (f32[64,128]{1,0:T(8,128)}, f32[64,128]{1,0:T(8,128)S(1)}, u32[]{:S(2)}, u32[]{:S(2)}) collective-permute-start(f32[64,128]{1,0:T(8,128)} %get-tuple-element.47), channel_id=1, source_target_pairs={{0,4},{4,8},{8,12},{12,16},{16,20},{20,24},{24,28},{28,0},{1,5},{5... | collective-permute-start | bytes 98312 | tf_op jit(solution)/shard_map/ppermute | solution.py:26
  85.3 5.8 %collective-permute-start.6 = (f32[72,256]{1,0:T(8,128)S(1)}, f32[72,256]{1,0:T(8,128)S(1)}, u32[]{:S(2)}, u32[]{:S(2)}) collective-permute-start(f32[72,256]{1,0:T(8,128)S(1)} %get-tuple-element.49), channel_id=1, source_target_pairs={{0,1},{1,2},{2,3},{3,0},{4,5},{5,6},{6,7},{7,4},{8,9},{9,10},{10,1... | collective-permute-start | bytes 221192 | tf_op jit(solution)/shard_map/ppermute | solution.py:26
  89.7 3.8 %collective-permute-start.7 = (f32[72,256]{1,0:T(8,128)S(1)}, f32[72,256]{1,0:T(8,128)S(1)}, u32[]{:S(2)}, u32[]{:S(2)}) collective-permute-start(f32[72,256]{1,0:T(8,128)S(1)} %get-tuple-element.50), channel_id=1, source_target_pairs={{0,3},{1,0},{2,1},{3,2},{4,7},{5,4},{6,5},{7,6},{8,11},{9,8},{10,9... | collective-permute-start | bytes 221192 | tf_op jit(solution)/shard_map/ppermute | solution.py:26
  94.4 1.5 %collective-permute-start.8 = (f32[72,256]{1,0:T(8,128)S(1)}, f32[72,256]{1,0:T(8,128)S(1)}, u32[]{:S(2)}, u32[]{:S(2)}) collective-permute-start(f32[72,256]{1,0:T(8,128)S(1)} %get-tuple-element.53), channel_id=1, source_target_pairs={{0,1},{1,2},{2,3},{3,0},{4,5},{5,6},{6,7},{7,4},{8,9},{9,10},{10,1... | collective-permute-start | bytes 221192 | tf_op jit(solution)/shard_map/ppermute | solution.py:26
  94.4 3.8 %collective-permute-start.9 = (f32[72,256]{1,0:T(8,128)S(1)}, f32[72,256]{1,0:T(8,128)S(1)}, u32[]{:S(2)}, u32[]{:S(2)}) collective-permute-start(f32[72,256]{1,0:T(8,128)S(1)} %get-tuple-element.54), channel_id=1, source_target_pairs={{0,3},{1,0},{2,1},{3,2},{4,7},{5,4},{6,5},{7,6},{8,11},{9,8},{10,9... | collective-permute-start | bytes 221192 | tf_op jit(solution)/shard_map/ppermute | solution.py:26
  99.2 1.3 %collective-permute-start.10 = (f32[72,128]{1,0:T(8,128)S(1)}, f32[72,128]{1,0:T(8,128)S(1)}, u32[]{:S(2)}, u32[]{:S(2)}) collective-permute-start(f32[72,128]{1,0:T(8,128)S(1)} %get-tuple-element.57), channel_id=1, source_target_pairs={{0,1},{1,2},{2,3},{3,0},{4,5},{5,6},{6,7},{7,4},{8,9},{9,10},{10,1... | collective-permute-start | bytes 110600 | tf_op jit(solution)/shard_map/ppermute | solution.py:26
  99.2 3.4 %collective-permute-start.11 = (f32[72,128]{1,0:T(8,128)S(1)}, f32[72,128]{1,0:T(8,128)S(1)}, u32[]{:S(2)}, u32[]{:S(2)}) collective-permute-start(f32[72,128]{1,0:T(8,128)S(1)} %get-tuple-element.58), channel_id=1, source_target_pairs={{0,3},{1,0},{2,1},{3,2},{4,7},{5,4},{6,5},{7,6},{8,11},{9,8},{10,9... | collective-permute-start | bytes 110600 | tf_op jit(solution)/shard_map/ppermute | solution.py:26

commit v9 on v8

--- a/solution.py
+++ b/solution.py
@@ -256,9 +256,10 @@
     lax.fori_loop(0, level_count, step, flux(0), unroll=4)
 
 
-def home_kernel(
-    first, state_ref, temp_ref, cosine_ref, ground_ref, day_ref, molecular_ref, table_ref,
-    heat_ref, optics_ref, weight_ref, terms_ref, right_ref, *scratch,
+def radiation_kernel(
+    state_ref, temp_ref, flow_ref, cosine_ref, ground_ref, day_ref, molecular_ref, table_ref,
+    edge_ref,
+    heat_ref, first_ref, last_ref, optics_ref, weight_ref, strip_ref, terms_ref, right_ref, *scratch,
 ):
     level_count, lines, lanes = state_ref.shape[1:]
     gpoints = weight_ref.shape[0]
@@ -267,25 +268,28 @@
     @pl.when(row == 0)
     def prepare():
         optics_matrices(molecular_ref, table_ref, optics_ref, weight_ref)
-        heat_ref[...] = jnp.zeros_like(heat_ref)
         prepare_terms(state_ref, temp_ref, terms_ref, right_ref)
 
-    line = first + row
     sweep_row(
-        row, line, lines, count, cosine_ref[pl.ds(line, 1), :], ground_ref[pl.ds(line, 1), :],
+        row, row, lines, count, cosine_ref[pl.ds(row, 1), :], ground_ref[pl.ds(row, 1), :],
         optics_ref, weight_ref, terms_ref, right_ref, *scratch,
     )
 
     @pl.when(row == count - 1)
     def finish():
-        size = heat_ref.shape[0] // level_count
-        rows = slice(first, first + size)
-        day = day_ref[rows, :] == 1
+        day = day_ref[...] == 1
 
         def write(level, value):
-            heat_ref[pl.ds(level * size, size), :] = jnp.where(day, value, 0.0)
-
-        level_heating(scratch[PARTIAL], level_count, gpoints, size, write)
+            start = pl.multiple_of(level * lines, 8)
+            heat_ref[pl.ds(start, lines), :] = jnp.where(day, value, 0.0)
+
+        level_heating(scratch[PARTIAL], level_count, gpoints, lines, write)
+        for n, ref in enumerate((heat_ref, temp_ref, flow_ref.at[0], flow_ref.at[1])):
+            for r in range(lines):
+                write_strip(ref, r, lines, strip_ref, 8 * (lines * n + r))
+        packed = split_dot(strip_ref[...], edge_ref[...])
+        first_ref[...] = packed[:, :lanes]
+        last_ref[...] = packed[:, lanes:]
 
 
 def prepare_terms(state_ref, temp_ref, terms_ref, right_ref):
@@ -297,86 +301,6 @@
         return carry
 
     lax.fori_loop(0, level_count, level, 0, unroll=4)
-
-
-def shared_places(lines):
-    low = lax.axis_index("gx") < lax.axis_size("gx") // 2
-    early, late = lines // 2, lines // 2 + lines // 4
-    return jnp.where(low, early, late), jnp.where(low, late, early)
-
-
-def pack_kernel(
-    state_ref, temp_ref, flow_ref, cosine_ref, ground_ref, edge_ref,
-    sent_ref, kept_ref, line_ref, first_ref, last_ref, own_ref, strip_ref,
-):
-    level_count, lines, lanes = state_ref.shape[1:]
-
-    def level(l, carry):
-        for k, value in enumerate(layer_terms(state_ref, temp_ref, l)):
-            own_ref[pl.ds(pl.multiple_of((5 * l + k) * lines, 8), lines), :] = value
-        return carry
-
-    lax.fori_loop(0, level_count, level, 0, unroll=4)
-    mine, theirs = shared_places(lines)
-    copies = ((kept_ref, mine), (sent_ref, theirs), (line_ref, lines // 2 - 1))
-
-    def copy(n, carry):
-        for ref, place in copies:
-            ref[n] = own_ref[pl.ds(n * lines + place, ref.shape[1]), :]
-        return carry
-
-    lax.fori_loop(0, 5 * level_count, copy, 0, unroll=8)
-    for ref, place in copies:
-        ref[5 * level_count] = cosine_ref[pl.ds(place, ref.shape[1]), :]
-        ref[5 * level_count + 1] = ground_ref[pl.ds(place, ref.shape[1]), :]
-    for n, ref in enumerate((temp_ref, flow_ref.at[0], flow_ref.at[1])):
-        for r in range(lines):
-            write_strip(ref, r, lines, strip_ref, 8 * (lines * n + r))
-    packed = split_dot(strip_ref[...], edge_ref[...])
-    first_ref[...] = packed[:, :lanes]
-    last_ref[...] = packed[:, lanes:]
-
-
-def shared_kernel(
-    kept_ref, received_ref, day_ref, optics_ref, weight_ref,
-    mine_ref, theirs_ref, surface_ref, terms_ref, right_ref, *scratch,
-):
-    level_count = kept_ref.shape[0] // 5
-    shared, lanes = kept_ref.shape[1:]
-    gpoints = weight_ref.shape[0]
-    row, count = pl.program_id(0), pl.num_programs(0)
-    first = shared_places(day_ref.shape[0])[0]
-    day = day_ref[pl.ds(first, shared), :] == 1
-
-    @pl.when(row == 0)
-    def prepare():
-        right_ref[...] = jnp.zeros_like(right_ref)
-
-        def level(l, carry):
-            values = [
-                jnp.where(day, kept_ref[5 * l + k], received_ref[5 * l + k]) for k in range(5)
-            ]
-            write_terms(terms_ref, l, values, shared)
-            return carry
-
-        lax.fori_loop(0, level_count, level, 0, unroll=4)
-        for n in range(2):
-            place = 5 * level_count + n
-            surface_ref[n, :shared, :] = jnp.where(day, kept_ref[place], received_ref[place])
-
-    sweep_row(
-        row, row, shared, count, surface_ref[0, pl.ds(row, 1), :],
-        surface_ref[1, pl.ds(row, 1), :], optics_ref, weight_ref, terms_ref, right_ref, *scratch,
-    )
-
-    @pl.when(row == count - 1)
-    def finish():
-        def write(level, value):
-            span = pl.ds(level * shared, shared)
-            mine_ref[span, :] = jnp.where(day, value, 0.0)
-            theirs_ref[span, :] = jnp.where(day, 0.0, value)
-
-        level_heating(scratch[PARTIAL], level_count, gpoints, shared, write)
 
 
 def write_strip(source_ref, r, lines, strip_ref, start):
@@ -387,144 +311,40 @@
         ]
 
 
-def last_home_kernel(
-    line_ref, day_ref, optics_ref, weight_ref, heat_ref, terms_ref, right_ref, *scratch,
-):
-    level_count = line_ref.shape[0] // 5
-    row = pl.program_id(0)
-    right_ref[...] = jnp.zeros_like(right_ref)
-
-    def level(l, carry):
-        write_terms(terms_ref, l, [line_ref[5 * l + k] for k in range(5)], 1)
-        return carry
-
-    lax.fori_loop(0, level_count, level, 0, unroll=4)
-    sweep_row(
-        row, 0, 1, 1, line_ref[5 * level_count], line_ref[5 * level_count + 1],
-        optics_ref, weight_ref, terms_ref, right_ref, *scratch,
-    )
-    line = day_ref.shape[0] // 2 - 1
-    day = day_ref[line : line + 1, :] == 1
-
-    def write(level, value):
-        heat_ref[pl.ds(level, 1), :] = jnp.where(day, value, 0.0)
-
-    level_heating(scratch[PARTIAL], level_count, weight_ref.shape[0], 1, write)
-
-
-def join_kernel(
-    home_ref, line_ref, mine_ref, returned_ref, edge_ref, heat_ref, first_ref, last_ref, strip_ref
-):
-    level_count, lanes = line_ref.shape
-    lines = heat_ref.shape[0] // level_count
-    home, shared = lines // 2, lines // 4
-    place = shared_places(lines)[0]
-    for r in range(lines):
-        if r < home - 1:
-            row = home_ref[pl.ds(r, level_count, stride=home - 1), :]
-        elif r == home - 1:
-            row = line_ref[...]
-        else:
-            n = (r - home) % shared
-            span = pl.ds(n, level_count, stride=shared)
-            row = jnp.where(place == r - n, mine_ref[span, :], returned_ref[span, :])
-        heat_ref[pl.ds(r, level_count, stride=lines), :] = row
-        for k in range(level_count // 8):
-            strip_ref[8 * r : 8 * (r + 1), lanes * k : lanes * (k + 1)] = row[8 * k : 8 * (k + 1)]
-    packed = split_dot(strip_ref[...], edge_ref[...])
-    first_ref[...] = packed[:, :lanes]
-    last_ref[...] = packed[:, lanes:]
-
-
 def radiation(state, temper, flow, cosine, ground, day, molecular, condensate):
-    level_count, rows, lanes = temper.shape
+    level_count, rows, lanes = state.shape[1:]
     gpoints = molecular.shape[1]
-    home, shared = rows // 2, rows // 4
-    partner = lax.axis_size("gx") // 2
-    temper = temper.reshape(level_count * rows, lanes)
-    flow = flow.reshape(2, level_count * rows, lanes)
     full = pltpu.VMEM((level_count, gpoints, lanes), jnp.float32)
     plane = pltpu.VMEM((gpoints, lanes), jnp.float32)
     whole = pl.BlockSpec(memory_space=pltpu.VMEM)
-    params = pltpu.CompilerParams(vmem_limit_bytes=60 * 1024 * 1024)
     part = (QUANTITIES * gpoints // CHUNKS, GROUP * TERMS)
-    strip = pltpu.VMEM((8 * rows, level_count // 8 * lanes), jnp.float32)
-
-    def field(lines):
-        return jax.ShapeDtypeStruct((level_count * lines, lanes), jnp.float32)
-
-    def scratch(lines, count):
-        return [
-            pltpu.VMEM((level_count * TERMS * lines, lanes), jnp.float32),
+    depths = pltpu.VMEM((BLOCK // 2, part[0], 2 * lanes), jnp.float32)
+    edge = jax.ShapeDtypeStruct((4 * 8 * rows, lanes), jnp.float32)
+    cells = level_count * gpoints * rows * lanes
+    return pl.pallas_call(
+        radiation_kernel,
+        out_shape=(jax.ShapeDtypeStruct((level_count * rows, lanes), jnp.float32), edge, edge),
+        grid=(rows,), in_specs=[whole] * 9, out_specs=(whole,) * 3,
+        scratch_shapes=[
+            pltpu.VMEM((level_count // GROUP, CHUNKS) + part, jnp.bfloat16),
+            plane,
+            pltpu.VMEM((4 * 8 * rows, level_count // 8 * lanes), jnp.float32),
+            pltpu.VMEM((level_count * TERMS * rows, lanes), jnp.float32),
             pltpu.VMEM((level_count // 2, GROUP * TERMS, 2 * lanes), jnp.bfloat16),
-            pltpu.VMEM((BLOCK // 2, part[0], 2 * lanes), jnp.float32),
-            pltpu.VMEM((BLOCK // 2, part[0], 2 * lanes), jnp.float32),
-            full, full, full,
-            pltpu.VMEM(((level_count + 1) * count * 8, lanes), jnp.float32),
+            depths, depths, full, full, full,
+            pltpu.VMEM(((level_count + 1) * rows * 8, lanes), jnp.float32),
             plane, plane,
             pltpu.VMEM((8, lanes), jnp.float32),
-        ]
-
-    def cost(count):
-        cells = level_count * gpoints * count * lanes
-        return pl.CostEstimate(
-            flops=10000 * cells, bytes_accessed=32 * temper.size, transcendentals=5 * cells
-        )
-
-    def state_rows(count):
-        return jax.ShapeDtypeStruct((5 * level_count + 2, count, lanes), jnp.float32)
-
-    edges = edge_matrix(level_count, lanes)
-    three = jax.ShapeDtypeStruct((3 * 8 * rows, lanes), jnp.float32)
-    sent, kept, line, fields_first, fields_last = pl.pallas_call(
-        pack_kernel,
-        out_shape=(state_rows(shared), state_rows(shared), state_rows(1), three, three),
-        in_specs=[whole] * 6, out_specs=(whole,) * 5,
-        scratch_shapes=[
-            pltpu.VMEM((5 * level_count * rows, lanes), jnp.float32),
-            pltpu.VMEM((3 * 8 * rows, level_count // 8 * lanes), jnp.float32),
         ],
-        compiler_params=params, name="pack",
-    )(state, temper, flow, cosine, ground, edges)
-    received = shifted(sent, "gx", partner)
-    fields_after, fields_before = shifted(fields_first, "gx", -1), shifted(fields_last, "gx", 1)
-    received, fields_after, fields_before = lax.optimization_barrier(
-        (received, fields_after, fields_before)
-    )
-    early = home - 1
-    home_heat, optics, weight = pl.pallas_call(
-        functools.partial(home_kernel, 0),
-        out_shape=(
-            field(early),
-            jax.ShapeDtypeStruct((level_count // GROUP, CHUNKS) + part, jnp.bfloat16),
-            jax.ShapeDtypeStruct((gpoints, lanes), jnp.float32),
+        compiler_params=pltpu.CompilerParams(vmem_limit_bytes=60 * 1024 * 1024),
+        cost_estimate=pl.CostEstimate(
+            flops=10000 * cells, bytes_accessed=4 * 9 * temper.size, transcendentals=5 * cells
         ),
-        grid=(early,), in_specs=[whole] * 7, out_specs=(whole,) * 3,
-        scratch_shapes=scratch(rows, early), compiler_params=params, cost_estimate=cost(early),
-        name="home_radiation",
-    )(state, temper, cosine, ground, day, molecular.transpose(0, 2, 1), condensate)
-    edge = jax.ShapeDtypeStruct((8 * rows, lanes), jnp.float32)
-    mine, theirs = pl.pallas_call(
-        shared_kernel,
-        out_shape=(field(shared), field(shared)),
-        grid=(shared,), in_specs=[whole] * 5, out_specs=(whole,) * 2,
-        scratch_shapes=[pltpu.VMEM((2, 8, lanes), jnp.float32)] + scratch(shared, shared),
-        compiler_params=params, cost_estimate=cost(shared), name="shared_radiation",
-    )(kept, received, day, optics, weight)
-    returned = shifted(theirs, "gx", partner)
-    line_heat = pl.pallas_call(
-        last_home_kernel,
-        out_shape=field(1),
-        grid=(1,), in_specs=[whole] * 4, out_specs=whole, scratch_shapes=scratch(1, 1),
-        compiler_params=params, cost_estimate=cost(1), name="last_home_radiation",
-    )(line, day, optics, weight)
-    heat, first, last = pl.pallas_call(
-        join_kernel, out_shape=(field(rows), edge, edge),
-        in_specs=[whole] * 5, out_specs=(whole,) * 3, scratch_shapes=[strip],
-        compiler_params=params, name="join",
-    )(home_heat, line_heat, mine, returned, edges)
-    after, before = shifted(first, "gx", -1), shifted(last, "gx", 1)
-    return heat, after, before, fields_after, fields_before
+        name="radiation",
+    )(
+        state, temper, flow, cosine, ground, day, molecular.transpose(0, 2, 1), condensate,
+        edge_matrix(level_count, lanes),
+    )
 
 
 def edge_matrix(level_count, lanes):
@@ -588,20 +408,17 @@
     return result
 
 
-def unpacked(after_ref, before_ref, edge_ref):
+def first_stage_kernel(
+    temp_ref, flow_ref, heat_ref, after_ref, before_ref, edge_ref, high_ref, low_ref, average_ref,
+    out_ref, first_ref, last_ref, wind_ref, temp_wide_ref, heat_wide_ref, slope_ref,
+):
+    level_count = first_ref.shape[0]
+    lanes = temp_ref.shape[-1]
     both = jnp.concatenate([after_ref[...], before_ref[...]], axis=1)
-    return split_dot(both, edge_ref[...])
-
-
-def own_change_kernel(
-    temp_ref, flow_ref, after_ref, before_ref, edge_ref, high_ref, low_ref,
-    change_ref, wind_ref, temp_wide_ref, slope_ref,
-):
-    level_count = change_ref.shape[0] // ROWS
-    lanes = temp_ref.shape[-1]
-    sides = unpacked(after_ref, before_ref, edge_ref)
+    sides = split_dot(both, edge_ref[...])
     fields = (
-        (temp_ref, temp_wide_ref), (flow_ref.at[0], wind_ref.at[0]), (flow_ref.at[1], wind_ref.at[1])
+        (heat_ref, heat_wide_ref), (temp_ref, temp_wide_ref),
+        (flow_ref.at[0], wind_ref.at[0]), (flow_ref.at[1], wind_ref.at[1]),
     )
     for n, (own, wide) in enumerate(fields):
         for r in range(ROWS):
@@ -613,7 +430,9 @@
                     here : here + 8, lanes * k : lanes * (k + 1)
                 ]
     slope_ref[...] = split_dot(temp_wide_ref[...], high_ref[...], low_ref[...])
-    advect(temp_wide_ref, slope_ref, wind_ref, change_ref, level_count)
+    advect(temp_wide_ref, slope_ref, wind_ref, temp_wide_ref, level_count)
+    change = temp_wide_ref[...] + TIME_INCREMENT * heat_wide_ref[...]
+    write_averaged(change, average_ref, out_ref, first_ref, last_ref)
 
 
 def advect(field_ref, slope_ref, wind_ref, change_ref, level_count):
@@ -633,24 +452,6 @@
     width = first_ref.shape[1]
     first_ref[...] = out_ref[:level_count, :width]
     last_ref[...] = out_ref[out_ref.shape[0] - level_count :, :width]
-
-
-def first_stage_kernel(
-    change_ref, heat_ref, after_ref, before_ref, edge_ref, average_ref,
-    out_ref, first_ref, last_ref, sum_ref,
-):
-    level_count = first_ref.shape[0]
-    lanes = heat_ref.shape[1]
-    sides = unpacked(after_ref, before_ref, edge_ref)
-    for r in range(ROWS):
-        rows = slice(r * level_count, (r + 1) * level_count)
-        own = heat_ref[pl.ds(r, level_count, stride=ROWS), :]
-        sum_ref[rows, :lanes] = change_ref[rows, :lanes] + TIME_INCREMENT * own
-        for k in range(level_count // 8):
-            side = sides[8 * r : 8 * (r + 1), lanes * k : lanes * (k + 1)]
-            here = slice(r * level_count + 8 * k, r * level_count + 8 * (k + 1))
-            sum_ref[here, lanes:] = change_ref[here, lanes:] + TIME_INCREMENT * side
-    write_averaged(sum_ref[...], average_ref, out_ref, first_ref, last_ref)
 
 
 def next_stage_kernel(
@@ -714,19 +515,16 @@
 
     slopes = slope_matrices(lanes)
     average = average_matrix(lanes)
-    heat, after, before, fields_after, fields_before = radiation(
-        atmospheric_constituents, thermal_ratio, flow_velocity, solar_elevation_factor,
+    heat, first, last = radiation(
+        atmospheric_constituents, temper, flow, solar_elevation_factor,
         ground_reflectivity, sunlit_indicator, molecular_optics_lookup, condensate_optics_lookup,
     )
+    after, before = shifted(first, "gx", -1), shifted(last, "gx", 1)
     back = edge_matrix(level_count, lanes).T
-    change, wind = call(
-        own_change_kernel, "own_change",
-        (wide, jax.ShapeDtypeStruct((2, size, 2 * lanes), jnp.float32)), 2,
-        temper, flow, fields_after, fields_before, back, *slopes,
-    )
-    wave, first, last = call(
-        first_stage_kernel, "first_stage", (wide, line, line), 1,
-        change, heat, after, before, back, average,
+    wave, first, last, wind = call(
+        first_stage_kernel, "first_stage",
+        (wide, line, line, jax.ShapeDtypeStruct((2, size, 2 * lanes), jnp.float32)), 3,
+        temper, flow, heat, after, before, back, *slopes, average,
     )
     below, above = shifted(last, "gy", 1), shifted(first, "gy", -1)
     wave, first, last, total = call(

time: 104 us -> 104 us (level)
  starting transfers between devices: 17.1 us -> 9.46 us
  Pallas kernels: 69.4 us -> 75.5 us
  waiting for transfers between devices: 14.8 us -> 16.8 us
    ppermute x12 -> x8, starting transfers between devices: 17.1 us -> 9.46 us  [shifted(): lax.ppermute(value, axis, [(i, (i + steps) % count) for i in range(count)])]
    pallas_call x5 -> x1, Pallas kernels: 65.4 us -> 71.4 us  [radiation(): pl.pallas_call(radiation_kernel, out_shape=(jax.ShapeDtypeStruct((level_c...]
    ppermute x12 -> x8, waiting for transfers between devices: 14.8 us -> 16.8 us  [shifted(): lax.ppermute(value, axis, [(i, (i + steps) % count) for i in range(count)])]
    pallas_call x5 -> x4, Pallas kernels: 4 us -> 4.05 us  [call(): pl.pallas_call(kernel, out_shape=outs, in_specs=[whole] * len(values), ou...]
  transfers between devices with their start and end apart: 12 -> 8, of which waited for: 8 -> 8; matrix products, arithmetic and copies ran while one was open for 0% -> 0% of each run, Pallas kernels for 39% -> 0%
where the time goes in v9:
time: 104 us; the launch traced here: 103 us
  Pallas kernels  75.5 us (73%)
  waiting for transfers between devices  16.8 us (16%)
  starting transfers between devices  9.46 us (9%)
    pallas_call x1, Pallas kernels, radiation(): pl.pallas_call(radiation_kernel, out_shape=(jax.ShapeDtypeStruct((level_c...  71.4 us
    ppermute x8, waiting for transfers between devices, shifted(): lax.ppermute(value, axis, [(i, (i + steps) % count) for i in range(count)])  16.8 us
    ppermute x8, starting transfers between devices, shifted(): lax.ppermute(value, axis, [(i, (i + steps) % count) for i in range(count)])  9.46 us
    pallas_call x4, Pallas kernels, call(): pl.pallas_call(kernel, out_shape=outs, in_specs=[whole] * len(values), ou...  4.05 us
  transfers between devices with their start and end apart: 8, of which 8 were waited for; matrix products, arithmetic and copies ran while one was open for 0% of the time, Pallas kernels for 0%

profile of v9, /device:TPU:1, one launch (start us, length us, event | category | flops | bytes accessed | tf_op | source)
XLA Modules:
  0.0 103.4 jit_solution(18440934402925378713)
XLA Ops:
  0.6 0.0 copy-start
  0.6 0.0 copy-start.1
  0.7 0.0 copy-start.2
  0.7 0.0 copy-start.3
  0.7 0.0 copy-start.4
  0.7 0.0 copy-start.5
  0.7 71.4 %radiation.1 = (f32[576,128]{1,0:T(8,128)}, f32[256,128]{1,0:T(8,128)}, f32[256,128]{1,0:T(8,128)}) custom-call(f32[5,72,8,128]{3,2,1,0:T(8,128)} %state_ref.1, f32[576,128]{1,0:T(8,128)} %bitcast.5, f32[2,576,128]{2,1,0:T(8,128)} %bitcast.8, f32[8,128]{1,0:T(8,128)} %cosine_ref.1, f32[8,128]{1,0:T(8,128)} %ground_ref.1, s32[8,128]{1,0:T(8,128)} %day_ref.1, ...), custom_call_target="tpu_custom_call" | custom-call | flops 82575360000 | bytes 2654208 | tf_op jit(solution)/shard_map/radiation/pallas_call | solution.py:324
  72.1 5.1 %collective-permute-start = (f32[256,128]{1,0:T(8,128)}, f32[256,128]{1,0:T(8,128)S(1)}, u32[]{:S(2)}, u32[]{:S(2)}) collective-permute-start(f32[256,128]{1,0:T(8,128)} %get-tuple-element.18), channel_id=1, source_target_pairs={{0,28},{4,0},{8,4},{12,8},{16,12},{20,16},{24,20},{28,24},{1,29},{... | collective-permute-start | bytes 393224 | tf_op jit(solution)/shard_map/ppermute | solution.py:26
  77.2 0.0 collective-permute-start.1
  77.2 2.5 %collective-permute-done.after_ref = f32[256,128]{1,0:T(8,128)S(1)} collective-permute-done((f32[256,128]{1,0:T(8,128)}, f32[256,128]{1,0:T(8,128)S(1)}, u32[]{:S(2)}, u32[]{:S(2)}) %collective-permute-start) | collective-permute-done | bytes 131104 | tf_op jit(solution)/shard_map/ppermute | solution.py:26
  79.7 4.2 %collective-permute-done.1.before_ref = f32[256,128]{1,0:T(8,128)S(1)} collective-permute-done((f32[256,128]{1,0:T(8,128)}, f32[256,128]{1,0:T(8,128)S(1)}, u32[]{:S(2)}, u32[]{:S(2)}) %collective-permute-start.1) | collective-permute-done | bytes 131104 | tf_op jit(solution)/shard_map/ppermute | solution.py:26
  83.9 0.0 copy-done
  83.9 0.0 copy-done.1
  83.9 0.0 copy-done.2
  83.9 0.0 copy-done.3
  84.0 0.0 copy-done.4
  84.0 0.0 copy-done.5
  84.0 0.0 copy-start.6
  84.0 1.0 copy-done.6
  84.9 1.4 %first_stage.1 = (f32[576,256]{1,0:T(8,128)S(1)}, f32[72,256]{1,0:T(8,128)S(1)}, f32[72,256]{1,0:T(8,128)S(1)}, f32[2,576,256]{2,1,0:T(8,128)S(1)}) custom-call(f32[576,128]{1,0:T(8,128)S(1)} %bitcast.6, f32[2,576,128]{2,1,0:T(8,128)S(1)} %bitcast.9, f32[576,128]{1,0:T(8,128)S(1)} %copy-done.6, f32[256,128]{1,0:T(8,128)S(1)} %collective-permute-done.after_ref, ...), custom_call_target="tpu_custom_call" | custom-call | tf_op jit(solution)/shard_map/first_stage/pallas_call | solution.py:509
  86.4 3.2 %collective-permute-start.2 = (f32[72,256]{1,0:T(8,128)S(1)}, f32[72,256]{1,0:T(8,128)S(1)}, u32[]{:S(2)}, u32[]{:S(2)}) collective-permute-start(f32[72,256]{1,0:T(8,128)S(1)} %get-tuple-element.21), channel_id=1, source_target_pairs={{0,1},{1,2},{2,3},{3,0},{4,5},{5,6},{6,7},{7,4},{8,9},{9,10},{10,1... | collective-permute-start | bytes 221192 | tf_op jit(solution)/shard_map/ppermute | solution.py:26
  89.6 0.0 collective-permute-start.3
  89.6 1.4 %collective-permute-done.2.below_ref = f32[72,256]{1,0:T(8,128)S(1)} collective-permute-done((f32[72,256]{1,0:T(8,128)S(1)}, f32[72,256]{1,0:T(8,128)S(1)}, u32[]{:S(2)}, u32[]{:S(2)}) %collective-permute-start.2) | collective-permute-done | bytes 73760 | tf_op jit(solution)/shard_map/ppermute | solution.py:26
  91.0 2.4 %collective-permute-done.3.above_ref = f32[72,256]{1,0:T(8,128)S(1)} collective-permute-done((f32[72,256]{1,0:T(8,128)S(1)}, f32[72,256]{1,0:T(8,128)S(1)}, u32[]{:S(2)}, u32[]{:S(2)}) %collective-permute-start.3) | collective-permute-done | bytes 73760 | tf_op jit(solution)/shard_map/ppermute | solution.py:26
  93.4 0.9 second_stage.1
  94.3 0.1 collective-permute-start.4
  94.4 0.5 collective-permute-start.5
  94.9 0.9 collective-permute-done.4.below_ref
  95.8 2.4 %collective-permute-done.5.above_ref = f32[72,256]{1,0:T(8,128)S(1)} collective-permute-done((f32[72,256]{1,0:T(8,128)S(1)}, f32[72,256]{1,0:T(8,128)S(1)}, u32[]{:S(2)}, u32[]{:S(2)}) %collective-permute-start.5) | collective-permute-done | bytes 73760 | tf_op jit(solution)/shard_map/ppermute | solution.py:26
  98.2 0.9 third_stage.1
  99.1 0.1 collective-permute-start.6
  99.2 0.5 collective-permute-start.7
  99.7 0.7 collective-permute-done.6.below_ref
  100.4 2.2 %collective-permute-done.7.above_ref = f32[72,128]{1,0:T(8,128)S(1)} collective-permute-done((f32[72,128]{1,0:T(8,128)S(1)}, f32[72,128]{1,0:T(8,128)S(1)}, u32[]{:S(2)}, u32[]{:S(2)}) %collective-permute-start.7) | collective-permute-done | bytes 36896 | tf_op jit(solution)/shard_map/ppermute | solution.py:26
  102.6 0.8 last_stage.1
Async XLA Ops:
  0.6 83.3 %copy-start = (f32[72,8,128]{2,1,0:T(8,128)S(1)}, f32[72,8,128]{2,1,0:T(8,128)}, u32[]{:S(2)}) copy-start(f32[72,8,128]{2,1,0:T(8,128)} %param.14) | copy-start | bytes 884740
  0.6 83.3 %copy-start.1 = (bf16[256,256]{1,0:T(8,128)(2,1)S(1)}, bf16[256,256]{1,0:T(8,128)(2,1)}, u32[]{:S(2)}) copy-start(bf16[256,256]{1,0:T(8,128)(2,1)} %constant.10.clone.average_ref) | copy-start | bytes 393220
  0.7 83.3 %copy-start.2 = (bf16[256,256]{1,0:T(8,128)(2,1)S(1)}, bf16[256,256]{1,0:T(8,128)(2,1)}, u32[]{:S(2)}) copy-start(bf16[256,256]{1,0:T(8,128)(2,1)} %constant.9.clone.low_ref) | copy-start | bytes 393220
  0.7 83.3 %copy-start.3 = (bf16[256,256]{1,0:T(8,128)(2,1)S(1)}, bf16[256,256]{1,0:T(8,128)(2,1)}, u32[]{:S(2)}) copy-start(bf16[256,256]{1,0:T(8,128)(2,1)} %constant.8.clone.high_ref) | copy-start | bytes 393220
  0.7 83.3 %copy-start.4 = (f32[2,72,8,128]{3,2,1,0:T(8,128)S(1)}, f32[2,72,8,128]{3,2,1,0:T(8,128)}, u32[]{:S(2)}) copy-start(f32[2,72,8,128]{3,2,1,0:T(8,128)} %param.15) | copy-start | bytes 1769476
  0.7 83.3 %copy-start.5 = (bf16[256,1152]{1,0:T(8,128)(2,1)S(1)}, bf16[256,1152]{1,0:T(8,128)(2,1)}, u32[]{:S(2)}) copy-start(bf16[256,1152]{1,0:T(8,128)(2,1)} %constant.12.edge_ref) | copy-start | bytes 1769476
  72.1 7.6 %collective-permute-start = (f32[256,128]{1,0:T(8,128)}, f32[256,128]{1,0:T(8,128)S(1)}, u32[]{:S(2)}, u32[]{:S(2)}) collective-permute-start(f32[256,128]{1,0:T(8,128)} %get-tuple-element.18), channel_id=1, source_target_pairs={{0,28},{4,0},{8,4},{12,8},{16,12},{20,16},{24,20},{28,24},{1,29},{... | collective-permute-start | bytes 393224 | tf_op jit(solution)/shard_map/ppermute | solution.py:26
  77.2 6.7 %collective-permute-start.1 = (f32[256,128]{1,0:T(8,128)}, f32[256,128]{1,0:T(8,128)S(1)}, u32[]{:S(2)}, u32[]{:S(2)}) collective-permute-start(f32[256,128]{1,0:T(8,128)} %get-tuple-element.19), channel_id=1, source_target_pairs={{0,4},{4,8},{8,12},{12,16},{16,20},{20,24},{24,28},{28,0},{1,5},{5... | collective-permute-start | bytes 393224 | tf_op jit(solution)/shard_map/ppermute | solution.py:26
  84.0 1.0 copy-start.6
  86.4 4.6 %collective-permute-start.2 = (f32[72,256]{1,0:T(8,128)S(1)}, f32[72,256]{1,0:T(8,128)S(1)}, u32[]{:S(2)}, u32[]{:S(2)}) collective-permute-start(f32[72,256]{1,0:T(8,128)S(1)} %get-tuple-element.21), channel_id=1, source_target_pairs={{0,1},{1,2},{2,3},{3,0},{4,5},{5,6},{6,7},{7,4},{8,9},{9,10},{10,1... | collective-permute-start | bytes 221192 | tf_op jit(solution)/shard_map/ppermute | solution.py:26
  89.6 3.8 %collective-permute-start.3 = (f32[72,256]{1,0:T(8,128)S(1)}, f32[72,256]{1,0:T(8,128)S(1)}, u32[]{:S(2)}, u32[]{:S(2)}) collective-permute-start(f32[72,256]{1,0:T(8,128)S(1)} %get-tuple-element.22), channel_id=1, source_target_pairs={{0,3},{1,0},{2,1},{3,2},{4,7},{5,4},{6,5},{7,6},{8,11},{9,8},{10,9... | collective-permute-start | bytes 221192 | tf_op jit(solution)/shard_map/ppermute | solution.py:26
  94.3 1.5 %collective-permute-start.4 = (f32[72,256]{1,0:T(8,128)S(1)}, f32[72,256]{1,0:T(8,128)S(1)}, u32[]{:S(2)}, u32[]{:S(2)}) collective-permute-start(f32[72,256]{1,0:T(8,128)S(1)} %get-tuple-element.25), channel_id=1, source_target_pairs={{0,1},{1,2},{2,3},{3,0},{4,5},{5,6},{6,7},{7,4},{8,9},{9,10},{10,1... | collective-permute-start | bytes 221192 | tf_op jit(solution)/shard_map/ppermute | solution.py:26
  94.4 3.8 %collective-permute-start.5 = (f32[72,256]{1,0:T(8,128)S(1)}, f32[72,256]{1,0:T(8,128)S(1)}, u32[]{:S(2)}, u32[]{:S(2)}) collective-permute-start(f32[72,256]{1,0:T(8,128)S(1)} %get-tuple-element.26), channel_id=1, source_target_pairs={{0,3},{1,0},{2,1},{3,2},{4,7},{5,4},{6,5},{7,6},{8,11},{9,8},{10,9... | collective-permute-start | bytes 221192 | tf_op jit(solution)/shard_map/ppermute | solution.py:26
  99.1 1.3 %collective-permute-start.6 = (f32[72,128]{1,0:T(8,128)S(1)}, f32[72,128]{1,0:T(8,128)S(1)}, u32[]{:S(2)}, u32[]{:S(2)}) collective-permute-start(f32[72,128]{1,0:T(8,128)S(1)} %get-tuple-element.29), channel_id=1, source_target_pairs={{0,1},{1,2},{2,3},{3,0},{4,5},{5,6},{6,7},{7,4},{8,9},{9,10},{10,1... | collective-permute-start | bytes 110600 | tf_op jit(solution)/shard_map/ppermute | solution.py:26
  99.2 3.4 %collective-permute-start.7 = (f32[72,128]{1,0:T(8,128)S(1)}, f32[72,128]{1,0:T(8,128)S(1)}, u32[]{:S(2)}, u32[]{:S(2)}) collective-permute-start(f32[72,128]{1,0:T(8,128)S(1)} %get-tuple-element.30), channel_id=1, source_target_pairs={{0,3},{1,0},{2,1},{3,2},{4,7},{5,4},{6,5},{7,6},{8,11},{9,8},{10,9... | collective-permute-start | bytes 110600 | tf_op jit(solution)/shard_map/ppermute | solution.py:26

commit v10 on v9

--- a/solution.py
+++ b/solution.py
@@ -17,6 +17,7 @@
 TERMS = 16
 BLOCK = 12
 PARTIAL = 5
+DOWN = 24
 CHUNKS = 2
 QUANTITIES = 4
 
@@ -141,7 +142,7 @@
     slots = (depths_0, depths_1)
     once = 1 + jnp.minimum(row, 0)
 
-    def place_group(group, carry):
+    def place_group(group, carry=None):
         for j in range(GROUP):
             start = (group * GROUP + j) * TERMS * lines + line
             tile = terms_ref[pl.ds(start, TERMS, stride=lines), :].astype(jnp.bfloat16)
@@ -150,7 +151,10 @@
             right_ref[pair, TERMS * j : TERMS * (j + 1), half : half + lanes] = tile
         return carry
 
-    lax.fori_loop(0, level_count // GROUP, place_group, 0)
+    groups = level_count // GROUP
+    ready = -(-BLOCK // GROUP)
+    for group in range(groups - ready, groups):
+        place_group(group)
     slant_ref[...] = jnp.broadcast_to((-0.5 * LOG2E) / cosine, (8, lanes))
 
     def over_rows(values):
@@ -216,6 +220,8 @@
         return carry
 
     fill(blocks - 1, 0)
+    for group in range(groups - ready):
+        place_group(group)
     lax.fori_loop(0, blocks, below_block, 0)
 
     def folded(net):
@@ -232,15 +238,15 @@
 
     def down_group(group, carry):
         net, beam = carry
-        for j in range(GROUP):
-            level = group * GROUP + j
+        for j in range(DOWN):
+            level = group * DOWN + j
             net = gain_ref[level] * net + offset_ref[level] * beam
             beam = beam * direct_ref[level]
             start = pl.multiple_of(((level + 1) * count + row) * 8, 8)
             partial_ref[pl.ds(start, 8), :] = folded(net) + folded(beam)
         return (net, beam)
 
-    lax.fori_loop(0, level_count // GROUP, down_group, carry)
+    lax.fori_loop(0, level_count // DOWN, down_group, carry)
 
 
 def level_heating(partial_ref, level_count, gpoints, count, write):
@@ -258,8 +264,9 @@
 
 def radiation_kernel(
     state_ref, temp_ref, flow_ref, cosine_ref, ground_ref, day_ref, molecular_ref, table_ref,
-    edge_ref,
-    heat_ref, first_ref, last_ref, optics_ref, weight_ref, strip_ref, terms_ref, right_ref, *scratch,
+    edge_ref, high_ref, low_ref,
+    heat_ref, change_ref, wind_ref, first_ref, last_ref,
+    optics_ref, weight_ref, strip_ref, slope_ref, terms_ref, right_ref, *scratch,
 ):
     level_count, lines, lanes = state_ref.shape[1:]
     gpoints = weight_ref.shape[0]
@@ -284,9 +291,25 @@
             heat_ref[pl.ds(start, lines), :] = jnp.where(day, value, 0.0)
 
         level_heating(scratch[PARTIAL], level_count, gpoints, lines, write)
-        for n, ref in enumerate((heat_ref, temp_ref, flow_ref.at[0], flow_ref.at[1])):
+        spans = [slice(r * level_count, (r + 1) * level_count) for r in range(lines)]
+        for r, span in enumerate(spans):
+            native = pl.ds(r, level_count, stride=lines)
+            change_ref[span, :] = temp_ref[native, :]
+            for n in range(2):
+                wind_ref[n, span, :] = flow_ref[n, native, :]
+        slope_ref[...] = split_dot(
+            change_ref[...], high_ref[:lanes, :lanes], low_ref[:lanes, :lanes]
+        )
+        changes = change_rows(change_ref, slope_ref, wind_ref, slice(0, lanes), spans)
+        for r, (span, change) in enumerate(zip(spans, changes)):
+            own = heat_ref[pl.ds(r, level_count, stride=lines), :]
+            change_ref[span, :] = change + TIME_INCREMENT * own
+        for n, ref in enumerate((change_ref, wind_ref.at[0], wind_ref.at[1])):
             for r in range(lines):
-                write_strip(ref, r, lines, strip_ref, 8 * (lines * n + r))
+                here = slice(8 * (lines * n + r), 8 * (lines * n + r + 1))
+                for k in range(level_count // 8):
+                    start = r * level_count + 8 * k
+                    strip_ref[here, lanes * k : lanes * (k + 1)] = ref[start : start + 8, :]
         packed = split_dot(strip_ref[...], edge_ref[...])
         first_ref[...] = packed[:, :lanes]
         last_ref[...] = packed[:, lanes:]
@@ -301,14 +324,6 @@
         return carry
 
     lax.fori_loop(0, level_count, level, 0, unroll=4)
-
-
-def write_strip(source_ref, r, lines, strip_ref, start):
-    lanes = source_ref.shape[1]
-    for k in range(strip_ref.shape[1] // lanes):
-        strip_ref[pl.ds(start, 8), lanes * k : lanes * (k + 1)] = source_ref[
-            pl.ds(8 * k * lines + r, 8, stride=lines), :
-        ]
 
 
 def radiation(state, temper, flow, cosine, ground, day, molecular, condensate):
@@ -319,16 +334,19 @@
     whole = pl.BlockSpec(memory_space=pltpu.VMEM)
     part = (QUANTITIES * gpoints // CHUNKS, GROUP * TERMS)
     depths = pltpu.VMEM((BLOCK // 2, part[0], 2 * lanes), jnp.float32)
-    edge = jax.ShapeDtypeStruct((4 * 8 * rows, lanes), jnp.float32)
+    field = jax.ShapeDtypeStruct((level_count * rows, lanes), jnp.float32)
+    wind = jax.ShapeDtypeStruct((2, level_count * rows, lanes), jnp.float32)
+    edge = jax.ShapeDtypeStruct((3 * 8 * rows, lanes), jnp.float32)
     cells = level_count * gpoints * rows * lanes
     return pl.pallas_call(
         radiation_kernel,
-        out_shape=(jax.ShapeDtypeStruct((level_count * rows, lanes), jnp.float32), edge, edge),
-        grid=(rows,), in_specs=[whole] * 9, out_specs=(whole,) * 3,
+        out_shape=(field, field, wind, edge, edge),
+        grid=(rows,), in_specs=[whole] * 11, out_specs=(whole,) * 5,
         scratch_shapes=[
             pltpu.VMEM((level_count // GROUP, CHUNKS) + part, jnp.bfloat16),
             plane,
-            pltpu.VMEM((4 * 8 * rows, level_count // 8 * lanes), jnp.float32),
+            pltpu.VMEM((3 * 8 * rows, level_count // 8 * lanes), jnp.float32),
+            pltpu.VMEM((level_count * rows, lanes), jnp.float32),
             pltpu.VMEM((level_count * TERMS * rows, lanes), jnp.float32),
             pltpu.VMEM((level_count // 2, GROUP * TERMS, 2 * lanes), jnp.bfloat16),
             depths, depths, full, full, full,
@@ -343,7 +361,7 @@
         name="radiation",
     )(
         state, temper, flow, cosine, ground, day, molecular.transpose(0, 2, 1), condensate,
-        edge_matrix(level_count, lanes),
+        edge_matrix(level_count, lanes), *slope_matrices(lanes),
     )
 
 
@@ -409,41 +427,32 @@
 
 
 def first_stage_kernel(
-    temp_ref, flow_ref, heat_ref, after_ref, before_ref, edge_ref, high_ref, low_ref, average_ref,
-    out_ref, first_ref, last_ref, wind_ref, temp_wide_ref, heat_wide_ref, slope_ref,
+    change_ref, after_ref, before_ref, edge_ref, average_ref,
+    out_ref, first_ref, last_ref, wind_side_ref, wide_ref,
 ):
     level_count = first_ref.shape[0]
-    lanes = temp_ref.shape[-1]
+    lanes = change_ref.shape[1]
     both = jnp.concatenate([after_ref[...], before_ref[...]], axis=1)
     sides = split_dot(both, edge_ref[...])
-    fields = (
-        (heat_ref, heat_wide_ref), (temp_ref, temp_wide_ref),
-        (flow_ref.at[0], wind_ref.at[0]), (flow_ref.at[1], wind_ref.at[1]),
-    )
-    for n, (own, wide) in enumerate(fields):
-        for r in range(ROWS):
-            start = r * level_count
-            wide[start : start + level_count, :lanes] = own[pl.ds(r, level_count, stride=ROWS), :]
-            here = 8 * (ROWS * n + r)
-            for k in range(level_count // 8):
-                wide[start + 8 * k : start + 8 * (k + 1), lanes:] = sides[
-                    here : here + 8, lanes * k : lanes * (k + 1)
-                ]
-    slope_ref[...] = split_dot(temp_wide_ref[...], high_ref[...], low_ref[...])
-    advect(temp_wide_ref, slope_ref, wind_ref, temp_wide_ref, level_count)
-    change = temp_wide_ref[...] + TIME_INCREMENT * heat_wide_ref[...]
-    write_averaged(change, average_ref, out_ref, first_ref, last_ref)
-
-
-def advect(field_ref, slope_ref, wind_ref, change_ref, level_count):
-    spans = [slice(r * level_count, (r + 1) * level_count) for r in range(ROWS)]
-    for half in range(2):
-        lanes = field_ref.shape[1] // 2
-        part = slice(half * lanes, (half + 1) * lanes)
-        slopes = slope_y([field_ref[span, part] for span in spans])
-        for span, slope in zip(spans, slopes):
-            change = wind_ref[0, span, part] * slope_ref[span, part]
-            change_ref[span, part] = -TIME_INCREMENT * (change + wind_ref[1, span, part] * slope)
+    wide_ref[:, :lanes] = change_ref[...]
+    for r in range(ROWS):
+        for k in range(level_count // 8):
+            span = slice(r * level_count + 8 * k, r * level_count + 8 * (k + 1))
+            part = slice(lanes * k, lanes * (k + 1))
+            wide_ref[span, lanes:] = sides[8 * r : 8 * (r + 1), part]
+            for n in range(2):
+                here = 8 * (ROWS * (n + 1) + r)
+                wind_side_ref[n, span, :] = sides[here : here + 8, part]
+    write_averaged(wide_ref[...], average_ref, out_ref, first_ref, last_ref)
+
+
+def change_rows(field_ref, slope_ref, wind_ref, part, spans):
+    slopes = slope_y([field_ref[span, part] for span in spans])
+    result = []
+    for span, slope in zip(spans, slopes):
+        change = wind_ref[0, span, :] * slope_ref[span, part] + wind_ref[1, span, :] * slope
+        result.append(-TIME_INCREMENT * change)
+    return result
 
 
 def write_averaged(change, average_ref, out_ref, first_ref, last_ref):
@@ -455,8 +464,8 @@
 
 
 def next_stage_kernel(
-    share, native, field_ref, below_ref, above_ref, wind_ref, sum_ref, high_ref, low_ref,
-    average_ref, out_ref, first_ref, last_ref, total_ref, wave_ref, slope_ref, change_ref,
+    share, native, field_ref, below_ref, above_ref, wind_ref, wind_side_ref, sum_ref, high_ref,
+    low_ref, average_ref, out_ref, first_ref, last_ref, total_ref, wave_ref, slope_ref, change_ref,
 ):
     level_count = below_ref.shape[0]
     lanes = sum_ref.shape[1]
@@ -472,7 +481,10 @@
                 before = sum_ref[pl.ds(r, level_count, stride=ROWS), :] if native else sum_ref[span]
                 total_ref[span] = before + share * row
     slope_ref[...] = split_dot(wave_ref[...], high_ref[...], low_ref[...])
-    advect(wave_ref, slope_ref, wind_ref, change_ref, level_count)
+    for half, wind in enumerate((wind_ref, wind_side_ref)):
+        part = slice(half * lanes, (half + 1) * lanes)
+        for span, change in zip(spans, change_rows(wave_ref, slope_ref, wind, part, spans)):
+            change_ref[span, part] = change
     write_averaged(change_ref[...], average_ref, out_ref, first_ref, last_ref)
 
 
@@ -515,26 +527,26 @@
 
     slopes = slope_matrices(lanes)
     average = average_matrix(lanes)
-    heat, first, last = radiation(
+    heat, change, wind, first, last = radiation(
         atmospheric_constituents, temper, flow, solar_elevation_factor,
         ground_reflectivity, sunlit_indicator, molecular_optics_lookup, condensate_optics_lookup,
     )
     after, before = shifted(first, "gx", -1), shifted(last, "gx", 1)
     back = edge_matrix(level_count, lanes).T
-    wave, first, last, wind = call(
+    wave, first, last, wind_side = call(
         first_stage_kernel, "first_stage",
-        (wide, line, line, jax.ShapeDtypeStruct((2, size, 2 * lanes), jnp.float32)), 3,
-        temper, flow, heat, after, before, back, *slopes, average,
+        (wide, line, line, jax.ShapeDtypeStruct((2, size, lanes), jnp.float32)), 1,
+        change, after, before, back, average,
     )
     below, above = shifted(last, "gy", 1), shifted(first, "gy", -1)
     wave, first, last, total = call(
         functools.partial(next_stage_kernel, 1.0, True), "second_stage",
-        (wide, line, line, field), 3, wave, below, above, wind, temper, *slopes, average,
+        (wide, line, line, field), 3, wave, below, above, wind, wind_side, temper, *slopes, average,
     )
     below, above = shifted(last, "gy", 1), shifted(first, "gy", -1)
     wave, first, last, total = call(
         functools.partial(next_stage_kernel, 0.5, False), "third_stage",
-        (wide, short, short, field), 3, wave, below, above, wind, total, *slopes, average,
+        (wide, short, short, field), 3, wave, below, above, wind, wind_side, total, *slopes, average,
     )
     below, above = shifted(last, "gy", 1), shifted(first, "gy", -1)
     total = call(

time: 104 us -> 102 us (0.981)
  Pallas kernels: 75.5 us -> 74 us
where the time goes in v10:
time: 102 us
  Pallas kernels  74 us (73%)
  waiting for transfers between devices  16.4 us (16%)
  starting transfers between devices  9.52 us (9%)
    pallas_call x1, Pallas kernels, radiation(): pl.pallas_call(radiation_kernel, out_shape=(field, field, wind, edge, edg...  70.8 us
    ppermute x8, waiting for transfers between devices, shifted(): lax.ppermute(value, axis, [(i, (i + steps) % count) for i in range(count)])  16.4 us
    ppermute x8, starting transfers between devices, shifted(): lax.ppermute(value, axis, [(i, (i + steps) % count) for i in range(count)])  9.52 us
    pallas_call x4, Pallas kernels, call(): pl.pallas_call(kernel, out_shape=outs, in_specs=[whole] * len(values), ou...  3.28 us
  transfers between devices with their start and end apart: 8, of which 8 were waited for; matrix products, arithmetic and copies ran while one was open for 0% of the time, Pallas kernels for 0%

profile of v10, /device:TPU:1, one launch (start us, length us, event | category | flops | bytes accessed | tf_op | source)
XLA Modules:
  0.0 101.7 jit_solution(14479579948052696435)
XLA Ops:
  0.6 0.0 copy-start.1
  0.6 0.0 copy-start.2
  0.7 0.0 copy-start.3
  0.7 0.0 copy-start.4
  0.7 0.0 copy-start.5
  0.7 70.8 %radiation.1 = (f32[576,128]{1,0:T(8,128)}, f32[576,128]{1,0:T(8,128)}, f32[2,576,128]{2,1,0:T(8,128)}, f32[192,128]{1,0:T(8,128)}, f32[192,128]{1,0:T(8,128)}) custom-call(f32[5,72,8,128]{3,2,1,0:T(8,128)} %state_ref.1, f32[576,128]{1,0:T(8,128)} %bitcast.5, f32[2,576,128]{2,1,0:T(8,128)} %bitcast.8, f32[8,128]{1,0:T(8,128)} %cosine_ref.1, ...), custom_call_target="tpu_custom_call" | custom-call | flops 82575360000 | bytes 2654208 | tf_op jit(solution)/shard_map/radiation/pallas_call | solution.py:341
  71.5 0.0 copy-start
  71.5 5.2 %collective-permute-start = (f32[192,128]{1,0:T(8,128)}, f32[192,128]{1,0:T(8,128)S(1)}, u32[]{:S(2)}, u32[]{:S(2)}) collective-permute-start(f32[192,128]{1,0:T(8,128)} %get-tuple-element.21), channel_id=1, source_target_pairs={{0,28},{4,0},{8,4},{12,8},{16,12},{20,16},{24,20},{28,24},{1,29},{... | collective-permute-start | bytes 294920 | tf_op jit(solution)/shard_map/ppermute | solution.py:27
  76.6 0.0 collective-permute-start.1
  76.6 2.0 %collective-permute-done.after_ref = f32[192,128]{1,0:T(8,128)S(1)} collective-permute-done((f32[192,128]{1,0:T(8,128)}, f32[192,128]{1,0:T(8,128)S(1)}, u32[]{:S(2)}, u32[]{:S(2)}) %collective-permute-start) | collective-permute-done | bytes 98336 | tf_op jit(solution)/shard_map/ppermute | solution.py:27
  78.6 4.4 %collective-permute-done.1.before_ref = f32[192,128]{1,0:T(8,128)S(1)} collective-permute-done((f32[192,128]{1,0:T(8,128)}, f32[192,128]{1,0:T(8,128)S(1)}, u32[]{:S(2)}, u32[]{:S(2)}) %collective-permute-start.1) | collective-permute-done | bytes 98336 | tf_op jit(solution)/shard_map/ppermute | solution.py:27
  83.0 0.0 copy-done.1
  83.0 0.0 copy-done.2
  83.0 0.0 copy-start.6
  83.0 1.0 copy-done.6
  84.0 0.7 first_stage.1
  84.6 3.3 %collective-permute-start.2 = (f32[72,256]{1,0:T(8,128)S(1)}, f32[72,256]{1,0:T(8,128)S(1)}, u32[]{:S(2)}, u32[]{:S(2)}) collective-permute-start(f32[72,256]{1,0:T(8,128)S(1)} %get-tuple-element.24), channel_id=1, source_target_pairs={{0,1},{1,2},{2,3},{3,0},{4,5},{5,6},{6,7},{7,4},{8,9},{9,10},{10,1... | collective-permute-start | bytes 221192 | tf_op jit(solution)/shard_map/ppermute | solution.py:27
  87.9 0.0 collective-permute-start.3
  87.9 1.4 %collective-permute-done.2.below_ref = f32[72,256]{1,0:T(8,128)S(1)} collective-permute-done((f32[72,256]{1,0:T(8,128)S(1)}, f32[72,256]{1,0:T(8,128)S(1)}, u32[]{:S(2)}, u32[]{:S(2)}) %collective-permute-start.2) | collective-permute-done | bytes 73760 | tf_op jit(solution)/shard_map/ppermute | solution.py:27
  89.3 2.4 %collective-permute-done.3.above_ref = f32[72,256]{1,0:T(8,128)S(1)} collective-permute-done((f32[72,256]{1,0:T(8,128)S(1)}, f32[72,256]{1,0:T(8,128)S(1)}, u32[]{:S(2)}, u32[]{:S(2)}) %collective-permute-start.3) | collective-permute-done | bytes 73760 | tf_op jit(solution)/shard_map/ppermute | solution.py:27
  91.7 0.0 copy-done.3
  91.7 0.0 copy-done.4
  91.7 0.0 copy-done.5
  91.7 0.0 copy-done
  91.7 0.9 second_stage.1
  92.6 0.1 collective-permute-start.4
  92.7 0.5 collective-permute-start.5
  93.2 0.9 collective-permute-done.4.below_ref
  94.1 2.4 %collective-permute-done.5.above_ref = f32[72,256]{1,0:T(8,128)S(1)} collective-permute-done((f32[72,256]{1,0:T(8,128)S(1)}, f32[72,256]{1,0:T(8,128)S(1)}, u32[]{:S(2)}, u32[]{:S(2)}) %collective-permute-start.5) | collective-permute-done | bytes 73760 | tf_op jit(solution)/shard_map/ppermute | solution.py:27
  96.5 0.9 third_stage.1
  97.4 0.1 collective-permute-start.6
  97.5 0.5 collective-permute-start.7
  98.0 0.7 collective-permute-done.6.below_ref
  98.7 2.2 %collective-permute-done.7.above_ref = f32[72,128]{1,0:T(8,128)S(1)} collective-permute-done((f32[72,128]{1,0:T(8,128)S(1)}, f32[72,128]{1,0:T(8,128)S(1)}, u32[]{:S(2)}, u32[]{:S(2)}) %collective-permute-start.7) | collective-permute-done | bytes 36896 | tf_op jit(solution)/shard_map/ppermute | solution.py:27
  100.9 0.8 last_stage.1
Async XLA Ops:
  0.6 82.4 %copy-start.1 = (bf16[256,256]{1,0:T(8,128)(2,1)S(1)}, bf16[256,256]{1,0:T(8,128)(2,1)}, u32[]{:S(2)}) copy-start(bf16[256,256]{1,0:T(8,128)(2,1)} %constant.10.clone.average_ref) | copy-start | bytes 393220
  0.6 82.4 %copy-start.2 = (bf16[256,1152]{1,0:T(8,128)(2,1)S(1)}, bf16[256,1152]{1,0:T(8,128)(2,1)}, u32[]{:S(2)}) copy-start(bf16[256,1152]{1,0:T(8,128)(2,1)} %constant.12.edge_ref) | copy-start | bytes 1769476
  0.7 91.0 %copy-start.3 = (bf16[256,256]{1,0:T(8,128)(2,1)S(1)}, bf16[256,256]{1,0:T(8,128)(2,1)}, u32[]{:S(2)}) copy-start(bf16[256,256]{1,0:T(8,128)(2,1)} %constant.9.clone.low_ref) | copy-start | bytes 393220
  0.7 91.0 %copy-start.4 = (bf16[256,256]{1,0:T(8,128)(2,1)S(1)}, bf16[256,256]{1,0:T(8,128)(2,1)}, u32[]{:S(2)}) copy-start(bf16[256,256]{1,0:T(8,128)(2,1)} %constant.8.clone.high_ref) | copy-start | bytes 393220
  0.7 91.0 %copy-start.5 = (f32[72,8,128]{2,1,0:T(8,128)S(1)}, f32[72,8,128]{2,1,0:T(8,128)}, u32[]{:S(2)}) copy-start(f32[72,8,128]{2,1,0:T(8,128)} %param.16) | copy-start | bytes 884740
  71.5 20.2 %copy-start = (f32[2,576,128]{2,1,0:T(8,128)S(1)}, f32[2,576,128]{2,1,0:T(8,128)}, u32[]{:S(2)}) copy-start(f32[2,576,128]{2,1,0:T(8,128)} %get-tuple-element.26.wind_ref) | copy-start | bytes 1769476
  71.5 7.1 %collective-permute-start = (f32[192,128]{1,0:T(8,128)}, f32[192,128]{1,0:T(8,128)S(1)}, u32[]{:S(2)}, u32[]{:S(2)}) collective-permute-start(f32[192,128]{1,0:T(8,128)} %get-tuple-element.21), channel_id=1, source_target_pairs={{0,28},{4,0},{8,4},{12,8},{16,12},{20,16},{24,20},{28,24},{1,29},{... | collective-permute-start | bytes 294920 | tf_op jit(solution)/shard_map/ppermute | solution.py:27
  76.6 6.4 %collective-permute-start.1 = (f32[192,128]{1,0:T(8,128)}, f32[192,128]{1,0:T(8,128)S(1)}, u32[]{:S(2)}, u32[]{:S(2)}) collective-permute-start(f32[192,128]{1,0:T(8,128)} %get-tuple-element.22), channel_id=1, source_target_pairs={{0,4},{4,8},{8,12},{12,16},{16,20},{20,24},{24,28},{28,0},{1,5},{5... | collective-permute-start | bytes 294920 | tf_op jit(solution)/shard_map/ppermute | solution.py:27
  83.0 1.0 copy-start.6
  84.6 4.7 %collective-permute-start.2 = (f32[72,256]{1,0:T(8,128)S(1)}, f32[72,256]{1,0:T(8,128)S(1)}, u32[]{:S(2)}, u32[]{:S(2)}) collective-permute-start(f32[72,256]{1,0:T(8,128)S(1)} %get-tuple-element.24), channel_id=1, source_target_pairs={{0,1},{1,2},{2,3},{3,0},{4,5},{5,6},{6,7},{7,4},{8,9},{9,10},{10,1... | collective-permute-start | bytes 221192 | tf_op jit(solution)/shard_map/ppermute | solution.py:27
  87.9 3.8 %collective-permute-start.3 = (f32[72,256]{1,0:T(8,128)S(1)}, f32[72,256]{1,0:T(8,128)S(1)}, u32[]{:S(2)}, u32[]{:S(2)}) collective-permute-start(f32[72,256]{1,0:T(8,128)S(1)} %get-tuple-element.25), channel_id=1, source_target_pairs={{0,3},{1,0},{2,1},{3,2},{4,7},{5,4},{6,5},{7,6},{8,11},{9,8},{10,9... | collective-permute-start | bytes 221192 | tf_op jit(solution)/shard_map/ppermute | solution.py:27
  92.6 1.5 %collective-permute-start.4 = (f32[72,256]{1,0:T(8,128)S(1)}, f32[72,256]{1,0:T(8,128)S(1)}, u32[]{:S(2)}, u32[]{:S(2)}) collective-permute-start(f32[72,256]{1,0:T(8,128)S(1)} %get-tuple-element.29), channel_id=1, source_target_pairs={{0,1},{1,2},{2,3},{3,0},{4,5},{5,6},{6,7},{7,4},{8,9},{9,10},{10,1... | collective-permute-start | bytes 221192 | tf_op jit(solution)/shard_map/ppermute | solution.py:27
  92.7 3.8 %collective-permute-start.5 = (f32[72,256]{1,0:T(8,128)S(1)}, f32[72,256]{1,0:T(8,128)S(1)}, u32[]{:S(2)}, u32[]{:S(2)}) collective-permute-start(f32[72,256]{1,0:T(8,128)S(1)} %get-tuple-element.30), channel_id=1, source_target_pairs={{0,3},{1,0},{2,1},{3,2},{4,7},{5,4},{6,5},{7,6},{8,11},{9,8},{10,9... | collective-permute-start | bytes 221192 | tf_op jit(solution)/shard_map/ppermute | solution.py:27
  97.4 1.3 %collective-permute-start.6 = (f32[72,128]{1,0:T(8,128)S(1)}, f32[72,128]{1,0:T(8,128)S(1)}, u32[]{:S(2)}, u32[]{:S(2)}) collective-permute-start(f32[72,128]{1,0:T(8,128)S(1)} %get-tuple-element.33), channel_id=1, source_target_pairs={{0,1},{1,2},{2,3},{3,0},{4,5},{5,6},{6,7},{7,4},{8,9},{9,10},{10,1... | collective-permute-start | bytes 110600 | tf_op jit(solution)/shard_map/ppermute | solution.py:27
  97.5 3.4 %collective-permute-start.7 = (f32[72,128]{1,0:T(8,128)S(1)}, f32[72,128]{1,0:T(8,128)S(1)}, u32[]{:S(2)}, u32[]{:S(2)}) collective-permute-start(f32[72,128]{1,0:T(8,128)S(1)} %get-tuple-element.34), channel_id=1, source_target_pairs={{0,3},{1,0},{2,1},{3,2},{4,7},{5,4},{6,5},{7,6},{8,11},{9,8},{10,9... | collective-permute-start | bytes 110600 | tf_op jit(solution)/shard_map/ppermute | solution.py:27

commit v11 on v10

--- a/solution.py
+++ b/solution.py
@@ -427,7 +427,7 @@
 
 
 def first_stage_kernel(
-    change_ref, after_ref, before_ref, edge_ref, average_ref,
+    change_ref, before_ref, after_ref, edge_ref, average_ref,
     out_ref, first_ref, last_ref, wind_side_ref, wide_ref,
 ):
     level_count = first_ref.shape[0]
@@ -531,12 +531,12 @@
         atmospheric_constituents, temper, flow, solar_elevation_factor,
         ground_reflectivity, sunlit_indicator, molecular_optics_lookup, condensate_optics_lookup,
     )
-    after, before = shifted(first, "gx", -1), shifted(last, "gx", 1)
+    before, after = shifted(last, "gx", 1), shifted(first, "gx", -1)
     back = edge_matrix(level_count, lanes).T
     wave, first, last, wind_side = call(
         first_stage_kernel, "first_stage",
         (wide, line, line, jax.ShapeDtypeStruct((2, size, lanes), jnp.float32)), 1,
-        change, after, before, back, average,
+        change, before, after, back, average,
     )
     below, above = shifted(last, "gy", 1), shifted(first, "gy", -1)
     wave, first, last, total = call(

time: 102 us -> 98.2 us (0.963)
  waiting for transfers between devices: 16.4 us -> 12.7 us
    ppermute x8, waiting for transfers between devices: 16.4 us -> 12.7 us  [shifted(): lax.ppermute(value, axis, [(i, (i + steps) % count) for i in range(count)])]
  transfers between devices with their start and end apart: 8 -> 8, of which waited for: 8 -> 7; matrix products, arithmetic and copies ran while one was open for 0% -> 0% of each run, Pallas kernels for 0% -> 0%
where the time goes in v11:
time: 98.2 us; the launch traced here: 98.1 us
  Pallas kernels  74.1 us (75%)
  waiting for transfers between devices  12.7 us (13%)
  starting transfers between devices  9.6 us (10%)
  local copies, waits for them, and re-layouts  0.99 us (1%)
    pallas_call x1, Pallas kernels, radiation(): pl.pallas_call(radiation_kernel, out_shape=(field, field, wind, edge, edg...  70.8 us
    ppermute x8, waiting for transfers between devices, shifted(): lax.ppermute(value, axis, [(i, (i + steps) % count) for i in range(count)])  12.7 us
    ppermute x8, starting transfers between devices, shifted(): lax.ppermute(value, axis, [(i, (i + steps) % count) for i in range(count)])  9.6 us
    pallas_call x4, Pallas kernels, call(): pl.pallas_call(kernel, out_shape=outs, in_specs=[whole] * len(values), ou...  3.28 us
  transfers between devices with their start and end apart: 8, of which 7 were waited for; matrix products, arithmetic and copies ran while one was open for 0% of the time, Pallas kernels for 0%

profile of v11, /device:TPU:1, one launch (start us, length us, event | category | flops | bytes accessed | tf_op | source)
XLA Modules:
  0.0 98.1 jit_solution(17819712565640394288)
XLA Ops:
  0.6 0.0 copy-start.1
  0.6 0.0 copy-start.2
  0.7 0.0 copy-start.3
  0.7 0.0 copy-start.4
  0.7 0.0 copy-start.5
  0.7 70.8 %radiation.1 = (f32[576,128]{1,0:T(8,128)}, f32[576,128]{1,0:T(8,128)}, f32[2,576,128]{2,1,0:T(8,128)}, f32[192,128]{1,0:T(8,128)}, f32[192,128]{1,0:T(8,128)}) custom-call(f32[5,72,8,128]{3,2,1,0:T(8,128)} %state_ref.1, f32[576,128]{1,0:T(8,128)} %bitcast.5, f32[2,576,128]{2,1,0:T(8,128)} %bitcast.8, f32[8,128]{1,0:T(8,128)} %cosine_ref.1, ...), custom_call_target="tpu_custom_call" | custom-call | flops 82575360000 | bytes 2654208 | tf_op jit(solution)/shard_map/radiation/pallas_call | solution.py:341
  71.5 0.0 copy-start
  71.5 2.1 %collective-permute-start = (f32[192,128]{1,0:T(8,128)}, f32[192,128]{1,0:T(8,128)S(1)}, u32[]{:S(2)}, u32[]{:S(2)}) collective-permute-start(f32[192,128]{1,0:T(8,128)} %get-tuple-element.21), channel_id=1, source_target_pairs={{0,4},{4,8},{8,12},{12,16},{16,20},{20,24},{24,28},{28,0},{1,5},{5... | collective-permute-start | bytes 294920 | tf_op jit(solution)/shard_map/ppermute | solution.py:27
  73.6 3.1 %collective-permute-start.1 = (f32[192,128]{1,0:T(8,128)}, f32[192,128]{1,0:T(8,128)S(1)}, u32[]{:S(2)}, u32[]{:S(2)}) collective-permute-start(f32[192,128]{1,0:T(8,128)} %get-tuple-element.22), channel_id=1, source_target_pairs={{0,28},{4,0},{8,4},{12,8},{16,12},{20,16},{24,20},{28,24},{1,29},{... | collective-permute-start | bytes 294920 | tf_op jit(solution)/shard_map/ppermute | solution.py:27
  76.7 2.7 %collective-permute-done.before_ref = f32[192,128]{1,0:T(8,128)S(1)} collective-permute-done((f32[192,128]{1,0:T(8,128)}, f32[192,128]{1,0:T(8,128)S(1)}, u32[]{:S(2)}, u32[]{:S(2)}) %collective-permute-start) | collective-permute-done | bytes 98336 | tf_op jit(solution)/shard_map/ppermute | solution.py:27
  79.4 0.0 collective-permute-done.1.after_ref
  79.4 0.0 copy-done.1
  79.4 0.0 copy-done.2
  79.4 0.0 copy-start.6
  79.4 1.0 copy-done.6
  80.3 0.7 first_stage.1
  81.0 3.3 %collective-permute-start.2 = (f32[72,256]{1,0:T(8,128)S(1)}, f32[72,256]{1,0:T(8,128)S(1)}, u32[]{:S(2)}, u32[]{:S(2)}) collective-permute-start(f32[72,256]{1,0:T(8,128)S(1)} %get-tuple-element.24), channel_id=1, source_target_pairs={{0,1},{1,2},{2,3},{3,0},{4,5},{5,6},{6,7},{7,4},{8,9},{9,10},{10,1... | collective-permute-start | bytes 221192 | tf_op jit(solution)/shard_map/ppermute | solution.py:27
  84.3 0.0 collective-permute-start.3
  84.3 1.4 %collective-permute-done.2.below_ref = f32[72,256]{1,0:T(8,128)S(1)} collective-permute-done((f32[72,256]{1,0:T(8,128)S(1)}, f32[72,256]{1,0:T(8,128)S(1)}, u32[]{:S(2)}, u32[]{:S(2)}) %collective-permute-start.2) | collective-permute-done | bytes 73760 | tf_op jit(solution)/shard_map/ppermute | solution.py:27
  85.7 2.4 %collective-permute-done.3.above_ref = f32[72,256]{1,0:T(8,128)S(1)} collective-permute-done((f32[72,256]{1,0:T(8,128)S(1)}, f32[72,256]{1,0:T(8,128)S(1)}, u32[]{:S(2)}, u32[]{:S(2)}) %collective-permute-start.3) | collective-permute-done | bytes 73760 | tf_op jit(solution)/shard_map/ppermute | solution.py:27
  88.0 0.0 copy-done.3
  88.1 0.0 copy-done.4
  88.1 0.0 copy-done.5
  88.1 0.0 copy-done
  88.1 0.9 second_stage.1
  89.0 0.1 collective-permute-start.4
  89.0 0.5 collective-permute-start.5
  89.5 0.9 collective-permute-done.4.below_ref
  90.4 2.4 %collective-permute-done.5.above_ref = f32[72,256]{1,0:T(8,128)S(1)} collective-permute-done((f32[72,256]{1,0:T(8,128)S(1)}, f32[72,256]{1,0:T(8,128)S(1)}, u32[]{:S(2)}, u32[]{:S(2)}) %collective-permute-start.5) | collective-permute-done | bytes 73760 | tf_op jit(solution)/shard_map/ppermute | solution.py:27
  92.9 0.9 third_stage.1
  93.8 0.1 collective-permute-start.6
  93.8 0.5 collective-permute-start.7
  94.3 0.7 collective-permute-done.6.below_ref
  95.0 2.2 %collective-permute-done.7.above_ref = f32[72,128]{1,0:T(8,128)S(1)} collective-permute-done((f32[72,128]{1,0:T(8,128)S(1)}, f32[72,128]{1,0:T(8,128)S(1)}, u32[]{:S(2)}, u32[]{:S(2)}) %collective-permute-start.7) | collective-permute-done | bytes 36896 | tf_op jit(solution)/shard_map/ppermute | solution.py:27
  97.3 0.8 last_stage.1
Async XLA Ops:
  0.6 78.7 %copy-start.1 = (bf16[256,256]{1,0:T(8,128)(2,1)S(1)}, bf16[256,256]{1,0:T(8,128)(2,1)}, u32[]{:S(2)}) copy-start(bf16[256,256]{1,0:T(8,128)(2,1)} %constant.10.clone.average_ref) | copy-start | bytes 393220
  0.6 78.7 %copy-start.2 = (bf16[256,1152]{1,0:T(8,128)(2,1)S(1)}, bf16[256,1152]{1,0:T(8,128)(2,1)}, u32[]{:S(2)}) copy-start(bf16[256,1152]{1,0:T(8,128)(2,1)} %constant.12.edge_ref) | copy-start | bytes 1769476
  0.7 87.4 %copy-start.3 = (bf16[256,256]{1,0:T(8,128)(2,1)S(1)}, bf16[256,256]{1,0:T(8,128)(2,1)}, u32[]{:S(2)}) copy-start(bf16[256,256]{1,0:T(8,128)(2,1)} %constant.9.clone.low_ref) | copy-start | bytes 393220
  0.7 87.4 %copy-start.4 = (bf16[256,256]{1,0:T(8,128)(2,1)S(1)}, bf16[256,256]{1,0:T(8,128)(2,1)}, u32[]{:S(2)}) copy-start(bf16[256,256]{1,0:T(8,128)(2,1)} %constant.8.clone.high_ref) | copy-start | bytes 393220
  0.7 87.4 %copy-start.5 = (f32[72,8,128]{2,1,0:T(8,128)S(1)}, f32[72,8,128]{2,1,0:T(8,128)}, u32[]{:S(2)}) copy-start(f32[72,8,128]{2,1,0:T(8,128)} %param.16) | copy-start | bytes 884740
  71.5 16.6 %copy-start = (f32[2,576,128]{2,1,0:T(8,128)S(1)}, f32[2,576,128]{2,1,0:T(8,128)}, u32[]{:S(2)}) copy-start(f32[2,576,128]{2,1,0:T(8,128)} %get-tuple-element.26.wind_ref) | copy-start | bytes 1769476
  71.5 7.9 %collective-permute-start = (f32[192,128]{1,0:T(8,128)}, f32[192,128]{1,0:T(8,128)S(1)}, u32[]{:S(2)}, u32[]{:S(2)}) collective-permute-start(f32[192,128]{1,0:T(8,128)} %get-tuple-element.21), channel_id=1, source_target_pairs={{0,4},{4,8},{8,12},{12,16},{16,20},{20,24},{24,28},{28,0},{1,5},{5... | collective-permute-start | bytes 294920 | tf_op jit(solution)/shard_map/ppermute | solution.py:27
  73.6 5.8 %collective-permute-start.1 = (f32[192,128]{1,0:T(8,128)}, f32[192,128]{1,0:T(8,128)S(1)}, u32[]{:S(2)}, u32[]{:S(2)}) collective-permute-start(f32[192,128]{1,0:T(8,128)} %get-tuple-element.22), channel_id=1, source_target_pairs={{0,28},{4,0},{8,4},{12,8},{16,12},{20,16},{24,20},{28,24},{1,29},{... | collective-permute-start | bytes 294920 | tf_op jit(solution)/shard_map/ppermute | solution.py:27
  79.4 1.0 copy-start.6
  81.0 4.7 %collective-permute-start.2 = (f32[72,256]{1,0:T(8,128)S(1)}, f32[72,256]{1,0:T(8,128)S(1)}, u32[]{:S(2)}, u32[]{:S(2)}) collective-permute-start(f32[72,256]{1,0:T(8,128)S(1)} %get-tuple-element.24), channel_id=1, source_target_pairs={{0,1},{1,2},{2,3},{3,0},{4,5},{5,6},{6,7},{7,4},{8,9},{9,10},{10,1... | collective-permute-start | bytes 221192 | tf_op jit(solution)/shard_map/ppermute | solution.py:27
  84.3 3.8 %collective-permute-start.3 = (f32[72,256]{1,0:T(8,128)S(1)}, f32[72,256]{1,0:T(8,128)S(1)}, u32[]{:S(2)}, u32[]{:S(2)}) collective-permute-start(f32[72,256]{1,0:T(8,128)S(1)} %get-tuple-element.25), channel_id=1, source_target_pairs={{0,3},{1,0},{2,1},{3,2},{4,7},{5,4},{6,5},{7,6},{8,11},{9,8},{10,9... | collective-permute-start | bytes 221192 | tf_op jit(solution)/shard_map/ppermute | solution.py:27
  89.0 1.5 %collective-permute-start.4 = (f32[72,256]{1,0:T(8,128)S(1)}, f32[72,256]{1,0:T(8,128)S(1)}, u32[]{:S(2)}, u32[]{:S(2)}) collective-permute-start(f32[72,256]{1,0:T(8,128)S(1)} %get-tuple-element.29), channel_id=1, source_target_pairs={{0,1},{1,2},{2,3},{3,0},{4,5},{5,6},{6,7},{7,4},{8,9},{9,10},{10,1... | collective-permute-start | bytes 221192 | tf_op jit(solution)/shard_map/ppermute | solution.py:27
  89.0 3.8 %collective-permute-start.5 = (f32[72,256]{1,0:T(8,128)S(1)}, f32[72,256]{1,0:T(8,128)S(1)}, u32[]{:S(2)}, u32[]{:S(2)}) collective-permute-start(f32[72,256]{1,0:T(8,128)S(1)} %get-tuple-element.30), channel_id=1, source_target_pairs={{0,3},{1,0},{2,1},{3,2},{4,7},{5,4},{6,5},{7,6},{8,11},{9,8},{10,9... | collective-permute-start | bytes 221192 | tf_op jit(solution)/shard_map/ppermute | solution.py:27
  93.8 1.3 %collective-permute-start.6 = (f32[72,128]{1,0:T(8,128)S(1)}, f32[72,128]{1,0:T(8,128)S(1)}, u32[]{:S(2)}, u32[]{:S(2)}) collective-permute-start(f32[72,128]{1,0:T(8,128)S(1)} %get-tuple-element.33), channel_id=1, source_target_pairs={{0,1},{1,2},{2,3},{3,0},{4,5},{5,6},{6,7},{7,4},{8,9},{9,10},{10,1... | collective-permute-start | bytes 110600 | tf_op jit(solution)/shard_map/ppermute | solution.py:27
  93.8 3.4 %collective-permute-start.7 = (f32[72,128]{1,0:T(8,128)S(1)}, f32[72,128]{1,0:T(8,128)S(1)}, u32[]{:S(2)}, u32[]{:S(2)}) collective-permute-start(f32[72,128]{1,0:T(8,128)S(1)} %get-tuple-element.34), channel_id=1, source_target_pairs={{0,3},{1,0},{2,1},{3,2},{4,7},{5,4},{6,5},{7,6},{8,11},{9,8},{10,9... | collective-permute-start | bytes 110600 | tf_op jit(solution)/shard_map/ppermute | solution.py:27

commit v12 on v11

--- a/solution.py
+++ b/solution.py
@@ -416,7 +416,9 @@
     return result
 
 
-def average_y(rows_of, below, above):
+def average_y(rows_of, far, near):
+    below = jnp.where(even_row(), far, near)
+    above = jnp.where(even_row(), near, far)
     result = list(rows_of)
     count = len(rows_of)
     for r in range(NODES - 1, count - 1, NODES):
@@ -428,9 +430,9 @@
 
 def first_stage_kernel(
     change_ref, before_ref, after_ref, edge_ref, average_ref,
-    out_ref, first_ref, last_ref, wind_side_ref, wide_ref,
+    out_ref, far_ref, near_ref, wind_side_ref, wide_ref,
 ):
-    level_count = first_ref.shape[0]
+    level_count = far_ref.shape[0]
     lanes = change_ref.shape[1]
     both = jnp.concatenate([after_ref[...], before_ref[...]], axis=1)
     sides = split_dot(both, edge_ref[...])
@@ -443,7 +445,7 @@
             for n in range(2):
                 here = 8 * (ROWS * (n + 1) + r)
                 wind_side_ref[n, span, :] = sides[here : here + 8, part]
-    write_averaged(wide_ref[...], average_ref, out_ref, first_ref, last_ref)
+    write_averaged(wide_ref[...], average_ref, out_ref, far_ref, near_ref)
 
 
 def change_rows(field_ref, slope_ref, wind_ref, part, spans):
@@ -455,25 +457,30 @@
     return result
 
 
-def write_averaged(change, average_ref, out_ref, first_ref, last_ref):
-    level_count = first_ref.shape[0]
+def even_row():
+    return lax.axis_index("gy") % 2 == 0
+
+
+def write_averaged(change, average_ref, out_ref, far_ref, near_ref):
+    level_count, width = far_ref.shape
     out_ref[...] = split_dot(change, average_ref[...])
-    width = first_ref.shape[1]
-    first_ref[...] = out_ref[:level_count, :width]
-    last_ref[...] = out_ref[out_ref.shape[0] - level_count :, :width]
+    first = out_ref[:level_count, :width]
+    last = out_ref[out_ref.shape[0] - level_count :, :width]
+    far_ref[...] = jnp.where(even_row(), first, last)
+    near_ref[...] = jnp.where(even_row(), last, first)
 
 
 def next_stage_kernel(
-    share, native, field_ref, below_ref, above_ref, wind_ref, wind_side_ref, sum_ref, high_ref,
-    low_ref, average_ref, out_ref, first_ref, last_ref, total_ref, wave_ref, slope_ref, change_ref,
+    share, native, field_ref, far_ref, near_ref, wind_ref, wind_side_ref, sum_ref, high_ref,
+    low_ref, average_ref, out_ref, far_out_ref, near_out_ref, total_ref, wave_ref, slope_ref, change_ref,
 ):
-    level_count = below_ref.shape[0]
+    level_count = far_ref.shape[0]
     lanes = sum_ref.shape[1]
     spans = [slice(r * level_count, (r + 1) * level_count) for r in range(ROWS)]
     for half in range(2):
         part = slice(half * lanes, (half + 1) * lanes)
         wave = average_y(
-            [field_ref[span, part] for span in spans], below_ref[:, part], above_ref[:, part]
+            [field_ref[span, part] for span in spans], far_ref[:, part], near_ref[:, part]
         )
         for r, (span, row) in enumerate(zip(spans, wave)):
             wave_ref[span, part] = row
@@ -485,15 +492,22 @@
         part = slice(half * lanes, (half + 1) * lanes)
         for span, change in zip(spans, change_rows(wave_ref, slope_ref, wind, part, spans)):
             change_ref[span, part] = change
-    write_averaged(change_ref[...], average_ref, out_ref, first_ref, last_ref)
-
-
-def last_kernel(share, field_ref, below_ref, above_ref, sum_ref, total_ref):
-    level_count, lanes = below_ref.shape
+    write_averaged(change_ref[...], average_ref, out_ref, far_out_ref, near_out_ref)
+
+
+def last_kernel(share, field_ref, far_ref, near_ref, sum_ref, total_ref):
+    level_count, lanes = far_ref.shape
     spans = [slice(r * level_count, (r + 1) * level_count) for r in range(ROWS)]
-    wave = average_y([field_ref[span, :lanes] for span in spans], below_ref[...], above_ref[...])
+    wave = average_y([field_ref[span, :lanes] for span in spans], far_ref[...], near_ref[...])
     for r, (span, row) in enumerate(zip(spans, wave)):
         total_ref[pl.ds(r, level_count, stride=ROWS), :] = sum_ref[span] + share * row
+
+
+def swapped(far, near):
+    count = lax.axis_size("gy")
+    far_pairs = [(i, (i - 1 if i % 2 == 0 else i + 1) % count) for i in range(count)]
+    near_pairs = [(i, i + 1 if i % 2 == 0 else i - 1) for i in range(count)]
+    return lax.ppermute(far, "gy", far_pairs), lax.ppermute(near, "gy", near_pairs)
 
 
 def local(
@@ -533,25 +547,25 @@
     )
     before, after = shifted(last, "gx", 1), shifted(first, "gx", -1)
     back = edge_matrix(level_count, lanes).T
-    wave, first, last, wind_side = call(
+    wave, far, near, wind_side = call(
         first_stage_kernel, "first_stage",
         (wide, line, line, jax.ShapeDtypeStruct((2, size, lanes), jnp.float32)), 1,
         change, before, after, back, average,
     )
-    below, above = shifted(last, "gy", 1), shifted(first, "gy", -1)
-    wave, first, last, total = call(
+    far, near = swapped(far, near)
+    wave, far, near, total = call(
         functools.partial(next_stage_kernel, 1.0, True), "second_stage",
-        (wide, line, line, field), 3, wave, below, above, wind, wind_side, temper, *slopes, average,
-    )
-    below, above = shifted(last, "gy", 1), shifted(first, "gy", -1)
-    wave, first, last, total = call(
+        (wide, line, line, field), 3, wave, far, near, wind, wind_side, temper, *slopes, average,
+    )
+    far, near = swapped(far, near)
+    wave, far, near, total = call(
         functools.partial(next_stage_kernel, 0.5, False), "third_stage",
-        (wide, short, short, field), 3, wave, below, above, wind, wind_side, total, *slopes, average,
-    )
-    below, above = shifted(last, "gy", 1), shifted(first, "gy", -1)
+        (wide, short, short, field), 3, wave, far, near, wind, wind_side, total, *slopes, average,
+    )
+    far, near = swapped(far, near)
     total = call(
         functools.partial(last_kernel, 1.0 / 6.0), "last_stage", field, 0,
-        wave, below, above, total,
+        wave, far, near, total,
     )
     return (heat.reshape(thermal_ratio.shape), total.reshape(thermal_ratio.shape))
 

time: 98.2 us -> 98.4 us (level)
    ppermute x8 -> x2, waiting for transfers between devices: 12.7 us -> 2.66 us  [shifted(): lax.ppermute(value, axis, [(i, (i + steps) % count) for i in range(count)])]
    ppermute x0 -> x6, waiting for transfers between devices: none -> 9.14 us  [the longest x3 9.13 us: swapped(): lax.ppermute(far, 'gy', far_pairs)]
    ppermute x0 -> x6, starting transfers between devices: none -> 5.06 us  [the longest x3 5.05 us: swapped(): lax.ppermute(far, 'gy', far_pairs)]
    ppermute x8 -> x2, starting transfers between devices: 9.6 us -> 5.22 us  [shifted(): lax.ppermute(value, axis, [(i, (i + steps) % count) for i in range(count)])]
  transfers between devices with their start and end apart: 8 -> 8, of which waited for: 7 -> 4; matrix products, arithmetic and copies ran while one was open for 0% -> 0% of each run, Pallas kernels for 0% -> 0%
where the time goes in v12:
time: 98.4 us; the launch traced here: 97.9 us
  Pallas kernels  74.1 us (75%)
  waiting for transfers between devices  11.8 us (12%)
  starting transfers between devices  10.3 us (10%)
  local copies, waits for them, and re-layouts  0.99 us (1%)
    pallas_call x1, Pallas kernels, radiation(): pl.pallas_call(radiation_kernel, out_shape=(field, field, wind, edge, edg...  70.8 us
    ppermute x3, waiting for transfers between devices, swapped(): lax.ppermute(far, 'gy', far_pairs)  9.13 us
    ppermute x2, starting transfers between devices, shifted(): lax.ppermute(value, axis, [(i, (i + steps) % count) for i in range(count)])  5.22 us
    ppermute x3, starting transfers between devices, swapped(): lax.ppermute(far, 'gy', far_pairs)  5.05 us
    pallas_call x4, Pallas kernels, call(): pl.pallas_call(kernel, out_shape=outs, in_specs=[whole] * len(values), ou...  3.3 us
    ppermute x2, waiting for transfers between devices, shifted(): lax.ppermute(value, axis, [(i, (i + steps) % count) for i in range(count)])  2.66 us
  transfers between devices with their start and end apart: 8, of which 4 were waited for; matrix products, arithmetic and copies ran while one was open for 0% of the time, Pallas kernels for 0%

profile of v12, /device:TPU:1, one launch (start us, length us, event | category | flops | bytes accessed | tf_op | source)
XLA Modules:
  0.0 97.9 jit_solution(9057924376651668062)
XLA Ops:
  0.6 0.0 copy-start.1
  0.6 0.0 copy-start.2
  0.7 0.0 copy-start.3
  0.7 0.0 copy-start.4
  0.7 0.0 copy-start.5
  0.7 70.8 %radiation.1 = (f32[576,128]{1,0:T(8,128)}, f32[576,128]{1,0:T(8,128)}, f32[2,576,128]{2,1,0:T(8,128)}, f32[192,128]{1,0:T(8,128)}, f32[192,128]{1,0:T(8,128)}) custom-call(f32[5,72,8,128]{3,2,1,0:T(8,128)} %state_ref.1, f32[576,128]{1,0:T(8,128)} %bitcast.5, f32[2,576,128]{2,1,0:T(8,128)} %bitcast.8, f32[8,128]{1,0:T(8,128)} %cosine_ref.1, ...), custom_call_target="tpu_custom_call" | custom-call | flops 82575360000 | bytes 2654208 | tf_op jit(solution)/shard_map/radiation/pallas_call | solution.py:341
  71.5 0.0 copy-start
  71.5 2.1 %collective-permute-start = (f32[192,128]{1,0:T(8,128)}, f32[192,128]{1,0:T(8,128)S(1)}, u32[]{:S(2)}, u32[]{:S(2)}) collective-permute-start(f32[192,128]{1,0:T(8,128)} %get-tuple-element.21), channel_id=1, source_target_pairs={{0,4},{4,8},{8,12},{12,16},{16,20},{20,24},{24,28},{28,0},{1,5},{5... | collective-permute-start | bytes 294920 | tf_op jit(solution)/shard_map/ppermute | solution.py:27
  73.6 3.1 %collective-permute-start.1 = (f32[192,128]{1,0:T(8,128)}, f32[192,128]{1,0:T(8,128)S(1)}, u32[]{:S(2)}, u32[]{:S(2)}) collective-permute-start(f32[192,128]{1,0:T(8,128)} %get-tuple-element.22), channel_id=1, source_target_pairs={{0,28},{4,0},{8,4},{12,8},{16,12},{20,16},{24,20},{28,24},{1,29},{... | collective-permute-start | bytes 294920 | tf_op jit(solution)/shard_map/ppermute | solution.py:27
  76.7 2.7 %collective-permute-done.before_ref = f32[192,128]{1,0:T(8,128)S(1)} collective-permute-done((f32[192,128]{1,0:T(8,128)}, f32[192,128]{1,0:T(8,128)S(1)}, u32[]{:S(2)}, u32[]{:S(2)}) %collective-permute-start) | collective-permute-done | bytes 98336 | tf_op jit(solution)/shard_map/ppermute | solution.py:27
  79.4 0.0 collective-permute-done.1.after_ref
  79.4 0.0 copy-done.1
  79.4 0.0 copy-done.2
  79.4 0.0 copy-start.6
  79.4 1.0 copy-done.6
  80.3 0.7 first_stage.1
  81.0 3.3 %collective-permute-start.2 = (f32[72,256]{1,0:T(8,128)S(1)}, f32[72,256]{1,0:T(8,128)S(1)}, u32[]{:S(2)}, u32[]{:S(2)}) collective-permute-start(f32[72,256]{1,0:T(8,128)S(1)} %get-tuple-element.24), channel_id=1, source_target_pairs={{0,3},{1,2},{2,1},{3,0},{4,7},{5,6},{6,5},{7,4},{8,11},{9,10},{10,... | collective-permute-start | bytes 221192 | tf_op jit(solution)/shard_map/ppermute | solution.py:510
  84.3 0.0 collective-permute-start.3
  84.3 3.0 %collective-permute-done.2.far_ref = f32[72,256]{1,0:T(8,128)S(1)} collective-permute-done((f32[72,256]{1,0:T(8,128)S(1)}, f32[72,256]{1,0:T(8,128)S(1)}, u32[]{:S(2)}, u32[]{:S(2)}) %collective-permute-start.2) | collective-permute-done | bytes 73760 | tf_op jit(solution)/shard_map/ppermute | solution.py:510
  87.3 0.0 collective-permute-done.3.near_ref
  87.3 0.0 copy-done.3
  87.3 0.0 copy-done.4
  87.3 0.0 copy-done.5
  87.3 0.0 copy-done
  87.3 0.9 second_stage.1
  88.3 0.8 collective-permute-start.4
  89.1 0.0 collective-permute-start.5
  89.1 3.5 %collective-permute-done.4.far_ref = f32[72,256]{1,0:T(8,128)S(1)} collective-permute-done((f32[72,256]{1,0:T(8,128)S(1)}, f32[72,256]{1,0:T(8,128)S(1)}, u32[]{:S(2)}, u32[]{:S(2)}) %collective-permute-start.4) | collective-permute-done | bytes 73760 | tf_op jit(solution)/shard_map/ppermute | solution.py:510
  92.6 0.0 collective-permute-done.5.near_ref
  92.6 0.9 third_stage.1
  93.5 0.9 collective-permute-start.6
  94.5 0.0 collective-permute-start.7
  94.5 2.6 %collective-permute-done.6.far_ref = f32[72,128]{1,0:T(8,128)S(1)} collective-permute-done((f32[72,128]{1,0:T(8,128)S(1)}, f32[72,128]{1,0:T(8,128)S(1)}, u32[]{:S(2)}, u32[]{:S(2)}) %collective-permute-start.6) | collective-permute-done | bytes 36896 | tf_op jit(solution)/shard_map/ppermute | solution.py:510
  97.1 0.0 collective-permute-done.7.near_ref
  97.1 0.8 last_stage.1
Async XLA Ops:
  0.6 78.7 %copy-start.1 = (bf16[256,256]{1,0:T(8,128)(2,1)S(1)}, bf16[256,256]{1,0:T(8,128)(2,1)}, u32[]{:S(2)}) copy-start(bf16[256,256]{1,0:T(8,128)(2,1)} %constant.10.clone.average_ref) | copy-start | bytes 393220
  0.6 78.7 %copy-start.2 = (bf16[256,1152]{1,0:T(8,128)(2,1)S(1)}, bf16[256,1152]{1,0:T(8,128)(2,1)}, u32[]{:S(2)}) copy-start(bf16[256,1152]{1,0:T(8,128)(2,1)} %constant.12.edge_ref) | copy-start | bytes 1769476
  0.7 86.7 %copy-start.3 = (bf16[256,256]{1,0:T(8,128)(2,1)S(1)}, bf16[256,256]{1,0:T(8,128)(2,1)}, u32[]{:S(2)}) copy-start(bf16[256,256]{1,0:T(8,128)(2,1)} %constant.9.clone.low_ref) | copy-start | bytes 393220
  0.7 86.6 %copy-start.4 = (bf16[256,256]{1,0:T(8,128)(2,1)S(1)}, bf16[256,256]{1,0:T(8,128)(2,1)}, u32[]{:S(2)}) copy-start(bf16[256,256]{1,0:T(8,128)(2,1)} %constant.8.clone.high_ref) | copy-start | bytes 393220
  0.7 86.6 %copy-start.5 = (f32[72,8,128]{2,1,0:T(8,128)S(1)}, f32[72,8,128]{2,1,0:T(8,128)}, u32[]{:S(2)}) copy-start(f32[72,8,128]{2,1,0:T(8,128)} %param.16) | copy-start | bytes 884740
  71.5 15.9 %copy-start = (f32[2,576,128]{2,1,0:T(8,128)S(1)}, f32[2,576,128]{2,1,0:T(8,128)}, u32[]{:S(2)}) copy-start(f32[2,576,128]{2,1,0:T(8,128)} %get-tuple-element.26.wind_ref) | copy-start | bytes 1769476
  71.5 7.9 %collective-permute-start = (f32[192,128]{1,0:T(8,128)}, f32[192,128]{1,0:T(8,128)S(1)}, u32[]{:S(2)}, u32[]{:S(2)}) collective-permute-start(f32[192,128]{1,0:T(8,128)} %get-tuple-element.21), channel_id=1, source_target_pairs={{0,4},{4,8},{8,12},{12,16},{16,20},{20,24},{24,28},{28,0},{1,5},{5... | collective-permute-start | bytes 294920 | tf_op jit(solution)/shard_map/ppermute | solution.py:27
  73.6 5.8 %collective-permute-start.1 = (f32[192,128]{1,0:T(8,128)}, f32[192,128]{1,0:T(8,128)S(1)}, u32[]{:S(2)}, u32[]{:S(2)}) collective-permute-start(f32[192,128]{1,0:T(8,128)} %get-tuple-element.22), channel_id=1, source_target_pairs={{0,28},{4,0},{8,4},{12,8},{16,12},{20,16},{24,20},{28,24},{1,29},{... | collective-permute-start | bytes 294920 | tf_op jit(solution)/shard_map/ppermute | solution.py:27
  79.4 1.0 copy-start.6
  81.0 6.3 %collective-permute-start.2 = (f32[72,256]{1,0:T(8,128)S(1)}, f32[72,256]{1,0:T(8,128)S(1)}, u32[]{:S(2)}, u32[]{:S(2)}) collective-permute-start(f32[72,256]{1,0:T(8,128)S(1)} %get-tuple-element.24), channel_id=1, source_target_pairs={{0,3},{1,2},{2,1},{3,0},{4,7},{5,6},{6,5},{7,4},{8,11},{9,10},{10,... | collective-permute-start | bytes 221192 | tf_op jit(solution)/shard_map/ppermute | solution.py:510
  84.3 3.0 %collective-permute-start.3 = (f32[72,256]{1,0:T(8,128)S(1)}, f32[72,256]{1,0:T(8,128)S(1)}, u32[]{:S(2)}, u32[]{:S(2)}) collective-permute-start(f32[72,256]{1,0:T(8,128)S(1)} %get-tuple-element.25), channel_id=1, source_target_pairs={{0,1},{1,0},{2,3},{3,2},{4,5},{5,4},{6,7},{7,6},{8,9},{9,8},{10,11... | collective-permute-start | bytes 221192 | tf_op jit(solution)/shard_map/ppermute | solution.py:510
  88.3 4.3 %collective-permute-start.4 = (f32[72,256]{1,0:T(8,128)S(1)}, f32[72,256]{1,0:T(8,128)S(1)}, u32[]{:S(2)}, u32[]{:S(2)}) collective-permute-start(f32[72,256]{1,0:T(8,128)S(1)} %get-tuple-element.29), channel_id=1, source_target_pairs={{0,3},{1,2},{2,1},{3,0},{4,7},{5,6},{6,5},{7,4},{8,11},{9,10},{10,... | collective-permute-start | bytes 221192 | tf_op jit(solution)/shard_map/ppermute | solution.py:510
  89.1 3.5 %collective-permute-start.5 = (f32[72,256]{1,0:T(8,128)S(1)}, f32[72,256]{1,0:T(8,128)S(1)}, u32[]{:S(2)}, u32[]{:S(2)}) collective-permute-start(f32[72,256]{1,0:T(8,128)S(1)} %get-tuple-element.30), channel_id=1, source_target_pairs={{0,1},{1,0},{2,3},{3,2},{4,5},{5,4},{6,7},{7,6},{8,9},{9,8},{10,11... | collective-permute-start | bytes 221192 | tf_op jit(solution)/shard_map/ppermute | solution.py:510
  93.5 3.5 %collective-permute-start.6 = (f32[72,128]{1,0:T(8,128)S(1)}, f32[72,128]{1,0:T(8,128)S(1)}, u32[]{:S(2)}, u32[]{:S(2)}) collective-permute-start(f32[72,128]{1,0:T(8,128)S(1)} %get-tuple-element.33), channel_id=1, source_target_pairs={{0,3},{1,2},{2,1},{3,0},{4,7},{5,6},{6,5},{7,4},{8,11},{9,10},{10,... | collective-permute-start | bytes 110600 | tf_op jit(solution)/shard_map/ppermute | solution.py:510
  94.5 2.6 %collective-permute-start.7 = (f32[72,128]{1,0:T(8,128)S(1)}, f32[72,128]{1,0:T(8,128)S(1)}, u32[]{:S(2)}, u32[]{:S(2)}) collective-permute-start(f32[72,128]{1,0:T(8,128)S(1)} %get-tuple-element.34), channel_id=1, source_target_pairs={{0,1},{1,0},{2,3},{3,2},{4,5},{5,4},{6,7},{7,6},{8,9},{9,8},{10,11... | collective-permute-start | bytes 110600 | tf_op jit(solution)/shard_map/ppermute | solution.py:510

commit v13 on v12

--- a/solution.py
+++ b/solution.py
@@ -11,6 +11,7 @@
 NODES = 4
 TIME_INCREMENT = 0.05
 ROWS = 8
+MARGIN = 8
 LOG2E = 1.4426950408889634
 
 GROUP = 8
@@ -432,11 +433,11 @@
     change_ref, before_ref, after_ref, edge_ref, average_ref,
     out_ref, far_ref, near_ref, wind_side_ref, wide_ref,
 ):
-    level_count = far_ref.shape[0]
     lanes = change_ref.shape[1]
+    level_count = change_ref.shape[0] // ROWS
+    wide_ref[:, :lanes] = change_ref[...]
     both = jnp.concatenate([after_ref[...], before_ref[...]], axis=1)
     sides = split_dot(both, edge_ref[...])
-    wide_ref[:, :lanes] = change_ref[...]
     for r in range(ROWS):
         for k in range(level_count // 8):
             span = slice(r * level_count + 8 * k, r * level_count + 8 * (k + 1))
@@ -445,7 +446,7 @@
             for n in range(2):
                 here = 8 * (ROWS * (n + 1) + r)
                 wind_side_ref[n, span, :] = sides[here : here + 8, part]
-    write_averaged(wide_ref[...], average_ref, out_ref, far_ref, near_ref)
+    write_averaged(wide_ref[...], average_ref, out_ref, far_ref, near_ref, level_count, True)
 
 
 def change_rows(field_ref, slope_ref, wind_ref, part, spans):
@@ -461,27 +462,61 @@
     return lax.axis_index("gy") % 2 == 0
 
 
-def write_averaged(change, average_ref, out_ref, far_ref, near_ref):
-    level_count, width = far_ref.shape
+def packed_side(side):
+    lanes = side.shape[1]
+    lane = lax.broadcasted_iota(jnp.int32, (8, lanes), 1)
+    fit = lanes // (2 * MARGIN)
+    tiles = []
+    for k in range(side.shape[0] // 8):
+        turned = pltpu.roll(side[8 * k : 8 * (k + 1)], (MARGIN + 2 * MARGIN * (k % fit)) % lanes, 1)
+        if k % fit == 0:
+            tiles.append(turned)
+        else:
+            tiles[-1] = jnp.where(lane // (2 * MARGIN) == k % fit, turned, tiles[-1])
+    return tiles
+
+
+def unpacked_side(tiles, level_count):
+    lanes = tiles.shape[1]
+    fit = lanes // (2 * MARGIN)
+    result = []
+    for k in range(level_count // 8):
+        tile = tiles[8 * (k // fit) : 8 * (k // fit + 1)]
+        result.append(pltpu.roll(tile, (lanes - MARGIN - 2 * MARGIN * (k % fit)) % lanes, 1))
+    return jnp.concatenate(result, axis=0)
+
+
+def write_averaged(change, average_ref, out_ref, far_ref, near_ref, level_count, with_side):
+    lanes = far_ref.shape[1]
     out_ref[...] = split_dot(change, average_ref[...])
-    first = out_ref[:level_count, :width]
-    last = out_ref[out_ref.shape[0] - level_count :, :width]
-    far_ref[...] = jnp.where(even_row(), first, last)
-    near_ref[...] = jnp.where(even_row(), last, first)
+    parts = [slice(0, lanes), slice(lanes, 2 * lanes)] if with_side else [slice(0, lanes)]
+    for n, part in enumerate(parts):
+        first = out_ref[:level_count, part]
+        last = out_ref[out_ref.shape[0] - level_count :, part]
+        far = jnp.where(even_row(), first, last)
+        near = jnp.where(even_row(), last, first)
+        for ref, line in ((far_ref, far), (near_ref, near)):
+            if n == 0:
+                ref[:level_count, :] = line
+                continue
+            for k, tile in enumerate(packed_side(line)):
+                ref[level_count + 8 * k : level_count + 8 * (k + 1), :] = tile
 
 
 def next_stage_kernel(
     share, native, field_ref, far_ref, near_ref, wind_ref, wind_side_ref, sum_ref, high_ref,
     low_ref, average_ref, out_ref, far_out_ref, near_out_ref, total_ref, wave_ref, slope_ref, change_ref,
 ):
-    level_count = far_ref.shape[0]
+    level_count = field_ref.shape[0] // ROWS
     lanes = sum_ref.shape[1]
     spans = [slice(r * level_count, (r + 1) * level_count) for r in range(ROWS)]
     for half in range(2):
         part = slice(half * lanes, (half + 1) * lanes)
-        wave = average_y(
-            [field_ref[span, part] for span in spans], far_ref[:, part], near_ref[:, part]
-        )
+        far, near = far_ref[:level_count, :], near_ref[:level_count, :]
+        if half:
+            far = unpacked_side(far_ref[level_count:, :], level_count)
+            near = unpacked_side(near_ref[level_count:, :], level_count)
+        wave = average_y([field_ref[span, part] for span in spans], far, near)
         for r, (span, row) in enumerate(zip(spans, wave)):
             wave_ref[span, part] = row
             if half == 0:
@@ -492,7 +527,9 @@
         part = slice(half * lanes, (half + 1) * lanes)
         for span, change in zip(spans, change_rows(wave_ref, slope_ref, wind, part, spans)):
             change_ref[span, part] = change
-    write_averaged(change_ref[...], average_ref, out_ref, far_out_ref, near_out_ref)
+    write_averaged(
+        change_ref[...], average_ref, out_ref, far_out_ref, near_out_ref, level_count, native
+    )
 
 
 def last_kernel(share, field_ref, far_ref, near_ref, sum_ref, total_ref):
@@ -526,7 +563,8 @@
     flow = flow_velocity.reshape(2, size, lanes)
     field = jax.ShapeDtypeStruct((size, lanes), jnp.float32)
     wide = jax.ShapeDtypeStruct((size, 2 * lanes), jnp.float32)
-    line = jax.ShapeDtypeStruct((level_count, 2 * lanes), jnp.float32)
+    extra = -(-(level_count // 8) * 2 * MARGIN // lanes) * 8
+    line = jax.ShapeDtypeStruct((level_count + extra, lanes), jnp.float32)
     short = jax.ShapeDtypeStruct((level_count, lanes), jnp.float32)
     wide_scratch = pltpu.VMEM(wide.shape, jnp.float32)
     whole = pl.BlockSpec(memory_space=pltpu.VMEM)

time: 98.4 us -> 97.3 us (0.989)
  waiting for transfers between devices: 11.8 us -> 10.3 us
    ppermute x3, waiting for transfers between devices: 9.13 us -> 7.59 us  [swapped(): lax.ppermute(far, 'gy', far_pairs)]
where the time goes in v13:
time: 97.3 us; the launch traced here: 96.8 us
  Pallas kernels  74.2 us (76%)
  starting transfers between devices  10.6 us (11%)
  waiting for transfers between devices  10.3 us (11%)
  local copies, waits for them, and re-layouts  0.99 us (1%)
    pallas_call x1, Pallas kernels, radiation(): pl.pallas_call(radiation_kernel, out_shape=(field, field, wind, edge, edg...  70.8 us
    ppermute x3, waiting for transfers between devices, swapped(): lax.ppermute(far, 'gy', far_pairs)  7.59 us
    ppermute x3, starting transfers between devices, swapped(): lax.ppermute(far, 'gy', far_pairs)  5.35 us
    ppermute x2, starting transfers between devices, shifted(): lax.ppermute(value, axis, [(i, (i + steps) % count) for i in range(count)])  5.22 us
    pallas_call x4, Pallas kernels, call(): pl.pallas_call(kernel, out_shape=outs, in_specs=[whole] * len(values), ou...  3.47 us
    ppermute x2, waiting for transfers between devices, shifted(): lax.ppermute(value, axis, [(i, (i + steps) % count) for i in range(count)])  2.66 us
  transfers between devices with their start and end apart: 8, of which 4 were waited for; matrix products, arithmetic and copies ran while one was open for 0% of the time, Pallas kernels for 0%

profile of v13, /device:TPU:1, one launch (start us, length us, event | category | flops | bytes accessed | tf_op | source)
XLA Modules:
  0.0 96.8 jit_solution(861057391803694567)
XLA Ops:
  0.6 0.0 copy-start.1
  0.6 0.0 copy-start.2
  0.7 0.0 copy-start.3
  0.7 0.0 copy-start.4
  0.7 0.0 copy-start.5
  0.7 70.8 %radiation.1 = (f32[576,128]{1,0:T(8,128)}, f32[576,128]{1,0:T(8,128)}, f32[2,576,128]{2,1,0:T(8,128)}, f32[192,128]{1,0:T(8,128)}, f32[192,128]{1,0:T(8,128)}) custom-call(f32[5,72,8,128]{3,2,1,0:T(8,128)} %state_ref.1, f32[576,128]{1,0:T(8,128)} %bitcast.5, f32[2,576,128]{2,1,0:T(8,128)} %bitcast.8, f32[8,128]{1,0:T(8,128)} %cosine_ref.1, ...), custom_call_target="tpu_custom_call" | custom-call | flops 82575360000 | bytes 2654208 | tf_op jit(solution)/shard_map/radiation/pallas_call | solution.py:342
  71.5 0.0 copy-start
  71.5 2.1 %collective-permute-start = (f32[192,128]{1,0:T(8,128)}, f32[192,128]{1,0:T(8,128)S(1)}, u32[]{:S(2)}, u32[]{:S(2)}) collective-permute-start(f32[192,128]{1,0:T(8,128)} %get-tuple-element.21), channel_id=1, source_target_pairs={{0,4},{4,8},{8,12},{12,16},{16,20},{20,24},{24,28},{28,0},{1,5},{5... | collective-permute-start | bytes 294920 | tf_op jit(solution)/shard_map/ppermute | solution.py:28
  73.6 3.1 %collective-permute-start.1 = (f32[192,128]{1,0:T(8,128)}, f32[192,128]{1,0:T(8,128)S(1)}, u32[]{:S(2)}, u32[]{:S(2)}) collective-permute-start(f32[192,128]{1,0:T(8,128)} %get-tuple-element.22), channel_id=1, source_target_pairs={{0,28},{4,0},{8,4},{12,8},{16,12},{20,16},{24,20},{28,24},{1,29},{... | collective-permute-start | bytes 294920 | tf_op jit(solution)/shard_map/ppermute | solution.py:28
  76.7 2.7 %collective-permute-done.before_ref = f32[192,128]{1,0:T(8,128)S(1)} collective-permute-done((f32[192,128]{1,0:T(8,128)}, f32[192,128]{1,0:T(8,128)S(1)}, u32[]{:S(2)}, u32[]{:S(2)}) %collective-permute-start) | collective-permute-done | bytes 98336 | tf_op jit(solution)/shard_map/ppermute | solution.py:28
  79.4 0.0 collective-permute-done.1.after_ref
  79.4 0.0 copy-done.1
  79.4 0.0 copy-done.2
  79.4 0.0 copy-start.6
  79.4 1.0 copy-done.6
  80.3 0.7 first_stage.1
  81.1 3.3 %collective-permute-start.2 = (f32[88,128]{1,0:T(8,128)S(1)}, f32[88,128]{1,0:T(8,128)S(1)}, u32[]{:S(2)}, u32[]{:S(2)}) collective-permute-start(f32[88,128]{1,0:T(8,128)S(1)} %get-tuple-element.24), channel_id=1, source_target_pairs={{0,3},{1,2},{2,1},{3,0},{4,7},{5,6},{6,5},{7,4},{8,11},{9,10},{10,... | collective-permute-start | bytes 135176 | tf_op jit(solution)/shard_map/ppermute | solution.py:547
  84.3 0.0 collective-permute-start.3
  84.3 2.4 %collective-permute-done.2.far_ref = f32[88,128]{1,0:T(8,128)S(1)} collective-permute-done((f32[88,128]{1,0:T(8,128)S(1)}, f32[88,128]{1,0:T(8,128)S(1)}, u32[]{:S(2)}, u32[]{:S(2)}) %collective-permute-start.2) | collective-permute-done | bytes 45088 | tf_op jit(solution)/shard_map/ppermute | solution.py:547
  86.7 0.0 collective-permute-done.3.near_ref
  86.8 0.0 copy-done.3
  86.8 0.0 copy-done.4
  86.8 0.0 copy-done.5
  86.8 0.0 copy-done
  86.8 1.0 %second_stage.1 = (f32[576,256]{1,0:T(8,128)S(1)}, f32[88,128]{1,0:T(8,128)S(1)}, f32[88,128]{1,0:T(8,128)S(1)}, f32[576,128]{1,0:T(8,128)S(1)}) custom-call(f32[576,256]{1,0:T(8,128)S(1)} %get-tuple-element.23.field_ref, f32[88,128]{1,0:T(8,128)S(1)} %collective-permute-done.2.far_ref, f32[88,128]{1,0:T(8,128)S(1)} %collective-permute-done.3.near_ref, ...), custom_call_target="tpu_custom_call" | custom-call | tf_op jit(solution)/shard_map/second_stage/pallas_call | solution.py:573
  87.8 1.1 %collective-permute-start.4 = (f32[88,128]{1,0:T(8,128)S(1)}, f32[88,128]{1,0:T(8,128)S(1)}, u32[]{:S(2)}, u32[]{:S(2)}) collective-permute-start(f32[88,128]{1,0:T(8,128)S(1)} %get-tuple-element.29), channel_id=1, source_target_pairs={{0,3},{1,2},{2,1},{3,0},{4,7},{5,6},{6,5},{7,4},{8,11},{9,10},{10,... | collective-permute-start | bytes 135176 | tf_op jit(solution)/shard_map/ppermute | solution.py:547
  88.9 0.0 collective-permute-start.5
  88.9 2.6 %collective-permute-done.4.far_ref = f32[88,128]{1,0:T(8,128)S(1)} collective-permute-done((f32[88,128]{1,0:T(8,128)S(1)}, f32[88,128]{1,0:T(8,128)S(1)}, u32[]{:S(2)}, u32[]{:S(2)}) %collective-permute-start.4) | collective-permute-done | bytes 45088 | tf_op jit(solution)/shard_map/ppermute | solution.py:547
  91.5 0.0 collective-permute-done.5.near_ref
  91.5 0.9 third_stage.1
  92.4 0.9 collective-permute-start.6
  93.4 0.0 collective-permute-start.7
  93.4 2.6 %collective-permute-done.6.far_ref = f32[72,128]{1,0:T(8,128)S(1)} collective-permute-done((f32[72,128]{1,0:T(8,128)S(1)}, f32[72,128]{1,0:T(8,128)S(1)}, u32[]{:S(2)}, u32[]{:S(2)}) %collective-permute-start.6) | collective-permute-done | bytes 36896 | tf_op jit(solution)/shard_map/ppermute | solution.py:547
  96.0 0.0 collective-permute-done.7.near_ref
  96.0 0.8 last_stage.1
Async XLA Ops:
  0.6 78.7 %copy-start.1 = (bf16[256,256]{1,0:T(8,128)(2,1)S(1)}, bf16[256,256]{1,0:T(8,128)(2,1)}, u32[]{:S(2)}) copy-start(bf16[256,256]{1,0:T(8,128)(2,1)} %constant.10.clone.average_ref) | copy-start | bytes 393220
  0.6 78.7 %copy-start.2 = (bf16[256,1152]{1,0:T(8,128)(2,1)S(1)}, bf16[256,1152]{1,0:T(8,128)(2,1)}, u32[]{:S(2)}) copy-start(bf16[256,1152]{1,0:T(8,128)(2,1)} %constant.12.edge_ref) | copy-start | bytes 1769476
  0.7 86.1 %copy-start.3 = (bf16[256,256]{1,0:T(8,128)(2,1)S(1)}, bf16[256,256]{1,0:T(8,128)(2,1)}, u32[]{:S(2)}) copy-start(bf16[256,256]{1,0:T(8,128)(2,1)} %constant.9.clone.low_ref) | copy-start | bytes 393220
  0.7 86.1 %copy-start.4 = (bf16[256,256]{1,0:T(8,128)(2,1)S(1)}, bf16[256,256]{1,0:T(8,128)(2,1)}, u32[]{:S(2)}) copy-start(bf16[256,256]{1,0:T(8,128)(2,1)} %constant.8.clone.high_ref) | copy-start | bytes 393220
  0.7 86.1 %copy-start.5 = (f32[72,8,128]{2,1,0:T(8,128)S(1)}, f32[72,8,128]{2,1,0:T(8,128)}, u32[]{:S(2)}) copy-start(f32[72,8,128]{2,1,0:T(8,128)} %param.16) | copy-start | bytes 884740
  71.5 15.3 %copy-start = (f32[2,576,128]{2,1,0:T(8,128)S(1)}, f32[2,576,128]{2,1,0:T(8,128)}, u32[]{:S(2)}) copy-start(f32[2,576,128]{2,1,0:T(8,128)} %get-tuple-element.26.wind_ref) | copy-start | bytes 1769476
  71.5 7.9 %collective-permute-start = (f32[192,128]{1,0:T(8,128)}, f32[192,128]{1,0:T(8,128)S(1)}, u32[]{:S(2)}, u32[]{:S(2)}) collective-permute-start(f32[192,128]{1,0:T(8,128)} %get-tuple-element.21), channel_id=1, source_target_pairs={{0,4},{4,8},{8,12},{12,16},{16,20},{20,24},{24,28},{28,0},{1,5},{5... | collective-permute-start | bytes 294920 | tf_op jit(solution)/shard_map/ppermute | solution.py:28
  73.6 5.8 %collective-permute-start.1 = (f32[192,128]{1,0:T(8,128)}, f32[192,128]{1,0:T(8,128)S(1)}, u32[]{:S(2)}, u32[]{:S(2)}) collective-permute-start(f32[192,128]{1,0:T(8,128)} %get-tuple-element.22), channel_id=1, source_target_pairs={{0,28},{4,0},{8,4},{12,8},{16,12},{20,16},{24,20},{28,24},{1,29},{... | collective-permute-start | bytes 294920 | tf_op jit(solution)/shard_map/ppermute | solution.py:28
  79.4 1.0 copy-start.6
  81.1 5.7 %collective-permute-start.2 = (f32[88,128]{1,0:T(8,128)S(1)}, f32[88,128]{1,0:T(8,128)S(1)}, u32[]{:S(2)}, u32[]{:S(2)}) collective-permute-start(f32[88,128]{1,0:T(8,128)S(1)} %get-tuple-element.24), channel_id=1, source_target_pairs={{0,3},{1,2},{2,1},{3,0},{4,7},{5,6},{6,5},{7,4},{8,11},{9,10},{10,... | collective-permute-start | bytes 135176 | tf_op jit(solution)/shard_map/ppermute | solution.py:547
  84.3 2.4 %collective-permute-start.3 = (f32[88,128]{1,0:T(8,128)S(1)}, f32[88,128]{1,0:T(8,128)S(1)}, u32[]{:S(2)}, u32[]{:S(2)}) collective-permute-start(f32[88,128]{1,0:T(8,128)S(1)} %get-tuple-element.25), channel_id=1, source_target_pairs={{0,1},{1,0},{2,3},{3,2},{4,5},{5,4},{6,7},{7,6},{8,9},{9,8},{10,11... | collective-permute-start | bytes 135176 | tf_op jit(solution)/shard_map/ppermute | solution.py:547
  87.8 3.7 %collective-permute-start.4 = (f32[88,128]{1,0:T(8,128)S(1)}, f32[88,128]{1,0:T(8,128)S(1)}, u32[]{:S(2)}, u32[]{:S(2)}) collective-permute-start(f32[88,128]{1,0:T(8,128)S(1)} %get-tuple-element.29), channel_id=1, source_target_pairs={{0,3},{1,2},{2,1},{3,0},{4,7},{5,6},{6,5},{7,4},{8,11},{9,10},{10,... | collective-permute-start | bytes 135176 | tf_op jit(solution)/shard_map/ppermute | solution.py:547
  88.9 2.6 %collective-permute-start.5 = (f32[88,128]{1,0:T(8,128)S(1)}, f32[88,128]{1,0:T(8,128)S(1)}, u32[]{:S(2)}, u32[]{:S(2)}) collective-permute-start(f32[88,128]{1,0:T(8,128)S(1)} %get-tuple-element.30), channel_id=1, source_target_pairs={{0,1},{1,0},{2,3},{3,2},{4,5},{5,4},{6,7},{7,6},{8,9},{9,8},{10,11... | collective-permute-start | bytes 135176 | tf_op jit(solution)/shard_map/ppermute | solution.py:547
  92.4 3.5 %collective-permute-start.6 = (f32[72,128]{1,0:T(8,128)S(1)}, f32[72,128]{1,0:T(8,128)S(1)}, u32[]{:S(2)}, u32[]{:S(2)}) collective-permute-start(f32[72,128]{1,0:T(8,128)S(1)} %get-tuple-element.33), channel_id=1, source_target_pairs={{0,3},{1,2},{2,1},{3,0},{4,7},{5,6},{6,5},{7,4},{8,11},{9,10},{10,... | collective-permute-start | bytes 110600 | tf_op jit(solution)/shard_map/ppermute | solution.py:547
  93.4 2.6 %collective-permute-start.7 = (f32[72,128]{1,0:T(8,128)S(1)}, f32[72,128]{1,0:T(8,128)S(1)}, u32[]{:S(2)}, u32[]{:S(2)}) collective-permute-start(f32[72,128]{1,0:T(8,128)S(1)} %get-tuple-element.34), channel_id=1, source_target_pairs={{0,1},{1,0},{2,3},{3,2},{4,5},{5,4},{6,7},{7,6},{8,9},{9,8},{10,11... | collective-permute-start | bytes 110600 | tf_op jit(solution)/shard_map/ppermute | solution.py:547

commit v14 on v13

--- a/solution.py
+++ b/solution.py
@@ -312,8 +312,15 @@
                     start = r * level_count + 8 * k
                     strip_ref[here, lanes * k : lanes * (k + 1)] = ref[start : start + 8, :]
         packed = split_dot(strip_ref[...], edge_ref[...])
-        first_ref[...] = packed[:, :lanes]
-        last_ref[...] = packed[:, lanes:]
+        size = 8 * lines
+        used = (MARGIN + 1) * (level_count // 8)
+        lane = lax.broadcasted_iota(jnp.int32, (size, lanes), 1)
+        for ref, part in ((first_ref, slice(0, lanes)), (last_ref, slice(lanes, 2 * lanes))):
+            one, two, three = [packed[size * n : size * (n + 1), part] for n in range(3)]
+            turned = pltpu.roll(two, used, 1)
+            ref[:size, :] = jnp.where(lane >= used, turned, one)
+            rest = 2 * used - lanes
+            ref[size:, :] = jnp.where(lane < rest, turned, pltpu.roll(three, rest, 1))
 
 
 def prepare_terms(state_ref, temp_ref, terms_ref, right_ref):
@@ -337,7 +344,7 @@
     depths = pltpu.VMEM((BLOCK // 2, part[0], 2 * lanes), jnp.float32)
     field = jax.ShapeDtypeStruct((level_count * rows, lanes), jnp.float32)
     wind = jax.ShapeDtypeStruct((2, level_count * rows, lanes), jnp.float32)
-    edge = jax.ShapeDtypeStruct((3 * 8 * rows, lanes), jnp.float32)
+    edge = jax.ShapeDtypeStruct((2 * 8 * rows, lanes), jnp.float32)
     cells = level_count * gpoints * rows * lanes
     return pl.pallas_call(
         radiation_kernel,
@@ -368,7 +375,7 @@
 
 def edge_matrix(level_count, lanes):
     parts = level_count // 8
-    width = lanes // parts
+    width = MARGIN + 1
     matrix = np.zeros((parts * lanes, 2 * lanes), np.float32)
     for k in range(parts):
         for c in range(width):
@@ -436,8 +443,16 @@
     lanes = change_ref.shape[1]
     level_count = change_ref.shape[0] // ROWS
     wide_ref[:, :lanes] = change_ref[...]
-    both = jnp.concatenate([after_ref[...], before_ref[...]], axis=1)
-    sides = split_dot(both, edge_ref[...])
+    size = 8 * ROWS
+    used = (MARGIN + 1) * (level_count // 8)
+    lane = lax.broadcasted_iota(jnp.int32, (size, lanes), 1)
+    fields = []
+    for ref in (after_ref, before_ref):
+        one, two = ref[:size, :], ref[size:, :]
+        middle = pltpu.roll(jnp.where(lane >= used, one, two), lanes - used, 1)
+        last = pltpu.roll(two, 2 * (lanes - used), 1)
+        fields.append(jnp.concatenate([one, middle, last], axis=0))
+    sides = split_dot(jnp.concatenate(fields, axis=1), edge_ref[...])
     for r in range(ROWS):
         for k in range(level_count // 8):
             span = slice(r * level_count + 8 * k, r * level_count + 8 * (k + 1))

time: 97.3 us -> 96.3 us (0.990)
  no operation moved by 1% of the time
where the time goes in v14:
time: 96.3 us; the launch traced here: 95.8 us
  Pallas kernels  74.3 us (77%)
  starting transfers between devices  10.3 us (11%)
  waiting for transfers between devices  9.52 us (10%)
  local copies, waits for them, and re-layouts  0.99 us (1%)
    pallas_call x1, Pallas kernels, radiation(): pl.pallas_call(radiation_kernel, out_shape=(field, field, wind, edge, edg...  70.8 us
    ppermute x3, waiting for transfers between devices, swapped(): lax.ppermute(far, 'gy', far_pairs)  7.61 us
    ppermute x2, starting transfers between devices, shifted(): lax.ppermute(value, axis, [(i, (i + steps) % count) for i in range(count)])  5.22 us
    ppermute x3, starting transfers between devices, swapped(): lax.ppermute(far, 'gy', far_pairs)  5.04 us
    pallas_call x4, Pallas kernels, call(): pl.pallas_call(kernel, out_shape=outs, in_specs=[whole] * len(values), ou...  3.48 us
  transfers between devices with their start and end apart: 8, of which 4 were waited for; matrix products, arithmetic and copies ran while one was open for 0% of the time, Pallas kernels for 0%

profile of v14, /device:TPU:1, one launch (start us, length us, event | category | flops | bytes accessed | tf_op | source)
XLA Modules:
  0.0 95.8 jit_solution(12933815709661042800)
XLA Ops:
  0.6 0.0 copy-start.1
  0.6 0.0 copy-start.2
  0.7 0.0 copy-start.3
  0.7 0.0 copy-start.4
  0.7 0.0 copy-start.5
  0.7 70.8 %radiation.1 = (f32[576,128]{1,0:T(8,128)}, f32[576,128]{1,0:T(8,128)}, f32[2,576,128]{2,1,0:T(8,128)}, f32[128,128]{1,0:T(8,128)}, f32[128,128]{1,0:T(8,128)}) custom-call(f32[5,72,8,128]{3,2,1,0:T(8,128)} %state_ref.1, f32[576,128]{1,0:T(8,128)} %bitcast.5, f32[2,576,128]{2,1,0:T(8,128)} %bitcast.8, f32[8,128]{1,0:T(8,128)} %cosine_ref.1, ...), custom_call_target="tpu_custom_call" | custom-call | flops 82575360000 | bytes 2654208 | tf_op jit(solution)/shard_map/radiation/pallas_call | solution.py:349
  71.5 0.0 copy-start
  71.5 2.1 %collective-permute-start = (f32[128,128]{1,0:T(8,128)}, f32[128,128]{1,0:T(8,128)S(1)}, u32[]{:S(2)}, u32[]{:S(2)}) collective-permute-start(f32[128,128]{1,0:T(8,128)} %get-tuple-element.21), channel_id=1, source_target_pairs={{0,4},{4,8},{8,12},{12,16},{16,20},{20,24},{24,28},{28,0},{1,5},{5... | collective-permute-start | bytes 196616 | tf_op jit(solution)/shard_map/ppermute | solution.py:28
  73.6 3.1 %collective-permute-start.1 = (f32[128,128]{1,0:T(8,128)}, f32[128,128]{1,0:T(8,128)S(1)}, u32[]{:S(2)}, u32[]{:S(2)}) collective-permute-start(f32[128,128]{1,0:T(8,128)} %get-tuple-element.22), channel_id=1, source_target_pairs={{0,28},{4,0},{8,4},{12,8},{16,12},{20,16},{24,20},{28,24},{1,29},{... | collective-permute-start | bytes 196616 | tf_op jit(solution)/shard_map/ppermute | solution.py:28
  76.7 1.9 %collective-permute-done.before_ref = f32[128,128]{1,0:T(8,128)S(1)} collective-permute-done((f32[128,128]{1,0:T(8,128)}, f32[128,128]{1,0:T(8,128)S(1)}, u32[]{:S(2)}, u32[]{:S(2)}) %collective-permute-start) | collective-permute-done | bytes 65568 | tf_op jit(solution)/shard_map/ppermute | solution.py:28
  78.7 0.0 collective-permute-done.1.after_ref
  78.7 0.0 copy-done.1
  78.7 0.0 copy-done.2
  78.7 0.0 copy-start.6
  78.7 1.0 copy-done.6
  79.6 0.8 first_stage.1
  80.4 3.0 %collective-permute-start.2 = (f32[88,128]{1,0:T(8,128)S(1)}, f32[88,128]{1,0:T(8,128)S(1)}, u32[]{:S(2)}, u32[]{:S(2)}) collective-permute-start(f32[88,128]{1,0:T(8,128)S(1)} %get-tuple-element.24), channel_id=1, source_target_pairs={{0,3},{1,2},{2,1},{3,0},{4,7},{5,6},{6,5},{7,4},{8,11},{9,10},{10,... | collective-permute-start | bytes 135176 | tf_op jit(solution)/shard_map/ppermute | solution.py:562
  83.4 0.0 collective-permute-start.3
  83.4 2.4 %collective-permute-done.2.far_ref = f32[88,128]{1,0:T(8,128)S(1)} collective-permute-done((f32[88,128]{1,0:T(8,128)S(1)}, f32[88,128]{1,0:T(8,128)S(1)}, u32[]{:S(2)}, u32[]{:S(2)}) %collective-permute-start.2) | collective-permute-done | bytes 45088 | tf_op jit(solution)/shard_map/ppermute | solution.py:562
  85.8 0.0 collective-permute-done.3.near_ref
  85.8 0.0 copy-done.3
  85.8 0.0 copy-done.4
  85.8 0.0 copy-done.5
  85.8 0.0 copy-done
  85.8 1.0 %second_stage.1 = (f32[576,256]{1,0:T(8,128)S(1)}, f32[88,128]{1,0:T(8,128)S(1)}, f32[88,128]{1,0:T(8,128)S(1)}, f32[576,128]{1,0:T(8,128)S(1)}) custom-call(f32[576,256]{1,0:T(8,128)S(1)} %get-tuple-element.23.field_ref, f32[88,128]{1,0:T(8,128)S(1)} %collective-permute-done.2.far_ref, f32[88,128]{1,0:T(8,128)S(1)} %collective-permute-done.3.near_ref, ...), custom_call_target="tpu_custom_call" | custom-call | tf_op jit(solution)/shard_map/second_stage/pallas_call | solution.py:588
  86.8 1.1 %collective-permute-start.4 = (f32[88,128]{1,0:T(8,128)S(1)}, f32[88,128]{1,0:T(8,128)S(1)}, u32[]{:S(2)}, u32[]{:S(2)}) collective-permute-start(f32[88,128]{1,0:T(8,128)S(1)} %get-tuple-element.29), channel_id=1, source_target_pairs={{0,3},{1,2},{2,1},{3,0},{4,7},{5,6},{6,5},{7,4},{8,11},{9,10},{10,... | collective-permute-start | bytes 135176 | tf_op jit(solution)/shard_map/ppermute | solution.py:562
  88.0 0.0 collective-permute-start.5
  88.0 2.6 %collective-permute-done.4.far_ref = f32[88,128]{1,0:T(8,128)S(1)} collective-permute-done((f32[88,128]{1,0:T(8,128)S(1)}, f32[88,128]{1,0:T(8,128)S(1)}, u32[]{:S(2)}, u32[]{:S(2)}) %collective-permute-start.4) | collective-permute-done | bytes 45088 | tf_op jit(solution)/shard_map/ppermute | solution.py:562
  90.6 0.0 collective-permute-done.5.near_ref
  90.6 0.9 third_stage.1
  91.5 0.9 collective-permute-start.6
  92.4 0.0 collective-permute-start.7
  92.4 2.6 %collective-permute-done.6.far_ref = f32[72,128]{1,0:T(8,128)S(1)} collective-permute-done((f32[72,128]{1,0:T(8,128)S(1)}, f32[72,128]{1,0:T(8,128)S(1)}, u32[]{:S(2)}, u32[]{:S(2)}) %collective-permute-start.6) | collective-permute-done | bytes 36896 | tf_op jit(solution)/shard_map/ppermute | solution.py:562
  95.0 0.0 collective-permute-done.7.near_ref
  95.0 0.8 last_stage.1
Async XLA Ops:
  0.6 78.0 %copy-start.1 = (bf16[256,256]{1,0:T(8,128)(2,1)S(1)}, bf16[256,256]{1,0:T(8,128)(2,1)}, u32[]{:S(2)}) copy-start(bf16[256,256]{1,0:T(8,128)(2,1)} %constant.10.clone.average_ref) | copy-start | bytes 393220
  0.6 78.0 %copy-start.2 = (bf16[256,1152]{1,0:T(8,128)(2,1)S(1)}, bf16[256,1152]{1,0:T(8,128)(2,1)}, u32[]{:S(2)}) copy-start(bf16[256,1152]{1,0:T(8,128)(2,1)} %constant.12.edge_ref) | copy-start | bytes 1769476
  0.7 85.2 %copy-start.3 = (bf16[256,256]{1,0:T(8,128)(2,1)S(1)}, bf16[256,256]{1,0:T(8,128)(2,1)}, u32[]{:S(2)}) copy-start(bf16[256,256]{1,0:T(8,128)(2,1)} %constant.9.clone.low_ref) | copy-start | bytes 393220
  0.7 85.1 %copy-start.4 = (bf16[256,256]{1,0:T(8,128)(2,1)S(1)}, bf16[256,256]{1,0:T(8,128)(2,1)}, u32[]{:S(2)}) copy-start(bf16[256,256]{1,0:T(8,128)(2,1)} %constant.8.clone.high_ref) | copy-start | bytes 393220
  0.7 85.1 %copy-start.5 = (f32[72,8,128]{2,1,0:T(8,128)S(1)}, f32[72,8,128]{2,1,0:T(8,128)}, u32[]{:S(2)}) copy-start(f32[72,8,128]{2,1,0:T(8,128)} %param.16) | copy-start | bytes 884740
  71.5 14.3 %copy-start = (f32[2,576,128]{2,1,0:T(8,128)S(1)}, f32[2,576,128]{2,1,0:T(8,128)}, u32[]{:S(2)}) copy-start(f32[2,576,128]{2,1,0:T(8,128)} %get-tuple-element.26.wind_ref) | copy-start | bytes 1769476
  71.5 7.1 %collective-permute-start = (f32[128,128]{1,0:T(8,128)}, f32[128,128]{1,0:T(8,128)S(1)}, u32[]{:S(2)}, u32[]{:S(2)}) collective-permute-start(f32[128,128]{1,0:T(8,128)} %get-tuple-element.21), channel_id=1, source_target_pairs={{0,4},{4,8},{8,12},{12,16},{16,20},{20,24},{24,28},{28,0},{1,5},{5... | collective-permute-start | bytes 196616 | tf_op jit(solution)/shard_map/ppermute | solution.py:28
  73.6 5.0 %collective-permute-start.1 = (f32[128,128]{1,0:T(8,128)}, f32[128,128]{1,0:T(8,128)S(1)}, u32[]{:S(2)}, u32[]{:S(2)}) collective-permute-start(f32[128,128]{1,0:T(8,128)} %get-tuple-element.22), channel_id=1, source_target_pairs={{0,28},{4,0},{8,4},{12,8},{16,12},{20,16},{24,20},{28,24},{1,29},{... | collective-permute-start | bytes 196616 | tf_op jit(solution)/shard_map/ppermute | solution.py:28
  78.7 1.0 %copy-start.6 = (f32[576,128]{1,0:T(8,128)S(1)}, f32[576,128]{1,0:T(8,128)}, u32[]{:S(2)}) copy-start(f32[576,128]{1,0:T(8,128)} %get-tuple-element.20.change_ref) | copy-start | bytes 884740
  80.4 5.4 %collective-permute-start.2 = (f32[88,128]{1,0:T(8,128)S(1)}, f32[88,128]{1,0:T(8,128)S(1)}, u32[]{:S(2)}, u32[]{:S(2)}) collective-permute-start(f32[88,128]{1,0:T(8,128)S(1)} %get-tuple-element.24), channel_id=1, source_target_pairs={{0,3},{1,2},{2,1},{3,0},{4,7},{5,6},{6,5},{7,4},{8,11},{9,10},{10,... | collective-permute-start | bytes 135176 | tf_op jit(solution)/shard_map/ppermute | solution.py:562
  83.4 2.4 %collective-permute-start.3 = (f32[88,128]{1,0:T(8,128)S(1)}, f32[88,128]{1,0:T(8,128)S(1)}, u32[]{:S(2)}, u32[]{:S(2)}) collective-permute-start(f32[88,128]{1,0:T(8,128)S(1)} %get-tuple-element.25), channel_id=1, source_target_pairs={{0,1},{1,0},{2,3},{3,2},{4,5},{5,4},{6,7},{7,6},{8,9},{9,8},{10,11... | collective-permute-start | bytes 135176 | tf_op jit(solution)/shard_map/ppermute | solution.py:562
  86.8 3.7 %collective-permute-start.4 = (f32[88,128]{1,0:T(8,128)S(1)}, f32[88,128]{1,0:T(8,128)S(1)}, u32[]{:S(2)}, u32[]{:S(2)}) collective-permute-start(f32[88,128]{1,0:T(8,128)S(1)} %get-tuple-element.29), channel_id=1, source_target_pairs={{0,3},{1,2},{2,1},{3,0},{4,7},{5,6},{6,5},{7,4},{8,11},{9,10},{10,... | collective-permute-start | bytes 135176 | tf_op jit(solution)/shard_map/ppermute | solution.py:562
  88.0 2.6 %collective-permute-start.5 = (f32[88,128]{1,0:T(8,128)S(1)}, f32[88,128]{1,0:T(8,128)S(1)}, u32[]{:S(2)}, u32[]{:S(2)}) collective-permute-start(f32[88,128]{1,0:T(8,128)S(1)} %get-tuple-element.30), channel_id=1, source_target_pairs={{0,1},{1,0},{2,3},{3,2},{4,5},{5,4},{6,7},{7,6},{8,9},{9,8},{10,11... | collective-permute-start | bytes 135176 | tf_op jit(solution)/shard_map/ppermute | solution.py:562
  91.5 3.5 %collective-permute-start.6 = (f32[72,128]{1,0:T(8,128)S(1)}, f32[72,128]{1,0:T(8,128)S(1)}, u32[]{:S(2)}, u32[]{:S(2)}) collective-permute-start(f32[72,128]{1,0:T(8,128)S(1)} %get-tuple-element.33), channel_id=1, source_target_pairs={{0,3},{1,2},{2,1},{3,0},{4,7},{5,6},{6,5},{7,4},{8,11},{9,10},{10,... | collective-permute-start | bytes 110600 | tf_op jit(solution)/shard_map/ppermute | solution.py:562
  92.4 2.6 %collective-permute-start.7 = (f32[72,128]{1,0:T(8,128)S(1)}, f32[72,128]{1,0:T(8,128)S(1)}, u32[]{:S(2)}, u32[]{:S(2)}) collective-permute-start(f32[72,128]{1,0:T(8,128)S(1)} %get-tuple-element.34), channel_id=1, source_target_pairs={{0,1},{1,0},{2,3},{3,2},{4,5},{5,4},{6,7},{7,6},{8,9},{9,8},{10,11... | collective-permute-start | bytes 110600 | tf_op jit(solution)/shard_map/ppermute | solution.py:562

commit v15 on v14

--- a/solution.py
+++ b/solution.py
@@ -362,7 +362,7 @@
             plane, plane,
             pltpu.VMEM((8, lanes), jnp.float32),
         ],
-        compiler_params=pltpu.CompilerParams(vmem_limit_bytes=60 * 1024 * 1024),
+        compiler_params=pltpu.CompilerParams(vmem_limit_bytes=40 * 1024 * 1024),
         cost_estimate=pl.CostEstimate(
             flops=10000 * cells, bytes_accessed=4 * 9 * temper.size, transcendentals=5 * cells
         ),

time: 96.3 us -> 103 us (1.070)
  local copies, waits for them, and re-layouts: 0.99 us -> 9.93 us
  Pallas kernels: 74.3 us -> 72.1 us
    unnamed x14 -> x32, local copies, waits for them, and re-layouts: 0.99 us -> 9.93 us
    pallas_call x1, Pallas kernels: 70.8 us -> 68.6 us  [radiation(): pl.pallas_call(radiation_kernel, out_shape=(field, field, wind, edge, edg...]
where the time goes in v15:
time: 103 us; the launch traced here: 102 us
  Pallas kernels  72.1 us (70%)
  starting transfers between devices  10.2 us (10%)
  local copies, waits for them, and re-layouts  9.93 us (10%)
  waiting for transfers between devices  9.35 us (9%)
    pallas_call x1, Pallas kernels, radiation(): pl.pallas_call(radiation_kernel, out_shape=(field, field, wind, edge, edg...  68.6 us
    unnamed x32, local copies, waits for them, and re-layouts  9.93 us
    ppermute x3, waiting for transfers between devices, swapped(): lax.ppermute(far, 'gy', far_pairs)  7.58 us
    ppermute x2, starting transfers between devices, shifted(): lax.ppermute(value, axis, [(i, (i + steps) % count) for i in range(count)])  5.11 us
    ppermute x3, starting transfers between devices, swapped(): lax.ppermute(far, 'gy', far_pairs)  5.07 us
    pallas_call x4, Pallas kernels, call(): pl.pallas_call(kernel, out_shape=outs, in_specs=[whole] * len(values), ou...  3.56 us
  transfers between devices with their start and end apart: 8, of which 4 were waited for; matrix products, arithmetic and copies ran while one was open for 0% of the time, Pallas kernels for 0%

profile of v15, /device:TPU:1, one launch (start us, length us, event | category | flops | bytes accessed | tf_op | source)
XLA Modules:
  0.0 102.3 jit_solution(6129390976505176153)
XLA Ops:
  0.6 0.0 copy-start.2
  0.6 0.9 copy-done.2
  1.5 0.0 copy-start.4
  1.5 0.9 copy-done.4
  2.4 0.0 copy-start.6
  2.4 1.0 copy-done.6
  3.4 0.0 copy-start.8
  3.4 1.4 %copy-done.8 = f32[5,72,8,128]{3,2,1,0:T(8,128)S(1)} copy-done((f32[5,72,8,128]{3,2,1,0:T(8,128)S(1)}, f32[5,72,8,128]{3,2,1,0:T(8,128)}, u32[]{:S(2)}) %copy-start.8) | copy-done | bytes 1474584
  4.8 0.0 copy-start.9
  4.8 1.1 %copy-done.9 = f32[2,72,8,128]{3,2,1,0:T(8,128)S(1)} copy-done((f32[2,72,8,128]{3,2,1,0:T(8,128)S(1)}, f32[2,72,8,128]{3,2,1,0:T(8,128)}, u32[]{:S(2)}) %copy-start.9) | copy-done | bytes 589848
  5.8 0.0 copy-start.10
  5.8 0.9 copy-done.10
  6.7 0.0 copy-start.11
  6.7 0.7 copy-done.11
  7.4 0.0 copy-start.12
  7.4 0.7 copy-done.12
  8.1 0.0 copy-start.13
  8.1 0.7 copy-done.13
  8.8 0.0 copy-start.14
  8.8 0.7 copy-done.14
  9.5 0.0 copy-start.15
  9.5 1.1 %copy-done.15 = bf16[1152,256]{1,0:T(8,128)(2,1)S(1)} copy-done((bf16[1152,256]{1,0:T(8,128)(2,1)S(1)}, bf16[1152,256]{1,0:T(8,128)(2,1)}, u32[]{:S(2)}) %copy-start.15) | copy-done | bytes 589848
  10.6 0.0 copy-start
  10.6 0.0 copy-start.1
  10.6 0.0 copy-start.3
  10.6 0.0 copy-start.5
  10.6 0.0 copy-start.7
  10.6 68.6 %radiation.1 = (f32[576,128]{1,0:T(8,128)}, f32[576,128]{1,0:T(8,128)S(1)}, f32[2,576,128]{2,1,0:T(8,128)S(1)}, f32[128,128]{1,0:T(8,128)S(1)}, f32[128,128]{1,0:T(8,128)S(1)}) custom-call(f32[5,72,8,128]{3,2,1,0:T(8,128)S(1)} %copy-done.8, f32[576,128]{1,0:T(8,128)S(1)} %bitcast.5, f32[2,576,128]{2,1,0:T(8,128)S(1)} %bitcast.7, f32[8,128]{1,0:T(8,128)S(1)} %copy-done.11, ...), custom_call_target="tpu_custom_call" | custom-call | flops 82575360000 | bytes 2654208 | tf_op jit(solution)/shard_map/radiation/pallas_call | solution.py:349
  79.1 2.1 %collective-permute-start = (f32[128,128]{1,0:T(8,128)S(1)}, f32[128,128]{1,0:T(8,128)S(1)}, u32[]{:S(2)}, u32[]{:S(2)}) collective-permute-start(f32[128,128]{1,0:T(8,128)S(1)} %get-tuple-element.21), channel_id=1, source_target_pairs={{0,4},{4,8},{8,12},{12,16},{16,20},{20,24},{24,28},{28,0},{1,5},{5... | collective-permute-start | bytes 196616 | tf_op jit(solution)/shard_map/ppermute | solution.py:28
  81.2 3.0 %collective-permute-start.1 = (f32[128,128]{1,0:T(8,128)S(1)}, f32[128,128]{1,0:T(8,128)S(1)}, u32[]{:S(2)}, u32[]{:S(2)}) collective-permute-start(f32[128,128]{1,0:T(8,128)S(1)} %get-tuple-element.22), channel_id=1, source_target_pairs={{0,28},{4,0},{8,4},{12,8},{16,12},{20,16},{24,20},{28,24},{1,29},{... | collective-permute-start | bytes 196616 | tf_op jit(solution)/shard_map/ppermute | solution.py:28
  84.3 1.8 %collective-permute-done.before_ref = f32[128,128]{1,0:T(8,128)S(1)} collective-permute-done((f32[128,128]{1,0:T(8,128)S(1)}, f32[128,128]{1,0:T(8,128)S(1)}, u32[]{:S(2)}, u32[]{:S(2)}) %collective-permute-start) | collective-permute-done | bytes 65568 | tf_op jit(solution)/shard_map/ppermute | solution.py:28
  86.0 0.0 collective-permute-done.1.after_ref
  86.0 0.0 copy-done
  86.0 0.0 copy-done.1
  86.0 0.8 first_stage.1
  86.8 3.0 %collective-permute-start.2 = (f32[88,128]{1,0:T(8,128)S(1)}, f32[88,128]{1,0:T(8,128)S(1)}, u32[]{:S(2)}, u32[]{:S(2)}) collective-permute-start(f32[88,128]{1,0:T(8,128)S(1)} %get-tuple-element.24), channel_id=1, source_target_pairs={{0,3},{1,2},{2,1},{3,0},{4,7},{5,6},{6,5},{7,4},{8,11},{9,10},{10,... | collective-permute-start | bytes 135176 | tf_op jit(solution)/shard_map/ppermute | solution.py:562
  89.8 0.0 collective-permute-start.3
  89.8 2.4 %collective-permute-done.2.far_ref = f32[88,128]{1,0:T(8,128)S(1)} collective-permute-done((f32[88,128]{1,0:T(8,128)S(1)}, f32[88,128]{1,0:T(8,128)S(1)}, u32[]{:S(2)}, u32[]{:S(2)}) %collective-permute-start.2) | collective-permute-done | bytes 45088 | tf_op jit(solution)/shard_map/ppermute | solution.py:562
  92.2 0.0 collective-permute-done.3.near_ref
  92.2 0.0 copy-done.3
  92.2 0.0 copy-done.5
  92.2 0.0 copy-done.7
  92.2 1.0 second_stage.1
  93.2 1.1 %collective-permute-start.4 = (f32[88,128]{1,0:T(8,128)S(1)}, f32[88,128]{1,0:T(8,128)S(1)}, u32[]{:S(2)}, u32[]{:S(2)}) collective-permute-start(f32[88,128]{1,0:T(8,128)S(1)} %get-tuple-element.29), channel_id=1, source_target_pairs={{0,3},{1,2},{2,1},{3,0},{4,7},{5,6},{6,5},{7,4},{8,11},{9,10},{10,... | collective-permute-start | bytes 135176 | tf_op jit(solution)/shard_map/ppermute | solution.py:562
  94.4 0.0 collective-permute-start.5
  94.4 2.6 %collective-permute-done.4.far_ref = f32[88,128]{1,0:T(8,128)S(1)} collective-permute-done((f32[88,128]{1,0:T(8,128)S(1)}, f32[88,128]{1,0:T(8,128)S(1)}, u32[]{:S(2)}, u32[]{:S(2)}) %collective-permute-start.4) | collective-permute-done | bytes 45088 | tf_op jit(solution)/shard_map/ppermute | solution.py:562
  97.0 0.0 collective-permute-done.5.near_ref
  97.0 0.9 third_stage.1
  97.9 0.9 collective-permute-start.6
  98.9 0.0 collective-permute-start.7
  98.9 2.6 %collective-permute-done.6.far_ref = f32[72,128]{1,0:T(8,128)S(1)} collective-permute-done((f32[72,128]{1,0:T(8,128)S(1)}, f32[72,128]{1,0:T(8,128)S(1)}, u32[]{:S(2)}, u32[]{:S(2)}) %collective-permute-start.6) | collective-permute-done | bytes 36896 | tf_op jit(solution)/shard_map/ppermute | solution.py:562
  101.5 0.0 collective-permute-done.7.near_ref
  101.5 0.8 last_stage.1
Async XLA Ops:
  0.6 0.9 copy-start.2
  1.5 0.9 copy-start.4
  2.4 1.0 copy-start.6
  3.4 1.4 %copy-start.8 = (f32[5,72,8,128]{3,2,1,0:T(8,128)S(1)}, f32[5,72,8,128]{3,2,1,0:T(8,128)}, u32[]{:S(2)}) copy-start(f32[5,72,8,128]{3,2,1,0:T(8,128)} %state_ref.1) | copy-start | bytes 4423684
  4.8 1.1 %copy-start.9 = (f32[2,72,8,128]{3,2,1,0:T(8,128)S(1)}, f32[2,72,8,128]{3,2,1,0:T(8,128)}, u32[]{:S(2)}) copy-start(f32[2,72,8,128]{3,2,1,0:T(8,128)} %param.17) | copy-start | bytes 1769476
  5.8 0.9 copy-start.10
  6.7 0.7 copy-start.11
  7.4 0.7 copy-start.12
  8.1 0.7 copy-start.13
  8.8 0.7 copy-start.14
  9.5 1.1 %copy-start.15 = (bf16[1152,256]{1,0:T(8,128)(2,1)S(1)}, bf16[1152,256]{1,0:T(8,128)(2,1)}, u32[]{:S(2)}) copy-start(bf16[1152,256]{1,0:T(8,128)(2,1)} %constant.11.clone.edge_ref) | copy-start | bytes 1769476
  10.6 75.5 %copy-start = (bf16[256,256]{1,0:T(8,128)(2,1)S(1)}, bf16[256,256]{1,0:T(8,128)(2,1)}, u32[]{:S(2)}) copy-start(bf16[256,256]{1,0:T(8,128)(2,1)} %constant.10.clone.average_ref) | copy-start | bytes 393220
  10.6 75.5 %copy-start.1 = (bf16[256,1152]{1,0:T(8,128)(2,1)S(1)}, bf16[256,1152]{1,0:T(8,128)(2,1)}, u32[]{:S(2)}) copy-start(bf16[256,1152]{1,0:T(8,128)(2,1)} %constant.12.edge_ref) | copy-start | bytes 1769476
  10.6 81.6 %copy-start.3 = (bf16[256,256]{1,0:T(8,128)(2,1)S(1)}, bf16[256,256]{1,0:T(8,128)(2,1)}, u32[]{:S(2)}) copy-start(bf16[256,256]{1,0:T(8,128)(2,1)} %constant.9.clone.low_ref) | copy-start | bytes 393220
  10.6 81.6 %copy-start.5 = (bf16[256,256]{1,0:T(8,128)(2,1)S(1)}, bf16[256,256]{1,0:T(8,128)(2,1)}, u32[]{:S(2)}) copy-start(bf16[256,256]{1,0:T(8,128)(2,1)} %constant.8.clone.high_ref) | copy-start | bytes 393220
  10.6 81.6 %copy-start.7 = (f32[72,8,128]{2,1,0:T(8,128)S(1)}, f32[72,8,128]{2,1,0:T(8,128)}, u32[]{:S(2)}) copy-start(f32[72,8,128]{2,1,0:T(8,128)} %param.16) | copy-start | bytes 884740
  79.1 6.9 %collective-permute-start = (f32[128,128]{1,0:T(8,128)S(1)}, f32[128,128]{1,0:T(8,128)S(1)}, u32[]{:S(2)}, u32[]{:S(2)}) collective-permute-start(f32[128,128]{1,0:T(8,128)S(1)} %get-tuple-element.21), channel_id=1, source_target_pairs={{0,4},{4,8},{8,12},{12,16},{16,20},{20,24},{24,28},{28,0},{1,5},{5... | collective-permute-start | bytes 196616 | tf_op jit(solution)/shard_map/ppermute | solution.py:28
  81.2 4.8 %collective-permute-start.1 = (f32[128,128]{1,0:T(8,128)S(1)}, f32[128,128]{1,0:T(8,128)S(1)}, u32[]{:S(2)}, u32[]{:S(2)}) collective-permute-start(f32[128,128]{1,0:T(8,128)S(1)} %get-tuple-element.22), channel_id=1, source_target_pairs={{0,28},{4,0},{8,4},{12,8},{16,12},{20,16},{24,20},{28,24},{1,29},{... | collective-permute-start | bytes 196616 | tf_op jit(solution)/shard_map/ppermute | solution.py:28
  86.8 5.4 %collective-permute-start.2 = (f32[88,128]{1,0:T(8,128)S(1)}, f32[88,128]{1,0:T(8,128)S(1)}, u32[]{:S(2)}, u32[]{:S(2)}) collective-permute-start(f32[88,128]{1,0:T(8,128)S(1)} %get-tuple-element.24), channel_id=1, source_target_pairs={{0,3},{1,2},{2,1},{3,0},{4,7},{5,6},{6,5},{7,4},{8,11},{9,10},{10,... | collective-permute-start | bytes 135176 | tf_op jit(solution)/shard_map/ppermute | solution.py:562
  89.8 2.4 %collective-permute-start.3 = (f32[88,128]{1,0:T(8,128)S(1)}, f32[88,128]{1,0:T(8,128)S(1)}, u32[]{:S(2)}, u32[]{:S(2)}) collective-permute-start(f32[88,128]{1,0:T(8,128)S(1)} %get-tuple-element.25), channel_id=1, source_target_pairs={{0,1},{1,0},{2,3},{3,2},{4,5},{5,4},{6,7},{7,6},{8,9},{9,8},{10,11... | collective-permute-start | bytes 135176 | tf_op jit(solution)/shard_map/ppermute | solution.py:562
  93.2 3.7 %collective-permute-start.4 = (f32[88,128]{1,0:T(8,128)S(1)}, f32[88,128]{1,0:T(8,128)S(1)}, u32[]{:S(2)}, u32[]{:S(2)}) collective-permute-start(f32[88,128]{1,0:T(8,128)S(1)} %get-tuple-element.29), channel_id=1, source_target_pairs={{0,3},{1,2},{2,1},{3,0},{4,7},{5,6},{6,5},{7,4},{8,11},{9,10},{10,... | collective-permute-start | bytes 135176 | tf_op jit(solution)/shard_map/ppermute | solution.py:562
  94.4 2.6 %collective-permute-start.5 = (f32[88,128]{1,0:T(8,128)S(1)}, f32[88,128]{1,0:T(8,128)S(1)}, u32[]{:S(2)}, u32[]{:S(2)}) collective-permute-start(f32[88,128]{1,0:T(8,128)S(1)} %get-tuple-element.30), channel_id=1, source_target_pairs={{0,1},{1,0},{2,3},{3,2},{4,5},{5,4},{6,7},{7,6},{8,9},{9,8},{10,11... | collective-permute-start | bytes 135176 | tf_op jit(solution)/shard_map/ppermute | solution.py:562
  97.9 3.5 %collective-permute-start.6 = (f32[72,128]{1,0:T(8,128)S(1)}, f32[72,128]{1,0:T(8,128)S(1)}, u32[]{:S(2)}, u32[]{:S(2)}) collective-permute-start(f32[72,128]{1,0:T(8,128)S(1)} %get-tuple-element.33), channel_id=1, source_target_pairs={{0,3},{1,2},{2,1},{3,0},{4,7},{5,6},{6,5},{7,4},{8,11},{9,10},{10,... | collective-permute-start | bytes 110600 | tf_op jit(solution)/shard_map/ppermute | solution.py:562
  98.9 2.6 %collective-permute-start.7 = (f32[72,128]{1,0:T(8,128)S(1)}, f32[72,128]{1,0:T(8,128)S(1)}, u32[]{:S(2)}, u32[]{:S(2)}) collective-permute-start(f32[72,128]{1,0:T(8,128)S(1)} %get-tuple-element.34), channel_id=1, source_target_pairs={{0,1},{1,0},{2,3},{3,2},{4,5},{5,4},{6,7},{7,6},{8,9},{9,8},{10,11... | collective-permute-start | bytes 110600 | tf_op jit(solution)/shard_map/ppermute | solution.py:562
